TPU v7x, 32 devices: a whole 2x2x4 slice. The times are simulated.
32 devices in a mesh: leaf: 8 (over z, y), rows: 4 (over x, core).
Axes of the slice: x: 2, y: 2, z: 4, core: 2. Of those that a mesh axis runs over, the one named last changes fastest.
Arguments:
- mixing: bfloat16 [24, 1024, 1024], P('leaf'), may hold values from 0.04 to 2048
- emission: bfloat16 [24, 256, 1024], P('leaf'), may hold values from 0.099609375 to 10
- prior: float32 [1024], replicated, may hold values from 0.1 to 10
- parent: int32 [24], P('leaf'), may hold values from -1 to 23, as said below
- observed: int32 [24, 512], P('leaf', 'rows'), may hold values from 0 to 255
Outputs:
- pair_counts: bfloat16 [24, 1024, 1024], P('leaf', 'rows')
- emit_counts: bfloat16 [24, 256, 1024], P('leaf', None, 'rows')
Inputs may be any that keep to these rules, and one draw needn't show every extreme that they name: Nodes are numbered 3 to an index of leaf, in order. Every parent has a smaller number than its child. A node that is not the first of its index of leaf has its parent among the nodes of the same index. The first node of index d > 0 has as parent the first node of index d with its lowest set binary digit cleared. Node 0 is the root.
All inputs are finite; a program needn't handle non-finite values.
Results may differ from a plain program's by a relative error of at most 0.009.
Values may be sent and summed in bfloat16 or wider, within the bound.
No kernel may reach another device: no remote copies, remote signals or barrier semaphores. Data moves between devices by JAX's collectives and lax.ppermute only.
A program may use at most 128 MiB of HBM per device.

v0:
```python
import functools
import jax
import jax.numpy as jnp
from jax import lax
from jax.experimental import pallas as pl
from jax.experimental.pallas import tpu as pltpu
from jax.sharding import PartitionSpec as P

F32 = jnp.float32
BF16 = jnp.bfloat16
PAD = 16
CHUNKS = 2
WORK = 10*10**8
LIMIT = 24 * 2**20
VM = pl.BlockSpec(memory_space=pltpu.VMEM)
SM = pl.BlockSpec(memory_space=pltpu.SMEM)
ANY = pl.BlockSpec(memory_space=pl.ANY)


def run(body, name, ins, outs, scratch=(), specs=None, out_specs=None, same=None, after=(), work=1.0):
    count, idle = len(ins), len(ins) + len(after)
    return pl.pallas_call(
        lambda *refs: body(*refs[:count], *refs[idle:]),
        name=name,
        in_specs=(specs or [VM] * count) + [VM] * len(after),
        out_specs=out_specs or tuple(VM for _ in outs),
        out_shape=tuple(outs),
        input_output_aliases=same or {},
        scratch_shapes=list(scratch),
        compiler_params=pltpu.CompilerParams(vmem_limit_bytes=LIMIT),
        cost_estimate=pl.CostEstimate(flops=int(work * WORK), bytes_accessed=2**21, transcendentals=0),
    )(*ins, *after)


def scaled(raw):
    return (raw * (1.0 / jnp.mean(raw, axis=1, keepdims=True))).astype(BF16)


def upward(lam, weight):
    rows = lam.shape[0]
    stacked = jnp.concatenate([lam, jnp.ones((PAD, lam.shape[1]), BF16)], axis=0)
    both = lax.dot_general(stacked, weight, (((1,), (1,)), ((), ())), preferred_element_type=F32)
    return both[:rows], both[rows : rows + 1]


def downward(q_par, raw_msg, lam, weight):
    ratio = (q_par / raw_msg).astype(BF16)
    post = lam.astype(F32) * jnp.dot(ratio, weight, preferred_element_type=F32)
    return ratio, post.astype(BF16)


def one_hot(row, values):
    return (lax.broadcasted_iota(jnp.int32, (values, row.shape[1]), 0) == row).astype(F32).astype(BF16)


def local_slot(parent_ref, node, nodes):
    return jnp.clip(parent_ref[node] - lax.axis_index("leaf") * nodes, 0, node - 1)


def is_upper(level):
    return jnp.bitwise_and(lax.axis_index("leaf"), (2 << level) - 1) == 0


def is_lower(level):
    return jnp.bitwise_and(lax.axis_index("leaf"), (2 << level) - 1) == (1 << level)


def prep_body(nodes, parent_hbm, obs_hbm, emission_hbm, mixing_hbm, *refs):
    w_ref, lam_ref, msg_ref = refs[:3]
    u_refs = refs[3 : 3 + CHUNKS]
    prods, tables, obs, parent_ref, sems = refs[3 + CHUNKS :]
    copy_obs = pltpu.make_async_copy(obs_hbm, obs, sems.at[2, 0])
    copy_parent = pltpu.make_async_copy(parent_hbm, parent_ref, sems.at[2, 1])
    copies_w = [pltpu.make_async_copy(mixing_hbm.at[n], w_ref.at[n], sems.at[0, n]) for n in range(nodes)]
    copies_e = [pltpu.make_async_copy(emission_hbm.at[n], tables.at[n], sems.at[1, n]) for n in range(nodes)]
    copy_obs.start()
    copy_parent.start()
    for n in reversed(range(nodes)):
        copies_e[n].start()
        copies_w[n].start()
    values = tables.shape[1]
    rows = obs.shape[1]
    part = rows // CHUNKS
    for n in range(nodes - 1):
        prods[n] = jnp.ones(prods.shape[1:], F32)
    copy_obs.wait()
    index = lax.broadcasted_iota(jnp.int32, (PAD, rows), 0)
    listed = jnp.zeros((PAD, rows), jnp.int32)
    for n in range(nodes):
        listed = jnp.where(index == n, obs[n : n + 1, :], listed)
    base = (nodes - 1) * rows
    lam_ref[base : base + PAD, :] = jnp.zeros((PAD, lam_ref.shape[1]), BF16)
    lam_ref[base : base + PAD, :rows] = listed.astype(F32).astype(BF16)
    copy_parent.wait()
    for n in reversed(range(nodes)):
        copies_e[n].wait()
        hot = one_hot(obs[n : n + 1, :], values)
        table = tables[n]
        picked = lax.dot_general(hot, table, (((0,), (0,)), ((), ())), preferred_element_type=F32)
        total = jnp.dot(jnp.ones((PAD, values), BF16), table, preferred_element_type=F32)[:1]
        raw = (picked * (1.0 / total)).astype(BF16).astype(F32)
        if n < nodes - 1:
            raw = raw * prods[n]
        if n > 0:
            lam = scaled(raw)
            copies_w[n].wait()
            raw_msg, sums = upward(lam, w_ref[n])
            lam_ref[(n - 1) * rows : n * rows, :] = lam
            msg_ref[n - 1] = raw_msg
            slot = local_slot(parent_ref, n, nodes)
            prods[slot] = prods[slot] * (raw_msg * (1.0 / sums))
        else:
            for c in range(CHUNKS):
                u_refs[c][...] = raw[c * part : (c + 1) * part]
    copies_w[0].wait()


def send_up(level, raw_ref, w_ref, send_ref):
    @pl.when(is_lower(level))
    def _():
        raw_msg, sums = upward(scaled(raw_ref[...]), w_ref[0])
        send_ref[...] = (raw_msg * (1.0 / sums)).astype(BF16)


def first_body(u_ref, w_ref, send_ref):
    send_up(0, u_ref, w_ref, send_ref)


def lift_body(level, u_ref, recv_ref, w_ref, u_out, send_ref):
    @pl.when(is_upper(level))
    def _():
        u_out[...] = u_ref[...] * recv_ref[...].astype(F32)

    send_up(level + 1, u_out, w_ref, send_ref)


def root_body(level, u_ref, recv_ref, w_ref, prior_ref, *refs):
    lam_ref, msg_ref, ratio_ref, post_ref = refs[-5:-1] if len(refs) > 4 else refs
    lam = scaled(u_ref[...] * jnp.where(is_upper(level), recv_ref[...].astype(F32), 1.0))
    raw_msg, sums = upward(lam, w_ref[0])
    lam_ref[...] = lam
    msg_ref[...] = raw_msg
    if len(refs) > 4:
        for c, block in enumerate([item[...] for item in refs[:-5]] + [lam]):
            refs[-1][c * lam.shape[0] : (c + 1) * lam.shape[0], :] = block

    @pl.when(lax.axis_index("leaf") == 0)
    def _():
        prior = prior_ref[...]
        weighted = (prior / jnp.sum(prior)) * (raw_msg * (1.0 / sums))
        share = weighted / jnp.sum(weighted, axis=1, keepdims=True)
        ratio, post = downward(share, raw_msg, lam, w_ref[0])
        ratio_ref[...] = ratio
        post_ref[...] = post


def settle_body(level, recv_ref, lam_ref, msg_ref, w_ref, ratio_in, post_in, ratio_ref, post_ref):
    got = is_lower(level)

    @pl.when(got)
    def _():
        ratio, post = downward(recv_ref[...].astype(F32), msg_ref[...], lam_ref[...], w_ref[0])
        ratio_ref[...] = ratio
        post_ref[...] = post

    @pl.when(jnp.logical_not(got))
    def _():
        ratio_ref[...] = ratio_in[...]
        post_ref[...] = post_in[...]


def last_body(nodes, groups, chunk, parent_ref, recv_ref, lam_ref, msg_ref, w_ref, ratio_in, post_in, lams_ref, msgs_ref, *refs):
    packs, posts = refs[:groups], refs[groups]
    rows, part = msgs_ref.shape[1], lam_ref.shape[0]
    share = lam_ref.shape[1] // groups
    got = is_lower(0)

    @pl.when(got)
    def _():
        ratio, post = downward(recv_ref[...].astype(F32), msg_ref[...], lam_ref[...], w_ref[0])
        posts[nodes] = ratio
        posts[0] = post

    @pl.when(jnp.logical_not(got))
    def _():
        posts[nodes] = ratio_in[...]
        posts[0] = post_in[...]

    for n in range(1, nodes):
        q_par = posts[local_slot(parent_ref, n, nodes)].astype(F32)
        low = (n - 1) * rows + chunk * part
        raw_msg = msgs_ref[n - 1, chunk * part : (chunk + 1) * part, :]
        _, posts[n] = downward(q_par, raw_msg, lams_ref[low : low + part, :], w_ref[n])
    own = lax.axis_index("rows")
    for mask in range(groups):
        start = pl.multiple_of(jnp.bitwise_xor(own, mask) * share, share)
        packs[mask][...] = posts[:, :, pl.ds(start, share)]


def ready_body(nodes, groups, w_ref, *refs):
    lams, (raw_ref, hot_ref) = refs[:groups], refs[groups:]
    chunks, merged, share = raw_ref.shape[1:]
    part = merged // groups
    rows = part * chunks
    values = hot_ref.shape[2]
    base = (nodes - 1) * rows
    start = pl.multiple_of(lax.axis_index("rows") * share, share)
    for n in range(nodes):
        observed = [lam[base : base + PAD, :rows].astype(F32).astype(jnp.int32)[n : n + 1] for lam in lams]
        for c in range(chunks):
            row = jnp.concatenate([item[:, c * part : (c + 1) * part] for item in observed], axis=1)
            hot_ref[n, c] = one_hot(row, values)
        if n > 0:
            weight = w_ref[n, pl.ds(start, share), :]
            for c in range(chunks):
                low = (n - 1) * rows + c * part
                lam = jnp.concatenate([item[low : low + part, :] for item in lams], axis=0)
                raw_ref[n - 1, c] = lax.dot_general(lam, weight, (((1,), (1,)), ((), ())), preferred_element_type=F32)


def counts_body(nodes, groups, chunk, parent_ref, raw_ref, hot_ref, *refs):
    lams, tops, posts = refs[:groups], refs[groups : 2 * groups], refs[2 * groups : 3 * groups]
    refs = refs[3 * groups :]
    chunks = raw_ref.shape[1]
    part = raw_ref.shape[2] // groups
    rows = part * chunks
    before = refs[:2] if chunk > 0 else None
    refs = refs[2:] if chunk > 0 else refs
    final = chunk == chunks - 1
    copies = []
    if final:
        w_ref, homes, refs, sems = refs[0], refs[1:3], refs[3:5], refs[5]
        share = refs[0].shape[1]
        samples = rows * groups
        start = pl.multiple_of(lax.axis_index("rows") * share, share)
    for n in range(nodes):
        low = (n - 1) * rows + chunk * part if n > 0 else chunk * part
        lam = jnp.concatenate([item[low : low + part, :] for item in (lams if n > 0 else tops)], axis=0)
        if n == 0:
            ratio = jnp.concatenate([item[nodes] for item in posts], axis=0)
        else:
            slot = local_slot(parent_ref, n, nodes)
            q_par = jnp.concatenate([item[slot] for item in posts], axis=0)
            ratio = (q_par.astype(F32) / raw_ref[n - 1, chunk]).astype(BF16)
        flow = lax.dot_general(ratio, lam, (((0,), (0,)), ((), ())), preferred_element_type=F32)
        post = jnp.concatenate([item[n] for item in posts], axis=0)
        tally = jnp.dot(hot_ref[n, chunk], post, preferred_element_type=F32)
        if before is not None:
            flow += before[0][n]
            tally += before[1][n]
        if final:
            states, values = flow.shape[1], tally.shape[0]
            weight = w_ref[n, pl.ds(start, share), :].astype(F32)
            flow = weight * flow * (states * states / samples)
            tally = tally * (values * states / samples)
        for k, value in enumerate((flow, tally)):
            refs[k][n] = value.astype(refs[k].dtype)
            if final:
                copies.append(pltpu.make_async_copy(refs[k].at[n], homes[k].at[n], sems.at[k, n]))
                copies[-1].start()
    for copy in copies:
        copy.wait()


def swap(value, mask):
    return lax.ppermute(value, "rows", [(s, s ^ mask) for s in range(lax.axis_size("rows"))])


def gather(value):
    blocks = {0: value}
    for bit in reversed(range(lax.axis_size("rows").bit_length() - 1)):
        blocks.update({place | (1 << bit): swap(block, 1 << bit) for place, block in blocks.items()})
    return [blocks[place] for place in range(len(blocks))]


def per_device(mixing, emission, prior, parent, observed):
    nodes, states = mixing.shape[:2]
    rows = observed.shape[1]
    values = emission.shape[1]
    leaves = lax.axis_size("leaf")
    groups = lax.axis_size("rows")
    levels = leaves.bit_length() - 1
    share = states // groups
    part = rows // CHUNKS
    every = range(CHUNKS)
    half = functools.partial(pltpu.VMEM, (part, states))

    outs = run(
        functools.partial(prep_body, nodes),
        "prep",
        tuple(pltpu.with_memory_space_constraint(x, pltpu.HBM) for x in (parent, observed, emission, mixing)),
        (
            pltpu.VMEM(mixing.shape, BF16),
            pltpu.VMEM(((nodes - 1) * rows + PAD, states), BF16),
            pltpu.VMEM((nodes - 1, rows, states), F32),
        )
        + (half(F32),) * CHUNKS,
        (
            pltpu.VMEM((nodes - 1, rows, states), F32),
            pltpu.VMEM(emission.shape, BF16),
            pltpu.VMEM(observed.shape, jnp.int32),
            pltpu.SMEM(parent.shape, jnp.int32),
            pltpu.SemaphoreType.DMA((3, max(nodes, 2))),
        ),
        [ANY] * 4,
    )
    weights, lams, msgs = outs[:3]
    raw, send = list(outs[3:]), []
    for c in every:
        (block,) = run(first_body, "first", (raw[c], weights), (half(BF16),), after=[lams] if c > 0 else ())
        send.append(block)
        if c == 0:
            (lams,) = run(
                lambda *refs: None, "pass", (lams,), (pltpu.VMEM(lams.shape, BF16),), same={0: 0}, after=(block,)
            )

    def up_pairs(level):
        step = 1 << level
        return [(s, s - step) for s in range(leaves) if s % (2 * step) == step]

    def down_pairs(level):
        return [(b, a) for a, b in up_pairs(level)]

    for level in range(levels - 1):
        for c in every:
            recv = lax.ppermute(send[c], "leaf", up_pairs(level))
            raw[c], send[c] = run(
                functools.partial(lift_body, level),
                "lift",
                (raw[c], recv, weights),
                (half(F32), half(BF16)),
                same={0: 0},
                after=send[:c][-1:],
            )
        if level == 0:
            all_lams = gather(lams)
    top_lam, top_msg, ratio, post = ([None] * CHUNKS for _ in range(4))
    for c in every:
        recv = lax.ppermute(send[c], "leaf", up_pairs(levels - 1))
        final = c == CHUNKS - 1
        top_lam[c], top_msg[c], ratio[c], post[c], *merged = run(
            functools.partial(root_body, levels - 1),
            "root",
            (raw[c], recv, weights, prior.reshape(1, states)) + (tuple(top_lam[:c]) if final else ()),
            (half(BF16), half(F32), half(BF16), half(BF16)) + ((pltpu.VMEM((rows, states), BF16),) if final else ()),
        )
    all_tops = gather(merged[0])
    raw_own, hots = run(
        functools.partial(ready_body, nodes, groups),
        "ready",
        (weights, *all_lams),
        (
            pltpu.VMEM((nodes - 1, CHUNKS, groups * part, share), F32),
            pltpu.VMEM((nodes, CHUNKS, values, groups * part), BF16),
        ),

    )
    for level in reversed(range(1, levels)):
        for c in every:
            recv = lax.ppermute(post[c], "leaf", down_pairs(level))
            ratio[c], post[c] = run(
                functools.partial(settle_body, level),
                "settle",
                (recv, top_lam[c], top_msg[c], weights, ratio[c], post[c]),
                (half(BF16), half(BF16)),
                after=post[:c][-1:] if c != 1 or level > 1 else (raw_own, *post[:c][-1:]),
            )
    own_posts = []
    for c in every:
        recv = lax.ppermute(post[c], "leaf", down_pairs(0))
        packs = run(
            functools.partial(last_body, nodes, groups, c),
            "last",
            (parent, recv, top_lam[c], top_msg[c], weights, ratio[c], post[c], lams, msgs),
            (pltpu.VMEM((nodes + 1, part, share), BF16),) * groups,
            (pltpu.VMEM((nodes + 1, part, states), BF16),),
            [SM] + [VM] * 8,
            after=own_posts[-1][:1] if c > 0 else tuple(all_tops),
        )
        order = sorted(range(1, groups), reverse=True)
        moved = {mask: swap(packs[mask], mask) for mask in order}
        own_posts.append([packs[0]] + [moved[mask] for mask in range(1, groups)])
    sums = ()
    for c in every:
        final = c == CHUNKS - 1
        ins = (parent, raw_own, hots, *all_lams, *all_tops, *own_posts[c], *sums) + ((weights,) if final else ())
        shapes = ((nodes, share, states), (nodes, values, share))
        sums = run(
            functools.partial(counts_body, nodes, groups, c),
            "counts",
            ins,
            tuple(jax.ShapeDtypeStruct(x, BF16) if final else pltpu.VMEM(x, F32) for x in shapes),
            tuple(pltpu.VMEM(x, BF16) for x in shapes) + (pltpu.SemaphoreType.DMA((2, nodes)),) if final else (),
            [SM] + [VM] * (len(ins) - 1),
            (ANY, ANY) if final else None,
        )
    return tuple(sums)


def solution(mesh):
    placed = (P("leaf", None, None), P("leaf", None, None), P(), P("leaf"), P("leaf", "rows"))
    return jax.shard_map(
        per_device,
        mesh=mesh,
        in_specs=placed,
        out_specs=(P("leaf", "rows", None), P("leaf", None, "rows")),
        check_vma=False,
    )
```

profile of v0, /device:TPU:5, one launch (start us, length us, event | category | flops | bytes accessed | tf_op | source)
XLA Modules:
  0.0 70.0 jit_solution(15117751999031536195)
XLA Ops:
  0.6 4.5 %prep.1 = (bf16[3,1024,1024]{2,1,0:T(8,128)(2,1)S(1)}, bf16[272,1024]{1,0:T(8,128)(2,1)S(1)}, f32[2,128,1024]{2,1,0:T(8,128)S(1)}, f32[64,1024]{1,0:T(8,128)S(1)}, f32[64,1024]{1,0:T(8,128)S(1)}) custom-call(s32[3]{0:T(128)} %refs_0_.9, s32[3,128]{1,0:T(4,128)} %refs_1_.1, bf16[3,256,1024]{2,1,0:T(8,128)(2,1)} %refs_2_.1, bf16[3,1024,1024]{2,1,0:T(8,128)(2,1)} %refs_3_.1), custom_call_target="tpu_custom_call" | custom-call | flops 1000000000 | bytes 2097152 | tf_op jit(solution)/shard_map/prep/pallas_call | solution.py:22
  5.1 0.8 %first.2.refs_1_ = bf16[64,1024]{1,0:T(8,128)(2,1)S(1)} custom-call(f32[64,1024]{1,0:T(8,128)S(1)} %get-tuple-element.46.refs_0_, bf16[3,1024,1024]{2,1,0:T(8,128)(2,1)S(1)} %get-tuple-element.44.refs_1_.refs_0_.refs_2_.refs_3_.refs_4_.refs_17_), custom_call_target="tpu_custom_call" | custom-call | flops 1000000000 | bytes 2097152 | tf_op jit(solution)/shard_map/first/pallas_call | solution.py:22
  6.0 1.3 %collective-permute-start.4 = (bf16[64,1024]{1,0:T(8,128)(2,1)S(1)}, bf16[64,1024]{1,0:T(8,128)(2,1)S(1)}, u32[]{:S(2)}, u32[]{:S(2)}) collective-permute-start(bf16[64,1024]{1,0:T(8,128)(2,1)S(1)} %first.2.refs_1_), channel_id=1, source_target_pairs={{4,0},{12,8},{20,16},{28,24},{5,1},{13,9},{21,17},{29,25},{6,2},{1... | collective-permute-start | bytes 393224 | tf_op jit(solution)/shard_map/ppermute | solution.py:326
  7.3 1.3 %collective-permute-start.1 = (bf16[272,1024]{1,0:T(8,128)(2,1)S(1)}, bf16[272,1024]{1,0:T(8,128)(2,1)S(1)}, u32[]{:S(2)}, u32[]{:S(2)}) collective-permute-start(bf16[272,1024]{1,0:T(8,128)(2,1)S(1)} %pass.1.refs_1_.refs_2_.refs_7_.refs_3_), channel_id=1, source_target_pairs={{0,2},{1,3},{2,0},{3,1},{4,6},{5,7},{6,4},{7,5},{8,10},{9,11},{10,... | collective-permute-start | bytes 1671176 | tf_op jit(solution)/shard_map/ppermute | solution.py:266
  8.6 0.8 %first.3 = bf16[64,1024]{1,0:T(8,128)(2,1)S(1)} custom-call(f32[64,1024]{1,0:T(8,128)S(1)} %get-tuple-element.49.refs_0_, bf16[3,1024,1024]{2,1,0:T(8,128)(2,1)S(1)} %get-tuple-element.44.refs_1_.refs_0_.refs_2_.refs_3_.refs_4_.refs_17_, bf16[272,1024]{1,0:T(8,128)(2,1)S(1)} %pass.1.refs_1_.refs_2_.refs_7_.refs_3_), custom_call_target="tpu_custom_call" | custom-call | flops 1000000000 | bytes 2097152 | tf_op jit(solution)/shard_map/first/pallas_call | solution.py:22
  9.4 1.3 %collective-permute-start.3 = (bf16[64,1024]{1,0:T(8,128)(2,1)S(1)}, bf16[64,1024]{1,0:T(8,128)(2,1)S(1)}, u32[]{:S(2)}, u32[]{:S(2)}) collective-permute-start(bf16[64,1024]{1,0:T(8,128)(2,1)S(1)} %first.3), channel_id=1, source_target_pairs={{4,0},{12,8},{20,16},{28,24},{5,1},{13,9},{21,17},{29,25},{6,2},{1... | collective-permute-start | bytes 393224 | tf_op jit(solution)/shard_map/ppermute | solution.py:326
  10.8 0.7 collective-permute-start.6
  11.4 1.2 %collective-permute-done.3.refs_1_ = bf16[64,1024]{1,0:T(8,128)(2,1)S(1)} collective-permute-done((bf16[64,1024]{1,0:T(8,128)(2,1)S(1)}, bf16[64,1024]{1,0:T(8,128)(2,1)S(1)}, u32[]{:S(2)}, u32[]{:S(2)}) %collective-permute-start.3) | collective-permute-done | bytes 131104 | tf_op jit(solution)/shard_map/ppermute | solution.py:326
  12.6 0.7 collective-permute-start.5
  13.3 0.0 collective-permute-done.6.refs_1_
  13.3 0.7 collective-permute-start.8
  14.0 0.0 copy-start
  14.1 0.7 collective-permute-start.7
  14.8 1.9 %collective-permute-start = (bf16[272,1024]{1,0:T(8,128)(2,1)S(1)}, bf16[272,1024]{1,0:T(8,128)(2,1)S(1)}, u32[]{:S(2)}, u32[]{:S(2)}) collective-permute-start(bf16[272,1024]{1,0:T(8,128)(2,1)S(1)} %pass.1.refs_1_.refs_2_.refs_7_.refs_3_), channel_id=1, source_target_pairs={{0,1},{1,0},{2,3},{3,2},{4,5},{5,4},{6,7},{7,6},{8,9},{9,8},{10,11... | collective-permute-start | bytes 1671176 | tf_op jit(solution)/shard_map/ppermute | solution.py:266
  16.6 4.2 %collective-permute-done.1.refs_3_.refs_5_ = bf16[272,1024]{1,0:T(8,128)(2,1)S(1)} collective-permute-done((bf16[272,1024]{1,0:T(8,128)(2,1)S(1)}, bf16[272,1024]{1,0:T(8,128)(2,1)S(1)}, u32[]{:S(2)}, u32[]{:S(2)}) %collective-permute-start.1) | collective-permute-done | bytes 557088 | tf_op jit(solution)/shard_map/ppermute | solution.py:266
  20.8 1.6 %collective-permute-start.2 = (bf16[272,1024]{1,0:T(8,128)(2,1)S(1)}, bf16[272,1024]{1,0:T(8,128)(2,1)S(1)}, u32[]{:S(2)}, u32[]{:S(2)}) collective-permute-start(bf16[272,1024]{1,0:T(8,128)(2,1)S(1)} %collective-permute-done.1.refs_3_.refs_5_), channel_id=1, source_target_pairs={{0,1},{1,0},{2,3},{3,2},{4,5},{5,4},{6,7},{7,6},{8,9},{9,8},{10,11... | collective-permute-start | bytes 1671176 | tf_op jit(solution)/shard_map/ppermute | solution.py:266
  22.4 0.8 %root.2 = (bf16[64,1024]{1,0:T(8,128)(2,1)S(1)}, f32[64,1024]{1,0:T(8,128)S(1)}, bf16[64,1024]{1,0:T(8,128)(2,1)S(1)}, bf16[64,1024]{1,0:T(8,128)(2,1)S(1)}) custom-call(f32[64,1024]{1,0:T(8,128)S(1)} %get-tuple-element.57.refs_0_, bf16[64,1024]{1,0:T(8,128)(2,1)S(1)} %collective-permute-done.8.refs_1_, ...), custom_call_target="tpu_custom_call" | custom-call | flops 1000000000 | bytes 2097152 | tf_op jit(solution)/shard_map/root/pallas_call | solution.py:22
  23.2 0.7 collective-permute-start.13
  23.9 0.0 collective-permute-done.7.refs_1_
  23.9 0.8 %root.3 = (bf16[64,1024]{1,0:T(8,128)(2,1)S(1)}, f32[64,1024]{1,0:T(8,128)S(1)}, bf16[64,1024]{1,0:T(8,128)(2,1)S(1)}, bf16[64,1024]{1,0:T(8,128)(2,1)S(1)}, bf16[128,1024]{1,0:T(8,128)(2,1)S(1)}) custom-call(f32[64,1024]{1,0:T(8,128)S(1)} %get-tuple-element.55.refs_0_, bf16[64,1024]{1,0:T(8,128)(2,1)S(1)} %collective-permute-done.7.refs_1_, ...), custom_call_target="tpu_custom_call" | custom-call | flops 1000000000 | bytes 2097152 | tf_op jit(solution)/shard_map/root/pallas_call | solution.py:22
  24.7 1.3 %collective-permute-start.10 = (bf16[128,1024]{1,0:T(8,128)(2,1)S(1)}, bf16[128,1024]{1,0:T(8,128)(2,1)S(1)}, u32[]{:S(2)}, u32[]{:S(2)}) collective-permute-start(bf16[128,1024]{1,0:T(8,128)(2,1)S(1)} %get-tuple-element.59.refs_9_.refs_7_), channel_id=1, source_target_pairs={{0,2},{1,3},{2,0},{3,1},{4,6},{5,7},{6,4},{7,5},{8,10},{9,11},{10,... | collective-permute-start | bytes 786440 | tf_op jit(solution)/shard_map/ppermute | solution.py:266
  26.0 0.7 collective-permute-start.12
  26.7 0.7 collective-permute-start.15
  27.4 0.0 collective-permute-done.12.refs_0_
  27.4 0.4 collective-permute-start.9
  27.8 0.0 collective-permute-done.15.refs_0_
  27.8 0.7 collective-permute-start.14
  28.5 4.2 %collective-permute-done.10.refs_11_.refs_9_ = bf16[128,1024]{1,0:T(8,128)(2,1)S(1)} collective-permute-done((bf16[128,1024]{1,0:T(8,128)(2,1)S(1)}, bf16[128,1024]{1,0:T(8,128)(2,1)S(1)}, u32[]{:S(2)}, u32[]{:S(2)}) %collective-permute-start.10) | collective-permute-done | bytes 262176 | tf_op jit(solution)/shard_map/ppermute | solution.py:266
  32.7 0.8 %collective-permute-start.11 = (bf16[128,1024]{1,0:T(8,128)(2,1)S(1)}, bf16[128,1024]{1,0:T(8,128)(2,1)S(1)}, u32[]{:S(2)}, u32[]{:S(2)}) collective-permute-start(bf16[128,1024]{1,0:T(8,128)(2,1)S(1)} %collective-permute-done.10.refs_11_.refs_9_), channel_id=1, source_target_pairs={{0,1},{1,0},{2,3},{3,2},{4,5},{5,4},{6,7},{7,6},{8,9},{9,8},{10,11... | collective-permute-start | bytes 786440 | tf_op jit(solution)/shard_map/ppermute | solution.py:266
  33.5 0.0 collective-permute-done.refs_2_.refs_4_
  33.5 1.3 %collective-permute-start.17 = (bf16[64,1024]{1,0:T(8,128)(2,1)S(1)}, bf16[64,1024]{1,0:T(8,128)(2,1)S(1)}, u32[]{:S(2)}, u32[]{:S(2)}) collective-permute-start(bf16[64,1024]{1,0:T(8,128)(2,1)S(1)} %get-tuple-element.71.refs_7_.refs_6_), channel_id=1, source_target_pairs={{0,4},{8,12},{16,20},{24,28},{1,5},{9,13},{17,21},{25,29},{2,6},{1... | collective-permute-start | bytes 393224 | tf_op jit(solution)/shard_map/ppermute | solution.py:370
  34.8 0.9 %ready.1 = (f32[2,2,256,256]{3,2,1,0:T(8,128)S(1)}, bf16[3,2,256,256]{3,2,1,0:T(8,128)(2,1)S(1)}) custom-call(bf16[3,1024,1024]{2,1,0:T(8,128)(2,1)S(1)} %get-tuple-element.44.refs_1_.refs_0_.refs_2_.refs_3_.refs_4_.refs_17_, bf16[272,1024]{1,0:T(8,128)(2,1)S(1)} %pass.1.refs_1_.refs_2_.refs_7_.refs_3_, ...), custom_call_target="tpu_custom_call" | custom-call | flops 1000000000 | bytes 2097152 | tf_op jit(solution)/shard_map/ready/pallas_call | solution.py:22
  35.8 0.0 copy-start.1
  35.8 1.3 %collective-permute-start.16 = (bf16[64,1024]{1,0:T(8,128)(2,1)S(1)}, bf16[64,1024]{1,0:T(8,128)(2,1)S(1)}, u32[]{:S(2)}, u32[]{:S(2)}) collective-permute-start(bf16[64,1024]{1,0:T(8,128)(2,1)S(1)} %get-tuple-element.72.refs_6_), channel_id=1, source_target_pairs={{0,4},{8,12},{16,20},{24,28},{1,5},{9,13},{17,21},{25,29},{2,6},{1... | collective-permute-start | bytes 393224 | tf_op jit(solution)/shard_map/ppermute | solution.py:370
  37.1 14.0 %collective-permute-done.17.refs_1_ = bf16[64,1024]{1,0:T(8,128)(2,1)S(1)} collective-permute-done((bf16[64,1024]{1,0:T(8,128)(2,1)S(1)}, bf16[64,1024]{1,0:T(8,128)(2,1)S(1)}, u32[]{:S(2)}, u32[]{:S(2)}) %collective-permute-start.17) | collective-permute-done | bytes 131104 | tf_op jit(solution)/shard_map/ppermute | solution.py:370
  51.1 2.1 %last.2 = (bf16[4,64,256]{2,1,0:T(8,128)(2,1)S(1)}, bf16[4,64,256]{2,1,0:T(8,128)(2,1)S(1)}, bf16[4,64,256]{2,1,0:T(8,128)(2,1)S(1)}, bf16[4,64,256]{2,1,0:T(8,128)(2,1)S(1)}) custom-call(s32[3]{0:T(128)S(1)} %copy-done.1, bf16[64,1024]{1,0:T(8,128)(2,1)S(1)} %collective-permute-done.17.refs_1_, ...), custom_call_target="tpu_custom_call" | custom-call | flops 1000000000 | bytes 2097152 | tf_op jit(solution)/shard_map/last/pallas_call | solution.py:22
  53.2 0.9 %collective-permute-start.21 = (bf16[4,64,256]{2,1,0:T(8,128)(2,1)S(1)}, bf16[4,64,256]{2,1,0:T(8,128)(2,1)S(1)}, u32[]{:S(2)}, u32[]{:S(2)}) collective-permute-start(bf16[4,64,256]{2,1,0:T(8,128)(2,1)S(1)} %get-tuple-element.81), channel_id=1, source_target_pairs={{0,1},{1,0},{2,3},{3,2},{4,5},{5,4},{6,7},{7,6},{8,9},{9,8},{10,11... | collective-permute-start | bytes 393224 | tf_op jit(solution)/shard_map/ppermute | solution.py:266
  54.0 0.9 %collective-permute-start.22 = (bf16[4,64,256]{2,1,0:T(8,128)(2,1)S(1)}, bf16[4,64,256]{2,1,0:T(8,128)(2,1)S(1)}, u32[]{:S(2)}, u32[]{:S(2)}) collective-permute-start(bf16[4,64,256]{2,1,0:T(8,128)(2,1)S(1)} %get-tuple-element.82), channel_id=1, source_target_pairs={{0,2},{1,3},{2,0},{3,1},{4,6},{5,7},{6,4},{7,5},{8,10},{9,11},{10,... | collective-permute-start | bytes 393224 | tf_op jit(solution)/shard_map/ppermute | solution.py:266
  55.0 0.8 %collective-permute-start.23 = (bf16[4,64,256]{2,1,0:T(8,128)(2,1)S(1)}, bf16[4,64,256]{2,1,0:T(8,128)(2,1)S(1)}, u32[]{:S(2)}, u32[]{:S(2)}) collective-permute-start(bf16[4,64,256]{2,1,0:T(8,128)(2,1)S(1)} %get-tuple-element.83), channel_id=1, source_target_pairs={{0,3},{1,2},{2,1},{3,0},{4,7},{5,6},{6,5},{7,4},{8,11},{9,10},{10,... | collective-permute-start | bytes 393224 | tf_op jit(solution)/shard_map/ppermute | solution.py:266
  55.8 2.1 %last.3 = (bf16[4,64,256]{2,1,0:T(8,128)(2,1)S(1)}, bf16[4,64,256]{2,1,0:T(8,128)(2,1)S(1)}, bf16[4,64,256]{2,1,0:T(8,128)(2,1)S(1)}, bf16[4,64,256]{2,1,0:T(8,128)(2,1)S(1)}) custom-call(s32[3]{0:T(128)S(1)} %copy-done.1, bf16[64,1024]{1,0:T(8,128)(2,1)S(1)} %collective-permute-done.16.refs_1_, bf16[64,1024]{1,0:T(8,128)(2,1)S(1)} %get-tuple-element.61.refs_1_.refs_2_, ...), custom_call_target="tpu_custom_call" | custom-call | flops 1000000000 | bytes 2097152 | tf_op jit(solution)/shard_map/last/pallas_call | solution.py:22
  57.8 0.2 collective-permute-start.18
  58.1 0.9 %collective-permute-start.19 = (bf16[4,64,256]{2,1,0:T(8,128)(2,1)S(1)}, bf16[4,64,256]{2,1,0:T(8,128)(2,1)S(1)}, u32[]{:S(2)}, u32[]{:S(2)}) collective-permute-start(bf16[4,64,256]{2,1,0:T(8,128)(2,1)S(1)} %get-tuple-element.79), channel_id=1, source_target_pairs={{0,2},{1,3},{2,0},{3,1},{4,6},{5,7},{6,4},{7,5},{8,10},{9,11},{10,... | collective-permute-start | bytes 393224 | tf_op jit(solution)/shard_map/ppermute | solution.py:266
  59.0 1.1 %collective-permute-start.20 = (bf16[4,64,256]{2,1,0:T(8,128)(2,1)S(1)}, bf16[4,64,256]{2,1,0:T(8,128)(2,1)S(1)}, u32[]{:S(2)}, u32[]{:S(2)}) collective-permute-start(bf16[4,64,256]{2,1,0:T(8,128)(2,1)S(1)} %get-tuple-element.80), channel_id=1, source_target_pairs={{0,3},{1,2},{2,1},{3,0},{4,7},{5,6},{6,5},{7,4},{8,11},{9,10},{10,... | collective-permute-start | bytes 393224 | tf_op jit(solution)/shard_map/ppermute | solution.py:266
  60.0 2.5 %collective-permute-done.23.refs_14_ = bf16[4,64,256]{2,1,0:T(8,128)(2,1)S(1)} collective-permute-done((bf16[4,64,256]{2,1,0:T(8,128)(2,1)S(1)}, bf16[4,64,256]{2,1,0:T(8,128)(2,1)S(1)}, u32[]{:S(2)}, u32[]{:S(2)}) %collective-permute-start.23) | collective-permute-done | bytes 131104 | tf_op jit(solution)/shard_map/ppermute | solution.py:266
  62.5 1.3 %counts.2 = (f32[3,256,1024]{2,1,0:T(8,128)S(1)}, f32[3,256,256]{2,1,0:T(8,128)S(1)}) custom-call(s32[3]{0:T(128)S(1)} %copy-done.1, f32[2,2,256,256]{3,2,1,0:T(8,128)S(1)} %get-tuple-element.47.refs_6_.refs_1_, bf16[3,2,256,256]{3,2,1,0:T(8,128)(2,1)S(1)} %get-tuple-element.48.refs_2_, bf16[272,1024]{1,0:T(8,128)(2,1)S(1)} %pass.1.refs_1_.refs_2_.refs_7_.refs_3_, ...), custom_call_target="tpu_custom_call" | custom-call | flops 1000000000 | bytes 2097152 | tf_op jit(solution)/shard_map/counts/pallas_call | solution.py:22
  63.8 0.9 %collective-permute-done.19.refs_13_ = bf16[4,64,256]{2,1,0:T(8,128)(2,1)S(1)} collective-permute-done((bf16[4,64,256]{2,1,0:T(8,128)(2,1)S(1)}, bf16[4,64,256]{2,1,0:T(8,128)(2,1)S(1)}, u32[]{:S(2)}, u32[]{:S(2)}) %collective-permute-start.19) | collective-permute-done | bytes 131104 | tf_op jit(solution)/shard_map/ppermute | solution.py:266
  64.7 3.0 %collective-permute-done.20.refs_14_ = bf16[4,64,256]{2,1,0:T(8,128)(2,1)S(1)} collective-permute-done((bf16[4,64,256]{2,1,0:T(8,128)(2,1)S(1)}, bf16[4,64,256]{2,1,0:T(8,128)(2,1)S(1)}, u32[]{:S(2)}, u32[]{:S(2)}) %collective-permute-start.20) | collective-permute-done | bytes 131104 | tf_op jit(solution)/shard_map/ppermute | solution.py:266
  67.7 2.3 %counts.3 = (bf16[3,256,1024]{2,1,0:T(8,128)(2,1)}, bf16[3,256,256]{2,1,0:T(8,128)(2,1)}) custom-call(s32[3]{0:T(128)S(1)} %copy-done.1, f32[2,2,256,256]{3,2,1,0:T(8,128)S(1)} %get-tuple-element.47.refs_6_.refs_1_, bf16[3,2,256,256]{3,2,1,0:T(8,128)(2,1)S(1)} %get-tuple-element.48.refs_2_, bf16[272,1024]{1,0:T(8,128)(2,1)S(1)} %pass.1.refs_1_.refs_2_.refs_7_.refs_3_, ...), custom_call_target="tpu_custom_call" | custom-call | flops 1000000000 | bytes 2097152 | tf_op jit(solution)/shard_map/counts/pallas_call | solution.py:22
  (23 shorter events, 0.2 us)
Async XLA Ops:
  6.0 4.7 %collective-permute-start.4 = (bf16[64,1024]{1,0:T(8,128)(2,1)S(1)}, bf16[64,1024]{1,0:T(8,128)(2,1)S(1)}, u32[]{:S(2)}, u32[]{:S(2)}) collective-permute-start(bf16[64,1024]{1,0:T(8,128)(2,1)S(1)} %first.2.refs_1_), channel_id=1, source_target_pairs={{4,0},{12,8},{20,16},{28,24},{5,1},{13,9},{21,17},{29,25},{6,2},{1... | collective-permute-start | bytes 393224 | tf_op jit(solution)/shard_map/ppermute | solution.py:326
  7.3 13.5 %collective-permute-start.1 = (bf16[272,1024]{1,0:T(8,128)(2,1)S(1)}, bf16[272,1024]{1,0:T(8,128)(2,1)S(1)}, u32[]{:S(2)}, u32[]{:S(2)}) collective-permute-start(bf16[272,1024]{1,0:T(8,128)(2,1)S(1)} %pass.1.refs_1_.refs_2_.refs_7_.refs_3_), channel_id=1, source_target_pairs={{0,2},{1,3},{2,0},{3,1},{4,6},{5,7},{6,4},{7,5},{8,10},{9,11},{10,... | collective-permute-start | bytes 1671176 | tf_op jit(solution)/shard_map/ppermute | solution.py:266
  9.4 3.2 %collective-permute-start.3 = (bf16[64,1024]{1,0:T(8,128)(2,1)S(1)}, bf16[64,1024]{1,0:T(8,128)(2,1)S(1)}, u32[]{:S(2)}, u32[]{:S(2)}) collective-permute-start(bf16[64,1024]{1,0:T(8,128)(2,1)S(1)} %first.3), channel_id=1, source_target_pairs={{4,0},{12,8},{20,16},{28,24},{5,1},{13,9},{21,17},{29,25},{6,2},{1... | collective-permute-start | bytes 393224 | tf_op jit(solution)/shard_map/ppermute | solution.py:326
  10.8 2.6 %collective-permute-start.6 = (bf16[64,1024]{1,0:T(8,128)(2,1)S(1)}, bf16[64,1024]{1,0:T(8,128)(2,1)S(1)}, u32[]{:S(2)}, u32[]{:S(2)}) collective-permute-start(bf16[64,1024]{1,0:T(8,128)(2,1)S(1)} %get-tuple-element.50.refs_3_), channel_id=1, source_target_pairs={{8,0},{24,16},{9,1},{25,17},{10,2},{26,18},{11,3},{27,19}} | collective-permute-start | bytes 393224 | tf_op jit(solution)/shard_map/ppermute | solution.py:326
  12.6 1.4 %collective-permute-start.5 = (bf16[64,1024]{1,0:T(8,128)(2,1)S(1)}, bf16[64,1024]{1,0:T(8,128)(2,1)S(1)}, u32[]{:S(2)}, u32[]{:S(2)}) collective-permute-start(bf16[64,1024]{1,0:T(8,128)(2,1)S(1)} %get-tuple-element.52), channel_id=1, source_target_pairs={{8,0},{24,16},{9,1},{25,17},{10,2},{26,18},{11,3},{27,19}} | collective-permute-start | bytes 393224 | tf_op jit(solution)/shard_map/ppermute | solution.py:326
  13.3 9.1 %collective-permute-start.8 = (bf16[64,1024]{1,0:T(8,128)(2,1)S(1)}, bf16[64,1024]{1,0:T(8,128)(2,1)S(1)}, u32[]{:S(2)}, u32[]{:S(2)}) collective-permute-start(bf16[64,1024]{1,0:T(8,128)(2,1)S(1)} %get-tuple-element.54.refs_3_), channel_id=1, source_target_pairs={{16,0},{17,1},{18,2},{19,3}} | collective-permute-start | bytes 393224 | tf_op jit(solution)/shard_map/ppermute | solution.py:339
  14.0 8.4 %copy-start = (f32[1024]{0:T(1024)S(1)}, f32[1024]{0:T(1024)}, u32[]{:S(2)}) copy-start(f32[1024]{0:T(1024)} %param.7) | copy-start | bytes 12292
  14.1 9.8 %collective-permute-start.7 = (bf16[64,1024]{1,0:T(8,128)(2,1)S(1)}, bf16[64,1024]{1,0:T(8,128)(2,1)S(1)}, u32[]{:S(2)}, u32[]{:S(2)}) collective-permute-start(bf16[64,1024]{1,0:T(8,128)(2,1)S(1)} %get-tuple-element.56), channel_id=1, source_target_pairs={{16,0},{17,1},{18,2},{19,3}} | collective-permute-start | bytes 393224 | tf_op jit(solution)/shard_map/ppermute | solution.py:339
  14.8 18.7 %collective-permute-start = (bf16[272,1024]{1,0:T(8,128)(2,1)S(1)}, bf16[272,1024]{1,0:T(8,128)(2,1)S(1)}, u32[]{:S(2)}, u32[]{:S(2)}) collective-permute-start(bf16[272,1024]{1,0:T(8,128)(2,1)S(1)} %pass.1.refs_1_.refs_2_.refs_7_.refs_3_), channel_id=1, source_target_pairs={{0,1},{1,0},{2,3},{3,2},{4,5},{5,4},{6,7},{7,6},{8,9},{9,8},{10,11... | collective-permute-start | bytes 1671176 | tf_op jit(solution)/shard_map/ppermute | solution.py:266
  20.8 14.0 %collective-permute-start.2 = (bf16[272,1024]{1,0:T(8,128)(2,1)S(1)}, bf16[272,1024]{1,0:T(8,128)(2,1)S(1)}, u32[]{:S(2)}, u32[]{:S(2)}) collective-permute-start(bf16[272,1024]{1,0:T(8,128)(2,1)S(1)} %collective-permute-done.1.refs_3_.refs_5_), channel_id=1, source_target_pairs={{0,1},{1,0},{2,3},{3,2},{4,5},{5,4},{6,7},{7,6},{8,9},{9,8},{10,11... | collective-permute-start | bytes 1671176 | tf_op jit(solution)/shard_map/ppermute | solution.py:266
  23.2 3.5 %collective-permute-start.13 = (bf16[64,1024]{1,0:T(8,128)(2,1)S(1)}, bf16[64,1024]{1,0:T(8,128)(2,1)S(1)}, u32[]{:S(2)}, u32[]{:S(2)}) collective-permute-start(bf16[64,1024]{1,0:T(8,128)(2,1)S(1)} %get-tuple-element.64.refs_5_), channel_id=1, source_target_pairs={{0,16},{1,17},{2,18},{3,19}} | collective-permute-start | bytes 393224 | tf_op jit(solution)/shard_map/ppermute | solution.py:360
  24.7 8.0 %collective-permute-start.10 = (bf16[128,1024]{1,0:T(8,128)(2,1)S(1)}, bf16[128,1024]{1,0:T(8,128)(2,1)S(1)}, u32[]{:S(2)}, u32[]{:S(2)}) collective-permute-start(bf16[128,1024]{1,0:T(8,128)(2,1)S(1)} %get-tuple-element.59.refs_9_.refs_7_), channel_id=1, source_target_pairs={{0,2},{1,3},{2,0},{3,1},{4,6},{5,7},{6,4},{7,5},{8,10},{9,11},{10,... | collective-permute-start | bytes 786440 | tf_op jit(solution)/shard_map/ppermute | solution.py:266
  26.0 1.4 %collective-permute-start.12 = (bf16[64,1024]{1,0:T(8,128)(2,1)S(1)}, bf16[64,1024]{1,0:T(8,128)(2,1)S(1)}, u32[]{:S(2)}, u32[]{:S(2)}) collective-permute-start(bf16[64,1024]{1,0:T(8,128)(2,1)S(1)} %get-tuple-element.60.refs_5_), channel_id=1, source_target_pairs={{0,16},{1,17},{2,18},{3,19}} | collective-permute-start | bytes 393224 | tf_op jit(solution)/shard_map/ppermute | solution.py:360
  26.7 1.1 %collective-permute-start.15 = (bf16[64,1024]{1,0:T(8,128)(2,1)S(1)}, bf16[64,1024]{1,0:T(8,128)(2,1)S(1)}, u32[]{:S(2)}, u32[]{:S(2)}) collective-permute-start(bf16[64,1024]{1,0:T(8,128)(2,1)S(1)} %get-tuple-element.67.refs_6_.refs_5_), channel_id=1, source_target_pairs={{0,8},{16,24},{1,9},{17,25},{2,10},{18,26},{3,11},{19,27}} | collective-permute-start | bytes 393224 | tf_op jit(solution)/shard_map/ppermute | solution.py:360
  27.4 9.7 %collective-permute-start.9 = (bf16[128,1024]{1,0:T(8,128)(2,1)S(1)}, bf16[128,1024]{1,0:T(8,128)(2,1)S(1)}, u32[]{:S(2)}, u32[]{:S(2)}) collective-permute-start(bf16[128,1024]{1,0:T(8,128)(2,1)S(1)} %get-tuple-element.59.refs_9_.refs_7_), channel_id=1, source_target_pairs={{0,1},{1,0},{2,3},{3,2},{4,5},{5,4},{6,7},{7,6},{8,9},{9,8},{10,11... | collective-permute-start | bytes 786440 | tf_op jit(solution)/shard_map/ppermute | solution.py:266
  27.8 8.0 %collective-permute-start.14 = (bf16[64,1024]{1,0:T(8,128)(2,1)S(1)}, bf16[64,1024]{1,0:T(8,128)(2,1)S(1)}, u32[]{:S(2)}, u32[]{:S(2)}) collective-permute-start(bf16[64,1024]{1,0:T(8,128)(2,1)S(1)} %get-tuple-element.68.refs_5_), channel_id=1, source_target_pairs={{0,8},{16,24},{1,9},{17,25},{2,10},{18,26},{3,11},{19,27}} | collective-permute-start | bytes 393224 | tf_op jit(solution)/shard_map/ppermute | solution.py:360
  32.7 18.4 %collective-permute-start.11 = (bf16[128,1024]{1,0:T(8,128)(2,1)S(1)}, bf16[128,1024]{1,0:T(8,128)(2,1)S(1)}, u32[]{:S(2)}, u32[]{:S(2)}) collective-permute-start(bf16[128,1024]{1,0:T(8,128)(2,1)S(1)} %collective-permute-done.10.refs_11_.refs_9_), channel_id=1, source_target_pairs={{0,1},{1,0},{2,3},{3,2},{4,5},{5,4},{6,7},{7,6},{8,9},{9,8},{10,11... | collective-permute-start | bytes 786440 | tf_op jit(solution)/shard_map/ppermute | solution.py:266
  33.5 17.6 %collective-permute-start.17 = (bf16[64,1024]{1,0:T(8,128)(2,1)S(1)}, bf16[64,1024]{1,0:T(8,128)(2,1)S(1)}, u32[]{:S(2)}, u32[]{:S(2)}) collective-permute-start(bf16[64,1024]{1,0:T(8,128)(2,1)S(1)} %get-tuple-element.71.refs_7_.refs_6_), channel_id=1, source_target_pairs={{0,4},{8,12},{16,20},{24,28},{1,5},{9,13},{17,21},{25,29},{2,6},{1... | collective-permute-start | bytes 393224 | tf_op jit(solution)/shard_map/ppermute | solution.py:370
  35.8 15.3 %copy-start.1 = (s32[3]{0:T(128)S(1)}, s32[3]{0:T(128)}, u32[]{:S(2)}) copy-start(s32[3]{0:T(128)} %refs_0_.9) | copy-start | bytes 40
  35.8 19.9 %collective-permute-start.16 = (bf16[64,1024]{1,0:T(8,128)(2,1)S(1)}, bf16[64,1024]{1,0:T(8,128)(2,1)S(1)}, u32[]{:S(2)}, u32[]{:S(2)}) collective-permute-start(bf16[64,1024]{1,0:T(8,128)(2,1)S(1)} %get-tuple-element.72.refs_6_), channel_id=1, source_target_pairs={{0,4},{8,12},{16,20},{24,28},{1,5},{9,13},{17,21},{25,29},{2,6},{1... | collective-permute-start | bytes 393224 | tf_op jit(solution)/shard_map/ppermute | solution.py:370
  53.2 5.8 %collective-permute-start.21 = (bf16[4,64,256]{2,1,0:T(8,128)(2,1)S(1)}, bf16[4,64,256]{2,1,0:T(8,128)(2,1)S(1)}, u32[]{:S(2)}, u32[]{:S(2)}) collective-permute-start(bf16[4,64,256]{2,1,0:T(8,128)(2,1)S(1)} %get-tuple-element.81), channel_id=1, source_target_pairs={{0,1},{1,0},{2,3},{3,2},{4,5},{5,4},{6,7},{7,6},{8,9},{9,8},{10,11... | collective-permute-start | bytes 393224 | tf_op jit(solution)/shard_map/ppermute | solution.py:266
  54.0 6.0 %collective-permute-start.22 = (bf16[4,64,256]{2,1,0:T(8,128)(2,1)S(1)}, bf16[4,64,256]{2,1,0:T(8,128)(2,1)S(1)}, u32[]{:S(2)}, u32[]{:S(2)}) collective-permute-start(bf16[4,64,256]{2,1,0:T(8,128)(2,1)S(1)} %get-tuple-element.82), channel_id=1, source_target_pairs={{0,2},{1,3},{2,0},{3,1},{4,6},{5,7},{6,4},{7,5},{8,10},{9,11},{10,... | collective-permute-start | bytes 393224 | tf_op jit(solution)/shard_map/ppermute | solution.py:266
  55.0 7.6 %collective-permute-start.23 = (bf16[4,64,256]{2,1,0:T(8,128)(2,1)S(1)}, bf16[4,64,256]{2,1,0:T(8,128)(2,1)S(1)}, u32[]{:S(2)}, u32[]{:S(2)}) collective-permute-start(bf16[4,64,256]{2,1,0:T(8,128)(2,1)S(1)} %get-tuple-element.83), channel_id=1, source_target_pairs={{0,3},{1,2},{2,1},{3,0},{4,7},{5,6},{6,5},{7,4},{8,11},{9,10},{10,... | collective-permute-start | bytes 393224 | tf_op jit(solution)/shard_map/ppermute | solution.py:266
  57.8 6.0 %collective-permute-start.18 = (bf16[4,64,256]{2,1,0:T(8,128)(2,1)S(1)}, bf16[4,64,256]{2,1,0:T(8,128)(2,1)S(1)}, u32[]{:S(2)}, u32[]{:S(2)}) collective-permute-start(bf16[4,64,256]{2,1,0:T(8,128)(2,1)S(1)} %get-tuple-element.78), channel_id=1, source_target_pairs={{0,1},{1,0},{2,3},{3,2},{4,5},{5,4},{6,7},{7,6},{8,9},{9,8},{10,11... | collective-permute-start | bytes 393224 | tf_op jit(solution)/shard_map/ppermute | solution.py:266
  58.1 6.7 %collective-permute-start.19 = (bf16[4,64,256]{2,1,0:T(8,128)(2,1)S(1)}, bf16[4,64,256]{2,1,0:T(8,128)(2,1)S(1)}, u32[]{:S(2)}, u32[]{:S(2)}) collective-permute-start(bf16[4,64,256]{2,1,0:T(8,128)(2,1)S(1)} %get-tuple-element.79), channel_id=1, source_target_pairs={{0,2},{1,3},{2,0},{3,1},{4,6},{5,7},{6,4},{7,5},{8,10},{9,11},{10,... | collective-permute-start | bytes 393224 | tf_op jit(solution)/shard_map/ppermute | solution.py:266
  59.0 8.7 %collective-permute-start.20 = (bf16[4,64,256]{2,1,0:T(8,128)(2,1)S(1)}, bf16[4,64,256]{2,1,0:T(8,128)(2,1)S(1)}, u32[]{:S(2)}, u32[]{:S(2)}) collective-permute-start(bf16[4,64,256]{2,1,0:T(8,128)(2,1)S(1)} %get-tuple-element.80), channel_id=1, source_target_pairs={{0,3},{1,2},{2,1},{3,0},{4,7},{5,6},{6,5},{7,4},{8,11},{9,10},{10,... | collective-permute-start | bytes 393224 | tf_op jit(solution)/shard_map/ppermute | solution.py:266
where the time goes:
time: 70.4 us; the launch traced here: 70 us
  waiting for transfers between devices  30 us (43%)
  starting transfers between devices  22.5 us (32%)
  Pallas kernels  16.5 us (23%)
  between operations  0.95 us (1%)
    pallas_call x19, Pallas kernels, run(): pl.pallas_call(lambda *refs: body(*refs[:count], *refs[idle:]), name=name...  16.5 us
    ppermute x12, waiting for transfers between devices, swap(): lax.ppermute(value, 'rows', [(s, s ^ mask) for s in range(lax.axis_size('...  14.8 us
    ppermute x2, waiting for transfers between devices, per_device(): recv = lax.ppermute(post[c], 'leaf', down_pairs(0))  14 us
    ppermute x12, starting transfers between devices, swap(): lax.ppermute(value, 'rows', [(s, s ^ mask) for s in range(lax.axis_size('...  12 us
    ppermute x4, starting transfers between devices, per_device(): recv = lax.ppermute(send[c], 'leaf', up_pairs(level))  3.92 us
    ppermute x4, starting transfers between devices, per_device(): recv = lax.ppermute(post[c], 'leaf', down_pairs(level))  2.66 us
    ppermute x2, starting transfers between devices, per_device(): recv = lax.ppermute(post[c], 'leaf', down_pairs(0))  2.58 us
  transfers between devices with their start and end apart: 24, of which 7 were waited for; matrix products, arithmetic and copies ran while one was open for 0% of the time, Pallas kernels for 13%

commit v1 on v0

--- a/solution.py
+++ b/solution.py
@@ -266,11 +266,23 @@
     return lax.ppermute(value, "rows", [(s, s ^ mask) for s in range(lax.axis_size("rows"))])
 
 
-def gather(value):
-    blocks = {0: value}
+def hold(value, after):
+    shape = pltpu.VMEM(value.shape, value.dtype)
+    return run(lambda *refs: None, "hold", (value,), (shape,), same={0: 0}, after=after)[0]
+
+
+def gather(blocks, after=()):
     for bit in reversed(range(lax.axis_size("rows").bit_length() - 1)):
-        blocks.update({place | (1 << bit): swap(block, 1 << bit) for place, block in blocks.items()})
+        if 1 << bit in blocks:
+            continue
+        for place, block in list(blocks.items()):
+            blocks[place | (1 << bit)] = swap(hold(block, after) if place and after else block, 1 << bit)
     return [blocks[place] for place in range(len(blocks))]
+
+
+def far(value):
+    half = lax.axis_size("rows") // 2
+    return {0: value, half: swap(value, half)} if half else {0: value}
 
 
 def per_device(mixing, emission, prior, parent, observed):
@@ -310,9 +322,7 @@
         (block,) = run(first_body, "first", (raw[c], weights), (half(BF16),), after=[lams] if c > 0 else ())
         send.append(block)
         if c == 0:
-            (lams,) = run(
-                lambda *refs: None, "pass", (lams,), (pltpu.VMEM(lams.shape, BF16),), same={0: 0}, after=(block,)
-            )
+            lams = hold(lams, (block,))
 
     def up_pairs(level):
         step = 1 << level
@@ -333,7 +343,7 @@
                 after=send[:c][-1:],
             )
         if level == 0:
-            all_lams = gather(lams)
+            near = far(lams)
     top_lam, top_msg, ratio, post = ([None] * CHUNKS for _ in range(4))
     for c in every:
         recv = lax.ppermute(send[c], "leaf", up_pairs(levels - 1))
@@ -344,7 +354,8 @@
             (raw[c], recv, weights, prior.reshape(1, states)) + (tuple(top_lam[:c]) if final else ()),
             (half(BF16), half(F32), half(BF16), half(BF16)) + ((pltpu.VMEM((rows, states), BF16),) if final else ()),
         )
-    all_tops = gather(merged[0])
+    all_tops = gather(far(merged[0]))
+    all_lams = gather(near, send[-1:])
     raw_own, hots = run(
         functools.partial(ready_body, nodes, groups),
         "ready",
@@ -353,6 +364,7 @@
             pltpu.VMEM((nodes - 1, CHUNKS, groups * part, share), F32),
             pltpu.VMEM((nodes, CHUNKS, values, groups * part), BF16),
         ),
+        work=0.1,
 
     )
     for level in reversed(range(1, levels)):
@@ -363,7 +375,7 @@
                 "settle",
                 (recv, top_lam[c], top_msg[c], weights, ratio[c], post[c]),
                 (half(BF16), half(BF16)),
-                after=post[:c][-1:] if c != 1 or level > 1 else (raw_own, *post[:c][-1:]),
+                after=post[:c][-1:] + ([raw_own] if level == 1 and c == 0 else []),
             )
     own_posts = []
     for c in every:
@@ -375,9 +387,9 @@
             (pltpu.VMEM((nodes + 1, part, share), BF16),) * groups,
             (pltpu.VMEM((nodes + 1, part, states), BF16),),
             [SM] + [VM] * 8,
-            after=own_posts[-1][:1] if c > 0 else tuple(all_tops),
+            after=own_posts[-1][:1] + all_tops if c > 0 else (),
         )
-        order = sorted(range(1, groups), reverse=True)
+        order = range(1, groups)
         moved = {mask: swap(packs[mask], mask) for mask in order}
         own_posts.append([packs[0]] + [moved[mask] for mask in range(1, groups)])
     sums = ()

time: 70.4 us -> 71 us (level)
  the two profiles are of different devices: /device:TPU:5 before, /device:TPU:23 now
where the time goes in v1:
time: 71 us; the launch traced here: 70.7 us
  waiting for transfers between devices  32.4 us (46%)
  starting transfers between devices  20.7 us (29%)
  Pallas kernels  16.5 us (23%)
  between operations  0.96 us (1%)
    pallas_call x20, Pallas kernels, run(): pl.pallas_call(lambda *refs: body(*refs[:count], *refs[idle:]), name=name...  16.5 us
    ppermute x12, waiting for transfers between devices, swap(): lax.ppermute(value, 'rows', [(s, s ^ mask) for s in range(lax.axis_size('...  15.5 us
    ppermute x2, waiting for transfers between devices, per_device(): recv = lax.ppermute(post[c], 'leaf', down_pairs(0))  14.4 us
    ppermute x12, starting transfers between devices, swap(): lax.ppermute(value, 'rows', [(s, s ^ mask) for s in range(lax.axis_size('...  10.2 us
    ppermute x4, starting transfers between devices, per_device(): recv = lax.ppermute(send[c], 'leaf', up_pairs(level))  3.95 us
    ppermute x4, starting transfers between devices, per_device(): recv = lax.ppermute(post[c], 'leaf', down_pairs(level))  2.66 us
    ppermute x2, starting transfers between devices, per_device(): recv = lax.ppermute(post[c], 'leaf', down_pairs(0))  2.58 us
    ppermute x4, waiting for transfers between devices, per_device(): recv = lax.ppermute(send[c], 'leaf', up_pairs(level))  2.54 us
  transfers between devices with their start and end apart: 24, of which 7 were waited for; matrix products, arithmetic and copies ran while one was open for 0% of the time, Pallas kernels for 13%

profile of v1, /device:TPU:23, one launch (start us, length us, event | category | flops | bytes accessed | tf_op | source)
XLA Modules:
  0.0 70.7 jit_solution(5848268440571210575)
XLA Ops:
  0.6 4.5 %prep.1 = (bf16[3,1024,1024]{2,1,0:T(8,128)(2,1)S(1)}, bf16[272,1024]{1,0:T(8,128)(2,1)S(1)}, f32[2,128,1024]{2,1,0:T(8,128)S(1)}, f32[64,1024]{1,0:T(8,128)S(1)}, f32[64,1024]{1,0:T(8,128)S(1)}) custom-call(s32[3]{0:T(128)} %refs_0_.9, s32[3,128]{1,0:T(4,128)} %refs_1_.1, bf16[3,256,1024]{2,1,0:T(8,128)(2,1)} %refs_2_.1, bf16[3,1024,1024]{2,1,0:T(8,128)(2,1)} %refs_3_.1), custom_call_target="tpu_custom_call" | custom-call | flops 1000000000 | bytes 2097152 | tf_op jit(solution)/shard_map/prep/pallas_call | solution.py:22
  5.1 0.8 %first.2.refs_1_ = bf16[64,1024]{1,0:T(8,128)(2,1)S(1)} custom-call(f32[64,1024]{1,0:T(8,128)S(1)} %get-tuple-element.46.refs_0_, bf16[3,1024,1024]{2,1,0:T(8,128)(2,1)S(1)} %get-tuple-element.44.refs_1_.refs_2_.refs_0_.refs_3_.refs_4_.refs_17_), custom_call_target="tpu_custom_call" | custom-call | flops 1000000000 | bytes 2097152 | tf_op jit(solution)/shard_map/first/pallas_call | solution.py:22
  6.0 0.3 collective-permute-start.1
  6.3 1.3 %collective-permute-start.3 = (bf16[64,1024]{1,0:T(8,128)(2,1)S(1)}, bf16[64,1024]{1,0:T(8,128)(2,1)S(1)}, u32[]{:S(2)}, u32[]{:S(2)}) collective-permute-start(bf16[64,1024]{1,0:T(8,128)(2,1)S(1)} %first.2.refs_1_), channel_id=1, source_target_pairs={{4,0},{12,8},{20,16},{28,24},{5,1},{13,9},{21,17},{29,25},{6,2},{1... | collective-permute-start | bytes 393224 | tf_op jit(solution)/shard_map/ppermute | solution.py:336
  7.6 0.8 %first.3 = bf16[64,1024]{1,0:T(8,128)(2,1)S(1)} custom-call(f32[64,1024]{1,0:T(8,128)S(1)} %get-tuple-element.47.refs_0_, bf16[3,1024,1024]{2,1,0:T(8,128)(2,1)S(1)} %get-tuple-element.44.refs_1_.refs_2_.refs_0_.refs_3_.refs_4_.refs_17_, bf16[272,1024]{1,0:T(8,128)(2,1)S(1)} %hold.2.refs_2_.refs_1_.refs_7_.refs_3_), custom_call_target="tpu_custom_call" | custom-call | flops 1000000000 | bytes 2097152 | tf_op jit(solution)/shard_map/first/pallas_call | solution.py:22
  8.4 1.3 %collective-permute-start.2 = (bf16[64,1024]{1,0:T(8,128)(2,1)S(1)}, bf16[64,1024]{1,0:T(8,128)(2,1)S(1)}, u32[]{:S(2)}, u32[]{:S(2)}) collective-permute-start(bf16[64,1024]{1,0:T(8,128)(2,1)S(1)} %first.3), channel_id=1, source_target_pairs={{4,0},{12,8},{20,16},{28,24},{5,1},{13,9},{21,17},{29,25},{6,2},{1... | collective-permute-start | bytes 393224 | tf_op jit(solution)/shard_map/ppermute | solution.py:336
  9.8 0.7 collective-permute-start.5
  10.5 2.5 %collective-permute-done.2.refs_1_ = bf16[64,1024]{1,0:T(8,128)(2,1)S(1)} collective-permute-done((bf16[64,1024]{1,0:T(8,128)(2,1)S(1)}, bf16[64,1024]{1,0:T(8,128)(2,1)S(1)}, u32[]{:S(2)}, u32[]{:S(2)}) %collective-permute-start.2) | collective-permute-done | bytes 131104 | tf_op jit(solution)/shard_map/ppermute | solution.py:336
  13.0 0.7 collective-permute-start.4
  13.7 1.2 %collective-permute-start = (bf16[272,1024]{1,0:T(8,128)(2,1)S(1)}, bf16[272,1024]{1,0:T(8,128)(2,1)S(1)}, u32[]{:S(2)}, u32[]{:S(2)}) collective-permute-start(bf16[272,1024]{1,0:T(8,128)(2,1)S(1)} %hold.2.refs_2_.refs_1_.refs_7_.refs_3_), channel_id=1, source_target_pairs={{0,1},{1,0},{2,3},{3,2},{4,5},{5,4},{6,7},{7,6},{8,9},{9,8},{10,11... | collective-permute-start | bytes 1671176 | tf_op jit(solution)/shard_map/ppermute | solution.py:266
  14.9 0.0 collective-permute-done.5.refs_1_
  14.9 0.7 collective-permute-start.8
  15.5 0.0 collective-permute-done.4.refs_1_
  15.6 0.0 copy-start
  15.6 3.9 %collective-permute-done.1.refs_3_.refs_5_ = bf16[272,1024]{1,0:T(8,128)(2,1)S(1)} collective-permute-done((bf16[272,1024]{1,0:T(8,128)(2,1)S(1)}, bf16[272,1024]{1,0:T(8,128)(2,1)S(1)}, u32[]{:S(2)}, u32[]{:S(2)}) %collective-permute-start.1) | collective-permute-done | bytes 557088 | tf_op jit(solution)/shard_map/ppermute | solution.py:266
  19.6 1.6 %collective-permute-start.6 = (bf16[272,1024]{1,0:T(8,128)(2,1)S(1)}, bf16[272,1024]{1,0:T(8,128)(2,1)S(1)}, u32[]{:S(2)}, u32[]{:S(2)}) collective-permute-start(bf16[272,1024]{1,0:T(8,128)(2,1)S(1)} %hold.3), channel_id=1, source_target_pairs={{0,1},{1,0},{2,3},{3,2},{4,5},{5,4},{6,7},{7,6},{8,9},{9,8},{10,11... | collective-permute-start | bytes 1671176 | tf_op jit(solution)/shard_map/ppermute | solution.py:266
  21.2 0.7 collective-permute-start.7
  21.9 0.8 %root.2 = (bf16[64,1024]{1,0:T(8,128)(2,1)S(1)}, f32[64,1024]{1,0:T(8,128)S(1)}, bf16[64,1024]{1,0:T(8,128)(2,1)S(1)}, bf16[64,1024]{1,0:T(8,128)(2,1)S(1)}) custom-call(f32[64,1024]{1,0:T(8,128)S(1)} %get-tuple-element.57.refs_0_, bf16[64,1024]{1,0:T(8,128)(2,1)S(1)} %collective-permute-done.8.refs_1_, ...), custom_call_target="tpu_custom_call" | custom-call | flops 1000000000 | bytes 2097152 | tf_op jit(solution)/shard_map/root/pallas_call | solution.py:22
  22.7 0.7 collective-permute-start.13
  23.4 0.8 %root.3 = (bf16[64,1024]{1,0:T(8,128)(2,1)S(1)}, f32[64,1024]{1,0:T(8,128)S(1)}, bf16[64,1024]{1,0:T(8,128)(2,1)S(1)}, bf16[64,1024]{1,0:T(8,128)(2,1)S(1)}, bf16[128,1024]{1,0:T(8,128)(2,1)S(1)}) custom-call(f32[64,1024]{1,0:T(8,128)S(1)} %get-tuple-element.56.refs_0_, bf16[64,1024]{1,0:T(8,128)(2,1)S(1)} %collective-permute-done.7.refs_1_, ...), custom_call_target="tpu_custom_call" | custom-call | flops 1000000000 | bytes 2097152 | tf_op jit(solution)/shard_map/root/pallas_call | solution.py:22
  24.2 0.3 collective-permute-start.10
  24.5 0.7 collective-permute-start.12
  25.2 0.7 collective-permute-start.15
  25.9 0.0 collective-permute-done.12.refs_0_
  25.9 0.4 collective-permute-start.9
  26.3 0.0 collective-permute-done.refs_2_.refs_4_
  26.3 0.7 collective-permute-start.14
  27.0 5.2 %collective-permute-done.10.refs_12_.refs_9_ = bf16[128,1024]{1,0:T(8,128)(2,1)S(1)} collective-permute-done((bf16[128,1024]{1,0:T(8,128)(2,1)S(1)}, bf16[128,1024]{1,0:T(8,128)(2,1)S(1)}, u32[]{:S(2)}, u32[]{:S(2)}) %collective-permute-start.10) | collective-permute-done | bytes 262176 | tf_op jit(solution)/shard_map/ppermute | solution.py:266
  32.1 0.8 %collective-permute-start.11 = (bf16[128,1024]{1,0:T(8,128)(2,1)S(1)}, bf16[128,1024]{1,0:T(8,128)(2,1)S(1)}, u32[]{:S(2)}, u32[]{:S(2)}) collective-permute-start(bf16[128,1024]{1,0:T(8,128)(2,1)S(1)} %collective-permute-done.10.refs_12_.refs_9_), channel_id=1, source_target_pairs={{0,1},{1,0},{2,3},{3,2},{4,5},{5,4},{6,7},{7,6},{8,9},{9,8},{10,11... | collective-permute-start | bytes 786440 | tf_op jit(solution)/shard_map/ppermute | solution.py:266
  33.0 0.9 %ready.1 = (f32[2,2,256,256]{3,2,1,0:T(8,128)S(1)}, bf16[3,2,256,256]{3,2,1,0:T(8,128)(2,1)S(1)}) custom-call(bf16[3,1024,1024]{2,1,0:T(8,128)(2,1)S(1)} %get-tuple-element.44.refs_1_.refs_2_.refs_0_.refs_3_.refs_4_.refs_17_, bf16[272,1024]{1,0:T(8,128)(2,1)S(1)} %hold.2.refs_2_.refs_1_.refs_7_.refs_3_, ...), custom_call_target="tpu_custom_call" | custom-call | flops 100000000 | bytes 2097152 | tf_op jit(solution)/shard_map/ready/pallas_call | solution.py:22
  33.9 0.0 collective-permute-done.15.refs_0_
  33.9 1.3 %collective-permute-start.17 = (bf16[64,1024]{1,0:T(8,128)(2,1)S(1)}, bf16[64,1024]{1,0:T(8,128)(2,1)S(1)}, u32[]{:S(2)}, u32[]{:S(2)}) collective-permute-start(bf16[64,1024]{1,0:T(8,128)(2,1)S(1)} %get-tuple-element.71.refs_6_), channel_id=1, source_target_pairs={{0,4},{8,12},{16,20},{24,28},{1,5},{9,13},{17,21},{25,29},{2,6},{1... | collective-permute-start | bytes 393224 | tf_op jit(solution)/shard_map/ppermute | solution.py:382
  35.3 0.0 copy-start.1
  35.3 1.3 %collective-permute-start.16 = (bf16[64,1024]{1,0:T(8,128)(2,1)S(1)}, bf16[64,1024]{1,0:T(8,128)(2,1)S(1)}, u32[]{:S(2)}, u32[]{:S(2)}) collective-permute-start(bf16[64,1024]{1,0:T(8,128)(2,1)S(1)} %get-tuple-element.72.refs_6_), channel_id=1, source_target_pairs={{0,4},{8,12},{16,20},{24,28},{1,5},{9,13},{17,21},{25,29},{2,6},{1... | collective-permute-start | bytes 393224 | tf_op jit(solution)/shard_map/ppermute | solution.py:382
  36.6 14.4 %collective-permute-done.17.refs_1_ = bf16[64,1024]{1,0:T(8,128)(2,1)S(1)} collective-permute-done((bf16[64,1024]{1,0:T(8,128)(2,1)S(1)}, bf16[64,1024]{1,0:T(8,128)(2,1)S(1)}, u32[]{:S(2)}, u32[]{:S(2)}) %collective-permute-start.17) | collective-permute-done | bytes 131104 | tf_op jit(solution)/shard_map/ppermute | solution.py:382
  51.0 2.1 %last.2 = (bf16[4,64,256]{2,1,0:T(8,128)(2,1)S(1)}, bf16[4,64,256]{2,1,0:T(8,128)(2,1)S(1)}, bf16[4,64,256]{2,1,0:T(8,128)(2,1)S(1)}, bf16[4,64,256]{2,1,0:T(8,128)(2,1)S(1)}) custom-call(s32[3]{0:T(128)S(1)} %copy-done.1, bf16[64,1024]{1,0:T(8,128)(2,1)S(1)} %collective-permute-done.17.refs_1_, ...), custom_call_target="tpu_custom_call" | custom-call | flops 1000000000 | bytes 2097152 | tf_op jit(solution)/shard_map/last/pallas_call | solution.py:22
  53.0 1.6 %collective-permute-start.21 = (bf16[4,64,256]{2,1,0:T(8,128)(2,1)S(1)}, bf16[4,64,256]{2,1,0:T(8,128)(2,1)S(1)}, u32[]{:S(2)}, u32[]{:S(2)}) collective-permute-start(bf16[4,64,256]{2,1,0:T(8,128)(2,1)S(1)} %get-tuple-element.81), channel_id=1, source_target_pairs={{0,1},{1,0},{2,3},{3,2},{4,5},{5,4},{6,7},{7,6},{8,9},{9,8},{10,11... | collective-permute-start | bytes 393224 | tf_op jit(solution)/shard_map/ppermute | solution.py:266
  54.7 0.0 collective-permute-done.9.refs_11_.refs_8_
  54.7 1.7 %collective-permute-start.23 = (bf16[4,64,256]{2,1,0:T(8,128)(2,1)S(1)}, bf16[4,64,256]{2,1,0:T(8,128)(2,1)S(1)}, u32[]{:S(2)}, u32[]{:S(2)}) collective-permute-start(bf16[4,64,256]{2,1,0:T(8,128)(2,1)S(1)} %get-tuple-element.83), channel_id=1, source_target_pairs={{0,3},{1,2},{2,1},{3,0},{4,7},{5,6},{6,5},{7,4},{8,11},{9,10},{10,... | collective-permute-start | bytes 393224 | tf_op jit(solution)/shard_map/ppermute | solution.py:266
  56.4 2.1 %last.3 = (bf16[4,64,256]{2,1,0:T(8,128)(2,1)S(1)}, bf16[4,64,256]{2,1,0:T(8,128)(2,1)S(1)}, bf16[4,64,256]{2,1,0:T(8,128)(2,1)S(1)}, bf16[4,64,256]{2,1,0:T(8,128)(2,1)S(1)}) custom-call(s32[3]{0:T(128)S(1)} %copy-done.1, bf16[64,1024]{1,0:T(8,128)(2,1)S(1)} %collective-permute-done.16.refs_1_, bf16[64,1024]{1,0:T(8,128)(2,1)S(1)} %get-tuple-element.61.refs_1_.refs_2_, ...), custom_call_target="tpu_custom_call" | custom-call | flops 1000000000 | bytes 2097152 | tf_op jit(solution)/shard_map/last/pallas_call | solution.py:22
  58.5 0.2 collective-permute-start.18
  58.7 0.0 collective-permute-start.19
  58.7 2.0 %collective-permute-start.20 = (bf16[4,64,256]{2,1,0:T(8,128)(2,1)S(1)}, bf16[4,64,256]{2,1,0:T(8,128)(2,1)S(1)}, u32[]{:S(2)}, u32[]{:S(2)}) collective-permute-start(bf16[4,64,256]{2,1,0:T(8,128)(2,1)S(1)} %get-tuple-element.80), channel_id=1, source_target_pairs={{0,3},{1,2},{2,1},{3,0},{4,7},{5,6},{6,5},{7,4},{8,11},{9,10},{10,... | collective-permute-start | bytes 393224 | tf_op jit(solution)/shard_map/ppermute | solution.py:266
  60.7 2.5 %collective-permute-done.23.refs_14_ = bf16[4,64,256]{2,1,0:T(8,128)(2,1)S(1)} collective-permute-done((bf16[4,64,256]{2,1,0:T(8,128)(2,1)S(1)}, bf16[4,64,256]{2,1,0:T(8,128)(2,1)S(1)}, u32[]{:S(2)}, u32[]{:S(2)}) %collective-permute-start.23) | collective-permute-done | bytes 131104 | tf_op jit(solution)/shard_map/ppermute | solution.py:266
  63.2 1.3 %counts.2 = (f32[3,256,1024]{2,1,0:T(8,128)S(1)}, f32[3,256,256]{2,1,0:T(8,128)S(1)}) custom-call(s32[3]{0:T(128)S(1)} %copy-done.1, f32[2,2,256,256]{3,2,1,0:T(8,128)S(1)} %get-tuple-element.54.refs_6_.refs_1_, bf16[3,2,256,256]{3,2,1,0:T(8,128)(2,1)S(1)} %get-tuple-element.55.refs_2_, bf16[272,1024]{1,0:T(8,128)(2,1)S(1)} %hold.2.refs_2_.refs_1_.refs_7_.refs_3_, ...), custom_call_target="tpu_custom_call" | custom-call | flops 1000000000 | bytes 2097152 | tf_op jit(solution)/shard_map/counts/pallas_call | solution.py:22
  64.5 0.9 %collective-permute-done.19.refs_13_ = bf16[4,64,256]{2,1,0:T(8,128)(2,1)S(1)} collective-permute-done((bf16[4,64,256]{2,1,0:T(8,128)(2,1)S(1)}, bf16[4,64,256]{2,1,0:T(8,128)(2,1)S(1)}, u32[]{:S(2)}, u32[]{:S(2)}) %collective-permute-start.19) | collective-permute-done | bytes 131104 | tf_op jit(solution)/shard_map/ppermute | solution.py:266
  65.4 3.0 %collective-permute-done.20.refs_14_ = bf16[4,64,256]{2,1,0:T(8,128)(2,1)S(1)} collective-permute-done((bf16[4,64,256]{2,1,0:T(8,128)(2,1)S(1)}, bf16[4,64,256]{2,1,0:T(8,128)(2,1)S(1)}, u32[]{:S(2)}, u32[]{:S(2)}) %collective-permute-start.20) | collective-permute-done | bytes 131104 | tf_op jit(solution)/shard_map/ppermute | solution.py:266
  68.4 2.3 %counts.3 = (bf16[3,256,1024]{2,1,0:T(8,128)(2,1)}, bf16[3,256,256]{2,1,0:T(8,128)(2,1)}) custom-call(s32[3]{0:T(128)S(1)} %copy-done.1, f32[2,2,256,256]{3,2,1,0:T(8,128)S(1)} %get-tuple-element.54.refs_6_.refs_1_, bf16[3,2,256,256]{3,2,1,0:T(8,128)(2,1)S(1)} %get-tuple-element.55.refs_2_, bf16[272,1024]{1,0:T(8,128)(2,1)S(1)} %hold.2.refs_2_.refs_1_.refs_7_.refs_3_, ...), custom_call_target="tpu_custom_call" | custom-call | flops 1000000000 | bytes 2097152 | tf_op jit(solution)/shard_map/counts/pallas_call | solution.py:22
  (25 shorter events, 0.2 us)
Async XLA Ops:
  6.0 13.5 %collective-permute-start.1 = (bf16[272,1024]{1,0:T(8,128)(2,1)S(1)}, bf16[272,1024]{1,0:T(8,128)(2,1)S(1)}, u32[]{:S(2)}, u32[]{:S(2)}) collective-permute-start(bf16[272,1024]{1,0:T(8,128)(2,1)S(1)} %hold.2.refs_2_.refs_1_.refs_7_.refs_3_), channel_id=1, source_target_pairs={{0,2},{1,3},{2,0},{3,1},{4,6},{5,7},{6,4},{7,5},{8,10},{9,11},{10,... | collective-permute-start | bytes 1671176 | tf_op jit(solution)/shard_map/ppermute | solution.py:266
  6.3 3.5 %collective-permute-start.3 = (bf16[64,1024]{1,0:T(8,128)(2,1)S(1)}, bf16[64,1024]{1,0:T(8,128)(2,1)S(1)}, u32[]{:S(2)}, u32[]{:S(2)}) collective-permute-start(bf16[64,1024]{1,0:T(8,128)(2,1)S(1)} %first.2.refs_1_), channel_id=1, source_target_pairs={{4,0},{12,8},{20,16},{28,24},{5,1},{13,9},{21,17},{29,25},{6,2},{1... | collective-permute-start | bytes 393224 | tf_op jit(solution)/shard_map/ppermute | solution.py:336
  8.4 4.6 %collective-permute-start.2 = (bf16[64,1024]{1,0:T(8,128)(2,1)S(1)}, bf16[64,1024]{1,0:T(8,128)(2,1)S(1)}, u32[]{:S(2)}, u32[]{:S(2)}) collective-permute-start(bf16[64,1024]{1,0:T(8,128)(2,1)S(1)} %first.3), channel_id=1, source_target_pairs={{4,0},{12,8},{20,16},{28,24},{5,1},{13,9},{21,17},{29,25},{6,2},{1... | collective-permute-start | bytes 393224 | tf_op jit(solution)/shard_map/ppermute | solution.py:336
  9.8 5.1 %collective-permute-start.5 = (bf16[64,1024]{1,0:T(8,128)(2,1)S(1)}, bf16[64,1024]{1,0:T(8,128)(2,1)S(1)}, u32[]{:S(2)}, u32[]{:S(2)}) collective-permute-start(bf16[64,1024]{1,0:T(8,128)(2,1)S(1)} %get-tuple-element.48.refs_3_), channel_id=1, source_target_pairs={{8,0},{24,16},{9,1},{25,17},{10,2},{26,18},{11,3},{27,19}} | collective-permute-start | bytes 393224 | tf_op jit(solution)/shard_map/ppermute | solution.py:336
  13.0 2.5 %collective-permute-start.4 = (bf16[64,1024]{1,0:T(8,128)(2,1)S(1)}, bf16[64,1024]{1,0:T(8,128)(2,1)S(1)}, u32[]{:S(2)}, u32[]{:S(2)}) collective-permute-start(bf16[64,1024]{1,0:T(8,128)(2,1)S(1)} %get-tuple-element.50), channel_id=1, source_target_pairs={{8,0},{24,16},{9,1},{25,17},{10,2},{26,18},{11,3},{27,19}} | collective-permute-start | bytes 393224 | tf_op jit(solution)/shard_map/ppermute | solution.py:336
  13.7 12.6 %collective-permute-start = (bf16[272,1024]{1,0:T(8,128)(2,1)S(1)}, bf16[272,1024]{1,0:T(8,128)(2,1)S(1)}, u32[]{:S(2)}, u32[]{:S(2)}) collective-permute-start(bf16[272,1024]{1,0:T(8,128)(2,1)S(1)} %hold.2.refs_2_.refs_1_.refs_7_.refs_3_), channel_id=1, source_target_pairs={{0,1},{1,0},{2,3},{3,2},{4,5},{5,4},{6,7},{7,6},{8,9},{9,8},{10,11... | collective-permute-start | bytes 1671176 | tf_op jit(solution)/shard_map/ppermute | solution.py:266
  14.9 7.0 %collective-permute-start.8 = (bf16[64,1024]{1,0:T(8,128)(2,1)S(1)}, bf16[64,1024]{1,0:T(8,128)(2,1)S(1)}, u32[]{:S(2)}, u32[]{:S(2)}) collective-permute-start(bf16[64,1024]{1,0:T(8,128)(2,1)S(1)} %get-tuple-element.52.refs_3_), channel_id=1, source_target_pairs={{16,0},{17,1},{18,2},{19,3}} | collective-permute-start | bytes 393224 | tf_op jit(solution)/shard_map/ppermute | solution.py:349
  15.6 6.3 %copy-start = (f32[1024]{0:T(1024)S(1)}, f32[1024]{0:T(1024)}, u32[]{:S(2)}) copy-start(f32[1024]{0:T(1024)} %param.7) | copy-start | bytes 12292
  19.6 13.4 %collective-permute-start.6 = (bf16[272,1024]{1,0:T(8,128)(2,1)S(1)}, bf16[272,1024]{1,0:T(8,128)(2,1)S(1)}, u32[]{:S(2)}, u32[]{:S(2)}) collective-permute-start(bf16[272,1024]{1,0:T(8,128)(2,1)S(1)} %hold.3), channel_id=1, source_target_pairs={{0,1},{1,0},{2,3},{3,2},{4,5},{5,4},{6,7},{7,6},{8,9},{9,8},{10,11... | collective-permute-start | bytes 1671176 | tf_op jit(solution)/shard_map/ppermute | solution.py:266
  21.2 2.2 %collective-permute-start.7 = (bf16[64,1024]{1,0:T(8,128)(2,1)S(1)}, bf16[64,1024]{1,0:T(8,128)(2,1)S(1)}, u32[]{:S(2)}, u32[]{:S(2)}) collective-permute-start(bf16[64,1024]{1,0:T(8,128)(2,1)S(1)} %get-tuple-element.53.refs_1_), channel_id=1, source_target_pairs={{16,0},{17,1},{18,2},{19,3}} | collective-permute-start | bytes 393224 | tf_op jit(solution)/shard_map/ppermute | solution.py:349
  22.7 2.5 %collective-permute-start.13 = (bf16[64,1024]{1,0:T(8,128)(2,1)S(1)}, bf16[64,1024]{1,0:T(8,128)(2,1)S(1)}, u32[]{:S(2)}, u32[]{:S(2)}) collective-permute-start(bf16[64,1024]{1,0:T(8,128)(2,1)S(1)} %get-tuple-element.64.refs_5_), channel_id=1, source_target_pairs={{0,16},{1,17},{2,18},{3,19}} | collective-permute-start | bytes 393224 | tf_op jit(solution)/shard_map/ppermute | solution.py:372
  24.2 8.0 %collective-permute-start.10 = (bf16[128,1024]{1,0:T(8,128)(2,1)S(1)}, bf16[128,1024]{1,0:T(8,128)(2,1)S(1)}, u32[]{:S(2)}, u32[]{:S(2)}) collective-permute-start(bf16[128,1024]{1,0:T(8,128)(2,1)S(1)} %get-tuple-element.59.refs_10_.refs_7_), channel_id=1, source_target_pairs={{0,2},{1,3},{2,0},{3,1},{4,6},{5,7},{6,4},{7,5},{8,10},{9,11},{10,... | collective-permute-start | bytes 786440 | tf_op jit(solution)/shard_map/ppermute | solution.py:266
  24.5 1.4 %collective-permute-start.12 = (bf16[64,1024]{1,0:T(8,128)(2,1)S(1)}, bf16[64,1024]{1,0:T(8,128)(2,1)S(1)}, u32[]{:S(2)}, u32[]{:S(2)}) collective-permute-start(bf16[64,1024]{1,0:T(8,128)(2,1)S(1)} %get-tuple-element.60.refs_5_), channel_id=1, source_target_pairs={{0,16},{1,17},{2,18},{3,19}} | collective-permute-start | bytes 393224 | tf_op jit(solution)/shard_map/ppermute | solution.py:372
  25.2 8.7 %collective-permute-start.15 = (bf16[64,1024]{1,0:T(8,128)(2,1)S(1)}, bf16[64,1024]{1,0:T(8,128)(2,1)S(1)}, u32[]{:S(2)}, u32[]{:S(2)}) collective-permute-start(bf16[64,1024]{1,0:T(8,128)(2,1)S(1)} %get-tuple-element.67.refs_6_.refs_5_), channel_id=1, source_target_pairs={{0,8},{16,24},{1,9},{17,25},{2,10},{18,26},{3,11},{19,27}} | collective-permute-start | bytes 393224 | tf_op jit(solution)/shard_map/ppermute | solution.py:372
  25.9 28.8 %collective-permute-start.9 = (bf16[128,1024]{1,0:T(8,128)(2,1)S(1)}, bf16[128,1024]{1,0:T(8,128)(2,1)S(1)}, u32[]{:S(2)}, u32[]{:S(2)}) collective-permute-start(bf16[128,1024]{1,0:T(8,128)(2,1)S(1)} %get-tuple-element.59.refs_10_.refs_7_), channel_id=1, source_target_pairs={{0,1},{1,0},{2,3},{3,2},{4,5},{5,4},{6,7},{7,6},{8,9},{9,8},{10,11... | collective-permute-start | bytes 786440 | tf_op jit(solution)/shard_map/ppermute | solution.py:266
  26.3 9.0 %collective-permute-start.14 = (bf16[64,1024]{1,0:T(8,128)(2,1)S(1)}, bf16[64,1024]{1,0:T(8,128)(2,1)S(1)}, u32[]{:S(2)}, u32[]{:S(2)}) collective-permute-start(bf16[64,1024]{1,0:T(8,128)(2,1)S(1)} %get-tuple-element.68.refs_5_), channel_id=1, source_target_pairs={{0,8},{16,24},{1,9},{17,25},{2,10},{18,26},{3,11},{19,27}} | collective-permute-start | bytes 393224 | tf_op jit(solution)/shard_map/ppermute | solution.py:372
  32.1 24.3 %collective-permute-start.11 = (bf16[128,1024]{1,0:T(8,128)(2,1)S(1)}, bf16[128,1024]{1,0:T(8,128)(2,1)S(1)}, u32[]{:S(2)}, u32[]{:S(2)}) collective-permute-start(bf16[128,1024]{1,0:T(8,128)(2,1)S(1)} %collective-permute-done.10.refs_12_.refs_9_), channel_id=1, source_target_pairs={{0,1},{1,0},{2,3},{3,2},{4,5},{5,4},{6,7},{7,6},{8,9},{9,8},{10,11... | collective-permute-start | bytes 786440 | tf_op jit(solution)/shard_map/ppermute | solution.py:266
  33.9 17.0 %collective-permute-start.17 = (bf16[64,1024]{1,0:T(8,128)(2,1)S(1)}, bf16[64,1024]{1,0:T(8,128)(2,1)S(1)}, u32[]{:S(2)}, u32[]{:S(2)}) collective-permute-start(bf16[64,1024]{1,0:T(8,128)(2,1)S(1)} %get-tuple-element.71.refs_6_), channel_id=1, source_target_pairs={{0,4},{8,12},{16,20},{24,28},{1,5},{9,13},{17,21},{25,29},{2,6},{1... | collective-permute-start | bytes 393224 | tf_op jit(solution)/shard_map/ppermute | solution.py:382
  35.3 15.7 %copy-start.1 = (s32[3]{0:T(128)S(1)}, s32[3]{0:T(128)}, u32[]{:S(2)}) copy-start(s32[3]{0:T(128)} %refs_0_.9) | copy-start | bytes 40
  35.3 21.1 %collective-permute-start.16 = (bf16[64,1024]{1,0:T(8,128)(2,1)S(1)}, bf16[64,1024]{1,0:T(8,128)(2,1)S(1)}, u32[]{:S(2)}, u32[]{:S(2)}) collective-permute-start(bf16[64,1024]{1,0:T(8,128)(2,1)S(1)} %get-tuple-element.72.refs_6_), channel_id=1, source_target_pairs={{0,4},{8,12},{16,20},{24,28},{1,5},{9,13},{17,21},{25,29},{2,6},{1... | collective-permute-start | bytes 393224 | tf_op jit(solution)/shard_map/ppermute | solution.py:382
  53.0 5.7 %collective-permute-start.21 = (bf16[4,64,256]{2,1,0:T(8,128)(2,1)S(1)}, bf16[4,64,256]{2,1,0:T(8,128)(2,1)S(1)}, u32[]{:S(2)}, u32[]{:S(2)}) collective-permute-start(bf16[4,64,256]{2,1,0:T(8,128)(2,1)S(1)} %get-tuple-element.81), channel_id=1, source_target_pairs={{0,1},{1,0},{2,3},{3,2},{4,5},{5,4},{6,7},{7,6},{8,9},{9,8},{10,11... | collective-permute-start | bytes 393224 | tf_op jit(solution)/shard_map/ppermute | solution.py:266
  54.7 6.0 %collective-permute-start.22 = (bf16[4,64,256]{2,1,0:T(8,128)(2,1)S(1)}, bf16[4,64,256]{2,1,0:T(8,128)(2,1)S(1)}, u32[]{:S(2)}, u32[]{:S(2)}) collective-permute-start(bf16[4,64,256]{2,1,0:T(8,128)(2,1)S(1)} %get-tuple-element.82), channel_id=1, source_target_pairs={{0,2},{1,3},{2,0},{3,1},{4,6},{5,7},{6,4},{7,5},{8,10},{9,11},{10,... | collective-permute-start | bytes 393224 | tf_op jit(solution)/shard_map/ppermute | solution.py:266
  54.7 8.5 %collective-permute-start.23 = (bf16[4,64,256]{2,1,0:T(8,128)(2,1)S(1)}, bf16[4,64,256]{2,1,0:T(8,128)(2,1)S(1)}, u32[]{:S(2)}, u32[]{:S(2)}) collective-permute-start(bf16[4,64,256]{2,1,0:T(8,128)(2,1)S(1)} %get-tuple-element.83), channel_id=1, source_target_pairs={{0,3},{1,2},{2,1},{3,0},{4,7},{5,6},{6,5},{7,4},{8,11},{9,10},{10,... | collective-permute-start | bytes 393224 | tf_op jit(solution)/shard_map/ppermute | solution.py:266
  58.5 6.0 %collective-permute-start.18 = (bf16[4,64,256]{2,1,0:T(8,128)(2,1)S(1)}, bf16[4,64,256]{2,1,0:T(8,128)(2,1)S(1)}, u32[]{:S(2)}, u32[]{:S(2)}) collective-permute-start(bf16[4,64,256]{2,1,0:T(8,128)(2,1)S(1)} %get-tuple-element.78), channel_id=1, source_target_pairs={{0,1},{1,0},{2,3},{3,2},{4,5},{5,4},{6,7},{7,6},{8,9},{9,8},{10,11... | collective-permute-start | bytes 393224 | tf_op jit(solution)/shard_map/ppermute | solution.py:266
  58.7 6.7 %collective-permute-start.19 = (bf16[4,64,256]{2,1,0:T(8,128)(2,1)S(1)}, bf16[4,64,256]{2,1,0:T(8,128)(2,1)S(1)}, u32[]{:S(2)}, u32[]{:S(2)}) collective-permute-start(bf16[4,64,256]{2,1,0:T(8,128)(2,1)S(1)} %get-tuple-element.79), channel_id=1, source_target_pairs={{0,2},{1,3},{2,0},{3,1},{4,6},{5,7},{6,4},{7,5},{8,10},{9,11},{10,... | collective-permute-start | bytes 393224 | tf_op jit(solution)/shard_map/ppermute | solution.py:266
  58.7 9.6 %collective-permute-start.20 = (bf16[4,64,256]{2,1,0:T(8,128)(2,1)S(1)}, bf16[4,64,256]{2,1,0:T(8,128)(2,1)S(1)}, u32[]{:S(2)}, u32[]{:S(2)}) collective-permute-start(bf16[4,64,256]{2,1,0:T(8,128)(2,1)S(1)} %get-tuple-element.80), channel_id=1, source_target_pairs={{0,3},{1,2},{2,1},{3,0},{4,7},{5,6},{6,5},{7,4},{8,11},{9,10},{10,... | collective-permute-start | bytes 393224 | tf_op jit(solution)/shard_map/ppermute | solution.py:266

commit v2 on v1

--- a/solution.py
+++ b/solution.py
@@ -10,7 +10,7 @@
 BF16 = jnp.bfloat16
 PAD = 16
 CHUNKS = 2
-WORK = 10*10**8
+WORK = 13*10**8
 LIMIT = 24 * 2**20
 VM = pl.BlockSpec(memory_space=pltpu.VMEM)
 SM = pl.BlockSpec(memory_space=pltpu.SMEM)
@@ -375,7 +375,7 @@
                 "settle",
                 (recv, top_lam[c], top_msg[c], weights, ratio[c], post[c]),
                 (half(BF16), half(BF16)),
-                after=post[:c][-1:] + ([raw_own] if level == 1 and c == 0 else []),
+                after=post[:c][-1:] + (all_lams if level == 1 and c == CHUNKS - 1 else []),
             )
     own_posts = []
     for c in every:
@@ -387,7 +387,7 @@
             (pltpu.VMEM((nodes + 1, part, share), BF16),) * groups,
             (pltpu.VMEM((nodes + 1, part, states), BF16),),
             [SM] + [VM] * 8,
-            after=own_posts[-1][:1] + all_tops if c > 0 else (),
+            after=[own_posts[-1][0], *all_tops, raw_own] if c > 0 else [],
         )
         order = range(1, groups)
         moved = {mask: swap(packs[mask], mask) for mask in order}

time: 71 us -> 66.9 us (0.942)
  the two profiles are of different devices: /device:TPU:23 before, /device:TPU:13 now
where the time goes in v2:
time: 66.9 us; the launch traced here: 66.3 us
  starting transfers between devices  26.9 us (40%)
  waiting for transfers between devices  21.9 us (33%)
  Pallas kernels  16.5 us (25%)
  between operations  0.95 us (1%)
    pallas_call x20, Pallas kernels, run(): pl.pallas_call(lambda *refs: body(*refs[:count], *refs[idle:]), name=name...  16.5 us
    ppermute x12, starting transfers between devices, swap(): lax.ppermute(value, 'rows', [(s, s ^ mask) for s in range(lax.axis_size('...  16.3 us
    ppermute x12, waiting for transfers between devices, swap(): lax.ppermute(value, 'rows', [(s, s ^ mask) for s in range(lax.axis_size('...  13.1 us
    ppermute x2, waiting for transfers between devices, per_device(): recv = lax.ppermute(post[c], 'leaf', down_pairs(0))  7.61 us
    ppermute x4, starting transfers between devices, per_device(): recv = lax.ppermute(send[c], 'leaf', up_pairs(level))  3.96 us
    ppermute x4, starting transfers between devices, per_device(): recv = lax.ppermute(post[c], 'leaf', down_pairs(level))  2.67 us
    ppermute x2, starting transfers between devices, per_device(): recv = lax.ppermute(post[c], 'leaf', down_pairs(0))  2.58 us
  transfers between devices with their start and end apart: 24, of which 7 were waited for; matrix products, arithmetic and copies ran while one was open for 0% of the time, Pallas kernels for 13%

profile of v2, /device:TPU:13, one launch (start us, length us, event | category | flops | bytes accessed | tf_op | source)
XLA Modules:
  0.0 66.3 jit_solution(912608532047971921)
XLA Ops:
  0.6 4.5 %prep.1 = (bf16[3,1024,1024]{2,1,0:T(8,128)(2,1)S(1)}, bf16[272,1024]{1,0:T(8,128)(2,1)S(1)}, f32[2,128,1024]{2,1,0:T(8,128)S(1)}, f32[64,1024]{1,0:T(8,128)S(1)}, f32[64,1024]{1,0:T(8,128)S(1)}) custom-call(s32[3]{0:T(128)} %refs_0_.9, s32[3,128]{1,0:T(4,128)} %refs_1_.1, bf16[3,256,1024]{2,1,0:T(8,128)(2,1)} %refs_2_.1, bf16[3,1024,1024]{2,1,0:T(8,128)(2,1)} %refs_3_.1), custom_call_target="tpu_custom_call" | custom-call | flops 1300000000 | bytes 2097152 | tf_op jit(solution)/shard_map/prep/pallas_call | solution.py:22
  5.1 0.8 %first.2.refs_1_ = bf16[64,1024]{1,0:T(8,128)(2,1)S(1)} custom-call(f32[64,1024]{1,0:T(8,128)S(1)} %get-tuple-element.46.refs_0_, bf16[3,1024,1024]{2,1,0:T(8,128)(2,1)S(1)} %get-tuple-element.44.refs_1_.refs_2_.refs_0_.refs_3_.refs_4_.refs_17_), custom_call_target="tpu_custom_call" | custom-call | flops 1300000000 | bytes 2097152 | tf_op jit(solution)/shard_map/first/pallas_call | solution.py:22
  6.0 1.3 %collective-permute-start.3 = (bf16[64,1024]{1,0:T(8,128)(2,1)S(1)}, bf16[64,1024]{1,0:T(8,128)(2,1)S(1)}, u32[]{:S(2)}, u32[]{:S(2)}) collective-permute-start(bf16[64,1024]{1,0:T(8,128)(2,1)S(1)} %first.2.refs_1_), channel_id=1, source_target_pairs={{4,0},{12,8},{20,16},{28,24},{5,1},{13,9},{21,17},{29,25},{6,2},{1... | collective-permute-start | bytes 393224 | tf_op jit(solution)/shard_map/ppermute | solution.py:336
  7.3 1.3 %collective-permute-start.1 = (bf16[272,1024]{1,0:T(8,128)(2,1)S(1)}, bf16[272,1024]{1,0:T(8,128)(2,1)S(1)}, u32[]{:S(2)}, u32[]{:S(2)}) collective-permute-start(bf16[272,1024]{1,0:T(8,128)(2,1)S(1)} %hold.2.refs_2_.refs_1_.refs_7_.refs_3_), channel_id=1, source_target_pairs={{0,2},{1,3},{2,0},{3,1},{4,6},{5,7},{6,4},{7,5},{8,10},{9,11},{10,... | collective-permute-start | bytes 1671176 | tf_op jit(solution)/shard_map/ppermute | solution.py:266
  8.6 0.8 %first.3 = bf16[64,1024]{1,0:T(8,128)(2,1)S(1)} custom-call(f32[64,1024]{1,0:T(8,128)S(1)} %get-tuple-element.47.refs_0_, bf16[3,1024,1024]{2,1,0:T(8,128)(2,1)S(1)} %get-tuple-element.44.refs_1_.refs_2_.refs_0_.refs_3_.refs_4_.refs_17_, bf16[272,1024]{1,0:T(8,128)(2,1)S(1)} %hold.2.refs_2_.refs_1_.refs_7_.refs_3_), custom_call_target="tpu_custom_call" | custom-call | flops 1300000000 | bytes 2097152 | tf_op jit(solution)/shard_map/first/pallas_call | solution.py:22
  9.4 1.3 %collective-permute-start.2 = (bf16[64,1024]{1,0:T(8,128)(2,1)S(1)}, bf16[64,1024]{1,0:T(8,128)(2,1)S(1)}, u32[]{:S(2)}, u32[]{:S(2)}) collective-permute-start(bf16[64,1024]{1,0:T(8,128)(2,1)S(1)} %first.3), channel_id=1, source_target_pairs={{4,0},{12,8},{20,16},{28,24},{5,1},{13,9},{21,17},{29,25},{6,2},{1... | collective-permute-start | bytes 393224 | tf_op jit(solution)/shard_map/ppermute | solution.py:336
  10.7 0.0 collective-permute-done.3.refs_1_
  10.7 0.7 %collective-permute-start.5 = (bf16[64,1024]{1,0:T(8,128)(2,1)S(1)}, bf16[64,1024]{1,0:T(8,128)(2,1)S(1)}, u32[]{:S(2)}, u32[]{:S(2)}) collective-permute-start(bf16[64,1024]{1,0:T(8,128)(2,1)S(1)} %get-tuple-element.48.refs_3_), channel_id=1, source_target_pairs={{8,0},{24,16},{9,1},{25,17},{10,2},{26,18},{11,3},{27,19}} | collective-permute-start | bytes 393224 | tf_op jit(solution)/shard_map/ppermute | solution.py:336
  11.4 1.2 %collective-permute-done.2.refs_1_ = bf16[64,1024]{1,0:T(8,128)(2,1)S(1)} collective-permute-done((bf16[64,1024]{1,0:T(8,128)(2,1)S(1)}, bf16[64,1024]{1,0:T(8,128)(2,1)S(1)}, u32[]{:S(2)}, u32[]{:S(2)}) %collective-permute-start.2) | collective-permute-done | bytes 131104 | tf_op jit(solution)/shard_map/ppermute | solution.py:336
  12.6 0.7 collective-permute-start.4
  13.3 1.9 %collective-permute-start = (bf16[272,1024]{1,0:T(8,128)(2,1)S(1)}, bf16[272,1024]{1,0:T(8,128)(2,1)S(1)}, u32[]{:S(2)}, u32[]{:S(2)}) collective-permute-start(bf16[272,1024]{1,0:T(8,128)(2,1)S(1)} %hold.2.refs_2_.refs_1_.refs_7_.refs_3_), channel_id=1, source_target_pairs={{0,1},{1,0},{2,3},{3,2},{4,5},{5,4},{6,7},{7,6},{8,9},{9,8},{10,11... | collective-permute-start | bytes 1671176 | tf_op jit(solution)/shard_map/ppermute | solution.py:266
  15.2 0.7 collective-permute-start.8
  15.9 0.0 copy-start
  15.9 0.7 %collective-permute-start.7 = (bf16[64,1024]{1,0:T(8,128)(2,1)S(1)}, bf16[64,1024]{1,0:T(8,128)(2,1)S(1)}, u32[]{:S(2)}, u32[]{:S(2)}) collective-permute-start(bf16[64,1024]{1,0:T(8,128)(2,1)S(1)} %get-tuple-element.53.refs_1_), channel_id=1, source_target_pairs={{16,0},{17,1},{18,2},{19,3}} | collective-permute-start | bytes 393224 | tf_op jit(solution)/shard_map/ppermute | solution.py:349
  16.6 4.0 %collective-permute-done.1.refs_3_.refs_9_.refs_5_ = bf16[272,1024]{1,0:T(8,128)(2,1)S(1)} collective-permute-done((bf16[272,1024]{1,0:T(8,128)(2,1)S(1)}, bf16[272,1024]{1,0:T(8,128)(2,1)S(1)}, u32[]{:S(2)}, u32[]{:S(2)}) %collective-permute-start.1) | collective-permute-done | bytes 557088 | tf_op jit(solution)/shard_map/ppermute | solution.py:266
  20.6 1.9 %collective-permute-start.6 = (bf16[272,1024]{1,0:T(8,128)(2,1)S(1)}, bf16[272,1024]{1,0:T(8,128)(2,1)S(1)}, u32[]{:S(2)}, u32[]{:S(2)}) collective-permute-start(bf16[272,1024]{1,0:T(8,128)(2,1)S(1)} %hold.3), channel_id=1, source_target_pairs={{0,1},{1,0},{2,3},{3,2},{4,5},{5,4},{6,7},{7,6},{8,9},{9,8},{10,11... | collective-permute-start | bytes 1671176 | tf_op jit(solution)/shard_map/ppermute | solution.py:266
  22.5 0.0 collective-permute-done.8.refs_1_
  22.5 0.8 %root.2 = (bf16[64,1024]{1,0:T(8,128)(2,1)S(1)}, f32[64,1024]{1,0:T(8,128)S(1)}, bf16[64,1024]{1,0:T(8,128)(2,1)S(1)}, bf16[64,1024]{1,0:T(8,128)(2,1)S(1)}) custom-call(f32[64,1024]{1,0:T(8,128)S(1)} %get-tuple-element.57.refs_0_, bf16[64,1024]{1,0:T(8,128)(2,1)S(1)} %collective-permute-done.8.refs_1_, ...), custom_call_target="tpu_custom_call" | custom-call | flops 1300000000 | bytes 2097152 | tf_op jit(solution)/shard_map/root/pallas_call | solution.py:22
  23.3 0.7 %collective-permute-start.13 = (bf16[64,1024]{1,0:T(8,128)(2,1)S(1)}, bf16[64,1024]{1,0:T(8,128)(2,1)S(1)}, u32[]{:S(2)}, u32[]{:S(2)}) collective-permute-start(bf16[64,1024]{1,0:T(8,128)(2,1)S(1)} %get-tuple-element.64.refs_5_), channel_id=1, source_target_pairs={{0,16},{1,17},{2,18},{3,19}} | collective-permute-start | bytes 393224 | tf_op jit(solution)/shard_map/ppermute | solution.py:372
  24.0 0.8 %root.3 = (bf16[64,1024]{1,0:T(8,128)(2,1)S(1)}, f32[64,1024]{1,0:T(8,128)S(1)}, bf16[64,1024]{1,0:T(8,128)(2,1)S(1)}, bf16[64,1024]{1,0:T(8,128)(2,1)S(1)}, bf16[128,1024]{1,0:T(8,128)(2,1)S(1)}) custom-call(f32[64,1024]{1,0:T(8,128)S(1)} %get-tuple-element.56.refs_0_, bf16[64,1024]{1,0:T(8,128)(2,1)S(1)} %collective-permute-done.7.refs_1_, ...), custom_call_target="tpu_custom_call" | custom-call | flops 1300000000 | bytes 2097152 | tf_op jit(solution)/shard_map/root/pallas_call | solution.py:22
  24.8 0.7 %collective-permute-start.12 = (bf16[64,1024]{1,0:T(8,128)(2,1)S(1)}, bf16[64,1024]{1,0:T(8,128)(2,1)S(1)}, u32[]{:S(2)}, u32[]{:S(2)}) collective-permute-start(bf16[64,1024]{1,0:T(8,128)(2,1)S(1)} %get-tuple-element.60.refs_5_), channel_id=1, source_target_pairs={{0,16},{1,17},{2,18},{3,19}} | collective-permute-start | bytes 393224 | tf_op jit(solution)/shard_map/ppermute | solution.py:372
  25.5 1.3 %collective-permute-start.10 = (bf16[128,1024]{1,0:T(8,128)(2,1)S(1)}, bf16[128,1024]{1,0:T(8,128)(2,1)S(1)}, u32[]{:S(2)}, u32[]{:S(2)}) collective-permute-start(bf16[128,1024]{1,0:T(8,128)(2,1)S(1)} %get-tuple-element.59.refs_10_.refs_7_), channel_id=1, source_target_pairs={{0,2},{1,3},{2,0},{3,1},{4,6},{5,7},{6,4},{7,5},{8,10},{9,11},{10,... | collective-permute-start | bytes 786440 | tf_op jit(solution)/shard_map/ppermute | solution.py:266
  26.8 0.0 collective-permute-done.13.refs_0_
  26.8 0.7 %collective-permute-start.15 = (bf16[64,1024]{1,0:T(8,128)(2,1)S(1)}, bf16[64,1024]{1,0:T(8,128)(2,1)S(1)}, u32[]{:S(2)}, u32[]{:S(2)}) collective-permute-start(bf16[64,1024]{1,0:T(8,128)(2,1)S(1)} %get-tuple-element.67.refs_6_.refs_5_), channel_id=1, source_target_pairs={{0,8},{16,24},{1,9},{17,25},{2,10},{18,26},{3,11},{19,27}} | collective-permute-start | bytes 393224 | tf_op jit(solution)/shard_map/ppermute | solution.py:372
  27.5 0.7 %collective-permute-start.14 = (bf16[64,1024]{1,0:T(8,128)(2,1)S(1)}, bf16[64,1024]{1,0:T(8,128)(2,1)S(1)}, u32[]{:S(2)}, u32[]{:S(2)}) collective-permute-start(bf16[64,1024]{1,0:T(8,128)(2,1)S(1)} %get-tuple-element.68.refs_5_), channel_id=1, source_target_pairs={{0,8},{16,24},{1,9},{17,25},{2,10},{18,26},{3,11},{19,27}} | collective-permute-start | bytes 393224 | tf_op jit(solution)/shard_map/ppermute | solution.py:372
  28.3 1.3 %collective-permute-start.17 = (bf16[64,1024]{1,0:T(8,128)(2,1)S(1)}, bf16[64,1024]{1,0:T(8,128)(2,1)S(1)}, u32[]{:S(2)}, u32[]{:S(2)}) collective-permute-start(bf16[64,1024]{1,0:T(8,128)(2,1)S(1)} %get-tuple-element.71.refs_6_), channel_id=1, source_target_pairs={{0,4},{8,12},{16,20},{24,28},{1,5},{9,13},{17,21},{25,29},{2,6},{1... | collective-permute-start | bytes 393224 | tf_op jit(solution)/shard_map/ppermute | solution.py:382
  29.6 0.0 collective-permute-done.refs_2_.refs_8_.refs_4_
  29.6 0.4 collective-permute-start.9
  30.0 3.5 %collective-permute-done.10.refs_12_.refs_9_ = bf16[128,1024]{1,0:T(8,128)(2,1)S(1)} collective-permute-done((bf16[128,1024]{1,0:T(8,128)(2,1)S(1)}, bf16[128,1024]{1,0:T(8,128)(2,1)S(1)}, u32[]{:S(2)}, u32[]{:S(2)}) %collective-permute-start.10) | collective-permute-done | bytes 262176 | tf_op jit(solution)/shard_map/ppermute | solution.py:266
  33.5 0.8 %collective-permute-start.11 = (bf16[128,1024]{1,0:T(8,128)(2,1)S(1)}, bf16[128,1024]{1,0:T(8,128)(2,1)S(1)}, u32[]{:S(2)}, u32[]{:S(2)}) collective-permute-start(bf16[128,1024]{1,0:T(8,128)(2,1)S(1)} %collective-permute-done.10.refs_12_.refs_9_), channel_id=1, source_target_pairs={{0,1},{1,0},{2,3},{3,2},{4,5},{5,4},{6,7},{7,6},{8,9},{9,8},{10,11... | collective-permute-start | bytes 786440 | tf_op jit(solution)/shard_map/ppermute | solution.py:266
  34.3 1.3 %collective-permute-start.16 = (bf16[64,1024]{1,0:T(8,128)(2,1)S(1)}, bf16[64,1024]{1,0:T(8,128)(2,1)S(1)}, u32[]{:S(2)}, u32[]{:S(2)}) collective-permute-start(bf16[64,1024]{1,0:T(8,128)(2,1)S(1)} %get-tuple-element.72.refs_6_), channel_id=1, source_target_pairs={{0,4},{8,12},{16,20},{24,28},{1,5},{9,13},{17,21},{25,29},{2,6},{1... | collective-permute-start | bytes 393224 | tf_op jit(solution)/shard_map/ppermute | solution.py:382
  35.6 7.6 %collective-permute-done.17.refs_1_ = bf16[64,1024]{1,0:T(8,128)(2,1)S(1)} collective-permute-done((bf16[64,1024]{1,0:T(8,128)(2,1)S(1)}, bf16[64,1024]{1,0:T(8,128)(2,1)S(1)}, u32[]{:S(2)}, u32[]{:S(2)}) %collective-permute-start.17) | collective-permute-done | bytes 131104 | tf_op jit(solution)/shard_map/ppermute | solution.py:382
  43.3 2.1 %last.2 = (bf16[4,64,256]{2,1,0:T(8,128)(2,1)S(1)}, bf16[4,64,256]{2,1,0:T(8,128)(2,1)S(1)}, bf16[4,64,256]{2,1,0:T(8,128)(2,1)S(1)}, bf16[4,64,256]{2,1,0:T(8,128)(2,1)S(1)}) custom-call(s32[3]{0:T(128)S(1)} %copy-done.1, bf16[64,1024]{1,0:T(8,128)(2,1)S(1)} %collective-permute-done.17.refs_1_, ...), custom_call_target="tpu_custom_call" | custom-call | flops 1300000000 | bytes 2097152 | tf_op jit(solution)/shard_map/last/pallas_call | solution.py:22
  45.3 4.4 %collective-permute-start.21 = (bf16[4,64,256]{2,1,0:T(8,128)(2,1)S(1)}, bf16[4,64,256]{2,1,0:T(8,128)(2,1)S(1)}, u32[]{:S(2)}, u32[]{:S(2)}) collective-permute-start(bf16[4,64,256]{2,1,0:T(8,128)(2,1)S(1)} %get-tuple-element.81), channel_id=1, source_target_pairs={{0,1},{1,0},{2,3},{3,2},{4,5},{5,4},{6,7},{7,6},{8,9},{9,8},{10,11... | collective-permute-start | bytes 393224 | tf_op jit(solution)/shard_map/ppermute | solution.py:266
  49.8 2.0 %collective-permute-start.22 = (bf16[4,64,256]{2,1,0:T(8,128)(2,1)S(1)}, bf16[4,64,256]{2,1,0:T(8,128)(2,1)S(1)}, u32[]{:S(2)}, u32[]{:S(2)}) collective-permute-start(bf16[4,64,256]{2,1,0:T(8,128)(2,1)S(1)} %get-tuple-element.82), channel_id=1, source_target_pairs={{0,2},{1,3},{2,0},{3,1},{4,6},{5,7},{6,4},{7,5},{8,10},{9,11},{10,... | collective-permute-start | bytes 393224 | tf_op jit(solution)/shard_map/ppermute | solution.py:266
  51.8 0.9 %ready.1 = (f32[2,2,256,256]{3,2,1,0:T(8,128)S(1)}, bf16[3,2,256,256]{3,2,1,0:T(8,128)(2,1)S(1)}) custom-call(bf16[3,1024,1024]{2,1,0:T(8,128)(2,1)S(1)} %get-tuple-element.44.refs_1_.refs_2_.refs_0_.refs_3_.refs_4_.refs_17_, bf16[272,1024]{1,0:T(8,128)(2,1)S(1)} %hold.2.refs_2_.refs_1_.refs_7_.refs_3_, ...), custom_call_target="tpu_custom_call" | custom-call | flops 130000000 | bytes 2097152 | tf_op jit(solution)/shard_map/ready/pallas_call | solution.py:22
  52.7 0.1 collective-permute-start.23
  52.8 0.0 collective-permute-done.11.refs_13_.refs_10_
  52.8 2.1 %last.3 = (bf16[4,64,256]{2,1,0:T(8,128)(2,1)S(1)}, bf16[4,64,256]{2,1,0:T(8,128)(2,1)S(1)}, bf16[4,64,256]{2,1,0:T(8,128)(2,1)S(1)}, bf16[4,64,256]{2,1,0:T(8,128)(2,1)S(1)}) custom-call(s32[3]{0:T(128)S(1)} %copy-done.1, bf16[64,1024]{1,0:T(8,128)(2,1)S(1)} %collective-permute-done.16.refs_1_, bf16[64,1024]{1,0:T(8,128)(2,1)S(1)} %get-tuple-element.61.refs_1_.refs_2_, ...), custom_call_target="tpu_custom_call" | custom-call | flops 1300000000 | bytes 2097152 | tf_op jit(solution)/shard_map/last/pallas_call | solution.py:22
  54.9 0.4 collective-permute-start.18
  55.3 1.5 %collective-permute-start.19 = (bf16[4,64,256]{2,1,0:T(8,128)(2,1)S(1)}, bf16[4,64,256]{2,1,0:T(8,128)(2,1)S(1)}, u32[]{:S(2)}, u32[]{:S(2)}) collective-permute-start(bf16[4,64,256]{2,1,0:T(8,128)(2,1)S(1)} %get-tuple-element.79), channel_id=1, source_target_pairs={{0,2},{1,3},{2,0},{3,1},{4,6},{5,7},{6,4},{7,5},{8,10},{9,11},{10,... | collective-permute-start | bytes 393224 | tf_op jit(solution)/shard_map/ppermute | solution.py:266
  56.8 0.0 collective-permute-done.21.refs_12_
  56.8 0.3 collective-permute-start.20
  57.1 1.5 %collective-permute-done.23.refs_14_ = bf16[4,64,256]{2,1,0:T(8,128)(2,1)S(1)} collective-permute-done((bf16[4,64,256]{2,1,0:T(8,128)(2,1)S(1)}, bf16[4,64,256]{2,1,0:T(8,128)(2,1)S(1)}, u32[]{:S(2)}, u32[]{:S(2)}) %collective-permute-start.23) | collective-permute-done | bytes 131104 | tf_op jit(solution)/shard_map/ppermute | solution.py:266
  58.6 1.3 %counts.2 = (f32[3,256,1024]{2,1,0:T(8,128)S(1)}, f32[3,256,256]{2,1,0:T(8,128)S(1)}) custom-call(s32[3]{0:T(128)S(1)} %copy-done.1, f32[2,2,256,256]{3,2,1,0:T(8,128)S(1)} %get-tuple-element.54.refs_14_.refs_1_, bf16[3,2,256,256]{3,2,1,0:T(8,128)(2,1)S(1)} %get-tuple-element.55.refs_2_, bf16[272,1024]{1,0:T(8,128)(2,1)S(1)} %hold.2.refs_2_.refs_1_.refs_7_.refs_3_, ...), custom_call_target="tpu_custom_call" | custom-call | flops 1300000000 | bytes 2097152 | tf_op jit(solution)/shard_map/counts/pallas_call | solution.py:22
  59.9 1.3 %collective-permute-done.19.refs_13_ = bf16[4,64,256]{2,1,0:T(8,128)(2,1)S(1)} collective-permute-done((bf16[4,64,256]{2,1,0:T(8,128)(2,1)S(1)}, bf16[4,64,256]{2,1,0:T(8,128)(2,1)S(1)}, u32[]{:S(2)}, u32[]{:S(2)}) %collective-permute-start.19) | collective-permute-done | bytes 131104 | tf_op jit(solution)/shard_map/ppermute | solution.py:266
  61.2 2.8 %collective-permute-done.20.refs_14_ = bf16[4,64,256]{2,1,0:T(8,128)(2,1)S(1)} collective-permute-done((bf16[4,64,256]{2,1,0:T(8,128)(2,1)S(1)}, bf16[4,64,256]{2,1,0:T(8,128)(2,1)S(1)}, u32[]{:S(2)}, u32[]{:S(2)}) %collective-permute-start.20) | collective-permute-done | bytes 131104 | tf_op jit(solution)/shard_map/ppermute | solution.py:266
  64.0 2.3 %counts.3 = (bf16[3,256,1024]{2,1,0:T(8,128)(2,1)}, bf16[3,256,256]{2,1,0:T(8,128)(2,1)}) custom-call(s32[3]{0:T(128)S(1)} %copy-done.1, f32[2,2,256,256]{3,2,1,0:T(8,128)S(1)} %get-tuple-element.54.refs_14_.refs_1_, bf16[3,2,256,256]{3,2,1,0:T(8,128)(2,1)S(1)} %get-tuple-element.55.refs_2_, bf16[272,1024]{1,0:T(8,128)(2,1)S(1)} %hold.2.refs_2_.refs_1_.refs_7_.refs_3_, ...), custom_call_target="tpu_custom_call" | custom-call | flops 1300000000 | bytes 2097152 | tf_op jit(solution)/shard_map/counts/pallas_call | solution.py:22
  (25 shorter events, 0.2 us)
Async XLA Ops:
  6.0 4.8 %collective-permute-start.3 = (bf16[64,1024]{1,0:T(8,128)(2,1)S(1)}, bf16[64,1024]{1,0:T(8,128)(2,1)S(1)}, u32[]{:S(2)}, u32[]{:S(2)}) collective-permute-start(bf16[64,1024]{1,0:T(8,128)(2,1)S(1)} %first.2.refs_1_), channel_id=1, source_target_pairs={{4,0},{12,8},{20,16},{28,24},{5,1},{13,9},{21,17},{29,25},{6,2},{1... | collective-permute-start | bytes 393224 | tf_op jit(solution)/shard_map/ppermute | solution.py:336
  7.3 13.2 %collective-permute-start.1 = (bf16[272,1024]{1,0:T(8,128)(2,1)S(1)}, bf16[272,1024]{1,0:T(8,128)(2,1)S(1)}, u32[]{:S(2)}, u32[]{:S(2)}) collective-permute-start(bf16[272,1024]{1,0:T(8,128)(2,1)S(1)} %hold.2.refs_2_.refs_1_.refs_7_.refs_3_), channel_id=1, source_target_pairs={{0,2},{1,3},{2,0},{3,1},{4,6},{5,7},{6,4},{7,5},{8,10},{9,11},{10,... | collective-permute-start | bytes 1671176 | tf_op jit(solution)/shard_map/ppermute | solution.py:266
  9.4 3.2 %collective-permute-start.2 = (bf16[64,1024]{1,0:T(8,128)(2,1)S(1)}, bf16[64,1024]{1,0:T(8,128)(2,1)S(1)}, u32[]{:S(2)}, u32[]{:S(2)}) collective-permute-start(bf16[64,1024]{1,0:T(8,128)(2,1)S(1)} %first.3), channel_id=1, source_target_pairs={{4,0},{12,8},{20,16},{28,24},{5,1},{13,9},{21,17},{29,25},{6,2},{1... | collective-permute-start | bytes 393224 | tf_op jit(solution)/shard_map/ppermute | solution.py:336
  10.7 4.4 %collective-permute-start.5 = (bf16[64,1024]{1,0:T(8,128)(2,1)S(1)}, bf16[64,1024]{1,0:T(8,128)(2,1)S(1)}, u32[]{:S(2)}, u32[]{:S(2)}) collective-permute-start(bf16[64,1024]{1,0:T(8,128)(2,1)S(1)} %get-tuple-element.48.refs_3_), channel_id=1, source_target_pairs={{8,0},{24,16},{9,1},{25,17},{10,2},{26,18},{11,3},{27,19}} | collective-permute-start | bytes 393224 | tf_op jit(solution)/shard_map/ppermute | solution.py:336
  12.6 3.2 %collective-permute-start.4 = (bf16[64,1024]{1,0:T(8,128)(2,1)S(1)}, bf16[64,1024]{1,0:T(8,128)(2,1)S(1)}, u32[]{:S(2)}, u32[]{:S(2)}) collective-permute-start(bf16[64,1024]{1,0:T(8,128)(2,1)S(1)} %get-tuple-element.50), channel_id=1, source_target_pairs={{8,0},{24,16},{9,1},{25,17},{10,2},{26,18},{11,3},{27,19}} | collective-permute-start | bytes 393224 | tf_op jit(solution)/shard_map/ppermute | solution.py:336
  13.3 16.3 %collective-permute-start = (bf16[272,1024]{1,0:T(8,128)(2,1)S(1)}, bf16[272,1024]{1,0:T(8,128)(2,1)S(1)}, u32[]{:S(2)}, u32[]{:S(2)}) collective-permute-start(bf16[272,1024]{1,0:T(8,128)(2,1)S(1)} %hold.2.refs_2_.refs_1_.refs_7_.refs_3_), channel_id=1, source_target_pairs={{0,1},{1,0},{2,3},{3,2},{4,5},{5,4},{6,7},{7,6},{8,9},{9,8},{10,11... | collective-permute-start | bytes 1671176 | tf_op jit(solution)/shard_map/ppermute | solution.py:266
  15.2 7.4 %collective-permute-start.8 = (bf16[64,1024]{1,0:T(8,128)(2,1)S(1)}, bf16[64,1024]{1,0:T(8,128)(2,1)S(1)}, u32[]{:S(2)}, u32[]{:S(2)}) collective-permute-start(bf16[64,1024]{1,0:T(8,128)(2,1)S(1)} %get-tuple-element.52.refs_3_), channel_id=1, source_target_pairs={{16,0},{17,1},{18,2},{19,3}} | collective-permute-start | bytes 393224 | tf_op jit(solution)/shard_map/ppermute | solution.py:349
  15.9 6.7 %copy-start = (f32[1024]{0:T(1024)S(1)}, f32[1024]{0:T(1024)}, u32[]{:S(2)}) copy-start(f32[1024]{0:T(1024)} %param.7) | copy-start | bytes 12292
  15.9 8.1 %collective-permute-start.7 = (bf16[64,1024]{1,0:T(8,128)(2,1)S(1)}, bf16[64,1024]{1,0:T(8,128)(2,1)S(1)}, u32[]{:S(2)}, u32[]{:S(2)}) collective-permute-start(bf16[64,1024]{1,0:T(8,128)(2,1)S(1)} %get-tuple-element.53.refs_1_), channel_id=1, source_target_pairs={{16,0},{17,1},{18,2},{19,3}} | collective-permute-start | bytes 393224 | tf_op jit(solution)/shard_map/ppermute | solution.py:349
  20.6 13.7 %collective-permute-start.6 = (bf16[272,1024]{1,0:T(8,128)(2,1)S(1)}, bf16[272,1024]{1,0:T(8,128)(2,1)S(1)}, u32[]{:S(2)}, u32[]{:S(2)}) collective-permute-start(bf16[272,1024]{1,0:T(8,128)(2,1)S(1)} %hold.3), channel_id=1, source_target_pairs={{0,1},{1,0},{2,3},{3,2},{4,5},{5,4},{6,7},{7,6},{8,9},{9,8},{10,11... | collective-permute-start | bytes 1671176 | tf_op jit(solution)/shard_map/ppermute | solution.py:266
  23.3 3.4 %collective-permute-start.13 = (bf16[64,1024]{1,0:T(8,128)(2,1)S(1)}, bf16[64,1024]{1,0:T(8,128)(2,1)S(1)}, u32[]{:S(2)}, u32[]{:S(2)}) collective-permute-start(bf16[64,1024]{1,0:T(8,128)(2,1)S(1)} %get-tuple-element.64.refs_5_), channel_id=1, source_target_pairs={{0,16},{1,17},{2,18},{3,19}} | collective-permute-start | bytes 393224 | tf_op jit(solution)/shard_map/ppermute | solution.py:372
  24.8 2.7 %collective-permute-start.12 = (bf16[64,1024]{1,0:T(8,128)(2,1)S(1)}, bf16[64,1024]{1,0:T(8,128)(2,1)S(1)}, u32[]{:S(2)}, u32[]{:S(2)}) collective-permute-start(bf16[64,1024]{1,0:T(8,128)(2,1)S(1)} %get-tuple-element.60.refs_5_), channel_id=1, source_target_pairs={{0,16},{1,17},{2,18},{3,19}} | collective-permute-start | bytes 393224 | tf_op jit(solution)/shard_map/ppermute | solution.py:372
  25.5 8.0 %collective-permute-start.10 = (bf16[128,1024]{1,0:T(8,128)(2,1)S(1)}, bf16[128,1024]{1,0:T(8,128)(2,1)S(1)}, u32[]{:S(2)}, u32[]{:S(2)}) collective-permute-start(bf16[128,1024]{1,0:T(8,128)(2,1)S(1)} %get-tuple-element.59.refs_10_.refs_7_), channel_id=1, source_target_pairs={{0,2},{1,3},{2,0},{3,1},{4,6},{5,7},{6,4},{7,5},{8,10},{9,11},{10,... | collective-permute-start | bytes 786440 | tf_op jit(solution)/shard_map/ppermute | solution.py:266
  26.8 1.4 %collective-permute-start.15 = (bf16[64,1024]{1,0:T(8,128)(2,1)S(1)}, bf16[64,1024]{1,0:T(8,128)(2,1)S(1)}, u32[]{:S(2)}, u32[]{:S(2)}) collective-permute-start(bf16[64,1024]{1,0:T(8,128)(2,1)S(1)} %get-tuple-element.67.refs_6_.refs_5_), channel_id=1, source_target_pairs={{0,8},{16,24},{1,9},{17,25},{2,10},{18,26},{3,11},{19,27}} | collective-permute-start | bytes 393224 | tf_op jit(solution)/shard_map/ppermute | solution.py:372
  27.5 6.8 %collective-permute-start.14 = (bf16[64,1024]{1,0:T(8,128)(2,1)S(1)}, bf16[64,1024]{1,0:T(8,128)(2,1)S(1)}, u32[]{:S(2)}, u32[]{:S(2)}) collective-permute-start(bf16[64,1024]{1,0:T(8,128)(2,1)S(1)} %get-tuple-element.68.refs_5_), channel_id=1, source_target_pairs={{0,8},{16,24},{1,9},{17,25},{2,10},{18,26},{3,11},{19,27}} | collective-permute-start | bytes 393224 | tf_op jit(solution)/shard_map/ppermute | solution.py:372
  28.3 15.0 %collective-permute-start.17 = (bf16[64,1024]{1,0:T(8,128)(2,1)S(1)}, bf16[64,1024]{1,0:T(8,128)(2,1)S(1)}, u32[]{:S(2)}, u32[]{:S(2)}) collective-permute-start(bf16[64,1024]{1,0:T(8,128)(2,1)S(1)} %get-tuple-element.71.refs_6_), channel_id=1, source_target_pairs={{0,4},{8,12},{16,20},{24,28},{1,5},{9,13},{17,21},{25,29},{2,6},{1... | collective-permute-start | bytes 393224 | tf_op jit(solution)/shard_map/ppermute | solution.py:382
  29.6 23.2 %collective-permute-start.9 = (bf16[128,1024]{1,0:T(8,128)(2,1)S(1)}, bf16[128,1024]{1,0:T(8,128)(2,1)S(1)}, u32[]{:S(2)}, u32[]{:S(2)}) collective-permute-start(bf16[128,1024]{1,0:T(8,128)(2,1)S(1)} %get-tuple-element.59.refs_10_.refs_7_), channel_id=1, source_target_pairs={{0,1},{1,0},{2,3},{3,2},{4,5},{5,4},{6,7},{7,6},{8,9},{9,8},{10,11... | collective-permute-start | bytes 786440 | tf_op jit(solution)/shard_map/ppermute | solution.py:266
  33.5 19.3 %collective-permute-start.11 = (bf16[128,1024]{1,0:T(8,128)(2,1)S(1)}, bf16[128,1024]{1,0:T(8,128)(2,1)S(1)}, u32[]{:S(2)}, u32[]{:S(2)}) collective-permute-start(bf16[128,1024]{1,0:T(8,128)(2,1)S(1)} %collective-permute-done.10.refs_12_.refs_9_), channel_id=1, source_target_pairs={{0,1},{1,0},{2,3},{3,2},{4,5},{5,4},{6,7},{7,6},{8,9},{9,8},{10,11... | collective-permute-start | bytes 786440 | tf_op jit(solution)/shard_map/ppermute | solution.py:266
  34.3 9.0 %copy-start.1 = (s32[3]{0:T(128)S(1)}, s32[3]{0:T(128)}, u32[]{:S(2)}) copy-start(s32[3]{0:T(128)} %refs_0_.9) | copy-start | bytes 40
  34.3 18.5 %collective-permute-start.16 = (bf16[64,1024]{1,0:T(8,128)(2,1)S(1)}, bf16[64,1024]{1,0:T(8,128)(2,1)S(1)}, u32[]{:S(2)}, u32[]{:S(2)}) collective-permute-start(bf16[64,1024]{1,0:T(8,128)(2,1)S(1)} %get-tuple-element.72.refs_6_), channel_id=1, source_target_pairs={{0,4},{8,12},{16,20},{24,28},{1,5},{9,13},{17,21},{25,29},{2,6},{1... | collective-permute-start | bytes 393224 | tf_op jit(solution)/shard_map/ppermute | solution.py:382
  45.3 11.5 %collective-permute-start.21 = (bf16[4,64,256]{2,1,0:T(8,128)(2,1)S(1)}, bf16[4,64,256]{2,1,0:T(8,128)(2,1)S(1)}, u32[]{:S(2)}, u32[]{:S(2)}) collective-permute-start(bf16[4,64,256]{2,1,0:T(8,128)(2,1)S(1)} %get-tuple-element.81), channel_id=1, source_target_pairs={{0,1},{1,0},{2,3},{3,2},{4,5},{5,4},{6,7},{7,6},{8,9},{9,8},{10,11... | collective-permute-start | bytes 393224 | tf_op jit(solution)/shard_map/ppermute | solution.py:266
  49.8 7.4 %collective-permute-start.22 = (bf16[4,64,256]{2,1,0:T(8,128)(2,1)S(1)}, bf16[4,64,256]{2,1,0:T(8,128)(2,1)S(1)}, u32[]{:S(2)}, u32[]{:S(2)}) collective-permute-start(bf16[4,64,256]{2,1,0:T(8,128)(2,1)S(1)} %get-tuple-element.82), channel_id=1, source_target_pairs={{0,2},{1,3},{2,0},{3,1},{4,6},{5,7},{6,4},{7,5},{8,10},{9,11},{10,... | collective-permute-start | bytes 393224 | tf_op jit(solution)/shard_map/ppermute | solution.py:266
  52.7 5.9 %collective-permute-start.23 = (bf16[4,64,256]{2,1,0:T(8,128)(2,1)S(1)}, bf16[4,64,256]{2,1,0:T(8,128)(2,1)S(1)}, u32[]{:S(2)}, u32[]{:S(2)}) collective-permute-start(bf16[4,64,256]{2,1,0:T(8,128)(2,1)S(1)} %get-tuple-element.83), channel_id=1, source_target_pairs={{0,3},{1,2},{2,1},{3,0},{4,7},{5,6},{6,5},{7,4},{8,11},{9,10},{10,... | collective-permute-start | bytes 393224 | tf_op jit(solution)/shard_map/ppermute | solution.py:266
  54.9 5.0 %collective-permute-start.18 = (bf16[4,64,256]{2,1,0:T(8,128)(2,1)S(1)}, bf16[4,64,256]{2,1,0:T(8,128)(2,1)S(1)}, u32[]{:S(2)}, u32[]{:S(2)}) collective-permute-start(bf16[4,64,256]{2,1,0:T(8,128)(2,1)S(1)} %get-tuple-element.78), channel_id=1, source_target_pairs={{0,1},{1,0},{2,3},{3,2},{4,5},{5,4},{6,7},{7,6},{8,9},{9,8},{10,11... | collective-permute-start | bytes 393224 | tf_op jit(solution)/shard_map/ppermute | solution.py:266
  55.3 5.9 %collective-permute-start.19 = (bf16[4,64,256]{2,1,0:T(8,128)(2,1)S(1)}, bf16[4,64,256]{2,1,0:T(8,128)(2,1)S(1)}, u32[]{:S(2)}, u32[]{:S(2)}) collective-permute-start(bf16[4,64,256]{2,1,0:T(8,128)(2,1)S(1)} %get-tuple-element.79), channel_id=1, source_target_pairs={{0,2},{1,3},{2,0},{3,1},{4,6},{5,7},{6,4},{7,5},{8,10},{9,11},{10,... | collective-permute-start | bytes 393224 | tf_op jit(solution)/shard_map/ppermute | solution.py:266
  56.8 7.2 %collective-permute-start.20 = (bf16[4,64,256]{2,1,0:T(8,128)(2,1)S(1)}, bf16[4,64,256]{2,1,0:T(8,128)(2,1)S(1)}, u32[]{:S(2)}, u32[]{:S(2)}) collective-permute-start(bf16[4,64,256]{2,1,0:T(8,128)(2,1)S(1)} %get-tuple-element.80), channel_id=1, source_target_pairs={{0,3},{1,2},{2,1},{3,0},{4,7},{5,6},{6,5},{7,4},{8,11},{9,10},{10,... | collective-permute-start | bytes 393224 | tf_op jit(solution)/shard_map/ppermute | solution.py:266

commit v3 on v2

--- a/solution.py
+++ b/solution.py
@@ -65,10 +65,24 @@
     return jnp.bitwise_and(lax.axis_index("leaf"), (2 << level) - 1) == (1 << level)
 
 
-def prep_body(nodes, parent_hbm, obs_hbm, emission_hbm, mixing_hbm, *refs):
-    w_ref, lam_ref, msg_ref = refs[:3]
-    u_refs = refs[3 : 3 + CHUNKS]
-    prods, tables, obs, parent_ref, sems = refs[3 + CHUNKS :]
+def root_base(w_ref, prior_ref, base_ref):
+    states = base_ref.shape[1]
+    sums = lax.dot_general(jnp.ones((PAD, states), BF16), w_ref[0], (((1,), (1,)), ((), ())), preferred_element_type=F32)
+    prior = prior_ref[...]
+    odds = (prior / jnp.sum(prior)) / sums[:1]
+    high = odds.astype(BF16).astype(F32)
+    index = lax.broadcasted_iota(jnp.int32, (PAD, states), 0)
+    stacked = jnp.where(index == 0, high, jnp.where(index == 1, odds - high, 0.0)).astype(BF16)
+    both = jnp.dot(stacked, w_ref[0], preferred_element_type=F32)
+    base_ref[0:1, :] = both[0:1] + both[1:2]
+    base_ref[1:2, :] = odds
+
+
+def prep_body(nodes, parent_hbm, obs_hbm, emission_hbm, mixing_hbm, prior_hbm, *refs):
+    w_ref, lam_ref, msg_ref, base_ref = refs[:4]
+    u_refs = refs[4 : 4 + CHUNKS]
+    prods, tables, obs, parent_ref, prior_ref, sems = refs[4 + CHUNKS :]
+    copy_prior = pltpu.make_async_copy(prior_hbm, prior_ref, sems.at[3, 0])
     copy_obs = pltpu.make_async_copy(obs_hbm, obs, sems.at[2, 0])
     copy_parent = pltpu.make_async_copy(parent_hbm, parent_ref, sems.at[2, 1])
     copies_w = [pltpu.make_async_copy(mixing_hbm.at[n], w_ref.at[n], sems.at[0, n]) for n in range(nodes)]
@@ -78,6 +92,7 @@
     for n in reversed(range(nodes)):
         copies_e[n].start()
         copies_w[n].start()
+    copy_prior.start()
     values = tables.shape[1]
     rows = obs.shape[1]
     part = rows // CHUNKS
@@ -113,6 +128,11 @@
             for c in range(CHUNKS):
                 u_refs[c][...] = raw[c * part : (c + 1) * part]
     copies_w[0].wait()
+    copy_prior.wait()
+
+    @pl.when(lax.axis_index("leaf") == 0)
+    def _():
+        root_base(w_ref, prior_ref, base_ref)
 
 
 def send_up(level, raw_ref, w_ref, send_ref):
@@ -134,24 +154,25 @@
     send_up(level + 1, u_out, w_ref, send_ref)
 
 
-def root_body(level, u_ref, recv_ref, w_ref, prior_ref, *refs):
+def root_body(level, u_ref, recv_ref, w_ref, base_ref, *refs):
     lam_ref, msg_ref, ratio_ref, post_ref = refs[-5:-1] if len(refs) > 4 else refs
     lam = scaled(u_ref[...] * jnp.where(is_upper(level), recv_ref[...].astype(F32), 1.0))
-    raw_msg, sums = upward(lam, w_ref[0])
     lam_ref[...] = lam
-    msg_ref[...] = raw_msg
     if len(refs) > 4:
         for c, block in enumerate([item[...] for item in refs[:-5]] + [lam]):
             refs[-1][c * lam.shape[0] : (c + 1) * lam.shape[0], :] = block
-
-    @pl.when(lax.axis_index("leaf") == 0)
-    def _():
-        prior = prior_ref[...]
-        weighted = (prior / jnp.sum(prior)) * (raw_msg * (1.0 / sums))
-        share = weighted / jnp.sum(weighted, axis=1, keepdims=True)
-        ratio, post = downward(share, raw_msg, lam, w_ref[0])
-        ratio_ref[...] = ratio
-        post_ref[...] = post
+    top = lax.axis_index("leaf") == 0
+
+    @pl.when(top)
+    def _():
+        terms = lam.astype(F32) * base_ref[0:1, :]
+        inverse = 1.0 / jnp.sum(terms, axis=1, keepdims=True)
+        ratio_ref[...] = (base_ref[1:2, :] * inverse).astype(BF16)
+        post_ref[...] = (terms * inverse).astype(BF16)
+
+    @pl.when(jnp.logical_not(top))
+    def _():
+        msg_ref[...] = lax.dot_general(lam, w_ref[0], (((1,), (1,)), ((), ())), preferred_element_type=F32)
 
 
 def settle_body(level, recv_ref, lam_ref, msg_ref, w_ref, ratio_in, post_in, ratio_ref, post_ref):
@@ -300,11 +321,12 @@
     outs = run(
         functools.partial(prep_body, nodes),
         "prep",
-        tuple(pltpu.with_memory_space_constraint(x, pltpu.HBM) for x in (parent, observed, emission, mixing)),
+        tuple(pltpu.with_memory_space_constraint(x, pltpu.HBM) for x in (parent, observed, emission, mixing, prior.reshape(1, states))),
         (
             pltpu.VMEM(mixing.shape, BF16),
             pltpu.VMEM(((nodes - 1) * rows + PAD, states), BF16),
             pltpu.VMEM((nodes - 1, rows, states), F32),
+            pltpu.VMEM((8, states), F32),
         )
         + (half(F32),) * CHUNKS,
         (
@@ -312,12 +334,13 @@
             pltpu.VMEM(emission.shape, BF16),
             pltpu.VMEM(observed.shape, jnp.int32),
             pltpu.SMEM(parent.shape, jnp.int32),
-            pltpu.SemaphoreType.DMA((3, max(nodes, 2))),
+            pltpu.VMEM((1, states), F32),
+            pltpu.SemaphoreType.DMA((4, max(nodes, 2))),
         ),
-        [ANY] * 4,
+        [ANY] * 5,
     )
-    weights, lams, msgs = outs[:3]
-    raw, send = list(outs[3:]), []
+    weights, lams, msgs, base = outs[:4]
+    raw, send = list(outs[4:]), []
     for c in every:
         (block,) = run(first_body, "first", (raw[c], weights), (half(BF16),), after=[lams] if c > 0 else ())
         send.append(block)
@@ -351,7 +374,7 @@
         top_lam[c], top_msg[c], ratio[c], post[c], *merged = run(
             functools.partial(root_body, levels - 1),
             "root",
-            (raw[c], recv, weights, prior.reshape(1, states)) + (tuple(top_lam[:c]) if final else ()),
+            (raw[c], recv, weights, base) + (tuple(top_lam[:c]) if final else ()),
             (half(BF16), half(F32), half(BF16), half(BF16)) + ((pltpu.VMEM((rows, states), BF16),) if final else ()),
         )
     all_tops = gather(far(merged[0]))
@@ -389,7 +412,7 @@
             [SM] + [VM] * 8,
             after=[own_posts[-1][0], *all_tops, raw_own] if c > 0 else [],
         )
-        order = range(1, groups)
+        order = sorted(range(1, groups), reverse=c < CHUNKS - 1)
         moved = {mask: swap(packs[mask], mask) for mask in order}
         own_posts.append([packs[0]] + [moved[mask] for mask in range(1, groups)])
     sums = ()

time: 66.9 us -> 67.5 us (level)
  waiting for transfers between devices: 21.9 us -> 23.2 us
  starting transfers between devices: 26.9 us -> 25.7 us
    ppermute x2, waiting for transfers between devices: 7.61 us -> 9.08 us  [per_device(): recv = lax.ppermute(post[c], 'leaf', down_pairs(0))]
    ppermute x12, starting transfers between devices: 16.3 us -> 15.2 us  [swap(): lax.ppermute(value, 'rows', [(s, s ^ mask) for s in range(lax.axis_size('...]
  transfers between devices with their start and end apart: 24 -> 24, of which waited for: 7 -> 7; matrix products, arithmetic and copies ran while one was open for 0% -> 0% of each run, Pallas kernels for 13% -> 14%
where the time goes in v3:
time: 67.5 us; the launch traced here: 66.7 us
  starting transfers between devices  25.7 us (38%)
  waiting for transfers between devices  23.2 us (34%)
  Pallas kernels  16.7 us (25%)
  between operations  0.92 us (1%)
    pallas_call x20, Pallas kernels, run(): pl.pallas_call(lambda *refs: body(*refs[:count], *refs[idle:]), name=name...  16.7 us
    ppermute x12, starting transfers between devices, swap(): lax.ppermute(value, 'rows', [(s, s ^ mask) for s in range(lax.axis_size('...  15.2 us
    ppermute x12, waiting for transfers between devices, swap(): lax.ppermute(value, 'rows', [(s, s ^ mask) for s in range(lax.axis_size('...  12.9 us
    ppermute x2, waiting for transfers between devices, per_device(): recv = lax.ppermute(post[c], 'leaf', down_pairs(0))  9.08 us
    ppermute x4, starting transfers between devices, per_device(): recv = lax.ppermute(send[c], 'leaf', up_pairs(level))  3.96 us
    ppermute x4, starting transfers between devices, per_device(): recv = lax.ppermute(post[c], 'leaf', down_pairs(level))  2.67 us
    ppermute x2, starting transfers between devices, per_device(): recv = lax.ppermute(post[c], 'leaf', down_pairs(0))  2.58 us
  transfers between devices with their start and end apart: 24, of which 7 were waited for; matrix products, arithmetic and copies ran while one was open for 0% of the time, Pallas kernels for 14%

profile of v3, /device:TPU:13, one launch (start us, length us, event | category | flops | bytes accessed | tf_op | source)
XLA Modules:
  0.0 66.7 jit_solution(8860288442091872452)
XLA Ops:
  0.6 4.5 %prep.1 = (bf16[3,1024,1024]{2,1,0:T(8,128)(2,1)S(1)}, bf16[272,1024]{1,0:T(8,128)(2,1)S(1)}, f32[2,128,1024]{2,1,0:T(8,128)S(1)}, f32[8,1024]{1,0:T(8,128)S(1)}...) custom-call(s32[3]{0:T(128)} %refs_0_.9, s32[3,128]{1,0:T(4,128)} %refs_1_.1, bf16[3,256,1024]{2,1,0:T(8,128)(2,1)} %refs_2_.1, ...), custom_call_target="tpu_custom_call" | custom-call | flops 1300000000 | bytes 2097152 | tf_op jit(solution)/shard_map/prep/pallas_call | solution.py:22
  5.2 0.8 %first.2.refs_1_ = bf16[64,1024]{1,0:T(8,128)(2,1)S(1)} custom-call(f32[64,1024]{1,0:T(8,128)S(1)} %get-tuple-element.47.refs_0_, bf16[3,1024,1024]{2,1,0:T(8,128)(2,1)S(1)} %get-tuple-element.45.refs_1_.refs_2_.refs_0_.refs_3_.refs_4_.refs_17_), custom_call_target="tpu_custom_call" | custom-call | flops 1300000000 | bytes 2097152 | tf_op jit(solution)/shard_map/first/pallas_call | solution.py:22
  6.0 1.3 %collective-permute-start.3 = (bf16[64,1024]{1,0:T(8,128)(2,1)S(1)}, bf16[64,1024]{1,0:T(8,128)(2,1)S(1)}, u32[]{:S(2)}, u32[]{:S(2)}) collective-permute-start(bf16[64,1024]{1,0:T(8,128)(2,1)S(1)} %first.2.refs_1_), channel_id=1, source_target_pairs={{4,0},{12,8},{20,16},{28,24},{5,1},{13,9},{21,17},{29,25},{6,2},{1... | collective-permute-start | bytes 393224 | tf_op jit(solution)/shard_map/ppermute | solution.py:359
  7.3 1.3 %collective-permute-start.1 = (bf16[272,1024]{1,0:T(8,128)(2,1)S(1)}, bf16[272,1024]{1,0:T(8,128)(2,1)S(1)}, u32[]{:S(2)}, u32[]{:S(2)}) collective-permute-start(bf16[272,1024]{1,0:T(8,128)(2,1)S(1)} %hold.2.refs_2_.refs_1_.refs_7_.refs_3_), channel_id=1, source_target_pairs={{0,2},{1,3},{2,0},{3,1},{4,6},{5,7},{6,4},{7,5},{8,10},{9,11},{10,... | collective-permute-start | bytes 1671176 | tf_op jit(solution)/shard_map/ppermute | solution.py:287
  8.6 0.8 %first.3 = bf16[64,1024]{1,0:T(8,128)(2,1)S(1)} custom-call(f32[64,1024]{1,0:T(8,128)S(1)} %get-tuple-element.48.refs_0_, bf16[3,1024,1024]{2,1,0:T(8,128)(2,1)S(1)} %get-tuple-element.45.refs_1_.refs_2_.refs_0_.refs_3_.refs_4_.refs_17_, bf16[272,1024]{1,0:T(8,128)(2,1)S(1)} %hold.2.refs_2_.refs_1_.refs_7_.refs_3_), custom_call_target="tpu_custom_call" | custom-call | flops 1300000000 | bytes 2097152 | tf_op jit(solution)/shard_map/first/pallas_call | solution.py:22
  9.4 1.3 %collective-permute-start.2 = (bf16[64,1024]{1,0:T(8,128)(2,1)S(1)}, bf16[64,1024]{1,0:T(8,128)(2,1)S(1)}, u32[]{:S(2)}, u32[]{:S(2)}) collective-permute-start(bf16[64,1024]{1,0:T(8,128)(2,1)S(1)} %first.3), channel_id=1, source_target_pairs={{4,0},{12,8},{20,16},{28,24},{5,1},{13,9},{21,17},{29,25},{6,2},{1... | collective-permute-start | bytes 393224 | tf_op jit(solution)/shard_map/ppermute | solution.py:359
  10.7 0.0 collective-permute-done.3.refs_1_
  10.8 0.7 %collective-permute-start.5 = (bf16[64,1024]{1,0:T(8,128)(2,1)S(1)}, bf16[64,1024]{1,0:T(8,128)(2,1)S(1)}, u32[]{:S(2)}, u32[]{:S(2)}) collective-permute-start(bf16[64,1024]{1,0:T(8,128)(2,1)S(1)} %get-tuple-element.49.refs_3_), channel_id=1, source_target_pairs={{8,0},{24,16},{9,1},{25,17},{10,2},{26,18},{11,3},{27,19}} | collective-permute-start | bytes 393224 | tf_op jit(solution)/shard_map/ppermute | solution.py:359
  11.5 1.2 %collective-permute-done.2.refs_1_ = bf16[64,1024]{1,0:T(8,128)(2,1)S(1)} collective-permute-done((bf16[64,1024]{1,0:T(8,128)(2,1)S(1)}, bf16[64,1024]{1,0:T(8,128)(2,1)S(1)}, u32[]{:S(2)}, u32[]{:S(2)}) %collective-permute-start.2) | collective-permute-done | bytes 131104 | tf_op jit(solution)/shard_map/ppermute | solution.py:359
  12.7 0.7 collective-permute-start.4
  13.3 1.9 %collective-permute-start = (bf16[272,1024]{1,0:T(8,128)(2,1)S(1)}, bf16[272,1024]{1,0:T(8,128)(2,1)S(1)}, u32[]{:S(2)}, u32[]{:S(2)}) collective-permute-start(bf16[272,1024]{1,0:T(8,128)(2,1)S(1)} %hold.2.refs_2_.refs_1_.refs_7_.refs_3_), channel_id=1, source_target_pairs={{0,1},{1,0},{2,3},{3,2},{4,5},{5,4},{6,7},{7,6},{8,9},{9,8},{10,11... | collective-permute-start | bytes 1671176 | tf_op jit(solution)/shard_map/ppermute | solution.py:287
  15.2 0.7 collective-permute-start.8
  15.9 0.7 %collective-permute-start.7 = (bf16[64,1024]{1,0:T(8,128)(2,1)S(1)}, bf16[64,1024]{1,0:T(8,128)(2,1)S(1)}, u32[]{:S(2)}, u32[]{:S(2)}) collective-permute-start(bf16[64,1024]{1,0:T(8,128)(2,1)S(1)} %get-tuple-element.54.refs_1_), channel_id=1, source_target_pairs={{16,0},{17,1},{18,2},{19,3}} | collective-permute-start | bytes 393224 | tf_op jit(solution)/shard_map/ppermute | solution.py:372
  16.6 4.0 %collective-permute-done.1.refs_3_.refs_9_.refs_5_ = bf16[272,1024]{1,0:T(8,128)(2,1)S(1)} collective-permute-done((bf16[272,1024]{1,0:T(8,128)(2,1)S(1)}, bf16[272,1024]{1,0:T(8,128)(2,1)S(1)}, u32[]{:S(2)}, u32[]{:S(2)}) %collective-permute-start.1) | collective-permute-done | bytes 557088 | tf_op jit(solution)/shard_map/ppermute | solution.py:287
  20.6 1.9 %collective-permute-start.6 = (bf16[272,1024]{1,0:T(8,128)(2,1)S(1)}, bf16[272,1024]{1,0:T(8,128)(2,1)S(1)}, u32[]{:S(2)}, u32[]{:S(2)}) collective-permute-start(bf16[272,1024]{1,0:T(8,128)(2,1)S(1)} %hold.3), channel_id=1, source_target_pairs={{0,1},{1,0},{2,3},{3,2},{4,5},{5,4},{6,7},{7,6},{8,9},{9,8},{10,11... | collective-permute-start | bytes 1671176 | tf_op jit(solution)/shard_map/ppermute | solution.py:287
  22.6 0.0 collective-permute-done.8.refs_1_
  22.6 0.9 %root.2 = (bf16[64,1024]{1,0:T(8,128)(2,1)S(1)}, f32[64,1024]{1,0:T(8,128)S(1)}, bf16[64,1024]{1,0:T(8,128)(2,1)S(1)}, bf16[64,1024]{1,0:T(8,128)(2,1)S(1)}) custom-call(f32[64,1024]{1,0:T(8,128)S(1)} %get-tuple-element.59.refs_0_, bf16[64,1024]{1,0:T(8,128)(2,1)S(1)} %collective-permute-done.8.refs_1_, ...), custom_call_target="tpu_custom_call" | custom-call | flops 1300000000 | bytes 2097152 | tf_op jit(solution)/shard_map/root/pallas_call | solution.py:22
  23.5 0.7 %collective-permute-start.13 = (bf16[64,1024]{1,0:T(8,128)(2,1)S(1)}, bf16[64,1024]{1,0:T(8,128)(2,1)S(1)}, u32[]{:S(2)}, u32[]{:S(2)}) collective-permute-start(bf16[64,1024]{1,0:T(8,128)(2,1)S(1)} %get-tuple-element.66.refs_5_), channel_id=1, source_target_pairs={{0,16},{1,17},{2,18},{3,19}} | collective-permute-start | bytes 393224 | tf_op jit(solution)/shard_map/ppermute | solution.py:395
  24.1 0.0 collective-permute-done.7.refs_1_
  24.1 0.9 %root.3 = (bf16[64,1024]{1,0:T(8,128)(2,1)S(1)}, f32[64,1024]{1,0:T(8,128)S(1)}, bf16[64,1024]{1,0:T(8,128)(2,1)S(1)}, bf16[64,1024]{1,0:T(8,128)(2,1)S(1)}, bf16[128,1024]{1,0:T(8,128)(2,1)S(1)}) custom-call(f32[64,1024]{1,0:T(8,128)S(1)} %get-tuple-element.57.refs_0_, bf16[64,1024]{1,0:T(8,128)(2,1)S(1)} %collective-permute-done.7.refs_1_, ...), custom_call_target="tpu_custom_call" | custom-call | flops 1300000000 | bytes 2097152 | tf_op jit(solution)/shard_map/root/pallas_call | solution.py:22
  25.0 0.7 collective-permute-start.12
  25.7 1.3 %collective-permute-start.10 = (bf16[128,1024]{1,0:T(8,128)(2,1)S(1)}, bf16[128,1024]{1,0:T(8,128)(2,1)S(1)}, u32[]{:S(2)}, u32[]{:S(2)}) collective-permute-start(bf16[128,1024]{1,0:T(8,128)(2,1)S(1)} %get-tuple-element.61.refs_10_.refs_7_), channel_id=1, source_target_pairs={{0,2},{1,3},{2,0},{3,1},{4,6},{5,7},{6,4},{7,5},{8,10},{9,11},{10,... | collective-permute-start | bytes 786440 | tf_op jit(solution)/shard_map/ppermute | solution.py:287
  27.0 0.0 collective-permute-done.13.refs_0_
  27.0 0.7 %collective-permute-start.15 = (bf16[64,1024]{1,0:T(8,128)(2,1)S(1)}, bf16[64,1024]{1,0:T(8,128)(2,1)S(1)}, u32[]{:S(2)}, u32[]{:S(2)}) collective-permute-start(bf16[64,1024]{1,0:T(8,128)(2,1)S(1)} %get-tuple-element.69.refs_6_.refs_5_), channel_id=1, source_target_pairs={{0,8},{16,24},{1,9},{17,25},{2,10},{18,26},{3,11},{19,27}} | collective-permute-start | bytes 393224 | tf_op jit(solution)/shard_map/ppermute | solution.py:395
  27.7 0.0 collective-permute-done.12.refs_0_
  27.7 0.7 %collective-permute-start.14 = (bf16[64,1024]{1,0:T(8,128)(2,1)S(1)}, bf16[64,1024]{1,0:T(8,128)(2,1)S(1)}, u32[]{:S(2)}, u32[]{:S(2)}) collective-permute-start(bf16[64,1024]{1,0:T(8,128)(2,1)S(1)} %get-tuple-element.70.refs_5_), channel_id=1, source_target_pairs={{0,8},{16,24},{1,9},{17,25},{2,10},{18,26},{3,11},{19,27}} | collective-permute-start | bytes 393224 | tf_op jit(solution)/shard_map/ppermute | solution.py:395
  28.4 0.0 collective-permute-done.15.refs_0_
  28.5 1.3 %collective-permute-start.17 = (bf16[64,1024]{1,0:T(8,128)(2,1)S(1)}, bf16[64,1024]{1,0:T(8,128)(2,1)S(1)}, u32[]{:S(2)}, u32[]{:S(2)}) collective-permute-start(bf16[64,1024]{1,0:T(8,128)(2,1)S(1)} %get-tuple-element.73.refs_6_), channel_id=1, source_target_pairs={{0,4},{8,12},{16,20},{24,28},{1,5},{9,13},{17,21},{25,29},{2,6},{1... | collective-permute-start | bytes 393224 | tf_op jit(solution)/shard_map/ppermute | solution.py:405
  29.8 0.0 collective-permute-done.refs_2_.refs_8_.refs_4_
  29.8 0.4 collective-permute-start.9
  30.2 3.5 %collective-permute-done.10.refs_12_.refs_9_ = bf16[128,1024]{1,0:T(8,128)(2,1)S(1)} collective-permute-done((bf16[128,1024]{1,0:T(8,128)(2,1)S(1)}, bf16[128,1024]{1,0:T(8,128)(2,1)S(1)}, u32[]{:S(2)}, u32[]{:S(2)}) %collective-permute-start.10) | collective-permute-done | bytes 262176 | tf_op jit(solution)/shard_map/ppermute | solution.py:287
  33.7 0.8 %collective-permute-start.11 = (bf16[128,1024]{1,0:T(8,128)(2,1)S(1)}, bf16[128,1024]{1,0:T(8,128)(2,1)S(1)}, u32[]{:S(2)}, u32[]{:S(2)}) collective-permute-start(bf16[128,1024]{1,0:T(8,128)(2,1)S(1)} %collective-permute-done.10.refs_12_.refs_9_), channel_id=1, source_target_pairs={{0,1},{1,0},{2,3},{3,2},{4,5},{5,4},{6,7},{7,6},{8,9},{9,8},{10,11... | collective-permute-start | bytes 786440 | tf_op jit(solution)/shard_map/ppermute | solution.py:287
  34.6 1.3 %collective-permute-start.16 = (bf16[64,1024]{1,0:T(8,128)(2,1)S(1)}, bf16[64,1024]{1,0:T(8,128)(2,1)S(1)}, u32[]{:S(2)}, u32[]{:S(2)}) collective-permute-start(bf16[64,1024]{1,0:T(8,128)(2,1)S(1)} %get-tuple-element.74.refs_6_), channel_id=1, source_target_pairs={{0,4},{8,12},{16,20},{24,28},{1,5},{9,13},{17,21},{25,29},{2,6},{1... | collective-permute-start | bytes 393224 | tf_op jit(solution)/shard_map/ppermute | solution.py:405
  35.9 9.1 %collective-permute-done.17.refs_1_ = bf16[64,1024]{1,0:T(8,128)(2,1)S(1)} collective-permute-done((bf16[64,1024]{1,0:T(8,128)(2,1)S(1)}, bf16[64,1024]{1,0:T(8,128)(2,1)S(1)}, u32[]{:S(2)}, u32[]{:S(2)}) %collective-permute-start.17) | collective-permute-done | bytes 131104 | tf_op jit(solution)/shard_map/ppermute | solution.py:405
  44.9 2.1 %last.2 = (bf16[4,64,256]{2,1,0:T(8,128)(2,1)S(1)}, bf16[4,64,256]{2,1,0:T(8,128)(2,1)S(1)}, bf16[4,64,256]{2,1,0:T(8,128)(2,1)S(1)}, bf16[4,64,256]{2,1,0:T(8,128)(2,1)S(1)}) custom-call(s32[3]{0:T(128)S(1)} %copy-done, bf16[64,1024]{1,0:T(8,128)(2,1)S(1)} %collective-permute-done.17.refs_1_, ...), custom_call_target="tpu_custom_call" | custom-call | flops 1300000000 | bytes 2097152 | tf_op jit(solution)/shard_map/last/pallas_call | solution.py:22
  47.0 3.7 %collective-permute-start.21 = (bf16[4,64,256]{2,1,0:T(8,128)(2,1)S(1)}, bf16[4,64,256]{2,1,0:T(8,128)(2,1)S(1)}, u32[]{:S(2)}, u32[]{:S(2)}) collective-permute-start(bf16[4,64,256]{2,1,0:T(8,128)(2,1)S(1)} %get-tuple-element.83), channel_id=1, source_target_pairs={{0,1},{1,0},{2,3},{3,2},{4,5},{5,4},{6,7},{7,6},{8,9},{9,8},{10,11... | collective-permute-start | bytes 393224 | tf_op jit(solution)/shard_map/ppermute | solution.py:287
  50.7 1.2 %collective-permute-start.22 = (bf16[4,64,256]{2,1,0:T(8,128)(2,1)S(1)}, bf16[4,64,256]{2,1,0:T(8,128)(2,1)S(1)}, u32[]{:S(2)}, u32[]{:S(2)}) collective-permute-start(bf16[4,64,256]{2,1,0:T(8,128)(2,1)S(1)} %get-tuple-element.84), channel_id=1, source_target_pairs={{0,2},{1,3},{2,0},{3,1},{4,6},{5,7},{6,4},{7,5},{8,10},{9,11},{10,... | collective-permute-start | bytes 393224 | tf_op jit(solution)/shard_map/ppermute | solution.py:287
  51.9 0.9 %ready.1 = (f32[2,2,256,256]{3,2,1,0:T(8,128)S(1)}, bf16[3,2,256,256]{3,2,1,0:T(8,128)(2,1)S(1)}) custom-call(bf16[3,1024,1024]{2,1,0:T(8,128)(2,1)S(1)} %get-tuple-element.45.refs_1_.refs_2_.refs_0_.refs_3_.refs_4_.refs_17_, bf16[272,1024]{1,0:T(8,128)(2,1)S(1)} %hold.2.refs_2_.refs_1_.refs_7_.refs_3_, ...), custom_call_target="tpu_custom_call" | custom-call | flops 130000000 | bytes 2097152 | tf_op jit(solution)/shard_map/ready/pallas_call | solution.py:22
  52.8 0.6 collective-permute-start.23
  53.4 2.1 %last.3 = (bf16[4,64,256]{2,1,0:T(8,128)(2,1)S(1)}, bf16[4,64,256]{2,1,0:T(8,128)(2,1)S(1)}, bf16[4,64,256]{2,1,0:T(8,128)(2,1)S(1)}, bf16[4,64,256]{2,1,0:T(8,128)(2,1)S(1)}) custom-call(s32[3]{0:T(128)S(1)} %copy-done, bf16[64,1024]{1,0:T(8,128)(2,1)S(1)} %collective-permute-done.16.refs_1_, bf16[64,1024]{1,0:T(8,128)(2,1)S(1)} %get-tuple-element.63.refs_1_.refs_2_, ...), custom_call_target="tpu_custom_call" | custom-call | flops 1300000000 | bytes 2097152 | tf_op jit(solution)/shard_map/last/pallas_call | solution.py:22
  55.5 0.2 collective-permute-start.18
  55.7 1.2 %collective-permute-start.19 = (bf16[4,64,256]{2,1,0:T(8,128)(2,1)S(1)}, bf16[4,64,256]{2,1,0:T(8,128)(2,1)S(1)}, u32[]{:S(2)}, u32[]{:S(2)}) collective-permute-start(bf16[4,64,256]{2,1,0:T(8,128)(2,1)S(1)} %get-tuple-element.81), channel_id=1, source_target_pairs={{0,2},{1,3},{2,0},{3,1},{4,6},{5,7},{6,4},{7,5},{8,10},{9,11},{10,... | collective-permute-start | bytes 393224 | tf_op jit(solution)/shard_map/ppermute | solution.py:287
  56.9 0.8 %collective-permute-start.20 = (bf16[4,64,256]{2,1,0:T(8,128)(2,1)S(1)}, bf16[4,64,256]{2,1,0:T(8,128)(2,1)S(1)}, u32[]{:S(2)}, u32[]{:S(2)}) collective-permute-start(bf16[4,64,256]{2,1,0:T(8,128)(2,1)S(1)} %get-tuple-element.82), channel_id=1, source_target_pairs={{0,3},{1,2},{2,1},{3,0},{4,7},{5,6},{6,5},{7,4},{8,11},{9,10},{10,... | collective-permute-start | bytes 393224 | tf_op jit(solution)/shard_map/ppermute | solution.py:287
  57.7 1.4 %collective-permute-done.23.refs_14_ = bf16[4,64,256]{2,1,0:T(8,128)(2,1)S(1)} collective-permute-done((bf16[4,64,256]{2,1,0:T(8,128)(2,1)S(1)}, bf16[4,64,256]{2,1,0:T(8,128)(2,1)S(1)}, u32[]{:S(2)}, u32[]{:S(2)}) %collective-permute-start.23) | collective-permute-done | bytes 131104 | tf_op jit(solution)/shard_map/ppermute | solution.py:287
  59.1 1.3 %counts.2 = (f32[3,256,1024]{2,1,0:T(8,128)S(1)}, f32[3,256,256]{2,1,0:T(8,128)S(1)}) custom-call(s32[3]{0:T(128)S(1)} %copy-done, f32[2,2,256,256]{3,2,1,0:T(8,128)S(1)} %get-tuple-element.55.refs_14_.refs_1_, bf16[3,2,256,256]{3,2,1,0:T(8,128)(2,1)S(1)} %get-tuple-element.56.refs_2_, bf16[272,1024]{1,0:T(8,128)(2,1)S(1)} %hold.2.refs_2_.refs_1_.refs_7_.refs_3_, ...), custom_call_target="tpu_custom_call" | custom-call | flops 1300000000 | bytes 2097152 | tf_op jit(solution)/shard_map/counts/pallas_call | solution.py:22
  60.3 1.2 %collective-permute-done.19.refs_13_ = bf16[4,64,256]{2,1,0:T(8,128)(2,1)S(1)} collective-permute-done((bf16[4,64,256]{2,1,0:T(8,128)(2,1)S(1)}, bf16[4,64,256]{2,1,0:T(8,128)(2,1)S(1)}, u32[]{:S(2)}, u32[]{:S(2)}) %collective-permute-start.19) | collective-permute-done | bytes 131104 | tf_op jit(solution)/shard_map/ppermute | solution.py:287
  61.5 2.8 %collective-permute-done.20.refs_14_ = bf16[4,64,256]{2,1,0:T(8,128)(2,1)S(1)} collective-permute-done((bf16[4,64,256]{2,1,0:T(8,128)(2,1)S(1)}, bf16[4,64,256]{2,1,0:T(8,128)(2,1)S(1)}, u32[]{:S(2)}, u32[]{:S(2)}) %collective-permute-start.20) | collective-permute-done | bytes 131104 | tf_op jit(solution)/shard_map/ppermute | solution.py:287
  64.4 2.3 %counts.3 = (bf16[3,256,1024]{2,1,0:T(8,128)(2,1)}, bf16[3,256,256]{2,1,0:T(8,128)(2,1)}) custom-call(s32[3]{0:T(128)S(1)} %copy-done, f32[2,2,256,256]{3,2,1,0:T(8,128)S(1)} %get-tuple-element.55.refs_14_.refs_1_, bf16[3,2,256,256]{3,2,1,0:T(8,128)(2,1)S(1)} %get-tuple-element.56.refs_2_, bf16[272,1024]{1,0:T(8,128)(2,1)S(1)} %hold.2.refs_2_.refs_1_.refs_7_.refs_3_, ...), custom_call_target="tpu_custom_call" | custom-call | flops 1300000000 | bytes 2097152 | tf_op jit(solution)/shard_map/counts/pallas_call | solution.py:22
  (23 shorter events, 0.2 us)
Async XLA Ops:
  6.0 4.7 %collective-permute-start.3 = (bf16[64,1024]{1,0:T(8,128)(2,1)S(1)}, bf16[64,1024]{1,0:T(8,128)(2,1)S(1)}, u32[]{:S(2)}, u32[]{:S(2)}) collective-permute-start(bf16[64,1024]{1,0:T(8,128)(2,1)S(1)} %first.2.refs_1_), channel_id=1, source_target_pairs={{4,0},{12,8},{20,16},{28,24},{5,1},{13,9},{21,17},{29,25},{6,2},{1... | collective-permute-start | bytes 393224 | tf_op jit(solution)/shard_map/ppermute | solution.py:359
  7.3 13.2 %collective-permute-start.1 = (bf16[272,1024]{1,0:T(8,128)(2,1)S(1)}, bf16[272,1024]{1,0:T(8,128)(2,1)S(1)}, u32[]{:S(2)}, u32[]{:S(2)}) collective-permute-start(bf16[272,1024]{1,0:T(8,128)(2,1)S(1)} %hold.2.refs_2_.refs_1_.refs_7_.refs_3_), channel_id=1, source_target_pairs={{0,2},{1,3},{2,0},{3,1},{4,6},{5,7},{6,4},{7,5},{8,10},{9,11},{10,... | collective-permute-start | bytes 1671176 | tf_op jit(solution)/shard_map/ppermute | solution.py:287
  9.4 3.2 %collective-permute-start.2 = (bf16[64,1024]{1,0:T(8,128)(2,1)S(1)}, bf16[64,1024]{1,0:T(8,128)(2,1)S(1)}, u32[]{:S(2)}, u32[]{:S(2)}) collective-permute-start(bf16[64,1024]{1,0:T(8,128)(2,1)S(1)} %first.3), channel_id=1, source_target_pairs={{4,0},{12,8},{20,16},{28,24},{5,1},{13,9},{21,17},{29,25},{6,2},{1... | collective-permute-start | bytes 393224 | tf_op jit(solution)/shard_map/ppermute | solution.py:359
  10.8 4.4 %collective-permute-start.5 = (bf16[64,1024]{1,0:T(8,128)(2,1)S(1)}, bf16[64,1024]{1,0:T(8,128)(2,1)S(1)}, u32[]{:S(2)}, u32[]{:S(2)}) collective-permute-start(bf16[64,1024]{1,0:T(8,128)(2,1)S(1)} %get-tuple-element.49.refs_3_), channel_id=1, source_target_pairs={{8,0},{24,16},{9,1},{25,17},{10,2},{26,18},{11,3},{27,19}} | collective-permute-start | bytes 393224 | tf_op jit(solution)/shard_map/ppermute | solution.py:359
  12.7 3.2 %collective-permute-start.4 = (bf16[64,1024]{1,0:T(8,128)(2,1)S(1)}, bf16[64,1024]{1,0:T(8,128)(2,1)S(1)}, u32[]{:S(2)}, u32[]{:S(2)}) collective-permute-start(bf16[64,1024]{1,0:T(8,128)(2,1)S(1)} %get-tuple-element.51), channel_id=1, source_target_pairs={{8,0},{24,16},{9,1},{25,17},{10,2},{26,18},{11,3},{27,19}} | collective-permute-start | bytes 393224 | tf_op jit(solution)/shard_map/ppermute | solution.py:359
  13.3 16.5 %collective-permute-start = (bf16[272,1024]{1,0:T(8,128)(2,1)S(1)}, bf16[272,1024]{1,0:T(8,128)(2,1)S(1)}, u32[]{:S(2)}, u32[]{:S(2)}) collective-permute-start(bf16[272,1024]{1,0:T(8,128)(2,1)S(1)} %hold.2.refs_2_.refs_1_.refs_7_.refs_3_), channel_id=1, source_target_pairs={{0,1},{1,0},{2,3},{3,2},{4,5},{5,4},{6,7},{7,6},{8,9},{9,8},{10,11... | collective-permute-start | bytes 1671176 | tf_op jit(solution)/shard_map/ppermute | solution.py:287
  15.2 7.4 %collective-permute-start.8 = (bf16[64,1024]{1,0:T(8,128)(2,1)S(1)}, bf16[64,1024]{1,0:T(8,128)(2,1)S(1)}, u32[]{:S(2)}, u32[]{:S(2)}) collective-permute-start(bf16[64,1024]{1,0:T(8,128)(2,1)S(1)} %get-tuple-element.53.refs_3_), channel_id=1, source_target_pairs={{16,0},{17,1},{18,2},{19,3}} | collective-permute-start | bytes 393224 | tf_op jit(solution)/shard_map/ppermute | solution.py:372
  15.9 8.2 %collective-permute-start.7 = (bf16[64,1024]{1,0:T(8,128)(2,1)S(1)}, bf16[64,1024]{1,0:T(8,128)(2,1)S(1)}, u32[]{:S(2)}, u32[]{:S(2)}) collective-permute-start(bf16[64,1024]{1,0:T(8,128)(2,1)S(1)} %get-tuple-element.54.refs_1_), channel_id=1, source_target_pairs={{16,0},{17,1},{18,2},{19,3}} | collective-permute-start | bytes 393224 | tf_op jit(solution)/shard_map/ppermute | solution.py:372
  20.6 13.9 %collective-permute-start.6 = (bf16[272,1024]{1,0:T(8,128)(2,1)S(1)}, bf16[272,1024]{1,0:T(8,128)(2,1)S(1)}, u32[]{:S(2)}, u32[]{:S(2)}) collective-permute-start(bf16[272,1024]{1,0:T(8,128)(2,1)S(1)} %hold.3), channel_id=1, source_target_pairs={{0,1},{1,0},{2,3},{3,2},{4,5},{5,4},{6,7},{7,6},{8,9},{9,8},{10,11... | collective-permute-start | bytes 1671176 | tf_op jit(solution)/shard_map/ppermute | solution.py:287
  23.5 3.5 %collective-permute-start.13 = (bf16[64,1024]{1,0:T(8,128)(2,1)S(1)}, bf16[64,1024]{1,0:T(8,128)(2,1)S(1)}, u32[]{:S(2)}, u32[]{:S(2)}) collective-permute-start(bf16[64,1024]{1,0:T(8,128)(2,1)S(1)} %get-tuple-element.66.refs_5_), channel_id=1, source_target_pairs={{0,16},{1,17},{2,18},{3,19}} | collective-permute-start | bytes 393224 | tf_op jit(solution)/shard_map/ppermute | solution.py:395
  25.0 2.7 %collective-permute-start.12 = (bf16[64,1024]{1,0:T(8,128)(2,1)S(1)}, bf16[64,1024]{1,0:T(8,128)(2,1)S(1)}, u32[]{:S(2)}, u32[]{:S(2)}) collective-permute-start(bf16[64,1024]{1,0:T(8,128)(2,1)S(1)} %get-tuple-element.62.refs_5_), channel_id=1, source_target_pairs={{0,16},{1,17},{2,18},{3,19}} | collective-permute-start | bytes 393224 | tf_op jit(solution)/shard_map/ppermute | solution.py:395
  25.7 8.0 %collective-permute-start.10 = (bf16[128,1024]{1,0:T(8,128)(2,1)S(1)}, bf16[128,1024]{1,0:T(8,128)(2,1)S(1)}, u32[]{:S(2)}, u32[]{:S(2)}) collective-permute-start(bf16[128,1024]{1,0:T(8,128)(2,1)S(1)} %get-tuple-element.61.refs_10_.refs_7_), channel_id=1, source_target_pairs={{0,2},{1,3},{2,0},{3,1},{4,6},{5,7},{6,4},{7,5},{8,10},{9,11},{10,... | collective-permute-start | bytes 786440 | tf_op jit(solution)/shard_map/ppermute | solution.py:287
  27.0 1.4 %collective-permute-start.15 = (bf16[64,1024]{1,0:T(8,128)(2,1)S(1)}, bf16[64,1024]{1,0:T(8,128)(2,1)S(1)}, u32[]{:S(2)}, u32[]{:S(2)}) collective-permute-start(bf16[64,1024]{1,0:T(8,128)(2,1)S(1)} %get-tuple-element.69.refs_6_.refs_5_), channel_id=1, source_target_pairs={{0,8},{16,24},{1,9},{17,25},{2,10},{18,26},{3,11},{19,27}} | collective-permute-start | bytes 393224 | tf_op jit(solution)/shard_map/ppermute | solution.py:395
  27.7 6.8 %collective-permute-start.14 = (bf16[64,1024]{1,0:T(8,128)(2,1)S(1)}, bf16[64,1024]{1,0:T(8,128)(2,1)S(1)}, u32[]{:S(2)}, u32[]{:S(2)}) collective-permute-start(bf16[64,1024]{1,0:T(8,128)(2,1)S(1)} %get-tuple-element.70.refs_5_), channel_id=1, source_target_pairs={{0,8},{16,24},{1,9},{17,25},{2,10},{18,26},{3,11},{19,27}} | collective-permute-start | bytes 393224 | tf_op jit(solution)/shard_map/ppermute | solution.py:395
  28.5 16.5 %collective-permute-start.17 = (bf16[64,1024]{1,0:T(8,128)(2,1)S(1)}, bf16[64,1024]{1,0:T(8,128)(2,1)S(1)}, u32[]{:S(2)}, u32[]{:S(2)}) collective-permute-start(bf16[64,1024]{1,0:T(8,128)(2,1)S(1)} %get-tuple-element.73.refs_6_), channel_id=1, source_target_pairs={{0,4},{8,12},{16,20},{24,28},{1,5},{9,13},{17,21},{25,29},{2,6},{1... | collective-permute-start | bytes 393224 | tf_op jit(solution)/shard_map/ppermute | solution.py:405
  29.8 23.0 %collective-permute-start.9 = (bf16[128,1024]{1,0:T(8,128)(2,1)S(1)}, bf16[128,1024]{1,0:T(8,128)(2,1)S(1)}, u32[]{:S(2)}, u32[]{:S(2)}) collective-permute-start(bf16[128,1024]{1,0:T(8,128)(2,1)S(1)} %get-tuple-element.61.refs_10_.refs_7_), channel_id=1, source_target_pairs={{0,1},{1,0},{2,3},{3,2},{4,5},{5,4},{6,7},{7,6},{8,9},{9,8},{10,11... | collective-permute-start | bytes 786440 | tf_op jit(solution)/shard_map/ppermute | solution.py:287
  33.7 19.7 %collective-permute-start.11 = (bf16[128,1024]{1,0:T(8,128)(2,1)S(1)}, bf16[128,1024]{1,0:T(8,128)(2,1)S(1)}, u32[]{:S(2)}, u32[]{:S(2)}) collective-permute-start(bf16[128,1024]{1,0:T(8,128)(2,1)S(1)} %collective-permute-done.10.refs_12_.refs_9_), channel_id=1, source_target_pairs={{0,1},{1,0},{2,3},{3,2},{4,5},{5,4},{6,7},{7,6},{8,9},{9,8},{10,11... | collective-permute-start | bytes 786440 | tf_op jit(solution)/shard_map/ppermute | solution.py:287
  34.5 10.4 %copy-start = (s32[3]{0:T(128)S(1)}, s32[3]{0:T(128)}, u32[]{:S(2)}) copy-start(s32[3]{0:T(128)} %refs_0_.9) | copy-start | bytes 40
  34.6 18.9 %collective-permute-start.16 = (bf16[64,1024]{1,0:T(8,128)(2,1)S(1)}, bf16[64,1024]{1,0:T(8,128)(2,1)S(1)}, u32[]{:S(2)}, u32[]{:S(2)}) collective-permute-start(bf16[64,1024]{1,0:T(8,128)(2,1)S(1)} %get-tuple-element.74.refs_6_), channel_id=1, source_target_pairs={{0,4},{8,12},{16,20},{24,28},{1,5},{9,13},{17,21},{25,29},{2,6},{1... | collective-permute-start | bytes 393224 | tf_op jit(solution)/shard_map/ppermute | solution.py:405
  47.0 9.9 %collective-permute-start.21 = (bf16[4,64,256]{2,1,0:T(8,128)(2,1)S(1)}, bf16[4,64,256]{2,1,0:T(8,128)(2,1)S(1)}, u32[]{:S(2)}, u32[]{:S(2)}) collective-permute-start(bf16[4,64,256]{2,1,0:T(8,128)(2,1)S(1)} %get-tuple-element.83), channel_id=1, source_target_pairs={{0,1},{1,0},{2,3},{3,2},{4,5},{5,4},{6,7},{7,6},{8,9},{9,8},{10,11... | collective-permute-start | bytes 393224 | tf_op jit(solution)/shard_map/ppermute | solution.py:287
  50.7 7.0 %collective-permute-start.22 = (bf16[4,64,256]{2,1,0:T(8,128)(2,1)S(1)}, bf16[4,64,256]{2,1,0:T(8,128)(2,1)S(1)}, u32[]{:S(2)}, u32[]{:S(2)}) collective-permute-start(bf16[4,64,256]{2,1,0:T(8,128)(2,1)S(1)} %get-tuple-element.84), channel_id=1, source_target_pairs={{0,2},{1,3},{2,0},{3,1},{4,6},{5,7},{6,4},{7,5},{8,10},{9,11},{10,... | collective-permute-start | bytes 393224 | tf_op jit(solution)/shard_map/ppermute | solution.py:287
  52.8 6.2 %collective-permute-start.23 = (bf16[4,64,256]{2,1,0:T(8,128)(2,1)S(1)}, bf16[4,64,256]{2,1,0:T(8,128)(2,1)S(1)}, u32[]{:S(2)}, u32[]{:S(2)}) collective-permute-start(bf16[4,64,256]{2,1,0:T(8,128)(2,1)S(1)} %get-tuple-element.85), channel_id=1, source_target_pairs={{0,3},{1,2},{2,1},{3,0},{4,7},{5,6},{6,5},{7,4},{8,11},{9,10},{10,... | collective-permute-start | bytes 393224 | tf_op jit(solution)/shard_map/ppermute | solution.py:287
  55.5 4.9 %collective-permute-start.18 = (bf16[4,64,256]{2,1,0:T(8,128)(2,1)S(1)}, bf16[4,64,256]{2,1,0:T(8,128)(2,1)S(1)}, u32[]{:S(2)}, u32[]{:S(2)}) collective-permute-start(bf16[4,64,256]{2,1,0:T(8,128)(2,1)S(1)} %get-tuple-element.80), channel_id=1, source_target_pairs={{0,1},{1,0},{2,3},{3,2},{4,5},{5,4},{6,7},{7,6},{8,9},{9,8},{10,11... | collective-permute-start | bytes 393224 | tf_op jit(solution)/shard_map/ppermute | solution.py:287
  55.7 5.8 %collective-permute-start.19 = (bf16[4,64,256]{2,1,0:T(8,128)(2,1)S(1)}, bf16[4,64,256]{2,1,0:T(8,128)(2,1)S(1)}, u32[]{:S(2)}, u32[]{:S(2)}) collective-permute-start(bf16[4,64,256]{2,1,0:T(8,128)(2,1)S(1)} %get-tuple-element.81), channel_id=1, source_target_pairs={{0,2},{1,3},{2,0},{3,1},{4,6},{5,7},{6,4},{7,5},{8,10},{9,11},{10,... | collective-permute-start | bytes 393224 | tf_op jit(solution)/shard_map/ppermute | solution.py:287
  56.9 7.5 %collective-permute-start.20 = (bf16[4,64,256]{2,1,0:T(8,128)(2,1)S(1)}, bf16[4,64,256]{2,1,0:T(8,128)(2,1)S(1)}, u32[]{:S(2)}, u32[]{:S(2)}) collective-permute-start(bf16[4,64,256]{2,1,0:T(8,128)(2,1)S(1)} %get-tuple-element.82), channel_id=1, source_target_pairs={{0,3},{1,2},{2,1},{3,0},{4,7},{5,6},{6,5},{7,4},{8,11},{9,10},{10,... | collective-permute-start | bytes 393224 | tf_op jit(solution)/shard_map/ppermute | solution.py:287

commit v4 on v3

--- a/solution.py
+++ b/solution.py
@@ -10,7 +10,7 @@
 BF16 = jnp.bfloat16
 PAD = 16
 CHUNKS = 2
-WORK = 13*10**8
+WORK = 10**9
 LIMIT = 24 * 2**20
 VM = pl.BlockSpec(memory_space=pltpu.VMEM)
 SM = pl.BlockSpec(memory_space=pltpu.SMEM)
@@ -154,25 +154,26 @@
     send_up(level + 1, u_out, w_ref, send_ref)
 
 
-def root_body(level, u_ref, recv_ref, w_ref, base_ref, *refs):
-    lam_ref, msg_ref, ratio_ref, post_ref = refs[-5:-1] if len(refs) > 4 else refs
+def root_body(level, u_ref, recv_ref, base_ref, *refs):
+    lam_ref, ratio_ref, post_ref = refs[-4:-1] if len(refs) > 3 else refs
     lam = scaled(u_ref[...] * jnp.where(is_upper(level), recv_ref[...].astype(F32), 1.0))
     lam_ref[...] = lam
-    if len(refs) > 4:
-        for c, block in enumerate([item[...] for item in refs[:-5]] + [lam]):
+    if len(refs) > 3:
+        for c, block in enumerate([item[...] for item in refs[:-4]] + [lam]):
             refs[-1][c * lam.shape[0] : (c + 1) * lam.shape[0], :] = block
-    top = lax.axis_index("leaf") == 0
-
-    @pl.when(top)
+
+    @pl.when(lax.axis_index("leaf") == 0)
     def _():
         terms = lam.astype(F32) * base_ref[0:1, :]
         inverse = 1.0 / jnp.sum(terms, axis=1, keepdims=True)
         ratio_ref[...] = (base_ref[1:2, :] * inverse).astype(BF16)
         post_ref[...] = (terms * inverse).astype(BF16)
 
-    @pl.when(jnp.logical_not(top))
-    def _():
-        msg_ref[...] = lax.dot_general(lam, w_ref[0], (((1,), (1,)), ((), ())), preferred_element_type=F32)
+
+def top_body(lam_ref, w_ref, msg_ref):
+    @pl.when(lax.axis_index("leaf") > 0)
+    def _():
+        msg_ref[...] = lax.dot_general(lam_ref[...], w_ref[0], (((1,), (1,)), ((), ())), preferred_element_type=F32)
 
 
 def settle_body(level, recv_ref, lam_ref, msg_ref, w_ref, ratio_in, post_in, ratio_ref, post_ref):
@@ -371,12 +372,13 @@
     for c in every:
         recv = lax.ppermute(send[c], "leaf", up_pairs(levels - 1))
         final = c == CHUNKS - 1
-        top_lam[c], top_msg[c], ratio[c], post[c], *merged = run(
+        top_lam[c], ratio[c], post[c], *merged = run(
             functools.partial(root_body, levels - 1),
             "root",
-            (raw[c], recv, weights, base) + (tuple(top_lam[:c]) if final else ()),
-            (half(BF16), half(F32), half(BF16), half(BF16)) + ((pltpu.VMEM((rows, states), BF16),) if final else ()),
+            (raw[c], recv, base) + (tuple(top_lam[:c]) if final else ()),
+            (half(BF16), half(BF16), half(BF16)) + ((pltpu.VMEM((rows, states), BF16),) if final else ()),
         )
+        (top_msg[c],) = run(top_body, "top", (top_lam[c], weights), (half(F32),), work=1.0)
     all_tops = gather(far(merged[0]))
     all_lams = gather(near, send[-1:])
     raw_own, hots = run(
@@ -387,8 +389,8 @@
             pltpu.VMEM((nodes - 1, CHUNKS, groups * part, share), F32),
             pltpu.VMEM((nodes, CHUNKS, values, groups * part), BF16),
         ),
-        work=0.1,
-
+        after=(),
+        work=1.0,
     )
     for level in reversed(range(1, levels)):
         for c in every:

time: 67.5 us -> 66.4 us (0.984)
    ppermute x12, waiting for transfers between devices: 12.9 us -> 10.6 us  [swap(): lax.ppermute(value, 'rows', [(s, s ^ mask) for s in range(lax.axis_size('...]
    ppermute x2, waiting for transfers between devices: 9.08 us -> 10.9 us  [per_device(): recv = lax.ppermute(post[c], 'leaf', down_pairs(0))]
    pallas_call x20 -> x22, Pallas kernels: 16.7 us -> 16.8 us  [run(): pl.pallas_call(lambda *refs: body(*refs[:count], *refs[idle:]), name=name...]
where the time goes in v4:
time: 66.4 us; the launch traced here: 66 us
  starting transfers between devices  25.6 us (39%)
  waiting for transfers between devices  22.7 us (34%)
  Pallas kernels  16.8 us (25%)
  between operations  0.94 us (1%)
    pallas_call x22, Pallas kernels, run(): pl.pallas_call(lambda *refs: body(*refs[:count], *refs[idle:]), name=name...  16.8 us
    ppermute x12, starting transfers between devices, swap(): lax.ppermute(value, 'rows', [(s, s ^ mask) for s in range(lax.axis_size('...  15.1 us
    ppermute x2, waiting for transfers between devices, per_device(): recv = lax.ppermute(post[c], 'leaf', down_pairs(0))  10.9 us
    ppermute x12, waiting for transfers between devices, swap(): lax.ppermute(value, 'rows', [(s, s ^ mask) for s in range(lax.axis_size('...  10.6 us
    ppermute x4, starting transfers between devices, per_device(): recv = lax.ppermute(send[c], 'leaf', up_pairs(level))  3.96 us
    ppermute x4, starting transfers between devices, per_device(): recv = lax.ppermute(post[c], 'leaf', down_pairs(level))  2.68 us
    ppermute x2, starting transfers between devices, per_device(): recv = lax.ppermute(post[c], 'leaf', down_pairs(0))  2.58 us
  transfers between devices with their start and end apart: 24, of which 7 were waited for; matrix products, arithmetic and copies ran while one was open for 0% of the time, Pallas kernels for 14%

profile of v4, /device:TPU:13, one launch (start us, length us, event | category | flops | bytes accessed | tf_op | source)
XLA Modules:
  0.0 66.0 jit_solution(17598220167577063568)
XLA Ops:
  0.6 4.5 %prep.1 = (bf16[3,1024,1024]{2,1,0:T(8,128)(2,1)S(1)}, bf16[272,1024]{1,0:T(8,128)(2,1)S(1)}, f32[2,128,1024]{2,1,0:T(8,128)S(1)}, f32[8,1024]{1,0:T(8,128)S(1)}...) custom-call(s32[3]{0:T(128)} %refs_0_.9, s32[3,128]{1,0:T(4,128)} %refs_1_.1, bf16[3,256,1024]{2,1,0:T(8,128)(2,1)} %refs_2_.1, ...), custom_call_target="tpu_custom_call" | custom-call | flops 1000000000 | bytes 2097152 | tf_op jit(solution)/shard_map/prep/pallas_call | solution.py:22
  5.2 0.8 %first.2.refs_1_ = bf16[64,1024]{1,0:T(8,128)(2,1)S(1)} custom-call(f32[64,1024]{1,0:T(8,128)S(1)} %get-tuple-element.45.refs_0_, bf16[3,1024,1024]{2,1,0:T(8,128)(2,1)S(1)} %get-tuple-element.43.refs_1_.refs_2_.refs_0_.refs_3_.refs_4_.refs_17_), custom_call_target="tpu_custom_call" | custom-call | flops 1000000000 | bytes 2097152 | tf_op jit(solution)/shard_map/first/pallas_call | solution.py:22
  6.0 1.3 %collective-permute-start.3 = (bf16[64,1024]{1,0:T(8,128)(2,1)S(1)}, bf16[64,1024]{1,0:T(8,128)(2,1)S(1)}, u32[]{:S(2)}, u32[]{:S(2)}) collective-permute-start(bf16[64,1024]{1,0:T(8,128)(2,1)S(1)} %first.2.refs_1_), channel_id=1, source_target_pairs={{4,0},{12,8},{20,16},{28,24},{5,1},{13,9},{21,17},{29,25},{6,2},{1... | collective-permute-start | bytes 393224 | tf_op jit(solution)/shard_map/ppermute | solution.py:360
  7.3 1.3 %collective-permute-start.1 = (bf16[272,1024]{1,0:T(8,128)(2,1)S(1)}, bf16[272,1024]{1,0:T(8,128)(2,1)S(1)}, u32[]{:S(2)}, u32[]{:S(2)}) collective-permute-start(bf16[272,1024]{1,0:T(8,128)(2,1)S(1)} %hold.2.refs_2_.refs_1_.refs_7_.refs_3_), channel_id=1, source_target_pairs={{0,2},{1,3},{2,0},{3,1},{4,6},{5,7},{6,4},{7,5},{8,10},{9,11},{10,... | collective-permute-start | bytes 1671176 | tf_op jit(solution)/shard_map/ppermute | solution.py:288
  8.6 0.8 %first.3 = bf16[64,1024]{1,0:T(8,128)(2,1)S(1)} custom-call(f32[64,1024]{1,0:T(8,128)S(1)} %get-tuple-element.46.refs_0_, bf16[3,1024,1024]{2,1,0:T(8,128)(2,1)S(1)} %get-tuple-element.43.refs_1_.refs_2_.refs_0_.refs_3_.refs_4_.refs_17_, bf16[272,1024]{1,0:T(8,128)(2,1)S(1)} %hold.2.refs_2_.refs_1_.refs_7_.refs_3_), custom_call_target="tpu_custom_call" | custom-call | flops 1000000000 | bytes 2097152 | tf_op jit(solution)/shard_map/first/pallas_call | solution.py:22
  9.4 1.3 %collective-permute-start.2 = (bf16[64,1024]{1,0:T(8,128)(2,1)S(1)}, bf16[64,1024]{1,0:T(8,128)(2,1)S(1)}, u32[]{:S(2)}, u32[]{:S(2)}) collective-permute-start(bf16[64,1024]{1,0:T(8,128)(2,1)S(1)} %first.3), channel_id=1, source_target_pairs={{4,0},{12,8},{20,16},{28,24},{5,1},{13,9},{21,17},{29,25},{6,2},{1... | collective-permute-start | bytes 393224 | tf_op jit(solution)/shard_map/ppermute | solution.py:360
  10.8 0.7 %collective-permute-start.5 = (bf16[64,1024]{1,0:T(8,128)(2,1)S(1)}, bf16[64,1024]{1,0:T(8,128)(2,1)S(1)}, u32[]{:S(2)}, u32[]{:S(2)}) collective-permute-start(bf16[64,1024]{1,0:T(8,128)(2,1)S(1)} %get-tuple-element.47.refs_3_), channel_id=1, source_target_pairs={{8,0},{24,16},{9,1},{25,17},{10,2},{26,18},{11,3},{27,19}} | collective-permute-start | bytes 393224 | tf_op jit(solution)/shard_map/ppermute | solution.py:360
  11.5 1.2 %collective-permute-done.2.refs_1_ = bf16[64,1024]{1,0:T(8,128)(2,1)S(1)} collective-permute-done((bf16[64,1024]{1,0:T(8,128)(2,1)S(1)}, bf16[64,1024]{1,0:T(8,128)(2,1)S(1)}, u32[]{:S(2)}, u32[]{:S(2)}) %collective-permute-start.2) | collective-permute-done | bytes 131104 | tf_op jit(solution)/shard_map/ppermute | solution.py:360
  12.7 0.7 collective-permute-start.4
  13.3 0.0 collective-permute-done.5.refs_1_
  13.4 0.7 %collective-permute-start.8 = (bf16[64,1024]{1,0:T(8,128)(2,1)S(1)}, bf16[64,1024]{1,0:T(8,128)(2,1)S(1)}, u32[]{:S(2)}, u32[]{:S(2)}) collective-permute-start(bf16[64,1024]{1,0:T(8,128)(2,1)S(1)} %get-tuple-element.51.refs_3_), channel_id=1, source_target_pairs={{16,0},{17,1},{18,2},{19,3}} | collective-permute-start | bytes 393224 | tf_op jit(solution)/shard_map/ppermute | solution.py:373
  14.0 1.9 %collective-permute-start = (bf16[272,1024]{1,0:T(8,128)(2,1)S(1)}, bf16[272,1024]{1,0:T(8,128)(2,1)S(1)}, u32[]{:S(2)}, u32[]{:S(2)}) collective-permute-start(bf16[272,1024]{1,0:T(8,128)(2,1)S(1)} %hold.2.refs_2_.refs_1_.refs_7_.refs_3_), channel_id=1, source_target_pairs={{0,1},{1,0},{2,3},{3,2},{4,5},{5,4},{6,7},{7,6},{8,9},{9,8},{10,11... | collective-permute-start | bytes 1671176 | tf_op jit(solution)/shard_map/ppermute | solution.py:288
  15.9 0.0 collective-permute-done.4.refs_1_
  15.9 0.7 collective-permute-start.7
  16.6 0.0 collective-permute-done.8.refs_1_
  16.6 0.1 root.2
  16.7 0.7 %collective-permute-start.13 = (bf16[64,1024]{1,0:T(8,128)(2,1)S(1)}, bf16[64,1024]{1,0:T(8,128)(2,1)S(1)}, u32[]{:S(2)}, u32[]{:S(2)}) collective-permute-start(bf16[64,1024]{1,0:T(8,128)(2,1)S(1)} %get-tuple-element.63.refs_5_), channel_id=1, source_target_pairs={{0,16},{1,17},{2,18},{3,19}} | collective-permute-start | bytes 393224 | tf_op jit(solution)/shard_map/ppermute | solution.py:397
  17.4 3.2 %collective-permute-done.1.refs_3_.refs_9_.refs_5_ = bf16[272,1024]{1,0:T(8,128)(2,1)S(1)} collective-permute-done((bf16[272,1024]{1,0:T(8,128)(2,1)S(1)}, bf16[272,1024]{1,0:T(8,128)(2,1)S(1)}, u32[]{:S(2)}, u32[]{:S(2)}) %collective-permute-start.1) | collective-permute-done | bytes 557088 | tf_op jit(solution)/shard_map/ppermute | solution.py:288
  20.6 1.9 %collective-permute-start.6 = (bf16[272,1024]{1,0:T(8,128)(2,1)S(1)}, bf16[272,1024]{1,0:T(8,128)(2,1)S(1)}, u32[]{:S(2)}, u32[]{:S(2)}) collective-permute-start(bf16[272,1024]{1,0:T(8,128)(2,1)S(1)} %hold.3), channel_id=1, source_target_pairs={{0,1},{1,0},{2,3},{3,2},{4,5},{5,4},{6,7},{7,6},{8,9},{9,8},{10,11... | collective-permute-start | bytes 1671176 | tf_op jit(solution)/shard_map/ppermute | solution.py:288
  22.6 0.1 root.3
  22.7 0.7 %collective-permute-start.12 = (bf16[64,1024]{1,0:T(8,128)(2,1)S(1)}, bf16[64,1024]{1,0:T(8,128)(2,1)S(1)}, u32[]{:S(2)}, u32[]{:S(2)}) collective-permute-start(bf16[64,1024]{1,0:T(8,128)(2,1)S(1)} %get-tuple-element.60.refs_5_), channel_id=1, source_target_pairs={{0,16},{1,17},{2,18},{3,19}} | collective-permute-start | bytes 393224 | tf_op jit(solution)/shard_map/ppermute | solution.py:397
  23.4 1.3 %collective-permute-start.10 = (bf16[128,1024]{1,0:T(8,128)(2,1)S(1)}, bf16[128,1024]{1,0:T(8,128)(2,1)S(1)}, u32[]{:S(2)}, u32[]{:S(2)}) collective-permute-start(bf16[128,1024]{1,0:T(8,128)(2,1)S(1)} %get-tuple-element.59.refs_10_.refs_7_), channel_id=1, source_target_pairs={{0,2},{1,3},{2,0},{3,1},{4,6},{5,7},{6,4},{7,5},{8,10},{9,11},{10,... | collective-permute-start | bytes 786440 | tf_op jit(solution)/shard_map/ppermute | solution.py:288
  24.7 0.8 %top.3.refs_2_.refs_3_ = f32[64,1024]{1,0:T(8,128)S(1)} custom-call(bf16[64,1024]{1,0:T(8,128)(2,1)S(1)} %get-tuple-element.58.refs_3_.refs_0_.refs_1_.refs_2_, bf16[3,1024,1024]{2,1,0:T(8,128)(2,1)S(1)} %get-tuple-element.43.refs_1_.refs_2_.refs_0_.refs_3_.refs_4_.refs_17_), custom_call_target="tpu_custom_call" | custom-call | flops 1000000000 | bytes 2097152 | tf_op jit(solution)/shard_map/top/pallas_call | solution.py:22
  25.5 0.7 %collective-permute-start.15 = (bf16[64,1024]{1,0:T(8,128)(2,1)S(1)}, bf16[64,1024]{1,0:T(8,128)(2,1)S(1)}, u32[]{:S(2)}, u32[]{:S(2)}) collective-permute-start(bf16[64,1024]{1,0:T(8,128)(2,1)S(1)} %get-tuple-element.65.refs_6_.refs_5_), channel_id=1, source_target_pairs={{0,8},{16,24},{1,9},{17,25},{2,10},{18,26},{3,11},{19,27}} | collective-permute-start | bytes 393224 | tf_op jit(solution)/shard_map/ppermute | solution.py:397
  26.1 0.8 %top.2.refs_2_.refs_3_ = f32[64,1024]{1,0:T(8,128)S(1)} custom-call(bf16[64,1024]{1,0:T(8,128)(2,1)S(1)} %get-tuple-element.61.refs_0_.refs_1_.refs_2_, bf16[3,1024,1024]{2,1,0:T(8,128)(2,1)S(1)} %get-tuple-element.43.refs_1_.refs_2_.refs_0_.refs_3_.refs_4_.refs_17_), custom_call_target="tpu_custom_call" | custom-call | flops 1000000000 | bytes 2097152 | tf_op jit(solution)/shard_map/top/pallas_call | solution.py:22
  26.9 0.0 collective-permute-done.12.refs_0_
  27.0 0.7 %collective-permute-start.14 = (bf16[64,1024]{1,0:T(8,128)(2,1)S(1)}, bf16[64,1024]{1,0:T(8,128)(2,1)S(1)}, u32[]{:S(2)}, u32[]{:S(2)}) collective-permute-start(bf16[64,1024]{1,0:T(8,128)(2,1)S(1)} %get-tuple-element.66.refs_5_), channel_id=1, source_target_pairs={{0,8},{16,24},{1,9},{17,25},{2,10},{18,26},{3,11},{19,27}} | collective-permute-start | bytes 393224 | tf_op jit(solution)/shard_map/ppermute | solution.py:397
  27.7 1.3 %collective-permute-start.17 = (bf16[64,1024]{1,0:T(8,128)(2,1)S(1)}, bf16[64,1024]{1,0:T(8,128)(2,1)S(1)}, u32[]{:S(2)}, u32[]{:S(2)}) collective-permute-start(bf16[64,1024]{1,0:T(8,128)(2,1)S(1)} %get-tuple-element.69.refs_6_), channel_id=1, source_target_pairs={{0,4},{8,12},{16,20},{24,28},{1,5},{9,13},{17,21},{25,29},{2,6},{1... | collective-permute-start | bytes 393224 | tf_op jit(solution)/shard_map/ppermute | solution.py:407
  29.0 0.0 collective-permute-done.refs_2_.refs_8_.refs_4_
  29.0 0.4 collective-permute-start.9
  29.4 2.0 %collective-permute-done.10.refs_12_.refs_9_ = bf16[128,1024]{1,0:T(8,128)(2,1)S(1)} collective-permute-done((bf16[128,1024]{1,0:T(8,128)(2,1)S(1)}, bf16[128,1024]{1,0:T(8,128)(2,1)S(1)}, u32[]{:S(2)}, u32[]{:S(2)}) %collective-permute-start.10) | collective-permute-done | bytes 262176 | tf_op jit(solution)/shard_map/ppermute | solution.py:288
  31.4 0.8 %collective-permute-start.11 = (bf16[128,1024]{1,0:T(8,128)(2,1)S(1)}, bf16[128,1024]{1,0:T(8,128)(2,1)S(1)}, u32[]{:S(2)}, u32[]{:S(2)}) collective-permute-start(bf16[128,1024]{1,0:T(8,128)(2,1)S(1)} %collective-permute-done.10.refs_12_.refs_9_), channel_id=1, source_target_pairs={{0,1},{1,0},{2,3},{3,2},{4,5},{5,4},{6,7},{7,6},{8,9},{9,8},{10,11... | collective-permute-start | bytes 786440 | tf_op jit(solution)/shard_map/ppermute | solution.py:288
  32.2 1.3 %collective-permute-start.16 = (bf16[64,1024]{1,0:T(8,128)(2,1)S(1)}, bf16[64,1024]{1,0:T(8,128)(2,1)S(1)}, u32[]{:S(2)}, u32[]{:S(2)}) collective-permute-start(bf16[64,1024]{1,0:T(8,128)(2,1)S(1)} %get-tuple-element.70.refs_6_), channel_id=1, source_target_pairs={{0,4},{8,12},{16,20},{24,28},{1,5},{9,13},{17,21},{25,29},{2,6},{1... | collective-permute-start | bytes 393224 | tf_op jit(solution)/shard_map/ppermute | solution.py:407
  33.5 10.9 %collective-permute-done.17.refs_1_ = bf16[64,1024]{1,0:T(8,128)(2,1)S(1)} collective-permute-done((bf16[64,1024]{1,0:T(8,128)(2,1)S(1)}, bf16[64,1024]{1,0:T(8,128)(2,1)S(1)}, u32[]{:S(2)}, u32[]{:S(2)}) %collective-permute-start.17) | collective-permute-done | bytes 131104 | tf_op jit(solution)/shard_map/ppermute | solution.py:407
  44.5 2.1 %last.2 = (bf16[4,64,256]{2,1,0:T(8,128)(2,1)S(1)}, bf16[4,64,256]{2,1,0:T(8,128)(2,1)S(1)}, bf16[4,64,256]{2,1,0:T(8,128)(2,1)S(1)}, bf16[4,64,256]{2,1,0:T(8,128)(2,1)S(1)}) custom-call(s32[3]{0:T(128)S(1)} %copy-done, bf16[64,1024]{1,0:T(8,128)(2,1)S(1)} %collective-permute-done.17.refs_1_, ...), custom_call_target="tpu_custom_call" | custom-call | flops 1000000000 | bytes 2097152 | tf_op jit(solution)/shard_map/last/pallas_call | solution.py:22
  46.5 3.6 %collective-permute-start.21 = (bf16[4,64,256]{2,1,0:T(8,128)(2,1)S(1)}, bf16[4,64,256]{2,1,0:T(8,128)(2,1)S(1)}, u32[]{:S(2)}, u32[]{:S(2)}) collective-permute-start(bf16[4,64,256]{2,1,0:T(8,128)(2,1)S(1)} %get-tuple-element.79), channel_id=1, source_target_pairs={{0,1},{1,0},{2,3},{3,2},{4,5},{5,4},{6,7},{7,6},{8,9},{9,8},{10,11... | collective-permute-start | bytes 393224 | tf_op jit(solution)/shard_map/ppermute | solution.py:288
  50.1 1.1 %collective-permute-start.22 = (bf16[4,64,256]{2,1,0:T(8,128)(2,1)S(1)}, bf16[4,64,256]{2,1,0:T(8,128)(2,1)S(1)}, u32[]{:S(2)}, u32[]{:S(2)}) collective-permute-start(bf16[4,64,256]{2,1,0:T(8,128)(2,1)S(1)} %get-tuple-element.80), channel_id=1, source_target_pairs={{0,2},{1,3},{2,0},{3,1},{4,6},{5,7},{6,4},{7,5},{8,10},{9,11},{10,... | collective-permute-start | bytes 393224 | tf_op jit(solution)/shard_map/ppermute | solution.py:288
  51.2 0.9 %ready.1 = (f32[2,2,256,256]{3,2,1,0:T(8,128)S(1)}, bf16[3,2,256,256]{3,2,1,0:T(8,128)(2,1)S(1)}) custom-call(bf16[3,1024,1024]{2,1,0:T(8,128)(2,1)S(1)} %get-tuple-element.43.refs_1_.refs_2_.refs_0_.refs_3_.refs_4_.refs_17_, bf16[272,1024]{1,0:T(8,128)(2,1)S(1)} %hold.2.refs_2_.refs_1_.refs_7_.refs_3_, ...), custom_call_target="tpu_custom_call" | custom-call | flops 1000000000 | bytes 2097152 | tf_op jit(solution)/shard_map/ready/pallas_call | solution.py:22
  52.1 0.7 collective-permute-start.23
  52.8 2.1 %last.3 = (bf16[4,64,256]{2,1,0:T(8,128)(2,1)S(1)}, bf16[4,64,256]{2,1,0:T(8,128)(2,1)S(1)}, bf16[4,64,256]{2,1,0:T(8,128)(2,1)S(1)}, bf16[4,64,256]{2,1,0:T(8,128)(2,1)S(1)}) custom-call(s32[3]{0:T(128)S(1)} %copy-done, bf16[64,1024]{1,0:T(8,128)(2,1)S(1)} %collective-permute-done.16.refs_1_, ...), custom_call_target="tpu_custom_call" | custom-call | flops 1000000000 | bytes 2097152 | tf_op jit(solution)/shard_map/last/pallas_call | solution.py:22
  54.9 0.2 collective-permute-start.18
  55.1 1.1 %collective-permute-start.19 = (bf16[4,64,256]{2,1,0:T(8,128)(2,1)S(1)}, bf16[4,64,256]{2,1,0:T(8,128)(2,1)S(1)}, u32[]{:S(2)}, u32[]{:S(2)}) collective-permute-start(bf16[4,64,256]{2,1,0:T(8,128)(2,1)S(1)} %get-tuple-element.77), channel_id=1, source_target_pairs={{0,2},{1,3},{2,0},{3,1},{4,6},{5,7},{6,4},{7,5},{8,10},{9,11},{10,... | collective-permute-start | bytes 393224 | tf_op jit(solution)/shard_map/ppermute | solution.py:288
  56.2 0.9 %collective-permute-start.20 = (bf16[4,64,256]{2,1,0:T(8,128)(2,1)S(1)}, bf16[4,64,256]{2,1,0:T(8,128)(2,1)S(1)}, u32[]{:S(2)}, u32[]{:S(2)}) collective-permute-start(bf16[4,64,256]{2,1,0:T(8,128)(2,1)S(1)} %get-tuple-element.78), channel_id=1, source_target_pairs={{0,3},{1,2},{2,1},{3,0},{4,7},{5,6},{6,5},{7,4},{8,11},{9,10},{10,... | collective-permute-start | bytes 393224 | tf_op jit(solution)/shard_map/ppermute | solution.py:288
  57.1 1.5 %collective-permute-done.23.refs_14_ = bf16[4,64,256]{2,1,0:T(8,128)(2,1)S(1)} collective-permute-done((bf16[4,64,256]{2,1,0:T(8,128)(2,1)S(1)}, bf16[4,64,256]{2,1,0:T(8,128)(2,1)S(1)}, u32[]{:S(2)}, u32[]{:S(2)}) %collective-permute-start.23) | collective-permute-done | bytes 131104 | tf_op jit(solution)/shard_map/ppermute | solution.py:288
  58.6 1.3 %counts.2 = (f32[3,256,1024]{2,1,0:T(8,128)S(1)}, f32[3,256,256]{2,1,0:T(8,128)S(1)}) custom-call(s32[3]{0:T(128)S(1)} %copy-done, f32[2,2,256,256]{3,2,1,0:T(8,128)S(1)} %get-tuple-element.53.refs_14_.refs_1_, bf16[3,2,256,256]{3,2,1,0:T(8,128)(2,1)S(1)} %get-tuple-element.54.refs_2_, bf16[272,1024]{1,0:T(8,128)(2,1)S(1)} %hold.2.refs_2_.refs_1_.refs_7_.refs_3_, ...), custom_call_target="tpu_custom_call" | custom-call | flops 1000000000 | bytes 2097152 | tf_op jit(solution)/shard_map/counts/pallas_call | solution.py:22
  59.9 0.9 %collective-permute-done.19.refs_13_ = bf16[4,64,256]{2,1,0:T(8,128)(2,1)S(1)} collective-permute-done((bf16[4,64,256]{2,1,0:T(8,128)(2,1)S(1)}, bf16[4,64,256]{2,1,0:T(8,128)(2,1)S(1)}, u32[]{:S(2)}, u32[]{:S(2)}) %collective-permute-start.19) | collective-permute-done | bytes 131104 | tf_op jit(solution)/shard_map/ppermute | solution.py:288
  60.8 3.0 %collective-permute-done.20.refs_14_ = bf16[4,64,256]{2,1,0:T(8,128)(2,1)S(1)} collective-permute-done((bf16[4,64,256]{2,1,0:T(8,128)(2,1)S(1)}, bf16[4,64,256]{2,1,0:T(8,128)(2,1)S(1)}, u32[]{:S(2)}, u32[]{:S(2)}) %collective-permute-start.20) | collective-permute-done | bytes 131104 | tf_op jit(solution)/shard_map/ppermute | solution.py:288
  63.7 2.3 %counts.3 = (bf16[3,256,1024]{2,1,0:T(8,128)(2,1)}, bf16[3,256,256]{2,1,0:T(8,128)(2,1)}) custom-call(s32[3]{0:T(128)S(1)} %copy-done, f32[2,2,256,256]{3,2,1,0:T(8,128)S(1)} %get-tuple-element.53.refs_14_.refs_1_, bf16[3,2,256,256]{3,2,1,0:T(8,128)(2,1)S(1)} %get-tuple-element.54.refs_2_, bf16[272,1024]{1,0:T(8,128)(2,1)S(1)} %hold.2.refs_2_.refs_1_.refs_7_.refs_3_, ...), custom_call_target="tpu_custom_call" | custom-call | flops 1000000000 | bytes 2097152 | tf_op jit(solution)/shard_map/counts/pallas_call | solution.py:22
  (25 shorter events, 0.3 us)
Async XLA Ops:
  6.0 4.7 %collective-permute-start.3 = (bf16[64,1024]{1,0:T(8,128)(2,1)S(1)}, bf16[64,1024]{1,0:T(8,128)(2,1)S(1)}, u32[]{:S(2)}, u32[]{:S(2)}) collective-permute-start(bf16[64,1024]{1,0:T(8,128)(2,1)S(1)} %first.2.refs_1_), channel_id=1, source_target_pairs={{4,0},{12,8},{20,16},{28,24},{5,1},{13,9},{21,17},{29,25},{6,2},{1... | collective-permute-start | bytes 393224 | tf_op jit(solution)/shard_map/ppermute | solution.py:360
  7.3 13.2 %collective-permute-start.1 = (bf16[272,1024]{1,0:T(8,128)(2,1)S(1)}, bf16[272,1024]{1,0:T(8,128)(2,1)S(1)}, u32[]{:S(2)}, u32[]{:S(2)}) collective-permute-start(bf16[272,1024]{1,0:T(8,128)(2,1)S(1)} %hold.2.refs_2_.refs_1_.refs_7_.refs_3_), channel_id=1, source_target_pairs={{0,2},{1,3},{2,0},{3,1},{4,6},{5,7},{6,4},{7,5},{8,10},{9,11},{10,... | collective-permute-start | bytes 1671176 | tf_op jit(solution)/shard_map/ppermute | solution.py:288
  9.4 3.2 %collective-permute-start.2 = (bf16[64,1024]{1,0:T(8,128)(2,1)S(1)}, bf16[64,1024]{1,0:T(8,128)(2,1)S(1)}, u32[]{:S(2)}, u32[]{:S(2)}) collective-permute-start(bf16[64,1024]{1,0:T(8,128)(2,1)S(1)} %first.3), channel_id=1, source_target_pairs={{4,0},{12,8},{20,16},{28,24},{5,1},{13,9},{21,17},{29,25},{6,2},{1... | collective-permute-start | bytes 393224 | tf_op jit(solution)/shard_map/ppermute | solution.py:360
  10.8 2.6 %collective-permute-start.5 = (bf16[64,1024]{1,0:T(8,128)(2,1)S(1)}, bf16[64,1024]{1,0:T(8,128)(2,1)S(1)}, u32[]{:S(2)}, u32[]{:S(2)}) collective-permute-start(bf16[64,1024]{1,0:T(8,128)(2,1)S(1)} %get-tuple-element.47.refs_3_), channel_id=1, source_target_pairs={{8,0},{24,16},{9,1},{25,17},{10,2},{26,18},{11,3},{27,19}} | collective-permute-start | bytes 393224 | tf_op jit(solution)/shard_map/ppermute | solution.py:360
  12.7 3.3 %collective-permute-start.4 = (bf16[64,1024]{1,0:T(8,128)(2,1)S(1)}, bf16[64,1024]{1,0:T(8,128)(2,1)S(1)}, u32[]{:S(2)}, u32[]{:S(2)}) collective-permute-start(bf16[64,1024]{1,0:T(8,128)(2,1)S(1)} %get-tuple-element.49), channel_id=1, source_target_pairs={{8,0},{24,16},{9,1},{25,17},{10,2},{26,18},{11,3},{27,19}} | collective-permute-start | bytes 393224 | tf_op jit(solution)/shard_map/ppermute | solution.py:360
  13.4 3.2 %collective-permute-start.8 = (bf16[64,1024]{1,0:T(8,128)(2,1)S(1)}, bf16[64,1024]{1,0:T(8,128)(2,1)S(1)}, u32[]{:S(2)}, u32[]{:S(2)}) collective-permute-start(bf16[64,1024]{1,0:T(8,128)(2,1)S(1)} %get-tuple-element.51.refs_3_), channel_id=1, source_target_pairs={{16,0},{17,1},{18,2},{19,3}} | collective-permute-start | bytes 393224 | tf_op jit(solution)/shard_map/ppermute | solution.py:373
  14.0 15.0 %collective-permute-start = (bf16[272,1024]{1,0:T(8,128)(2,1)S(1)}, bf16[272,1024]{1,0:T(8,128)(2,1)S(1)}, u32[]{:S(2)}, u32[]{:S(2)}) collective-permute-start(bf16[272,1024]{1,0:T(8,128)(2,1)S(1)} %hold.2.refs_2_.refs_1_.refs_7_.refs_3_), channel_id=1, source_target_pairs={{0,1},{1,0},{2,3},{3,2},{4,5},{5,4},{6,7},{7,6},{8,9},{9,8},{10,11... | collective-permute-start | bytes 1671176 | tf_op jit(solution)/shard_map/ppermute | solution.py:288
  15.9 6.7 %collective-permute-start.7 = (bf16[64,1024]{1,0:T(8,128)(2,1)S(1)}, bf16[64,1024]{1,0:T(8,128)(2,1)S(1)}, u32[]{:S(2)}, u32[]{:S(2)}) collective-permute-start(bf16[64,1024]{1,0:T(8,128)(2,1)S(1)} %get-tuple-element.52.refs_1_), channel_id=1, source_target_pairs={{16,0},{17,1},{18,2},{19,3}} | collective-permute-start | bytes 393224 | tf_op jit(solution)/shard_map/ppermute | solution.py:373
  16.7 8.7 %collective-permute-start.13 = (bf16[64,1024]{1,0:T(8,128)(2,1)S(1)}, bf16[64,1024]{1,0:T(8,128)(2,1)S(1)}, u32[]{:S(2)}, u32[]{:S(2)}) collective-permute-start(bf16[64,1024]{1,0:T(8,128)(2,1)S(1)} %get-tuple-element.63.refs_5_), channel_id=1, source_target_pairs={{0,16},{1,17},{2,18},{3,19}} | collective-permute-start | bytes 393224 | tf_op jit(solution)/shard_map/ppermute | solution.py:397
  20.6 11.5 %collective-permute-start.6 = (bf16[272,1024]{1,0:T(8,128)(2,1)S(1)}, bf16[272,1024]{1,0:T(8,128)(2,1)S(1)}, u32[]{:S(2)}, u32[]{:S(2)}) collective-permute-start(bf16[272,1024]{1,0:T(8,128)(2,1)S(1)} %hold.3), channel_id=1, source_target_pairs={{0,1},{1,0},{2,3},{3,2},{4,5},{5,4},{6,7},{7,6},{8,9},{9,8},{10,11... | collective-permute-start | bytes 1671176 | tf_op jit(solution)/shard_map/ppermute | solution.py:288
  22.7 4.2 %collective-permute-start.12 = (bf16[64,1024]{1,0:T(8,128)(2,1)S(1)}, bf16[64,1024]{1,0:T(8,128)(2,1)S(1)}, u32[]{:S(2)}, u32[]{:S(2)}) collective-permute-start(bf16[64,1024]{1,0:T(8,128)(2,1)S(1)} %get-tuple-element.60.refs_5_), channel_id=1, source_target_pairs={{0,16},{1,17},{2,18},{3,19}} | collective-permute-start | bytes 393224 | tf_op jit(solution)/shard_map/ppermute | solution.py:397
  23.4 8.0 %collective-permute-start.10 = (bf16[128,1024]{1,0:T(8,128)(2,1)S(1)}, bf16[128,1024]{1,0:T(8,128)(2,1)S(1)}, u32[]{:S(2)}, u32[]{:S(2)}) collective-permute-start(bf16[128,1024]{1,0:T(8,128)(2,1)S(1)} %get-tuple-element.59.refs_10_.refs_7_), channel_id=1, source_target_pairs={{0,2},{1,3},{2,0},{3,1},{4,6},{5,7},{6,4},{7,5},{8,10},{9,11},{10,... | collective-permute-start | bytes 786440 | tf_op jit(solution)/shard_map/ppermute | solution.py:288
  25.5 2.2 %collective-permute-start.15 = (bf16[64,1024]{1,0:T(8,128)(2,1)S(1)}, bf16[64,1024]{1,0:T(8,128)(2,1)S(1)}, u32[]{:S(2)}, u32[]{:S(2)}) collective-permute-start(bf16[64,1024]{1,0:T(8,128)(2,1)S(1)} %get-tuple-element.65.refs_6_.refs_5_), channel_id=1, source_target_pairs={{0,8},{16,24},{1,9},{17,25},{2,10},{18,26},{3,11},{19,27}} | collective-permute-start | bytes 393224 | tf_op jit(solution)/shard_map/ppermute | solution.py:397
  27.0 5.2 %collective-permute-start.14 = (bf16[64,1024]{1,0:T(8,128)(2,1)S(1)}, bf16[64,1024]{1,0:T(8,128)(2,1)S(1)}, u32[]{:S(2)}, u32[]{:S(2)}) collective-permute-start(bf16[64,1024]{1,0:T(8,128)(2,1)S(1)} %get-tuple-element.66.refs_5_), channel_id=1, source_target_pairs={{0,8},{16,24},{1,9},{17,25},{2,10},{18,26},{3,11},{19,27}} | collective-permute-start | bytes 393224 | tf_op jit(solution)/shard_map/ppermute | solution.py:397
  27.7 16.8 %collective-permute-start.17 = (bf16[64,1024]{1,0:T(8,128)(2,1)S(1)}, bf16[64,1024]{1,0:T(8,128)(2,1)S(1)}, u32[]{:S(2)}, u32[]{:S(2)}) collective-permute-start(bf16[64,1024]{1,0:T(8,128)(2,1)S(1)} %get-tuple-element.69.refs_6_), channel_id=1, source_target_pairs={{0,4},{8,12},{16,20},{24,28},{1,5},{9,13},{17,21},{25,29},{2,6},{1... | collective-permute-start | bytes 393224 | tf_op jit(solution)/shard_map/ppermute | solution.py:407
  29.0 23.1 %collective-permute-start.9 = (bf16[128,1024]{1,0:T(8,128)(2,1)S(1)}, bf16[128,1024]{1,0:T(8,128)(2,1)S(1)}, u32[]{:S(2)}, u32[]{:S(2)}) collective-permute-start(bf16[128,1024]{1,0:T(8,128)(2,1)S(1)} %get-tuple-element.59.refs_10_.refs_7_), channel_id=1, source_target_pairs={{0,1},{1,0},{2,3},{3,2},{4,5},{5,4},{6,7},{7,6},{8,9},{9,8},{10,11... | collective-permute-start | bytes 786440 | tf_op jit(solution)/shard_map/ppermute | solution.py:288
  31.4 21.4 %collective-permute-start.11 = (bf16[128,1024]{1,0:T(8,128)(2,1)S(1)}, bf16[128,1024]{1,0:T(8,128)(2,1)S(1)}, u32[]{:S(2)}, u32[]{:S(2)}) collective-permute-start(bf16[128,1024]{1,0:T(8,128)(2,1)S(1)} %collective-permute-done.10.refs_12_.refs_9_), channel_id=1, source_target_pairs={{0,1},{1,0},{2,3},{3,2},{4,5},{5,4},{6,7},{7,6},{8,9},{9,8},{10,11... | collective-permute-start | bytes 786440 | tf_op jit(solution)/shard_map/ppermute | solution.py:288
  32.2 12.3 %copy-start = (s32[3]{0:T(128)S(1)}, s32[3]{0:T(128)}, u32[]{:S(2)}) copy-start(s32[3]{0:T(128)} %refs_0_.9) | copy-start | bytes 40
  32.2 20.6 %collective-permute-start.16 = (bf16[64,1024]{1,0:T(8,128)(2,1)S(1)}, bf16[64,1024]{1,0:T(8,128)(2,1)S(1)}, u32[]{:S(2)}, u32[]{:S(2)}) collective-permute-start(bf16[64,1024]{1,0:T(8,128)(2,1)S(1)} %get-tuple-element.70.refs_6_), channel_id=1, source_target_pairs={{0,4},{8,12},{16,20},{24,28},{1,5},{9,13},{17,21},{25,29},{2,6},{1... | collective-permute-start | bytes 393224 | tf_op jit(solution)/shard_map/ppermute | solution.py:407
  46.5 9.7 %collective-permute-start.21 = (bf16[4,64,256]{2,1,0:T(8,128)(2,1)S(1)}, bf16[4,64,256]{2,1,0:T(8,128)(2,1)S(1)}, u32[]{:S(2)}, u32[]{:S(2)}) collective-permute-start(bf16[4,64,256]{2,1,0:T(8,128)(2,1)S(1)} %get-tuple-element.79), channel_id=1, source_target_pairs={{0,1},{1,0},{2,3},{3,2},{4,5},{5,4},{6,7},{7,6},{8,9},{9,8},{10,11... | collective-permute-start | bytes 393224 | tf_op jit(solution)/shard_map/ppermute | solution.py:288
  50.1 7.0 %collective-permute-start.22 = (bf16[4,64,256]{2,1,0:T(8,128)(2,1)S(1)}, bf16[4,64,256]{2,1,0:T(8,128)(2,1)S(1)}, u32[]{:S(2)}, u32[]{:S(2)}) collective-permute-start(bf16[4,64,256]{2,1,0:T(8,128)(2,1)S(1)} %get-tuple-element.80), channel_id=1, source_target_pairs={{0,2},{1,3},{2,0},{3,1},{4,6},{5,7},{6,4},{7,5},{8,10},{9,11},{10,... | collective-permute-start | bytes 393224 | tf_op jit(solution)/shard_map/ppermute | solution.py:288
  52.1 6.4 %collective-permute-start.23 = (bf16[4,64,256]{2,1,0:T(8,128)(2,1)S(1)}, bf16[4,64,256]{2,1,0:T(8,128)(2,1)S(1)}, u32[]{:S(2)}, u32[]{:S(2)}) collective-permute-start(bf16[4,64,256]{2,1,0:T(8,128)(2,1)S(1)} %get-tuple-element.81), channel_id=1, source_target_pairs={{0,3},{1,2},{2,1},{3,0},{4,7},{5,6},{6,5},{7,4},{8,11},{9,10},{10,... | collective-permute-start | bytes 393224 | tf_op jit(solution)/shard_map/ppermute | solution.py:288
  54.9 5.0 %collective-permute-start.18 = (bf16[4,64,256]{2,1,0:T(8,128)(2,1)S(1)}, bf16[4,64,256]{2,1,0:T(8,128)(2,1)S(1)}, u32[]{:S(2)}, u32[]{:S(2)}) collective-permute-start(bf16[4,64,256]{2,1,0:T(8,128)(2,1)S(1)} %get-tuple-element.76), channel_id=1, source_target_pairs={{0,1},{1,0},{2,3},{3,2},{4,5},{5,4},{6,7},{7,6},{8,9},{9,8},{10,11... | collective-permute-start | bytes 393224 | tf_op jit(solution)/shard_map/ppermute | solution.py:288
  55.1 5.7 %collective-permute-start.19 = (bf16[4,64,256]{2,1,0:T(8,128)(2,1)S(1)}, bf16[4,64,256]{2,1,0:T(8,128)(2,1)S(1)}, u32[]{:S(2)}, u32[]{:S(2)}) collective-permute-start(bf16[4,64,256]{2,1,0:T(8,128)(2,1)S(1)} %get-tuple-element.77), channel_id=1, source_target_pairs={{0,2},{1,3},{2,0},{3,1},{4,6},{5,7},{6,4},{7,5},{8,10},{9,11},{10,... | collective-permute-start | bytes 393224 | tf_op jit(solution)/shard_map/ppermute | solution.py:288
  56.2 7.5 %collective-permute-start.20 = (bf16[4,64,256]{2,1,0:T(8,128)(2,1)S(1)}, bf16[4,64,256]{2,1,0:T(8,128)(2,1)S(1)}, u32[]{:S(2)}, u32[]{:S(2)}) collective-permute-start(bf16[4,64,256]{2,1,0:T(8,128)(2,1)S(1)} %get-tuple-element.78), channel_id=1, source_target_pairs={{0,3},{1,2},{2,1},{3,0},{4,7},{5,6},{6,5},{7,4},{8,11},{9,10},{10,... | collective-permute-start | bytes 393224 | tf_op jit(solution)/shard_map/ppermute | solution.py:288

commit v5 on v4

--- a/solution.py
+++ b/solution.py
@@ -10,7 +10,7 @@
 BF16 = jnp.bfloat16
 PAD = 16
 CHUNKS = 2
-WORK = 10**9
+WORK = 8*10**8
 LIMIT = 24 * 2**20
 VM = pl.BlockSpec(memory_space=pltpu.VMEM)
 SM = pl.BlockSpec(memory_space=pltpu.SMEM)
@@ -378,20 +378,9 @@
             (raw[c], recv, base) + (tuple(top_lam[:c]) if final else ()),
             (half(BF16), half(BF16), half(BF16)) + ((pltpu.VMEM((rows, states), BF16),) if final else ()),
         )
-        (top_msg[c],) = run(top_body, "top", (top_lam[c], weights), (half(F32),), work=1.0)
+        (top_msg[c],) = run(top_body, "top", (top_lam[c], weights), (half(F32),), work=2.0)
     all_tops = gather(far(merged[0]))
     all_lams = gather(near, send[-1:])
-    raw_own, hots = run(
-        functools.partial(ready_body, nodes, groups),
-        "ready",
-        (weights, *all_lams),
-        (
-            pltpu.VMEM((nodes - 1, CHUNKS, groups * part, share), F32),
-            pltpu.VMEM((nodes, CHUNKS, values, groups * part), BF16),
-        ),
-        after=(),
-        work=1.0,
-    )
     for level in reversed(range(1, levels)):
         for c in every:
             recv = lax.ppermute(post[c], "leaf", down_pairs(level))
@@ -412,11 +401,22 @@
             (pltpu.VMEM((nodes + 1, part, share), BF16),) * groups,
             (pltpu.VMEM((nodes + 1, part, states), BF16),),
             [SM] + [VM] * 8,
-            after=[own_posts[-1][0], *all_tops, raw_own] if c > 0 else [],
+            after=[own_posts[-1][0], *all_tops] if c > 0 else [],
         )
         order = sorted(range(1, groups), reverse=c < CHUNKS - 1)
         moved = {mask: swap(packs[mask], mask) for mask in order}
         own_posts.append([packs[0]] + [moved[mask] for mask in range(1, groups)])
+    raw_own, hots = run(
+        functools.partial(ready_body, nodes, groups),
+        "ready",
+        (weights, *all_lams),
+        (
+            pltpu.VMEM((nodes - 1, CHUNKS, groups * part, share), F32),
+            pltpu.VMEM((nodes, CHUNKS, values, groups * part), BF16),
+        ),
+        after=own_posts[0][-1:],
+        work=0.1,
+    )
     sums = ()
     for c in every:
         final = c == CHUNKS - 1

time: 66.4 us -> 68.1 us (1.026)
  waiting for transfers between devices: 22.7 us -> 24.1 us
    ppermute x2, waiting for transfers between devices: 10.9 us -> 15 us  [per_device(): recv = lax.ppermute(post[c], 'leaf', down_pairs(0))]
    ppermute x12, waiting for transfers between devices: 10.6 us -> 7.73 us  [swap(): lax.ppermute(value, 'rows', [(s, s ^ mask) for s in range(lax.axis_size('...]
  transfers between devices with their start and end apart: 24 -> 24, of which waited for: 7 -> 5; matrix products, arithmetic and copies ran while one was open for 0% -> 0% of each run, Pallas kernels for 14% -> 14%
where the time goes in v5:
time: 68.1 us; the launch traced here: 67.7 us
  starting transfers between devices  25.5 us (37%)
  waiting for transfers between devices  24.1 us (35%)
  Pallas kernels  16.9 us (25%)
  between operations  1.12 us (2%)
    pallas_call x22, Pallas kernels, run(): pl.pallas_call(lambda *refs: body(*refs[:count], *refs[idle:]), name=name...  16.9 us
    ppermute x2, waiting for transfers between devices, per_device(): recv = lax.ppermute(post[c], 'leaf', down_pairs(0))  15 us
    ppermute x12, starting transfers between devices, swap(): lax.ppermute(value, 'rows', [(s, s ^ mask) for s in range(lax.axis_size('...  15 us
    ppermute x12, waiting for transfers between devices, swap(): lax.ppermute(value, 'rows', [(s, s ^ mask) for s in range(lax.axis_size('...  7.73 us
    ppermute x4, starting transfers between devices, per_device(): recv = lax.ppermute(send[c], 'leaf', up_pairs(level))  3.95 us
    ppermute x4, starting transfers between devices, per_device(): recv = lax.ppermute(post[c], 'leaf', down_pairs(level))  2.68 us
    ppermute x2, starting transfers between devices, per_device(): recv = lax.ppermute(post[c], 'leaf', down_pairs(0))  2.58 us
  transfers between devices with their start and end apart: 24, of which 5 were waited for; matrix products, arithmetic and copies ran while one was open for 0% of the time, Pallas kernels for 14%

profile of v5, /device:TPU:13, one launch (start us, length us, event | category | flops | bytes accessed | tf_op | source)
XLA Modules:
  0.0 67.7 jit_solution(14254141723102181769)
XLA Ops:
  0.6 4.5 %prep.1 = (bf16[3,1024,1024]{2,1,0:T(8,128)(2,1)S(1)}, bf16[272,1024]{1,0:T(8,128)(2,1)S(1)}, f32[2,128,1024]{2,1,0:T(8,128)S(1)}, f32[8,1024]{1,0:T(8,128)S(1)}...) custom-call(s32[3]{0:T(128)} %refs_0_.9, s32[3,128]{1,0:T(4,128)} %refs_1_.1, bf16[3,256,1024]{2,1,0:T(8,128)(2,1)} %refs_2_.1, ...), custom_call_target="tpu_custom_call" | custom-call | flops 800000000 | bytes 2097152 | tf_op jit(solution)/shard_map/prep/pallas_call | solution.py:22
  5.2 0.8 %first.2.refs_1_ = bf16[64,1024]{1,0:T(8,128)(2,1)S(1)} custom-call(f32[64,1024]{1,0:T(8,128)S(1)} %get-tuple-element.45.refs_0_, bf16[3,1024,1024]{2,1,0:T(8,128)(2,1)S(1)} %get-tuple-element.43.refs_1_.refs_2_.refs_3_.refs_4_.refs_0_.refs_17_), custom_call_target="tpu_custom_call" | custom-call | flops 800000000 | bytes 2097152 | tf_op jit(solution)/shard_map/first/pallas_call | solution.py:22
  6.0 1.3 %collective-permute-start.3 = (bf16[64,1024]{1,0:T(8,128)(2,1)S(1)}, bf16[64,1024]{1,0:T(8,128)(2,1)S(1)}, u32[]{:S(2)}, u32[]{:S(2)}) collective-permute-start(bf16[64,1024]{1,0:T(8,128)(2,1)S(1)} %first.2.refs_1_), channel_id=1, source_target_pairs={{4,0},{12,8},{20,16},{28,24},{5,1},{13,9},{21,17},{29,25},{6,2},{1... | collective-permute-start | bytes 393224 | tf_op jit(solution)/shard_map/ppermute | solution.py:360
  7.3 0.8 %first.3 = bf16[64,1024]{1,0:T(8,128)(2,1)S(1)} custom-call(f32[64,1024]{1,0:T(8,128)S(1)} %get-tuple-element.46.refs_0_, bf16[3,1024,1024]{2,1,0:T(8,128)(2,1)S(1)} %get-tuple-element.43.refs_1_.refs_2_.refs_3_.refs_4_.refs_0_.refs_17_, bf16[272,1024]{1,0:T(8,128)(2,1)S(1)} %hold.2.refs_2_.refs_7_.refs_1_.refs_3_), custom_call_target="tpu_custom_call" | custom-call | flops 800000000 | bytes 2097152 | tf_op jit(solution)/shard_map/first/pallas_call | solution.py:22
  8.2 1.3 %collective-permute-start.2 = (bf16[64,1024]{1,0:T(8,128)(2,1)S(1)}, bf16[64,1024]{1,0:T(8,128)(2,1)S(1)}, u32[]{:S(2)}, u32[]{:S(2)}) collective-permute-start(bf16[64,1024]{1,0:T(8,128)(2,1)S(1)} %first.3), channel_id=1, source_target_pairs={{4,0},{12,8},{20,16},{28,24},{5,1},{13,9},{21,17},{29,25},{6,2},{1... | collective-permute-start | bytes 393224 | tf_op jit(solution)/shard_map/ppermute | solution.py:360
  9.5 1.3 %collective-permute-start.1 = (bf16[272,1024]{1,0:T(8,128)(2,1)S(1)}, bf16[272,1024]{1,0:T(8,128)(2,1)S(1)}, u32[]{:S(2)}, u32[]{:S(2)}) collective-permute-start(bf16[272,1024]{1,0:T(8,128)(2,1)S(1)} %hold.2.refs_2_.refs_7_.refs_1_.refs_3_), channel_id=1, source_target_pairs={{0,2},{1,3},{2,0},{3,1},{4,6},{5,7},{6,4},{7,5},{8,10},{9,11},{10,... | collective-permute-start | bytes 1671176 | tf_op jit(solution)/shard_map/ppermute | solution.py:288
  10.8 0.0 collective-permute-done.3.refs_1_
  10.8 0.7 collective-permute-start.5
  11.4 1.3 %collective-permute-done.2.refs_1_ = bf16[64,1024]{1,0:T(8,128)(2,1)S(1)} collective-permute-done((bf16[64,1024]{1,0:T(8,128)(2,1)S(1)}, bf16[64,1024]{1,0:T(8,128)(2,1)S(1)}, u32[]{:S(2)}, u32[]{:S(2)}) %collective-permute-start.2) | collective-permute-done | bytes 131104 | tf_op jit(solution)/shard_map/ppermute | solution.py:360
  12.8 0.7 collective-permute-start.4
  13.5 0.7 collective-permute-start.7
  14.2 0.7 collective-permute-start.12
  14.9 1.1 %collective-permute-start = (bf16[272,1024]{1,0:T(8,128)(2,1)S(1)}, bf16[272,1024]{1,0:T(8,128)(2,1)S(1)}, u32[]{:S(2)}, u32[]{:S(2)}) collective-permute-start(bf16[272,1024]{1,0:T(8,128)(2,1)S(1)} %hold.2.refs_2_.refs_7_.refs_1_.refs_3_), channel_id=1, source_target_pairs={{0,1},{1,0},{2,3},{3,2},{4,5},{5,4},{6,7},{7,6},{8,9},{9,8},{10,11... | collective-permute-start | bytes 1671176 | tf_op jit(solution)/shard_map/ppermute | solution.py:288
  16.0 0.1 root.2
  16.1 0.7 collective-permute-start.8
  16.8 0.1 root.3
  17.0 0.7 collective-permute-start.16
  17.6 1.3 %collective-permute-start.14 = (bf16[128,1024]{1,0:T(8,128)(2,1)S(1)}, bf16[128,1024]{1,0:T(8,128)(2,1)S(1)}, u32[]{:S(2)}, u32[]{:S(2)}) collective-permute-start(bf16[128,1024]{1,0:T(8,128)(2,1)S(1)} %get-tuple-element.67.refs_10_.refs_7_), channel_id=1, source_target_pairs={{0,2},{1,3},{2,0},{3,1},{4,6},{5,7},{6,4},{7,5},{8,10},{9,11},{10,... | collective-permute-start | bytes 786440 | tf_op jit(solution)/shard_map/ppermute | solution.py:288
  18.9 3.8 %collective-permute-done.1.refs_3_.refs_9_.refs_5_ = bf16[272,1024]{1,0:T(8,128)(2,1)S(1)} collective-permute-done((bf16[272,1024]{1,0:T(8,128)(2,1)S(1)}, bf16[272,1024]{1,0:T(8,128)(2,1)S(1)}, u32[]{:S(2)}, u32[]{:S(2)}) %collective-permute-start.1) | collective-permute-done | bytes 557088 | tf_op jit(solution)/shard_map/ppermute | solution.py:288
  22.8 3.4 %collective-permute-start.6 = (bf16[272,1024]{1,0:T(8,128)(2,1)S(1)}, bf16[272,1024]{1,0:T(8,128)(2,1)S(1)}, u32[]{:S(2)}, u32[]{:S(2)}) collective-permute-start(bf16[272,1024]{1,0:T(8,128)(2,1)S(1)} %hold.3), channel_id=1, source_target_pairs={{0,1},{1,0},{2,3},{3,2},{4,5},{5,4},{6,7},{7,6},{8,9},{9,8},{10,11... | collective-permute-start | bytes 1671176 | tf_op jit(solution)/shard_map/ppermute | solution.py:288
  26.2 0.8 %top.2.refs_2_.refs_3_ = f32[64,1024]{1,0:T(8,128)S(1)} custom-call(bf16[64,1024]{1,0:T(8,128)(2,1)S(1)} %get-tuple-element.56.refs_0_.refs_1_.refs_2_.refs_3_, bf16[3,1024,1024]{2,1,0:T(8,128)(2,1)S(1)} %get-tuple-element.43.refs_1_.refs_2_.refs_3_.refs_4_.refs_0_.refs_17_), custom_call_target="tpu_custom_call" | custom-call | flops 1600000000 | bytes 2097152 | tf_op jit(solution)/shard_map/top/pallas_call | solution.py:22
  26.9 0.0 collective-permute-done.8.refs_0_
  27.0 0.7 collective-permute-start.9
  27.6 0.8 %top.3.refs_2_.refs_3_ = f32[64,1024]{1,0:T(8,128)S(1)} custom-call(bf16[64,1024]{1,0:T(8,128)(2,1)S(1)} %get-tuple-element.69.refs_0_.refs_1_.refs_2_, bf16[3,1024,1024]{2,1,0:T(8,128)(2,1)S(1)} %get-tuple-element.43.refs_1_.refs_2_.refs_3_.refs_4_.refs_0_.refs_17_), custom_call_target="tpu_custom_call" | custom-call | flops 1600000000 | bytes 2097152 | tf_op jit(solution)/shard_map/top/pallas_call | solution.py:22
  28.5 0.7 collective-permute-start.17
  29.1 0.0 collective-permute-done.9.refs_0_
  29.2 0.1 collective-permute-start.13
  29.2 0.0 collective-permute-done.14.refs_12_.refs_9_
  29.3 0.9 %collective-permute-start.15 = (bf16[128,1024]{1,0:T(8,128)(2,1)S(1)}, bf16[128,1024]{1,0:T(8,128)(2,1)S(1)}, u32[]{:S(2)}, u32[]{:S(2)}) collective-permute-start(bf16[128,1024]{1,0:T(8,128)(2,1)S(1)} %collective-permute-done.14.refs_12_.refs_9_), channel_id=1, source_target_pairs={{0,1},{1,0},{2,3},{3,2},{4,5},{5,4},{6,7},{7,6},{8,9},{9,8},{10,11... | collective-permute-start | bytes 786440 | tf_op jit(solution)/shard_map/ppermute | solution.py:288
  30.2 0.0 collective-permute-done.refs_2_.refs_8_.refs_4_
  30.2 1.3 %collective-permute-start.10 = (bf16[64,1024]{1,0:T(8,128)(2,1)S(1)}, bf16[64,1024]{1,0:T(8,128)(2,1)S(1)}, u32[]{:S(2)}, u32[]{:S(2)}) collective-permute-start(bf16[64,1024]{1,0:T(8,128)(2,1)S(1)} %get-tuple-element.60.refs_6_), channel_id=1, source_target_pairs={{0,4},{8,12},{16,20},{24,28},{1,5},{9,13},{17,21},{25,29},{2,6},{1... | collective-permute-start | bytes 393224 | tf_op jit(solution)/shard_map/ppermute | solution.py:396
  31.5 0.0 collective-permute-done.17.refs_0_
  31.5 0.0 copy-start
  31.6 1.3 %collective-permute-start.18 = (bf16[64,1024]{1,0:T(8,128)(2,1)S(1)}, bf16[64,1024]{1,0:T(8,128)(2,1)S(1)}, u32[]{:S(2)}, u32[]{:S(2)}) collective-permute-start(bf16[64,1024]{1,0:T(8,128)(2,1)S(1)} %get-tuple-element.73.refs_6_), channel_id=1, source_target_pairs={{0,4},{8,12},{16,20},{24,28},{1,5},{9,13},{17,21},{25,29},{2,6},{1... | collective-permute-start | bytes 393224 | tf_op jit(solution)/shard_map/ppermute | solution.py:396
  32.9 15.0 %collective-permute-done.10.refs_1_ = bf16[64,1024]{1,0:T(8,128)(2,1)S(1)} collective-permute-done((bf16[64,1024]{1,0:T(8,128)(2,1)S(1)}, bf16[64,1024]{1,0:T(8,128)(2,1)S(1)}, u32[]{:S(2)}, u32[]{:S(2)}) %collective-permute-start.10) | collective-permute-done | bytes 131104 | tf_op jit(solution)/shard_map/ppermute | solution.py:396
  47.9 2.0 %last.2 = (bf16[4,64,256]{2,1,0:T(8,128)(2,1)S(1)}, bf16[4,64,256]{2,1,0:T(8,128)(2,1)S(1)}, bf16[4,64,256]{2,1,0:T(8,128)(2,1)S(1)}, bf16[4,64,256]{2,1,0:T(8,128)(2,1)S(1)}) custom-call(s32[3]{0:T(128)S(1)} %copy-done, bf16[64,1024]{1,0:T(8,128)(2,1)S(1)} %collective-permute-done.10.refs_1_, ...), custom_call_target="tpu_custom_call" | custom-call | flops 800000000 | bytes 2097152 | tf_op jit(solution)/shard_map/last/pallas_call | solution.py:22
  50.0 3.3 %collective-permute-start.11 = (bf16[4,64,256]{2,1,0:T(8,128)(2,1)S(1)}, bf16[4,64,256]{2,1,0:T(8,128)(2,1)S(1)}, u32[]{:S(2)}, u32[]{:S(2)}) collective-permute-start(bf16[4,64,256]{2,1,0:T(8,128)(2,1)S(1)} %get-tuple-element.63), channel_id=1, source_target_pairs={{0,3},{1,2},{2,1},{3,0},{4,7},{5,6},{6,5},{7,4},{8,11},{9,10},{10,... | collective-permute-start | bytes 393224 | tf_op jit(solution)/shard_map/ppermute | solution.py:288
  53.3 0.2 collective-permute-start.23
  53.5 2.2 %last.3 = (bf16[4,64,256]{2,1,0:T(8,128)(2,1)S(1)}, bf16[4,64,256]{2,1,0:T(8,128)(2,1)S(1)}, bf16[4,64,256]{2,1,0:T(8,128)(2,1)S(1)}, bf16[4,64,256]{2,1,0:T(8,128)(2,1)S(1)}) custom-call(s32[3]{0:T(128)S(1)} %copy-done, bf16[64,1024]{1,0:T(8,128)(2,1)S(1)} %collective-permute-done.18.refs_1_, ...), custom_call_target="tpu_custom_call" | custom-call | flops 800000000 | bytes 2097152 | tf_op jit(solution)/shard_map/last/pallas_call | solution.py:22
  55.8 0.4 collective-permute-start.19
  56.2 1.7 %collective-permute-start.20 = (bf16[4,64,256]{2,1,0:T(8,128)(2,1)S(1)}, bf16[4,64,256]{2,1,0:T(8,128)(2,1)S(1)}, u32[]{:S(2)}, u32[]{:S(2)}) collective-permute-start(bf16[4,64,256]{2,1,0:T(8,128)(2,1)S(1)} %get-tuple-element.78), channel_id=1, source_target_pairs={{0,2},{1,3},{2,0},{3,1},{4,6},{5,7},{6,4},{7,5},{8,10},{9,11},{10,... | collective-permute-start | bytes 393224 | tf_op jit(solution)/shard_map/ppermute | solution.py:288
  57.9 0.0 collective-permute-done.11.refs_5_.refs_14_
  57.9 1.2 %collective-permute-start.21 = (bf16[4,64,256]{2,1,0:T(8,128)(2,1)S(1)}, bf16[4,64,256]{2,1,0:T(8,128)(2,1)S(1)}, u32[]{:S(2)}, u32[]{:S(2)}) collective-permute-start(bf16[4,64,256]{2,1,0:T(8,128)(2,1)S(1)} %get-tuple-element.79), channel_id=1, source_target_pairs={{0,3},{1,2},{2,1},{3,0},{4,7},{5,6},{6,5},{7,4},{8,11},{9,10},{10,... | collective-permute-start | bytes 393224 | tf_op jit(solution)/shard_map/ppermute | solution.py:288
  59.1 0.9 %ready.1 = (f32[2,2,256,256]{3,2,1,0:T(8,128)S(1)}, bf16[3,2,256,256]{3,2,1,0:T(8,128)(2,1)S(1)}) custom-call(bf16[3,1024,1024]{2,1,0:T(8,128)(2,1)S(1)} %get-tuple-element.43.refs_1_.refs_2_.refs_3_.refs_4_.refs_0_.refs_17_, bf16[272,1024]{1,0:T(8,128)(2,1)S(1)} %hold.2.refs_2_.refs_7_.refs_1_.refs_3_, ...), custom_call_target="tpu_custom_call" | custom-call | flops 80000000 | bytes 2097152 | tf_op jit(solution)/shard_map/ready/pallas_call | solution.py:22
  60.1 1.3 %counts.2 = (f32[3,256,1024]{2,1,0:T(8,128)S(1)}, f32[3,256,256]{2,1,0:T(8,128)S(1)}) custom-call(s32[3]{0:T(128)S(1)} %copy-done, f32[2,2,256,256]{3,2,1,0:T(8,128)S(1)} %get-tuple-element.64.refs_1_, bf16[3,2,256,256]{3,2,1,0:T(8,128)(2,1)S(1)} %get-tuple-element.65.refs_2_, bf16[272,1024]{1,0:T(8,128)(2,1)S(1)} %hold.2.refs_2_.refs_7_.refs_1_.refs_3_, ...), custom_call_target="tpu_custom_call" | custom-call | flops 800000000 | bytes 2097152 | tf_op jit(solution)/shard_map/counts/pallas_call | solution.py:22
  61.4 1.0 %collective-permute-done.20.refs_13_ = bf16[4,64,256]{2,1,0:T(8,128)(2,1)S(1)} collective-permute-done((bf16[4,64,256]{2,1,0:T(8,128)(2,1)S(1)}, bf16[4,64,256]{2,1,0:T(8,128)(2,1)S(1)}, u32[]{:S(2)}, u32[]{:S(2)}) %collective-permute-start.20) | collective-permute-done | bytes 131104 | tf_op jit(solution)/shard_map/ppermute | solution.py:288
  62.3 3.0 %collective-permute-done.21.refs_14_ = bf16[4,64,256]{2,1,0:T(8,128)(2,1)S(1)} collective-permute-done((bf16[4,64,256]{2,1,0:T(8,128)(2,1)S(1)}, bf16[4,64,256]{2,1,0:T(8,128)(2,1)S(1)}, u32[]{:S(2)}, u32[]{:S(2)}) %collective-permute-start.21) | collective-permute-done | bytes 131104 | tf_op jit(solution)/shard_map/ppermute | solution.py:288
  65.3 2.3 %counts.3 = (bf16[3,256,1024]{2,1,0:T(8,128)(2,1)}, bf16[3,256,256]{2,1,0:T(8,128)(2,1)}) custom-call(s32[3]{0:T(128)S(1)} %copy-done, f32[2,2,256,256]{3,2,1,0:T(8,128)S(1)} %get-tuple-element.64.refs_1_, bf16[3,2,256,256]{3,2,1,0:T(8,128)(2,1)S(1)} %get-tuple-element.65.refs_2_, bf16[272,1024]{1,0:T(8,128)(2,1)S(1)} %hold.2.refs_2_.refs_7_.refs_1_.refs_3_, ...), custom_call_target="tpu_custom_call" | custom-call | flops 800000000 | bytes 2097152 | tf_op jit(solution)/shard_map/counts/pallas_call | solution.py:22
  (25 shorter events, 0.3 us)
Async XLA Ops:
  6.0 4.8 %collective-permute-start.3 = (bf16[64,1024]{1,0:T(8,128)(2,1)S(1)}, bf16[64,1024]{1,0:T(8,128)(2,1)S(1)}, u32[]{:S(2)}, u32[]{:S(2)}) collective-permute-start(bf16[64,1024]{1,0:T(8,128)(2,1)S(1)} %first.2.refs_1_), channel_id=1, source_target_pairs={{4,0},{12,8},{20,16},{28,24},{5,1},{13,9},{21,17},{29,25},{6,2},{1... | collective-permute-start | bytes 393224 | tf_op jit(solution)/shard_map/ppermute | solution.py:360
  8.2 4.6 %collective-permute-start.2 = (bf16[64,1024]{1,0:T(8,128)(2,1)S(1)}, bf16[64,1024]{1,0:T(8,128)(2,1)S(1)}, u32[]{:S(2)}, u32[]{:S(2)}) collective-permute-start(bf16[64,1024]{1,0:T(8,128)(2,1)S(1)} %first.3), channel_id=1, source_target_pairs={{4,0},{12,8},{20,16},{28,24},{5,1},{13,9},{21,17},{29,25},{6,2},{1... | collective-permute-start | bytes 393224 | tf_op jit(solution)/shard_map/ppermute | solution.py:360
  9.5 13.2 %collective-permute-start.1 = (bf16[272,1024]{1,0:T(8,128)(2,1)S(1)}, bf16[272,1024]{1,0:T(8,128)(2,1)S(1)}, u32[]{:S(2)}, u32[]{:S(2)}) collective-permute-start(bf16[272,1024]{1,0:T(8,128)(2,1)S(1)} %hold.2.refs_2_.refs_7_.refs_1_.refs_3_), channel_id=1, source_target_pairs={{0,2},{1,3},{2,0},{3,1},{4,6},{5,7},{6,4},{7,5},{8,10},{9,11},{10,... | collective-permute-start | bytes 1671176 | tf_op jit(solution)/shard_map/ppermute | solution.py:288
  10.8 2.7 %collective-permute-start.5 = (bf16[64,1024]{1,0:T(8,128)(2,1)S(1)}, bf16[64,1024]{1,0:T(8,128)(2,1)S(1)}, u32[]{:S(2)}, u32[]{:S(2)}) collective-permute-start(bf16[64,1024]{1,0:T(8,128)(2,1)S(1)} %get-tuple-element.47.refs_3_), channel_id=1, source_target_pairs={{8,0},{24,16},{9,1},{25,17},{10,2},{26,18},{11,3},{27,19}} | collective-permute-start | bytes 393224 | tf_op jit(solution)/shard_map/ppermute | solution.py:360
  12.8 1.4 %collective-permute-start.4 = (bf16[64,1024]{1,0:T(8,128)(2,1)S(1)}, bf16[64,1024]{1,0:T(8,128)(2,1)S(1)}, u32[]{:S(2)}, u32[]{:S(2)}) collective-permute-start(bf16[64,1024]{1,0:T(8,128)(2,1)S(1)} %get-tuple-element.49), channel_id=1, source_target_pairs={{8,0},{24,16},{9,1},{25,17},{10,2},{26,18},{11,3},{27,19}} | collective-permute-start | bytes 393224 | tf_op jit(solution)/shard_map/ppermute | solution.py:360
  13.5 2.5 %collective-permute-start.7 = (bf16[64,1024]{1,0:T(8,128)(2,1)S(1)}, bf16[64,1024]{1,0:T(8,128)(2,1)S(1)}, u32[]{:S(2)}, u32[]{:S(2)}) collective-permute-start(bf16[64,1024]{1,0:T(8,128)(2,1)S(1)} %get-tuple-element.51.refs_3_), channel_id=1, source_target_pairs={{16,0},{17,1},{18,2},{19,3}} | collective-permute-start | bytes 393224 | tf_op jit(solution)/shard_map/ppermute | solution.py:373
  14.2 2.6 %collective-permute-start.12 = (bf16[64,1024]{1,0:T(8,128)(2,1)S(1)}, bf16[64,1024]{1,0:T(8,128)(2,1)S(1)}, u32[]{:S(2)}, u32[]{:S(2)}) collective-permute-start(bf16[64,1024]{1,0:T(8,128)(2,1)S(1)} %get-tuple-element.52.refs_1_), channel_id=1, source_target_pairs={{16,0},{17,1},{18,2},{19,3}} | collective-permute-start | bytes 393224 | tf_op jit(solution)/shard_map/ppermute | solution.py:373
  14.9 15.4 %collective-permute-start = (bf16[272,1024]{1,0:T(8,128)(2,1)S(1)}, bf16[272,1024]{1,0:T(8,128)(2,1)S(1)}, u32[]{:S(2)}, u32[]{:S(2)}) collective-permute-start(bf16[272,1024]{1,0:T(8,128)(2,1)S(1)} %hold.2.refs_2_.refs_7_.refs_1_.refs_3_), channel_id=1, source_target_pairs={{0,1},{1,0},{2,3},{3,2},{4,5},{5,4},{6,7},{7,6},{8,9},{9,8},{10,11... | collective-permute-start | bytes 1671176 | tf_op jit(solution)/shard_map/ppermute | solution.py:288
  16.1 10.8 %collective-permute-start.8 = (bf16[64,1024]{1,0:T(8,128)(2,1)S(1)}, bf16[64,1024]{1,0:T(8,128)(2,1)S(1)}, u32[]{:S(2)}, u32[]{:S(2)}) collective-permute-start(bf16[64,1024]{1,0:T(8,128)(2,1)S(1)} %get-tuple-element.55.refs_5_), channel_id=1, source_target_pairs={{0,16},{1,17},{2,18},{3,19}} | collective-permute-start | bytes 393224 | tf_op jit(solution)/shard_map/ppermute | solution.py:386
  17.0 11.5 %collective-permute-start.16 = (bf16[64,1024]{1,0:T(8,128)(2,1)S(1)}, bf16[64,1024]{1,0:T(8,128)(2,1)S(1)}, u32[]{:S(2)}, u32[]{:S(2)}) collective-permute-start(bf16[64,1024]{1,0:T(8,128)(2,1)S(1)} %get-tuple-element.68.refs_5_), channel_id=1, source_target_pairs={{0,16},{1,17},{2,18},{3,19}} | collective-permute-start | bytes 393224 | tf_op jit(solution)/shard_map/ppermute | solution.py:386
  17.6 11.6 %collective-permute-start.14 = (bf16[128,1024]{1,0:T(8,128)(2,1)S(1)}, bf16[128,1024]{1,0:T(8,128)(2,1)S(1)}, u32[]{:S(2)}, u32[]{:S(2)}) collective-permute-start(bf16[128,1024]{1,0:T(8,128)(2,1)S(1)} %get-tuple-element.67.refs_10_.refs_7_), channel_id=1, source_target_pairs={{0,2},{1,3},{2,0},{3,1},{4,6},{5,7},{6,4},{7,5},{8,10},{9,11},{10,... | collective-permute-start | bytes 786440 | tf_op jit(solution)/shard_map/ppermute | solution.py:288
  22.8 8.8 %collective-permute-start.6 = (bf16[272,1024]{1,0:T(8,128)(2,1)S(1)}, bf16[272,1024]{1,0:T(8,128)(2,1)S(1)}, u32[]{:S(2)}, u32[]{:S(2)}) collective-permute-start(bf16[272,1024]{1,0:T(8,128)(2,1)S(1)} %hold.3), channel_id=1, source_target_pairs={{0,1},{1,0},{2,3},{3,2},{4,5},{5,4},{6,7},{7,6},{8,9},{9,8},{10,11... | collective-permute-start | bytes 1671176 | tf_op jit(solution)/shard_map/ppermute | solution.py:288
  27.0 2.2 %collective-permute-start.9 = (bf16[64,1024]{1,0:T(8,128)(2,1)S(1)}, bf16[64,1024]{1,0:T(8,128)(2,1)S(1)}, u32[]{:S(2)}, u32[]{:S(2)}) collective-permute-start(bf16[64,1024]{1,0:T(8,128)(2,1)S(1)} %get-tuple-element.58.refs_5_.refs_6_), channel_id=1, source_target_pairs={{0,8},{16,24},{1,9},{17,25},{2,10},{18,26},{3,11},{19,27}} | collective-permute-start | bytes 393224 | tf_op jit(solution)/shard_map/ppermute | solution.py:386
  28.5 3.1 %collective-permute-start.17 = (bf16[64,1024]{1,0:T(8,128)(2,1)S(1)}, bf16[64,1024]{1,0:T(8,128)(2,1)S(1)}, u32[]{:S(2)}, u32[]{:S(2)}) collective-permute-start(bf16[64,1024]{1,0:T(8,128)(2,1)S(1)} %get-tuple-element.71.refs_5_), channel_id=1, source_target_pairs={{0,8},{16,24},{1,9},{17,25},{2,10},{18,26},{3,11},{19,27}} | collective-permute-start | bytes 393224 | tf_op jit(solution)/shard_map/ppermute | solution.py:386
  29.2 24.2 %collective-permute-start.13 = (bf16[128,1024]{1,0:T(8,128)(2,1)S(1)}, bf16[128,1024]{1,0:T(8,128)(2,1)S(1)}, u32[]{:S(2)}, u32[]{:S(2)}) collective-permute-start(bf16[128,1024]{1,0:T(8,128)(2,1)S(1)} %get-tuple-element.67.refs_10_.refs_7_), channel_id=1, source_target_pairs={{0,1},{1,0},{2,3},{3,2},{4,5},{5,4},{6,7},{7,6},{8,9},{9,8},{10,11... | collective-permute-start | bytes 786440 | tf_op jit(solution)/shard_map/ppermute | solution.py:288
  29.3 24.3 %collective-permute-start.15 = (bf16[128,1024]{1,0:T(8,128)(2,1)S(1)}, bf16[128,1024]{1,0:T(8,128)(2,1)S(1)}, u32[]{:S(2)}, u32[]{:S(2)}) collective-permute-start(bf16[128,1024]{1,0:T(8,128)(2,1)S(1)} %collective-permute-done.14.refs_12_.refs_9_), channel_id=1, source_target_pairs={{0,1},{1,0},{2,3},{3,2},{4,5},{5,4},{6,7},{7,6},{8,9},{9,8},{10,11... | collective-permute-start | bytes 786440 | tf_op jit(solution)/shard_map/ppermute | solution.py:288
  30.2 17.7 %collective-permute-start.10 = (bf16[64,1024]{1,0:T(8,128)(2,1)S(1)}, bf16[64,1024]{1,0:T(8,128)(2,1)S(1)}, u32[]{:S(2)}, u32[]{:S(2)}) collective-permute-start(bf16[64,1024]{1,0:T(8,128)(2,1)S(1)} %get-tuple-element.60.refs_6_), channel_id=1, source_target_pairs={{0,4},{8,12},{16,20},{24,28},{1,5},{9,13},{17,21},{25,29},{2,6},{1... | collective-permute-start | bytes 393224 | tf_op jit(solution)/shard_map/ppermute | solution.py:396
  31.5 16.4 %copy-start = (s32[3]{0:T(128)S(1)}, s32[3]{0:T(128)}, u32[]{:S(2)}) copy-start(s32[3]{0:T(128)} %refs_0_.9) | copy-start | bytes 40
  31.6 21.9 %collective-permute-start.18 = (bf16[64,1024]{1,0:T(8,128)(2,1)S(1)}, bf16[64,1024]{1,0:T(8,128)(2,1)S(1)}, u32[]{:S(2)}, u32[]{:S(2)}) collective-permute-start(bf16[64,1024]{1,0:T(8,128)(2,1)S(1)} %get-tuple-element.73.refs_6_), channel_id=1, source_target_pairs={{0,4},{8,12},{16,20},{24,28},{1,5},{9,13},{17,21},{25,29},{2,6},{1... | collective-permute-start | bytes 393224 | tf_op jit(solution)/shard_map/ppermute | solution.py:396
  50.0 7.9 %collective-permute-start.11 = (bf16[4,64,256]{2,1,0:T(8,128)(2,1)S(1)}, bf16[4,64,256]{2,1,0:T(8,128)(2,1)S(1)}, u32[]{:S(2)}, u32[]{:S(2)}) collective-permute-start(bf16[4,64,256]{2,1,0:T(8,128)(2,1)S(1)} %get-tuple-element.63), channel_id=1, source_target_pairs={{0,3},{1,2},{2,1},{3,0},{4,7},{5,6},{6,5},{7,4},{8,11},{9,10},{10,... | collective-permute-start | bytes 393224 | tf_op jit(solution)/shard_map/ppermute | solution.py:288
  53.3 6.7 %collective-permute-start.22 = (bf16[4,64,256]{2,1,0:T(8,128)(2,1)S(1)}, bf16[4,64,256]{2,1,0:T(8,128)(2,1)S(1)}, u32[]{:S(2)}, u32[]{:S(2)}) collective-permute-start(bf16[4,64,256]{2,1,0:T(8,128)(2,1)S(1)} %get-tuple-element.80), channel_id=1, source_target_pairs={{0,1},{1,0},{2,3},{3,2},{4,5},{5,4},{6,7},{7,6},{8,9},{9,8},{10,11... | collective-permute-start | bytes 393224 | tf_op jit(solution)/shard_map/ppermute | solution.py:288
  53.3 6.7 %collective-permute-start.23 = (bf16[4,64,256]{2,1,0:T(8,128)(2,1)S(1)}, bf16[4,64,256]{2,1,0:T(8,128)(2,1)S(1)}, u32[]{:S(2)}, u32[]{:S(2)}) collective-permute-start(bf16[4,64,256]{2,1,0:T(8,128)(2,1)S(1)} %get-tuple-element.81), channel_id=1, source_target_pairs={{0,2},{1,3},{2,0},{3,1},{4,6},{5,7},{6,4},{7,5},{8,10},{9,11},{10,... | collective-permute-start | bytes 393224 | tf_op jit(solution)/shard_map/ppermute | solution.py:288
  55.8 5.6 %collective-permute-start.19 = (bf16[4,64,256]{2,1,0:T(8,128)(2,1)S(1)}, bf16[4,64,256]{2,1,0:T(8,128)(2,1)S(1)}, u32[]{:S(2)}, u32[]{:S(2)}) collective-permute-start(bf16[4,64,256]{2,1,0:T(8,128)(2,1)S(1)} %get-tuple-element.77), channel_id=1, source_target_pairs={{0,1},{1,0},{2,3},{3,2},{4,5},{5,4},{6,7},{7,6},{8,9},{9,8},{10,11... | collective-permute-start | bytes 393224 | tf_op jit(solution)/shard_map/ppermute | solution.py:288
  56.2 6.1 %collective-permute-start.20 = (bf16[4,64,256]{2,1,0:T(8,128)(2,1)S(1)}, bf16[4,64,256]{2,1,0:T(8,128)(2,1)S(1)}, u32[]{:S(2)}, u32[]{:S(2)}) collective-permute-start(bf16[4,64,256]{2,1,0:T(8,128)(2,1)S(1)} %get-tuple-element.78), channel_id=1, source_target_pairs={{0,2},{1,3},{2,0},{3,1},{4,6},{5,7},{6,4},{7,5},{8,10},{9,11},{10,... | collective-permute-start | bytes 393224 | tf_op jit(solution)/shard_map/ppermute | solution.py:288
  57.9 7.4 %collective-permute-start.21 = (bf16[4,64,256]{2,1,0:T(8,128)(2,1)S(1)}, bf16[4,64,256]{2,1,0:T(8,128)(2,1)S(1)}, u32[]{:S(2)}, u32[]{:S(2)}) collective-permute-start(bf16[4,64,256]{2,1,0:T(8,128)(2,1)S(1)} %get-tuple-element.79), channel_id=1, source_target_pairs={{0,3},{1,2},{2,1},{3,0},{4,7},{5,6},{6,5},{7,4},{8,11},{9,10},{10,... | collective-permute-start | bytes 393224 | tf_op jit(solution)/shard_map/ppermute | solution.py:288

commit v6 on v4

--- a/solution.py
+++ b/solution.py
@@ -10,7 +10,7 @@
 BF16 = jnp.bfloat16
 PAD = 16
 CHUNKS = 2
-WORK = 10**9
+WORK = 10*10**8
 LIMIT = 24 * 2**20
 VM = pl.BlockSpec(memory_space=pltpu.VMEM)
 SM = pl.BlockSpec(memory_space=pltpu.SMEM)
@@ -390,7 +390,7 @@
             pltpu.VMEM((nodes, CHUNKS, values, groups * part), BF16),
         ),
         after=(),
-        work=1.0,
+        work=0.1,
     )
     for level in reversed(range(1, levels)):
         for c in every:
@@ -400,7 +400,7 @@
                 "settle",
                 (recv, top_lam[c], top_msg[c], weights, ratio[c], post[c]),
                 (half(BF16), half(BF16)),
-                after=post[:c][-1:] + (all_lams if level == 1 and c == CHUNKS - 1 else []),
+                after=post[:c][-1:] + ([raw_own] if level == 1 and c == CHUNKS - 1 else []),
             )
     own_posts = []
     for c in every:
@@ -412,7 +412,7 @@
             (pltpu.VMEM((nodes + 1, part, share), BF16),) * groups,
             (pltpu.VMEM((nodes + 1, part, states), BF16),),
             [SM] + [VM] * 8,
-            after=[own_posts[-1][0], *all_tops, raw_own] if c > 0 else [],
+            after=[own_posts[-1][0], *all_tops] if c > 0 else [],
         )
         order = sorted(range(1, groups), reverse=c < CHUNKS - 1)
         moved = {mask: swap(packs[mask], mask) for mask in order}

time: 66.4 us -> 67.8 us (1.021)
  waiting for transfers between devices: 22.7 us -> 26.5 us
  starting transfers between devices: 25.6 us -> 23.1 us
    ppermute x12, starting transfers between devices: 15.1 us -> 12.5 us  [swap(): lax.ppermute(value, 'rows', [(s, s ^ mask) for s in range(lax.axis_size('...]
    ppermute x12, waiting for transfers between devices: 10.6 us -> 12.9 us  [swap(): lax.ppermute(value, 'rows', [(s, s ^ mask) for s in range(lax.axis_size('...]
    ppermute x2, waiting for transfers between devices: 10.9 us -> 12.3 us  [per_device(): recv = lax.ppermute(post[c], 'leaf', down_pairs(0))]
  transfers between devices with their start and end apart: 24 -> 24, of which waited for: 7 -> 7; matrix products, arithmetic and copies ran while one was open for 0% -> 0% of each run, Pallas kernels for 14% -> 13%
where the time goes in v6:
time: 67.8 us; the launch traced here: 67.3 us
  waiting for transfers between devices  26.5 us (39%)
  starting transfers between devices  23.1 us (34%)
  Pallas kernels  16.7 us (25%)
  between operations  0.95 us (1%)
    pallas_call x22, Pallas kernels, run(): pl.pallas_call(lambda *refs: body(*refs[:count], *refs[idle:]), name=name...  16.7 us
    ppermute x12, waiting for transfers between devices, swap(): lax.ppermute(value, 'rows', [(s, s ^ mask) for s in range(lax.axis_size('...  12.9 us
    ppermute x12, starting transfers between devices, swap(): lax.ppermute(value, 'rows', [(s, s ^ mask) for s in range(lax.axis_size('...  12.5 us
    ppermute x2, waiting for transfers between devices, per_device(): recv = lax.ppermute(post[c], 'leaf', down_pairs(0))  12.3 us
    ppermute x4, starting transfers between devices, per_device(): recv = lax.ppermute(send[c], 'leaf', up_pairs(level))  3.96 us
    ppermute x4, starting transfers between devices, per_device(): recv = lax.ppermute(post[c], 'leaf', down_pairs(level))  2.68 us
    ppermute x2, starting transfers between devices, per_device(): recv = lax.ppermute(post[c], 'leaf', down_pairs(0))  2.58 us
  transfers between devices with their start and end apart: 24, of which 7 were waited for; matrix products, arithmetic and copies ran while one was open for 0% of the time, Pallas kernels for 13%

profile of v6, /device:TPU:13, one launch (start us, length us, event | category | flops | bytes accessed | tf_op | source)
XLA Modules:
  0.0 67.3 jit_solution(13378375072653112501)
XLA Ops:
  0.6 4.5 %prep.1 = (bf16[3,1024,1024]{2,1,0:T(8,128)(2,1)S(1)}, bf16[272,1024]{1,0:T(8,128)(2,1)S(1)}, f32[2,128,1024]{2,1,0:T(8,128)S(1)}, f32[8,1024]{1,0:T(8,128)S(1)}...) custom-call(s32[3]{0:T(128)} %refs_0_.9, s32[3,128]{1,0:T(4,128)} %refs_1_.1, bf16[3,256,1024]{2,1,0:T(8,128)(2,1)} %refs_2_.1, ...), custom_call_target="tpu_custom_call" | custom-call | flops 1000000000 | bytes 2097152 | tf_op jit(solution)/shard_map/prep/pallas_call | solution.py:22
  5.2 0.8 %first.2.refs_1_ = bf16[64,1024]{1,0:T(8,128)(2,1)S(1)} custom-call(f32[64,1024]{1,0:T(8,128)S(1)} %get-tuple-element.45.refs_0_, bf16[3,1024,1024]{2,1,0:T(8,128)(2,1)S(1)} %get-tuple-element.43.refs_1_.refs_2_.refs_0_.refs_3_.refs_4_.refs_17_), custom_call_target="tpu_custom_call" | custom-call | flops 1000000000 | bytes 2097152 | tf_op jit(solution)/shard_map/first/pallas_call | solution.py:22
  6.0 1.3 %collective-permute-start.3 = (bf16[64,1024]{1,0:T(8,128)(2,1)S(1)}, bf16[64,1024]{1,0:T(8,128)(2,1)S(1)}, u32[]{:S(2)}, u32[]{:S(2)}) collective-permute-start(bf16[64,1024]{1,0:T(8,128)(2,1)S(1)} %first.2.refs_1_), channel_id=1, source_target_pairs={{4,0},{12,8},{20,16},{28,24},{5,1},{13,9},{21,17},{29,25},{6,2},{1... | collective-permute-start | bytes 393224 | tf_op jit(solution)/shard_map/ppermute | solution.py:360
  7.3 1.3 %collective-permute-start.1 = (bf16[272,1024]{1,0:T(8,128)(2,1)S(1)}, bf16[272,1024]{1,0:T(8,128)(2,1)S(1)}, u32[]{:S(2)}, u32[]{:S(2)}) collective-permute-start(bf16[272,1024]{1,0:T(8,128)(2,1)S(1)} %hold.2.refs_2_.refs_1_.refs_7_.refs_3_), channel_id=1, source_target_pairs={{0,2},{1,3},{2,0},{3,1},{4,6},{5,7},{6,4},{7,5},{8,10},{9,11},{10,... | collective-permute-start | bytes 1671176 | tf_op jit(solution)/shard_map/ppermute | solution.py:288
  8.6 0.8 %first.3 = bf16[64,1024]{1,0:T(8,128)(2,1)S(1)} custom-call(f32[64,1024]{1,0:T(8,128)S(1)} %get-tuple-element.46.refs_0_, bf16[3,1024,1024]{2,1,0:T(8,128)(2,1)S(1)} %get-tuple-element.43.refs_1_.refs_2_.refs_0_.refs_3_.refs_4_.refs_17_, bf16[272,1024]{1,0:T(8,128)(2,1)S(1)} %hold.2.refs_2_.refs_1_.refs_7_.refs_3_), custom_call_target="tpu_custom_call" | custom-call | flops 1000000000 | bytes 2097152 | tf_op jit(solution)/shard_map/first/pallas_call | solution.py:22
  9.4 1.3 %collective-permute-start.2 = (bf16[64,1024]{1,0:T(8,128)(2,1)S(1)}, bf16[64,1024]{1,0:T(8,128)(2,1)S(1)}, u32[]{:S(2)}, u32[]{:S(2)}) collective-permute-start(bf16[64,1024]{1,0:T(8,128)(2,1)S(1)} %first.3), channel_id=1, source_target_pairs={{4,0},{12,8},{20,16},{28,24},{5,1},{13,9},{21,17},{29,25},{6,2},{1... | collective-permute-start | bytes 393224 | tf_op jit(solution)/shard_map/ppermute | solution.py:360
  10.7 0.0 collective-permute-done.3.refs_1_
  10.8 0.7 collective-permute-start.5
  11.5 1.2 %collective-permute-done.2.refs_1_ = bf16[64,1024]{1,0:T(8,128)(2,1)S(1)} collective-permute-done((bf16[64,1024]{1,0:T(8,128)(2,1)S(1)}, bf16[64,1024]{1,0:T(8,128)(2,1)S(1)}, u32[]{:S(2)}, u32[]{:S(2)}) %collective-permute-start.2) | collective-permute-done | bytes 131104 | tf_op jit(solution)/shard_map/ppermute | solution.py:360
  12.7 0.7 collective-permute-start.4
  13.4 0.7 collective-permute-start.8
  14.0 1.9 %collective-permute-start = (bf16[272,1024]{1,0:T(8,128)(2,1)S(1)}, bf16[272,1024]{1,0:T(8,128)(2,1)S(1)}, u32[]{:S(2)}, u32[]{:S(2)}) collective-permute-start(bf16[272,1024]{1,0:T(8,128)(2,1)S(1)} %hold.2.refs_2_.refs_1_.refs_7_.refs_3_), channel_id=1, source_target_pairs={{0,1},{1,0},{2,3},{3,2},{4,5},{5,4},{6,7},{7,6},{8,9},{9,8},{10,11... | collective-permute-start | bytes 1671176 | tf_op jit(solution)/shard_map/ppermute | solution.py:288
  15.9 0.7 collective-permute-start.7
  16.6 0.1 root.2
  16.7 0.7 collective-permute-start.13
  17.4 3.2 %collective-permute-done.1.refs_3_.refs_5_ = bf16[272,1024]{1,0:T(8,128)(2,1)S(1)} collective-permute-done((bf16[272,1024]{1,0:T(8,128)(2,1)S(1)}, bf16[272,1024]{1,0:T(8,128)(2,1)S(1)}, u32[]{:S(2)}, u32[]{:S(2)}) %collective-permute-start.1) | collective-permute-done | bytes 557088 | tf_op jit(solution)/shard_map/ppermute | solution.py:288
  20.6 1.9 %collective-permute-start.6 = (bf16[272,1024]{1,0:T(8,128)(2,1)S(1)}, bf16[272,1024]{1,0:T(8,128)(2,1)S(1)}, u32[]{:S(2)}, u32[]{:S(2)}) collective-permute-start(bf16[272,1024]{1,0:T(8,128)(2,1)S(1)} %hold.3), channel_id=1, source_target_pairs={{0,1},{1,0},{2,3},{3,2},{4,5},{5,4},{6,7},{7,6},{8,9},{9,8},{10,11... | collective-permute-start | bytes 1671176 | tf_op jit(solution)/shard_map/ppermute | solution.py:288
  22.6 0.0 collective-permute-done.7.refs_1_
  22.6 0.1 root.3
  22.7 0.7 collective-permute-start.12
  23.4 1.3 %collective-permute-start.10 = (bf16[128,1024]{1,0:T(8,128)(2,1)S(1)}, bf16[128,1024]{1,0:T(8,128)(2,1)S(1)}, u32[]{:S(2)}, u32[]{:S(2)}) collective-permute-start(bf16[128,1024]{1,0:T(8,128)(2,1)S(1)} %get-tuple-element.59.refs_10_.refs_7_), channel_id=1, source_target_pairs={{0,2},{1,3},{2,0},{3,1},{4,6},{5,7},{6,4},{7,5},{8,10},{9,11},{10,... | collective-permute-start | bytes 786440 | tf_op jit(solution)/shard_map/ppermute | solution.py:288
  24.7 0.8 %top.3.refs_2_.refs_3_ = f32[64,1024]{1,0:T(8,128)S(1)} custom-call(bf16[64,1024]{1,0:T(8,128)(2,1)S(1)} %get-tuple-element.58.refs_3_.refs_0_.refs_1_.refs_2_, bf16[3,1024,1024]{2,1,0:T(8,128)(2,1)S(1)} %get-tuple-element.43.refs_1_.refs_2_.refs_0_.refs_3_.refs_4_.refs_17_), custom_call_target="tpu_custom_call" | custom-call | flops 1000000000 | bytes 2097152 | tf_op jit(solution)/shard_map/top/pallas_call | solution.py:22
  25.4 0.0 collective-permute-done.13.refs_0_
  25.5 0.7 collective-permute-start.15
  26.1 0.8 %top.2.refs_2_.refs_3_ = f32[64,1024]{1,0:T(8,128)S(1)} custom-call(bf16[64,1024]{1,0:T(8,128)(2,1)S(1)} %get-tuple-element.61.refs_0_.refs_1_.refs_2_, bf16[3,1024,1024]{2,1,0:T(8,128)(2,1)S(1)} %get-tuple-element.43.refs_1_.refs_2_.refs_0_.refs_3_.refs_4_.refs_17_), custom_call_target="tpu_custom_call" | custom-call | flops 1000000000 | bytes 2097152 | tf_op jit(solution)/shard_map/top/pallas_call | solution.py:22
  27.0 0.7 collective-permute-start.14
  27.6 0.0 collective-permute-done.15.refs_0_
  27.7 0.4 collective-permute-start.9
  28.0 3.3 %collective-permute-done.10.refs_12_.refs_9_ = bf16[128,1024]{1,0:T(8,128)(2,1)S(1)} collective-permute-done((bf16[128,1024]{1,0:T(8,128)(2,1)S(1)}, bf16[128,1024]{1,0:T(8,128)(2,1)S(1)}, u32[]{:S(2)}, u32[]{:S(2)}) %collective-permute-start.10) | collective-permute-done | bytes 262176 | tf_op jit(solution)/shard_map/ppermute | solution.py:288
  31.4 0.8 %collective-permute-start.11 = (bf16[128,1024]{1,0:T(8,128)(2,1)S(1)}, bf16[128,1024]{1,0:T(8,128)(2,1)S(1)}, u32[]{:S(2)}, u32[]{:S(2)}) collective-permute-start(bf16[128,1024]{1,0:T(8,128)(2,1)S(1)} %collective-permute-done.10.refs_12_.refs_9_), channel_id=1, source_target_pairs={{0,1},{1,0},{2,3},{3,2},{4,5},{5,4},{6,7},{7,6},{8,9},{9,8},{10,11... | collective-permute-start | bytes 786440 | tf_op jit(solution)/shard_map/ppermute | solution.py:288
  32.2 1.3 %collective-permute-start.17 = (bf16[64,1024]{1,0:T(8,128)(2,1)S(1)}, bf16[64,1024]{1,0:T(8,128)(2,1)S(1)}, u32[]{:S(2)}, u32[]{:S(2)}) collective-permute-start(bf16[64,1024]{1,0:T(8,128)(2,1)S(1)} %get-tuple-element.69.refs_6_), channel_id=1, source_target_pairs={{0,4},{8,12},{16,20},{24,28},{1,5},{9,13},{17,21},{25,29},{2,6},{1... | collective-permute-start | bytes 393224 | tf_op jit(solution)/shard_map/ppermute | solution.py:407
  33.5 0.9 %ready.1 = (f32[2,2,256,256]{3,2,1,0:T(8,128)S(1)}, bf16[3,2,256,256]{3,2,1,0:T(8,128)(2,1)S(1)}) custom-call(bf16[3,1024,1024]{2,1,0:T(8,128)(2,1)S(1)} %get-tuple-element.43.refs_1_.refs_2_.refs_0_.refs_3_.refs_4_.refs_17_, bf16[272,1024]{1,0:T(8,128)(2,1)S(1)} %hold.2.refs_2_.refs_1_.refs_7_.refs_3_, ...), custom_call_target="tpu_custom_call" | custom-call | flops 100000000 | bytes 2097152 | tf_op jit(solution)/shard_map/ready/pallas_call | solution.py:22
  34.5 0.0 copy-start
  34.5 1.3 %collective-permute-start.16 = (bf16[64,1024]{1,0:T(8,128)(2,1)S(1)}, bf16[64,1024]{1,0:T(8,128)(2,1)S(1)}, u32[]{:S(2)}, u32[]{:S(2)}) collective-permute-start(bf16[64,1024]{1,0:T(8,128)(2,1)S(1)} %get-tuple-element.70.refs_6_), channel_id=1, source_target_pairs={{0,4},{8,12},{16,20},{24,28},{1,5},{9,13},{17,21},{25,29},{2,6},{1... | collective-permute-start | bytes 393224 | tf_op jit(solution)/shard_map/ppermute | solution.py:407
  35.8 12.3 %collective-permute-done.17.refs_1_ = bf16[64,1024]{1,0:T(8,128)(2,1)S(1)} collective-permute-done((bf16[64,1024]{1,0:T(8,128)(2,1)S(1)}, bf16[64,1024]{1,0:T(8,128)(2,1)S(1)}, u32[]{:S(2)}, u32[]{:S(2)}) %collective-permute-start.17) | collective-permute-done | bytes 131104 | tf_op jit(solution)/shard_map/ppermute | solution.py:407
  48.1 2.1 %last.2 = (bf16[4,64,256]{2,1,0:T(8,128)(2,1)S(1)}, bf16[4,64,256]{2,1,0:T(8,128)(2,1)S(1)}, bf16[4,64,256]{2,1,0:T(8,128)(2,1)S(1)}, bf16[4,64,256]{2,1,0:T(8,128)(2,1)S(1)}) custom-call(s32[3]{0:T(128)S(1)} %copy-done, bf16[64,1024]{1,0:T(8,128)(2,1)S(1)} %collective-permute-done.17.refs_1_, ...), custom_call_target="tpu_custom_call" | custom-call | flops 1000000000 | bytes 2097152 | tf_op jit(solution)/shard_map/last/pallas_call | solution.py:22
  50.2 1.1 %collective-permute-start.21 = (bf16[4,64,256]{2,1,0:T(8,128)(2,1)S(1)}, bf16[4,64,256]{2,1,0:T(8,128)(2,1)S(1)}, u32[]{:S(2)}, u32[]{:S(2)}) collective-permute-start(bf16[4,64,256]{2,1,0:T(8,128)(2,1)S(1)} %get-tuple-element.79), channel_id=1, source_target_pairs={{0,1},{1,0},{2,3},{3,2},{4,5},{5,4},{6,7},{7,6},{8,9},{9,8},{10,11... | collective-permute-start | bytes 393224 | tf_op jit(solution)/shard_map/ppermute | solution.py:288
  51.3 1.1 %collective-permute-start.22 = (bf16[4,64,256]{2,1,0:T(8,128)(2,1)S(1)}, bf16[4,64,256]{2,1,0:T(8,128)(2,1)S(1)}, u32[]{:S(2)}, u32[]{:S(2)}) collective-permute-start(bf16[4,64,256]{2,1,0:T(8,128)(2,1)S(1)} %get-tuple-element.80), channel_id=1, source_target_pairs={{0,2},{1,3},{2,0},{3,1},{4,6},{5,7},{6,4},{7,5},{8,10},{9,11},{10,... | collective-permute-start | bytes 393224 | tf_op jit(solution)/shard_map/ppermute | solution.py:288
  52.4 0.6 collective-permute-start.23
  53.0 2.1 %last.3 = (bf16[4,64,256]{2,1,0:T(8,128)(2,1)S(1)}, bf16[4,64,256]{2,1,0:T(8,128)(2,1)S(1)}, bf16[4,64,256]{2,1,0:T(8,128)(2,1)S(1)}, bf16[4,64,256]{2,1,0:T(8,128)(2,1)S(1)}) custom-call(s32[3]{0:T(128)S(1)} %copy-done, bf16[64,1024]{1,0:T(8,128)(2,1)S(1)} %collective-permute-done.16.refs_1_, ...), custom_call_target="tpu_custom_call" | custom-call | flops 1000000000 | bytes 2097152 | tf_op jit(solution)/shard_map/last/pallas_call | solution.py:22
  55.1 0.2 collective-permute-start.18
  55.3 1.1 %collective-permute-start.19 = (bf16[4,64,256]{2,1,0:T(8,128)(2,1)S(1)}, bf16[4,64,256]{2,1,0:T(8,128)(2,1)S(1)}, u32[]{:S(2)}, u32[]{:S(2)}) collective-permute-start(bf16[4,64,256]{2,1,0:T(8,128)(2,1)S(1)} %get-tuple-element.77), channel_id=1, source_target_pairs={{0,2},{1,3},{2,0},{3,1},{4,6},{5,7},{6,4},{7,5},{8,10},{9,11},{10,... | collective-permute-start | bytes 393224 | tf_op jit(solution)/shard_map/ppermute | solution.py:288
  56.4 0.9 %collective-permute-start.20 = (bf16[4,64,256]{2,1,0:T(8,128)(2,1)S(1)}, bf16[4,64,256]{2,1,0:T(8,128)(2,1)S(1)}, u32[]{:S(2)}, u32[]{:S(2)}) collective-permute-start(bf16[4,64,256]{2,1,0:T(8,128)(2,1)S(1)} %get-tuple-element.78), channel_id=1, source_target_pairs={{0,3},{1,2},{2,1},{3,0},{4,7},{5,6},{6,5},{7,4},{8,11},{9,10},{10,... | collective-permute-start | bytes 393224 | tf_op jit(solution)/shard_map/ppermute | solution.py:288
  57.3 2.5 %collective-permute-done.23.refs_14_ = bf16[4,64,256]{2,1,0:T(8,128)(2,1)S(1)} collective-permute-done((bf16[4,64,256]{2,1,0:T(8,128)(2,1)S(1)}, bf16[4,64,256]{2,1,0:T(8,128)(2,1)S(1)}, u32[]{:S(2)}, u32[]{:S(2)}) %collective-permute-start.23) | collective-permute-done | bytes 131104 | tf_op jit(solution)/shard_map/ppermute | solution.py:288
  59.8 1.3 %counts.2 = (f32[3,256,1024]{2,1,0:T(8,128)S(1)}, f32[3,256,256]{2,1,0:T(8,128)S(1)}) custom-call(s32[3]{0:T(128)S(1)} %copy-done, f32[2,2,256,256]{3,2,1,0:T(8,128)S(1)} %get-tuple-element.53.refs_7_.refs_1_, bf16[3,2,256,256]{3,2,1,0:T(8,128)(2,1)S(1)} %get-tuple-element.54.refs_2_, bf16[272,1024]{1,0:T(8,128)(2,1)S(1)} %hold.2.refs_2_.refs_1_.refs_7_.refs_3_, ...), custom_call_target="tpu_custom_call" | custom-call | flops 1000000000 | bytes 2097152 | tf_op jit(solution)/shard_map/counts/pallas_call | solution.py:22
  61.1 0.9 %collective-permute-done.19.refs_13_ = bf16[4,64,256]{2,1,0:T(8,128)(2,1)S(1)} collective-permute-done((bf16[4,64,256]{2,1,0:T(8,128)(2,1)S(1)}, bf16[4,64,256]{2,1,0:T(8,128)(2,1)S(1)}, u32[]{:S(2)}, u32[]{:S(2)}) %collective-permute-start.19) | collective-permute-done | bytes 131104 | tf_op jit(solution)/shard_map/ppermute | solution.py:288
  62.0 3.0 %collective-permute-done.20.refs_14_ = bf16[4,64,256]{2,1,0:T(8,128)(2,1)S(1)} collective-permute-done((bf16[4,64,256]{2,1,0:T(8,128)(2,1)S(1)}, bf16[4,64,256]{2,1,0:T(8,128)(2,1)S(1)}, u32[]{:S(2)}, u32[]{:S(2)}) %collective-permute-start.20) | collective-permute-done | bytes 131104 | tf_op jit(solution)/shard_map/ppermute | solution.py:288
  65.0 2.3 %counts.3 = (bf16[3,256,1024]{2,1,0:T(8,128)(2,1)}, bf16[3,256,256]{2,1,0:T(8,128)(2,1)}) custom-call(s32[3]{0:T(128)S(1)} %copy-done, f32[2,2,256,256]{3,2,1,0:T(8,128)S(1)} %get-tuple-element.53.refs_7_.refs_1_, bf16[3,2,256,256]{3,2,1,0:T(8,128)(2,1)S(1)} %get-tuple-element.54.refs_2_, bf16[272,1024]{1,0:T(8,128)(2,1)S(1)} %hold.2.refs_2_.refs_1_.refs_7_.refs_3_, ...), custom_call_target="tpu_custom_call" | custom-call | flops 1000000000 | bytes 2097152 | tf_op jit(solution)/shard_map/counts/pallas_call | solution.py:22
  (25 shorter events, 0.2 us)
Async XLA Ops:
  6.0 4.7 %collective-permute-start.3 = (bf16[64,1024]{1,0:T(8,128)(2,1)S(1)}, bf16[64,1024]{1,0:T(8,128)(2,1)S(1)}, u32[]{:S(2)}, u32[]{:S(2)}) collective-permute-start(bf16[64,1024]{1,0:T(8,128)(2,1)S(1)} %first.2.refs_1_), channel_id=1, source_target_pairs={{4,0},{12,8},{20,16},{28,24},{5,1},{13,9},{21,17},{29,25},{6,2},{1... | collective-permute-start | bytes 393224 | tf_op jit(solution)/shard_map/ppermute | solution.py:360
  7.3 13.2 %collective-permute-start.1 = (bf16[272,1024]{1,0:T(8,128)(2,1)S(1)}, bf16[272,1024]{1,0:T(8,128)(2,1)S(1)}, u32[]{:S(2)}, u32[]{:S(2)}) collective-permute-start(bf16[272,1024]{1,0:T(8,128)(2,1)S(1)} %hold.2.refs_2_.refs_1_.refs_7_.refs_3_), channel_id=1, source_target_pairs={{0,2},{1,3},{2,0},{3,1},{4,6},{5,7},{6,4},{7,5},{8,10},{9,11},{10,... | collective-permute-start | bytes 1671176 | tf_op jit(solution)/shard_map/ppermute | solution.py:288
  9.4 3.2 %collective-permute-start.2 = (bf16[64,1024]{1,0:T(8,128)(2,1)S(1)}, bf16[64,1024]{1,0:T(8,128)(2,1)S(1)}, u32[]{:S(2)}, u32[]{:S(2)}) collective-permute-start(bf16[64,1024]{1,0:T(8,128)(2,1)S(1)} %first.3), channel_id=1, source_target_pairs={{4,0},{12,8},{20,16},{28,24},{5,1},{13,9},{21,17},{29,25},{6,2},{1... | collective-permute-start | bytes 393224 | tf_op jit(solution)/shard_map/ppermute | solution.py:360
  10.8 2.6 %collective-permute-start.5 = (bf16[64,1024]{1,0:T(8,128)(2,1)S(1)}, bf16[64,1024]{1,0:T(8,128)(2,1)S(1)}, u32[]{:S(2)}, u32[]{:S(2)}) collective-permute-start(bf16[64,1024]{1,0:T(8,128)(2,1)S(1)} %get-tuple-element.47.refs_3_), channel_id=1, source_target_pairs={{8,0},{24,16},{9,1},{25,17},{10,2},{26,18},{11,3},{27,19}} | collective-permute-start | bytes 393224 | tf_op jit(solution)/shard_map/ppermute | solution.py:360
  12.7 3.3 %collective-permute-start.4 = (bf16[64,1024]{1,0:T(8,128)(2,1)S(1)}, bf16[64,1024]{1,0:T(8,128)(2,1)S(1)}, u32[]{:S(2)}, u32[]{:S(2)}) collective-permute-start(bf16[64,1024]{1,0:T(8,128)(2,1)S(1)} %get-tuple-element.49), channel_id=1, source_target_pairs={{8,0},{24,16},{9,1},{25,17},{10,2},{26,18},{11,3},{27,19}} | collective-permute-start | bytes 393224 | tf_op jit(solution)/shard_map/ppermute | solution.py:360
  13.4 3.2 %collective-permute-start.8 = (bf16[64,1024]{1,0:T(8,128)(2,1)S(1)}, bf16[64,1024]{1,0:T(8,128)(2,1)S(1)}, u32[]{:S(2)}, u32[]{:S(2)}) collective-permute-start(bf16[64,1024]{1,0:T(8,128)(2,1)S(1)} %get-tuple-element.51.refs_3_), channel_id=1, source_target_pairs={{16,0},{17,1},{18,2},{19,3}} | collective-permute-start | bytes 393224 | tf_op jit(solution)/shard_map/ppermute | solution.py:373
  14.0 18.1 %collective-permute-start = (bf16[272,1024]{1,0:T(8,128)(2,1)S(1)}, bf16[272,1024]{1,0:T(8,128)(2,1)S(1)}, u32[]{:S(2)}, u32[]{:S(2)}) collective-permute-start(bf16[272,1024]{1,0:T(8,128)(2,1)S(1)} %hold.2.refs_2_.refs_1_.refs_7_.refs_3_), channel_id=1, source_target_pairs={{0,1},{1,0},{2,3},{3,2},{4,5},{5,4},{6,7},{7,6},{8,9},{9,8},{10,11... | collective-permute-start | bytes 1671176 | tf_op jit(solution)/shard_map/ppermute | solution.py:288
  15.9 6.7 %collective-permute-start.7 = (bf16[64,1024]{1,0:T(8,128)(2,1)S(1)}, bf16[64,1024]{1,0:T(8,128)(2,1)S(1)}, u32[]{:S(2)}, u32[]{:S(2)}) collective-permute-start(bf16[64,1024]{1,0:T(8,128)(2,1)S(1)} %get-tuple-element.52.refs_1_), channel_id=1, source_target_pairs={{16,0},{17,1},{18,2},{19,3}} | collective-permute-start | bytes 393224 | tf_op jit(solution)/shard_map/ppermute | solution.py:373
  16.7 8.7 %collective-permute-start.13 = (bf16[64,1024]{1,0:T(8,128)(2,1)S(1)}, bf16[64,1024]{1,0:T(8,128)(2,1)S(1)}, u32[]{:S(2)}, u32[]{:S(2)}) collective-permute-start(bf16[64,1024]{1,0:T(8,128)(2,1)S(1)} %get-tuple-element.63.refs_5_), channel_id=1, source_target_pairs={{0,16},{1,17},{2,18},{3,19}} | collective-permute-start | bytes 393224 | tf_op jit(solution)/shard_map/ppermute | solution.py:397
  20.6 12.9 %collective-permute-start.6 = (bf16[272,1024]{1,0:T(8,128)(2,1)S(1)}, bf16[272,1024]{1,0:T(8,128)(2,1)S(1)}, u32[]{:S(2)}, u32[]{:S(2)}) collective-permute-start(bf16[272,1024]{1,0:T(8,128)(2,1)S(1)} %hold.3), channel_id=1, source_target_pairs={{0,1},{1,0},{2,3},{3,2},{4,5},{5,4},{6,7},{7,6},{8,9},{9,8},{10,11... | collective-permute-start | bytes 1671176 | tf_op jit(solution)/shard_map/ppermute | solution.py:288
  22.7 4.2 %collective-permute-start.12 = (bf16[64,1024]{1,0:T(8,128)(2,1)S(1)}, bf16[64,1024]{1,0:T(8,128)(2,1)S(1)}, u32[]{:S(2)}, u32[]{:S(2)}) collective-permute-start(bf16[64,1024]{1,0:T(8,128)(2,1)S(1)} %get-tuple-element.60.refs_5_), channel_id=1, source_target_pairs={{0,16},{1,17},{2,18},{3,19}} | collective-permute-start | bytes 393224 | tf_op jit(solution)/shard_map/ppermute | solution.py:397
  23.4 8.0 %collective-permute-start.10 = (bf16[128,1024]{1,0:T(8,128)(2,1)S(1)}, bf16[128,1024]{1,0:T(8,128)(2,1)S(1)}, u32[]{:S(2)}, u32[]{:S(2)}) collective-permute-start(bf16[128,1024]{1,0:T(8,128)(2,1)S(1)} %get-tuple-element.59.refs_10_.refs_7_), channel_id=1, source_target_pairs={{0,2},{1,3},{2,0},{3,1},{4,6},{5,7},{6,4},{7,5},{8,10},{9,11},{10,... | collective-permute-start | bytes 786440 | tf_op jit(solution)/shard_map/ppermute | solution.py:288
  25.5 2.2 %collective-permute-start.15 = (bf16[64,1024]{1,0:T(8,128)(2,1)S(1)}, bf16[64,1024]{1,0:T(8,128)(2,1)S(1)}, u32[]{:S(2)}, u32[]{:S(2)}) collective-permute-start(bf16[64,1024]{1,0:T(8,128)(2,1)S(1)} %get-tuple-element.65.refs_6_.refs_5_), channel_id=1, source_target_pairs={{0,8},{16,24},{1,9},{17,25},{2,10},{18,26},{3,11},{19,27}} | collective-permute-start | bytes 393224 | tf_op jit(solution)/shard_map/ppermute | solution.py:397
  27.0 7.5 %collective-permute-start.14 = (bf16[64,1024]{1,0:T(8,128)(2,1)S(1)}, bf16[64,1024]{1,0:T(8,128)(2,1)S(1)}, u32[]{:S(2)}, u32[]{:S(2)}) collective-permute-start(bf16[64,1024]{1,0:T(8,128)(2,1)S(1)} %get-tuple-element.66.refs_5_), channel_id=1, source_target_pairs={{0,8},{16,24},{1,9},{17,25},{2,10},{18,26},{3,11},{19,27}} | collective-permute-start | bytes 393224 | tf_op jit(solution)/shard_map/ppermute | solution.py:397
  27.7 24.8 %collective-permute-start.9 = (bf16[128,1024]{1,0:T(8,128)(2,1)S(1)}, bf16[128,1024]{1,0:T(8,128)(2,1)S(1)}, u32[]{:S(2)}, u32[]{:S(2)}) collective-permute-start(bf16[128,1024]{1,0:T(8,128)(2,1)S(1)} %get-tuple-element.59.refs_10_.refs_7_), channel_id=1, source_target_pairs={{0,1},{1,0},{2,3},{3,2},{4,5},{5,4},{6,7},{7,6},{8,9},{9,8},{10,11... | collective-permute-start | bytes 786440 | tf_op jit(solution)/shard_map/ppermute | solution.py:288
  31.4 21.7 %collective-permute-start.11 = (bf16[128,1024]{1,0:T(8,128)(2,1)S(1)}, bf16[128,1024]{1,0:T(8,128)(2,1)S(1)}, u32[]{:S(2)}, u32[]{:S(2)}) collective-permute-start(bf16[128,1024]{1,0:T(8,128)(2,1)S(1)} %collective-permute-done.10.refs_12_.refs_9_), channel_id=1, source_target_pairs={{0,1},{1,0},{2,3},{3,2},{4,5},{5,4},{6,7},{7,6},{8,9},{9,8},{10,11... | collective-permute-start | bytes 786440 | tf_op jit(solution)/shard_map/ppermute | solution.py:288
  32.2 15.9 %collective-permute-start.17 = (bf16[64,1024]{1,0:T(8,128)(2,1)S(1)}, bf16[64,1024]{1,0:T(8,128)(2,1)S(1)}, u32[]{:S(2)}, u32[]{:S(2)}) collective-permute-start(bf16[64,1024]{1,0:T(8,128)(2,1)S(1)} %get-tuple-element.69.refs_6_), channel_id=1, source_target_pairs={{0,4},{8,12},{16,20},{24,28},{1,5},{9,13},{17,21},{25,29},{2,6},{1... | collective-permute-start | bytes 393224 | tf_op jit(solution)/shard_map/ppermute | solution.py:407
  34.5 13.7 %copy-start = (s32[3]{0:T(128)S(1)}, s32[3]{0:T(128)}, u32[]{:S(2)}) copy-start(s32[3]{0:T(128)} %refs_0_.9) | copy-start | bytes 40
  34.5 18.5 %collective-permute-start.16 = (bf16[64,1024]{1,0:T(8,128)(2,1)S(1)}, bf16[64,1024]{1,0:T(8,128)(2,1)S(1)}, u32[]{:S(2)}, u32[]{:S(2)}) collective-permute-start(bf16[64,1024]{1,0:T(8,128)(2,1)S(1)} %get-tuple-element.70.refs_6_), channel_id=1, source_target_pairs={{0,4},{8,12},{16,20},{24,28},{1,5},{9,13},{17,21},{25,29},{2,6},{1... | collective-permute-start | bytes 393224 | tf_op jit(solution)/shard_map/ppermute | solution.py:407
  50.2 6.2 %collective-permute-start.21 = (bf16[4,64,256]{2,1,0:T(8,128)(2,1)S(1)}, bf16[4,64,256]{2,1,0:T(8,128)(2,1)S(1)}, u32[]{:S(2)}, u32[]{:S(2)}) collective-permute-start(bf16[4,64,256]{2,1,0:T(8,128)(2,1)S(1)} %get-tuple-element.79), channel_id=1, source_target_pairs={{0,1},{1,0},{2,3},{3,2},{4,5},{5,4},{6,7},{7,6},{8,9},{9,8},{10,11... | collective-permute-start | bytes 393224 | tf_op jit(solution)/shard_map/ppermute | solution.py:288
  51.3 6.0 %collective-permute-start.22 = (bf16[4,64,256]{2,1,0:T(8,128)(2,1)S(1)}, bf16[4,64,256]{2,1,0:T(8,128)(2,1)S(1)}, u32[]{:S(2)}, u32[]{:S(2)}) collective-permute-start(bf16[4,64,256]{2,1,0:T(8,128)(2,1)S(1)} %get-tuple-element.80), channel_id=1, source_target_pairs={{0,2},{1,3},{2,0},{3,1},{4,6},{5,7},{6,4},{7,5},{8,10},{9,11},{10,... | collective-permute-start | bytes 393224 | tf_op jit(solution)/shard_map/ppermute | solution.py:288
  52.4 7.4 %collective-permute-start.23 = (bf16[4,64,256]{2,1,0:T(8,128)(2,1)S(1)}, bf16[4,64,256]{2,1,0:T(8,128)(2,1)S(1)}, u32[]{:S(2)}, u32[]{:S(2)}) collective-permute-start(bf16[4,64,256]{2,1,0:T(8,128)(2,1)S(1)} %get-tuple-element.81), channel_id=1, source_target_pairs={{0,3},{1,2},{2,1},{3,0},{4,7},{5,6},{6,5},{7,4},{8,11},{9,10},{10,... | collective-permute-start | bytes 393224 | tf_op jit(solution)/shard_map/ppermute | solution.py:288
  55.1 6.0 %collective-permute-start.18 = (bf16[4,64,256]{2,1,0:T(8,128)(2,1)S(1)}, bf16[4,64,256]{2,1,0:T(8,128)(2,1)S(1)}, u32[]{:S(2)}, u32[]{:S(2)}) collective-permute-start(bf16[4,64,256]{2,1,0:T(8,128)(2,1)S(1)} %get-tuple-element.76), channel_id=1, source_target_pairs={{0,1},{1,0},{2,3},{3,2},{4,5},{5,4},{6,7},{7,6},{8,9},{9,8},{10,11... | collective-permute-start | bytes 393224 | tf_op jit(solution)/shard_map/ppermute | solution.py:288
  55.3 6.7 %collective-permute-start.19 = (bf16[4,64,256]{2,1,0:T(8,128)(2,1)S(1)}, bf16[4,64,256]{2,1,0:T(8,128)(2,1)S(1)}, u32[]{:S(2)}, u32[]{:S(2)}) collective-permute-start(bf16[4,64,256]{2,1,0:T(8,128)(2,1)S(1)} %get-tuple-element.77), channel_id=1, source_target_pairs={{0,2},{1,3},{2,0},{3,1},{4,6},{5,7},{6,4},{7,5},{8,10},{9,11},{10,... | collective-permute-start | bytes 393224 | tf_op jit(solution)/shard_map/ppermute | solution.py:288
  56.4 8.5 %collective-permute-start.20 = (bf16[4,64,256]{2,1,0:T(8,128)(2,1)S(1)}, bf16[4,64,256]{2,1,0:T(8,128)(2,1)S(1)}, u32[]{:S(2)}, u32[]{:S(2)}) collective-permute-start(bf16[4,64,256]{2,1,0:T(8,128)(2,1)S(1)} %get-tuple-element.78), channel_id=1, source_target_pairs={{0,3},{1,2},{2,1},{3,0},{4,7},{5,6},{6,5},{7,4},{8,11},{9,10},{10,... | collective-permute-start | bytes 393224 | tf_op jit(solution)/shard_map/ppermute | solution.py:288

commit v7 on v4

--- a/solution.py
+++ b/solution.py
@@ -414,7 +414,7 @@
             [SM] + [VM] * 8,
             after=[own_posts[-1][0], *all_tops, raw_own] if c > 0 else [],
         )
-        order = sorted(range(1, groups), reverse=c < CHUNKS - 1)
+        order = sorted(range(1, groups), reverse=True)
         moved = {mask: swap(packs[mask], mask) for mask in order}
         own_posts.append([packs[0]] + [moved[mask] for mask in range(1, groups)])
     sums = ()

time: 66.4 us -> 66.4 us (level)
  no operation moved by 1% of the time
where the time goes in v7:
time: 66.4 us; the launch traced here: 66 us
  starting transfers between devices  25.6 us (39%)
  waiting for transfers between devices  22.7 us (34%)
  Pallas kernels  16.8 us (25%)
  between operations  0.94 us (1%)
    pallas_call x22, Pallas kernels, run(): pl.pallas_call(lambda *refs: body(*refs[:count], *refs[idle:]), name=name...  16.8 us
    ppermute x12, starting transfers between devices, swap(): lax.ppermute(value, 'rows', [(s, s ^ mask) for s in range(lax.axis_size('...  15.1 us
    ppermute x2, waiting for transfers between devices, per_device(): recv = lax.ppermute(post[c], 'leaf', down_pairs(0))  10.9 us
    ppermute x12, waiting for transfers between devices, swap(): lax.ppermute(value, 'rows', [(s, s ^ mask) for s in range(lax.axis_size('...  10.6 us
    ppermute x4, starting transfers between devices, per_device(): recv = lax.ppermute(send[c], 'leaf', up_pairs(level))  3.96 us
    ppermute x4, starting transfers between devices, per_device(): recv = lax.ppermute(post[c], 'leaf', down_pairs(level))  2.68 us
    ppermute x2, starting transfers between devices, per_device(): recv = lax.ppermute(post[c], 'leaf', down_pairs(0))  2.58 us
  transfers between devices with their start and end apart: 24, of which 7 were waited for; matrix products, arithmetic and copies ran while one was open for 0% of the time, Pallas kernels for 14%

profile of v7, /device:TPU:13, one launch (start us, length us, event | category | flops | bytes accessed | tf_op | source)
XLA Modules:
  0.0 66.0 jit_solution(17598220167577063568)
XLA Ops:
  0.6 4.5 %prep.1 = (bf16[3,1024,1024]{2,1,0:T(8,128)(2,1)S(1)}, bf16[272,1024]{1,0:T(8,128)(2,1)S(1)}, f32[2,128,1024]{2,1,0:T(8,128)S(1)}, f32[8,1024]{1,0:T(8,128)S(1)}...) custom-call(s32[3]{0:T(128)} %refs_0_.9, s32[3,128]{1,0:T(4,128)} %refs_1_.1, bf16[3,256,1024]{2,1,0:T(8,128)(2,1)} %refs_2_.1, ...), custom_call_target="tpu_custom_call" | custom-call | flops 1000000000 | bytes 2097152 | tf_op jit(solution)/shard_map/prep/pallas_call | solution.py:22
  5.2 0.8 %first.2.refs_1_ = bf16[64,1024]{1,0:T(8,128)(2,1)S(1)} custom-call(f32[64,1024]{1,0:T(8,128)S(1)} %get-tuple-element.45.refs_0_, bf16[3,1024,1024]{2,1,0:T(8,128)(2,1)S(1)} %get-tuple-element.43.refs_1_.refs_2_.refs_0_.refs_3_.refs_4_.refs_17_), custom_call_target="tpu_custom_call" | custom-call | flops 1000000000 | bytes 2097152 | tf_op jit(solution)/shard_map/first/pallas_call | solution.py:22
  6.0 1.3 %collective-permute-start.3 = (bf16[64,1024]{1,0:T(8,128)(2,1)S(1)}, bf16[64,1024]{1,0:T(8,128)(2,1)S(1)}, u32[]{:S(2)}, u32[]{:S(2)}) collective-permute-start(bf16[64,1024]{1,0:T(8,128)(2,1)S(1)} %first.2.refs_1_), channel_id=1, source_target_pairs={{4,0},{12,8},{20,16},{28,24},{5,1},{13,9},{21,17},{29,25},{6,2},{1... | collective-permute-start | bytes 393224 | tf_op jit(solution)/shard_map/ppermute | solution.py:360
  7.3 1.3 %collective-permute-start.1 = (bf16[272,1024]{1,0:T(8,128)(2,1)S(1)}, bf16[272,1024]{1,0:T(8,128)(2,1)S(1)}, u32[]{:S(2)}, u32[]{:S(2)}) collective-permute-start(bf16[272,1024]{1,0:T(8,128)(2,1)S(1)} %hold.2.refs_2_.refs_1_.refs_7_.refs_3_), channel_id=1, source_target_pairs={{0,2},{1,3},{2,0},{3,1},{4,6},{5,7},{6,4},{7,5},{8,10},{9,11},{10,... | collective-permute-start | bytes 1671176 | tf_op jit(solution)/shard_map/ppermute | solution.py:288
  8.6 0.8 %first.3 = bf16[64,1024]{1,0:T(8,128)(2,1)S(1)} custom-call(f32[64,1024]{1,0:T(8,128)S(1)} %get-tuple-element.46.refs_0_, bf16[3,1024,1024]{2,1,0:T(8,128)(2,1)S(1)} %get-tuple-element.43.refs_1_.refs_2_.refs_0_.refs_3_.refs_4_.refs_17_, bf16[272,1024]{1,0:T(8,128)(2,1)S(1)} %hold.2.refs_2_.refs_1_.refs_7_.refs_3_), custom_call_target="tpu_custom_call" | custom-call | flops 1000000000 | bytes 2097152 | tf_op jit(solution)/shard_map/first/pallas_call | solution.py:22
  9.4 1.3 %collective-permute-start.2 = (bf16[64,1024]{1,0:T(8,128)(2,1)S(1)}, bf16[64,1024]{1,0:T(8,128)(2,1)S(1)}, u32[]{:S(2)}, u32[]{:S(2)}) collective-permute-start(bf16[64,1024]{1,0:T(8,128)(2,1)S(1)} %first.3), channel_id=1, source_target_pairs={{4,0},{12,8},{20,16},{28,24},{5,1},{13,9},{21,17},{29,25},{6,2},{1... | collective-permute-start | bytes 393224 | tf_op jit(solution)/shard_map/ppermute | solution.py:360
  10.8 0.7 %collective-permute-start.5 = (bf16[64,1024]{1,0:T(8,128)(2,1)S(1)}, bf16[64,1024]{1,0:T(8,128)(2,1)S(1)}, u32[]{:S(2)}, u32[]{:S(2)}) collective-permute-start(bf16[64,1024]{1,0:T(8,128)(2,1)S(1)} %get-tuple-element.47.refs_3_), channel_id=1, source_target_pairs={{8,0},{24,16},{9,1},{25,17},{10,2},{26,18},{11,3},{27,19}} | collective-permute-start | bytes 393224 | tf_op jit(solution)/shard_map/ppermute | solution.py:360
  11.5 1.2 %collective-permute-done.2.refs_1_ = bf16[64,1024]{1,0:T(8,128)(2,1)S(1)} collective-permute-done((bf16[64,1024]{1,0:T(8,128)(2,1)S(1)}, bf16[64,1024]{1,0:T(8,128)(2,1)S(1)}, u32[]{:S(2)}, u32[]{:S(2)}) %collective-permute-start.2) | collective-permute-done | bytes 131104 | tf_op jit(solution)/shard_map/ppermute | solution.py:360
  12.7 0.7 collective-permute-start.4
  13.3 0.0 collective-permute-done.5.refs_1_
  13.4 0.7 %collective-permute-start.8 = (bf16[64,1024]{1,0:T(8,128)(2,1)S(1)}, bf16[64,1024]{1,0:T(8,128)(2,1)S(1)}, u32[]{:S(2)}, u32[]{:S(2)}) collective-permute-start(bf16[64,1024]{1,0:T(8,128)(2,1)S(1)} %get-tuple-element.51.refs_3_), channel_id=1, source_target_pairs={{16,0},{17,1},{18,2},{19,3}} | collective-permute-start | bytes 393224 | tf_op jit(solution)/shard_map/ppermute | solution.py:373
  14.0 1.9 %collective-permute-start = (bf16[272,1024]{1,0:T(8,128)(2,1)S(1)}, bf16[272,1024]{1,0:T(8,128)(2,1)S(1)}, u32[]{:S(2)}, u32[]{:S(2)}) collective-permute-start(bf16[272,1024]{1,0:T(8,128)(2,1)S(1)} %hold.2.refs_2_.refs_1_.refs_7_.refs_3_), channel_id=1, source_target_pairs={{0,1},{1,0},{2,3},{3,2},{4,5},{5,4},{6,7},{7,6},{8,9},{9,8},{10,11... | collective-permute-start | bytes 1671176 | tf_op jit(solution)/shard_map/ppermute | solution.py:288
  15.9 0.0 collective-permute-done.4.refs_1_
  15.9 0.7 collective-permute-start.7
  16.6 0.0 collective-permute-done.8.refs_1_
  16.6 0.1 root.2
  16.7 0.7 %collective-permute-start.13 = (bf16[64,1024]{1,0:T(8,128)(2,1)S(1)}, bf16[64,1024]{1,0:T(8,128)(2,1)S(1)}, u32[]{:S(2)}, u32[]{:S(2)}) collective-permute-start(bf16[64,1024]{1,0:T(8,128)(2,1)S(1)} %get-tuple-element.63.refs_5_), channel_id=1, source_target_pairs={{0,16},{1,17},{2,18},{3,19}} | collective-permute-start | bytes 393224 | tf_op jit(solution)/shard_map/ppermute | solution.py:397
  17.4 3.2 %collective-permute-done.1.refs_3_.refs_9_.refs_5_ = bf16[272,1024]{1,0:T(8,128)(2,1)S(1)} collective-permute-done((bf16[272,1024]{1,0:T(8,128)(2,1)S(1)}, bf16[272,1024]{1,0:T(8,128)(2,1)S(1)}, u32[]{:S(2)}, u32[]{:S(2)}) %collective-permute-start.1) | collective-permute-done | bytes 557088 | tf_op jit(solution)/shard_map/ppermute | solution.py:288
  20.6 1.9 %collective-permute-start.6 = (bf16[272,1024]{1,0:T(8,128)(2,1)S(1)}, bf16[272,1024]{1,0:T(8,128)(2,1)S(1)}, u32[]{:S(2)}, u32[]{:S(2)}) collective-permute-start(bf16[272,1024]{1,0:T(8,128)(2,1)S(1)} %hold.3), channel_id=1, source_target_pairs={{0,1},{1,0},{2,3},{3,2},{4,5},{5,4},{6,7},{7,6},{8,9},{9,8},{10,11... | collective-permute-start | bytes 1671176 | tf_op jit(solution)/shard_map/ppermute | solution.py:288
  22.6 0.1 root.3
  22.7 0.7 %collective-permute-start.12 = (bf16[64,1024]{1,0:T(8,128)(2,1)S(1)}, bf16[64,1024]{1,0:T(8,128)(2,1)S(1)}, u32[]{:S(2)}, u32[]{:S(2)}) collective-permute-start(bf16[64,1024]{1,0:T(8,128)(2,1)S(1)} %get-tuple-element.60.refs_5_), channel_id=1, source_target_pairs={{0,16},{1,17},{2,18},{3,19}} | collective-permute-start | bytes 393224 | tf_op jit(solution)/shard_map/ppermute | solution.py:397
  23.4 1.3 %collective-permute-start.10 = (bf16[128,1024]{1,0:T(8,128)(2,1)S(1)}, bf16[128,1024]{1,0:T(8,128)(2,1)S(1)}, u32[]{:S(2)}, u32[]{:S(2)}) collective-permute-start(bf16[128,1024]{1,0:T(8,128)(2,1)S(1)} %get-tuple-element.59.refs_10_.refs_7_), channel_id=1, source_target_pairs={{0,2},{1,3},{2,0},{3,1},{4,6},{5,7},{6,4},{7,5},{8,10},{9,11},{10,... | collective-permute-start | bytes 786440 | tf_op jit(solution)/shard_map/ppermute | solution.py:288
  24.7 0.8 %top.3.refs_2_.refs_3_ = f32[64,1024]{1,0:T(8,128)S(1)} custom-call(bf16[64,1024]{1,0:T(8,128)(2,1)S(1)} %get-tuple-element.58.refs_3_.refs_0_.refs_1_.refs_2_, bf16[3,1024,1024]{2,1,0:T(8,128)(2,1)S(1)} %get-tuple-element.43.refs_1_.refs_2_.refs_0_.refs_3_.refs_4_.refs_17_), custom_call_target="tpu_custom_call" | custom-call | flops 1000000000 | bytes 2097152 | tf_op jit(solution)/shard_map/top/pallas_call | solution.py:22
  25.5 0.7 %collective-permute-start.15 = (bf16[64,1024]{1,0:T(8,128)(2,1)S(1)}, bf16[64,1024]{1,0:T(8,128)(2,1)S(1)}, u32[]{:S(2)}, u32[]{:S(2)}) collective-permute-start(bf16[64,1024]{1,0:T(8,128)(2,1)S(1)} %get-tuple-element.65.refs_6_.refs_5_), channel_id=1, source_target_pairs={{0,8},{16,24},{1,9},{17,25},{2,10},{18,26},{3,11},{19,27}} | collective-permute-start | bytes 393224 | tf_op jit(solution)/shard_map/ppermute | solution.py:397
  26.1 0.8 %top.2.refs_2_.refs_3_ = f32[64,1024]{1,0:T(8,128)S(1)} custom-call(bf16[64,1024]{1,0:T(8,128)(2,1)S(1)} %get-tuple-element.61.refs_0_.refs_1_.refs_2_, bf16[3,1024,1024]{2,1,0:T(8,128)(2,1)S(1)} %get-tuple-element.43.refs_1_.refs_2_.refs_0_.refs_3_.refs_4_.refs_17_), custom_call_target="tpu_custom_call" | custom-call | flops 1000000000 | bytes 2097152 | tf_op jit(solution)/shard_map/top/pallas_call | solution.py:22
  26.9 0.0 collective-permute-done.12.refs_0_
  27.0 0.7 %collective-permute-start.14 = (bf16[64,1024]{1,0:T(8,128)(2,1)S(1)}, bf16[64,1024]{1,0:T(8,128)(2,1)S(1)}, u32[]{:S(2)}, u32[]{:S(2)}) collective-permute-start(bf16[64,1024]{1,0:T(8,128)(2,1)S(1)} %get-tuple-element.66.refs_5_), channel_id=1, source_target_pairs={{0,8},{16,24},{1,9},{17,25},{2,10},{18,26},{3,11},{19,27}} | collective-permute-start | bytes 393224 | tf_op jit(solution)/shard_map/ppermute | solution.py:397
  27.7 1.3 %collective-permute-start.17 = (bf16[64,1024]{1,0:T(8,128)(2,1)S(1)}, bf16[64,1024]{1,0:T(8,128)(2,1)S(1)}, u32[]{:S(2)}, u32[]{:S(2)}) collective-permute-start(bf16[64,1024]{1,0:T(8,128)(2,1)S(1)} %get-tuple-element.69.refs_6_), channel_id=1, source_target_pairs={{0,4},{8,12},{16,20},{24,28},{1,5},{9,13},{17,21},{25,29},{2,6},{1... | collective-permute-start | bytes 393224 | tf_op jit(solution)/shard_map/ppermute | solution.py:407
  29.0 0.0 collective-permute-done.refs_2_.refs_8_.refs_4_
  29.0 0.4 collective-permute-start.9
  29.4 2.0 %collective-permute-done.10.refs_12_.refs_9_ = bf16[128,1024]{1,0:T(8,128)(2,1)S(1)} collective-permute-done((bf16[128,1024]{1,0:T(8,128)(2,1)S(1)}, bf16[128,1024]{1,0:T(8,128)(2,1)S(1)}, u32[]{:S(2)}, u32[]{:S(2)}) %collective-permute-start.10) | collective-permute-done | bytes 262176 | tf_op jit(solution)/shard_map/ppermute | solution.py:288
  31.4 0.8 %collective-permute-start.11 = (bf16[128,1024]{1,0:T(8,128)(2,1)S(1)}, bf16[128,1024]{1,0:T(8,128)(2,1)S(1)}, u32[]{:S(2)}, u32[]{:S(2)}) collective-permute-start(bf16[128,1024]{1,0:T(8,128)(2,1)S(1)} %collective-permute-done.10.refs_12_.refs_9_), channel_id=1, source_target_pairs={{0,1},{1,0},{2,3},{3,2},{4,5},{5,4},{6,7},{7,6},{8,9},{9,8},{10,11... | collective-permute-start | bytes 786440 | tf_op jit(solution)/shard_map/ppermute | solution.py:288
  32.2 1.3 %collective-permute-start.16 = (bf16[64,1024]{1,0:T(8,128)(2,1)S(1)}, bf16[64,1024]{1,0:T(8,128)(2,1)S(1)}, u32[]{:S(2)}, u32[]{:S(2)}) collective-permute-start(bf16[64,1024]{1,0:T(8,128)(2,1)S(1)} %get-tuple-element.70.refs_6_), channel_id=1, source_target_pairs={{0,4},{8,12},{16,20},{24,28},{1,5},{9,13},{17,21},{25,29},{2,6},{1... | collective-permute-start | bytes 393224 | tf_op jit(solution)/shard_map/ppermute | solution.py:407
  33.5 10.9 %collective-permute-done.17.refs_1_ = bf16[64,1024]{1,0:T(8,128)(2,1)S(1)} collective-permute-done((bf16[64,1024]{1,0:T(8,128)(2,1)S(1)}, bf16[64,1024]{1,0:T(8,128)(2,1)S(1)}, u32[]{:S(2)}, u32[]{:S(2)}) %collective-permute-start.17) | collective-permute-done | bytes 131104 | tf_op jit(solution)/shard_map/ppermute | solution.py:407
  44.5 2.1 %last.2 = (bf16[4,64,256]{2,1,0:T(8,128)(2,1)S(1)}, bf16[4,64,256]{2,1,0:T(8,128)(2,1)S(1)}, bf16[4,64,256]{2,1,0:T(8,128)(2,1)S(1)}, bf16[4,64,256]{2,1,0:T(8,128)(2,1)S(1)}) custom-call(s32[3]{0:T(128)S(1)} %copy-done, bf16[64,1024]{1,0:T(8,128)(2,1)S(1)} %collective-permute-done.17.refs_1_, ...), custom_call_target="tpu_custom_call" | custom-call | flops 1000000000 | bytes 2097152 | tf_op jit(solution)/shard_map/last/pallas_call | solution.py:22
  46.5 3.6 %collective-permute-start.21 = (bf16[4,64,256]{2,1,0:T(8,128)(2,1)S(1)}, bf16[4,64,256]{2,1,0:T(8,128)(2,1)S(1)}, u32[]{:S(2)}, u32[]{:S(2)}) collective-permute-start(bf16[4,64,256]{2,1,0:T(8,128)(2,1)S(1)} %get-tuple-element.79), channel_id=1, source_target_pairs={{0,1},{1,0},{2,3},{3,2},{4,5},{5,4},{6,7},{7,6},{8,9},{9,8},{10,11... | collective-permute-start | bytes 393224 | tf_op jit(solution)/shard_map/ppermute | solution.py:288
  50.1 1.1 %collective-permute-start.22 = (bf16[4,64,256]{2,1,0:T(8,128)(2,1)S(1)}, bf16[4,64,256]{2,1,0:T(8,128)(2,1)S(1)}, u32[]{:S(2)}, u32[]{:S(2)}) collective-permute-start(bf16[4,64,256]{2,1,0:T(8,128)(2,1)S(1)} %get-tuple-element.80), channel_id=1, source_target_pairs={{0,2},{1,3},{2,0},{3,1},{4,6},{5,7},{6,4},{7,5},{8,10},{9,11},{10,... | collective-permute-start | bytes 393224 | tf_op jit(solution)/shard_map/ppermute | solution.py:288
  51.2 0.9 %ready.1 = (f32[2,2,256,256]{3,2,1,0:T(8,128)S(1)}, bf16[3,2,256,256]{3,2,1,0:T(8,128)(2,1)S(1)}) custom-call(bf16[3,1024,1024]{2,1,0:T(8,128)(2,1)S(1)} %get-tuple-element.43.refs_1_.refs_2_.refs_0_.refs_3_.refs_4_.refs_17_, bf16[272,1024]{1,0:T(8,128)(2,1)S(1)} %hold.2.refs_2_.refs_1_.refs_7_.refs_3_, ...), custom_call_target="tpu_custom_call" | custom-call | flops 1000000000 | bytes 2097152 | tf_op jit(solution)/shard_map/ready/pallas_call | solution.py:22
  52.1 0.7 collective-permute-start.23
  52.8 2.1 %last.3 = (bf16[4,64,256]{2,1,0:T(8,128)(2,1)S(1)}, bf16[4,64,256]{2,1,0:T(8,128)(2,1)S(1)}, bf16[4,64,256]{2,1,0:T(8,128)(2,1)S(1)}, bf16[4,64,256]{2,1,0:T(8,128)(2,1)S(1)}) custom-call(s32[3]{0:T(128)S(1)} %copy-done, bf16[64,1024]{1,0:T(8,128)(2,1)S(1)} %collective-permute-done.16.refs_1_, ...), custom_call_target="tpu_custom_call" | custom-call | flops 1000000000 | bytes 2097152 | tf_op jit(solution)/shard_map/last/pallas_call | solution.py:22
  54.9 0.2 collective-permute-start.18
  55.1 1.1 %collective-permute-start.19 = (bf16[4,64,256]{2,1,0:T(8,128)(2,1)S(1)}, bf16[4,64,256]{2,1,0:T(8,128)(2,1)S(1)}, u32[]{:S(2)}, u32[]{:S(2)}) collective-permute-start(bf16[4,64,256]{2,1,0:T(8,128)(2,1)S(1)} %get-tuple-element.77), channel_id=1, source_target_pairs={{0,2},{1,3},{2,0},{3,1},{4,6},{5,7},{6,4},{7,5},{8,10},{9,11},{10,... | collective-permute-start | bytes 393224 | tf_op jit(solution)/shard_map/ppermute | solution.py:288
  56.2 0.9 %collective-permute-start.20 = (bf16[4,64,256]{2,1,0:T(8,128)(2,1)S(1)}, bf16[4,64,256]{2,1,0:T(8,128)(2,1)S(1)}, u32[]{:S(2)}, u32[]{:S(2)}) collective-permute-start(bf16[4,64,256]{2,1,0:T(8,128)(2,1)S(1)} %get-tuple-element.78), channel_id=1, source_target_pairs={{0,3},{1,2},{2,1},{3,0},{4,7},{5,6},{6,5},{7,4},{8,11},{9,10},{10,... | collective-permute-start | bytes 393224 | tf_op jit(solution)/shard_map/ppermute | solution.py:288
  57.1 1.5 %collective-permute-done.23.refs_14_ = bf16[4,64,256]{2,1,0:T(8,128)(2,1)S(1)} collective-permute-done((bf16[4,64,256]{2,1,0:T(8,128)(2,1)S(1)}, bf16[4,64,256]{2,1,0:T(8,128)(2,1)S(1)}, u32[]{:S(2)}, u32[]{:S(2)}) %collective-permute-start.23) | collective-permute-done | bytes 131104 | tf_op jit(solution)/shard_map/ppermute | solution.py:288
  58.6 1.3 %counts.2 = (f32[3,256,1024]{2,1,0:T(8,128)S(1)}, f32[3,256,256]{2,1,0:T(8,128)S(1)}) custom-call(s32[3]{0:T(128)S(1)} %copy-done, f32[2,2,256,256]{3,2,1,0:T(8,128)S(1)} %get-tuple-element.53.refs_14_.refs_1_, bf16[3,2,256,256]{3,2,1,0:T(8,128)(2,1)S(1)} %get-tuple-element.54.refs_2_, bf16[272,1024]{1,0:T(8,128)(2,1)S(1)} %hold.2.refs_2_.refs_1_.refs_7_.refs_3_, ...), custom_call_target="tpu_custom_call" | custom-call | flops 1000000000 | bytes 2097152 | tf_op jit(solution)/shard_map/counts/pallas_call | solution.py:22
  59.9 0.9 %collective-permute-done.19.refs_13_ = bf16[4,64,256]{2,1,0:T(8,128)(2,1)S(1)} collective-permute-done((bf16[4,64,256]{2,1,0:T(8,128)(2,1)S(1)}, bf16[4,64,256]{2,1,0:T(8,128)(2,1)S(1)}, u32[]{:S(2)}, u32[]{:S(2)}) %collective-permute-start.19) | collective-permute-done | bytes 131104 | tf_op jit(solution)/shard_map/ppermute | solution.py:288
  60.8 3.0 %collective-permute-done.20.refs_14_ = bf16[4,64,256]{2,1,0:T(8,128)(2,1)S(1)} collective-permute-done((bf16[4,64,256]{2,1,0:T(8,128)(2,1)S(1)}, bf16[4,64,256]{2,1,0:T(8,128)(2,1)S(1)}, u32[]{:S(2)}, u32[]{:S(2)}) %collective-permute-start.20) | collective-permute-done | bytes 131104 | tf_op jit(solution)/shard_map/ppermute | solution.py:288
  63.7 2.3 %counts.3 = (bf16[3,256,1024]{2,1,0:T(8,128)(2,1)}, bf16[3,256,256]{2,1,0:T(8,128)(2,1)}) custom-call(s32[3]{0:T(128)S(1)} %copy-done, f32[2,2,256,256]{3,2,1,0:T(8,128)S(1)} %get-tuple-element.53.refs_14_.refs_1_, bf16[3,2,256,256]{3,2,1,0:T(8,128)(2,1)S(1)} %get-tuple-element.54.refs_2_, bf16[272,1024]{1,0:T(8,128)(2,1)S(1)} %hold.2.refs_2_.refs_1_.refs_7_.refs_3_, ...), custom_call_target="tpu_custom_call" | custom-call | flops 1000000000 | bytes 2097152 | tf_op jit(solution)/shard_map/counts/pallas_call | solution.py:22
  (25 shorter events, 0.3 us)
Async XLA Ops:
  6.0 4.7 %collective-permute-start.3 = (bf16[64,1024]{1,0:T(8,128)(2,1)S(1)}, bf16[64,1024]{1,0:T(8,128)(2,1)S(1)}, u32[]{:S(2)}, u32[]{:S(2)}) collective-permute-start(bf16[64,1024]{1,0:T(8,128)(2,1)S(1)} %first.2.refs_1_), channel_id=1, source_target_pairs={{4,0},{12,8},{20,16},{28,24},{5,1},{13,9},{21,17},{29,25},{6,2},{1... | collective-permute-start | bytes 393224 | tf_op jit(solution)/shard_map/ppermute | solution.py:360
  7.3 13.2 %collective-permute-start.1 = (bf16[272,1024]{1,0:T(8,128)(2,1)S(1)}, bf16[272,1024]{1,0:T(8,128)(2,1)S(1)}, u32[]{:S(2)}, u32[]{:S(2)}) collective-permute-start(bf16[272,1024]{1,0:T(8,128)(2,1)S(1)} %hold.2.refs_2_.refs_1_.refs_7_.refs_3_), channel_id=1, source_target_pairs={{0,2},{1,3},{2,0},{3,1},{4,6},{5,7},{6,4},{7,5},{8,10},{9,11},{10,... | collective-permute-start | bytes 1671176 | tf_op jit(solution)/shard_map/ppermute | solution.py:288
  9.4 3.2 %collective-permute-start.2 = (bf16[64,1024]{1,0:T(8,128)(2,1)S(1)}, bf16[64,1024]{1,0:T(8,128)(2,1)S(1)}, u32[]{:S(2)}, u32[]{:S(2)}) collective-permute-start(bf16[64,1024]{1,0:T(8,128)(2,1)S(1)} %first.3), channel_id=1, source_target_pairs={{4,0},{12,8},{20,16},{28,24},{5,1},{13,9},{21,17},{29,25},{6,2},{1... | collective-permute-start | bytes 393224 | tf_op jit(solution)/shard_map/ppermute | solution.py:360
  10.8 2.6 %collective-permute-start.5 = (bf16[64,1024]{1,0:T(8,128)(2,1)S(1)}, bf16[64,1024]{1,0:T(8,128)(2,1)S(1)}, u32[]{:S(2)}, u32[]{:S(2)}) collective-permute-start(bf16[64,1024]{1,0:T(8,128)(2,1)S(1)} %get-tuple-element.47.refs_3_), channel_id=1, source_target_pairs={{8,0},{24,16},{9,1},{25,17},{10,2},{26,18},{11,3},{27,19}} | collective-permute-start | bytes 393224 | tf_op jit(solution)/shard_map/ppermute | solution.py:360
  12.7 3.3 %collective-permute-start.4 = (bf16[64,1024]{1,0:T(8,128)(2,1)S(1)}, bf16[64,1024]{1,0:T(8,128)(2,1)S(1)}, u32[]{:S(2)}, u32[]{:S(2)}) collective-permute-start(bf16[64,1024]{1,0:T(8,128)(2,1)S(1)} %get-tuple-element.49), channel_id=1, source_target_pairs={{8,0},{24,16},{9,1},{25,17},{10,2},{26,18},{11,3},{27,19}} | collective-permute-start | bytes 393224 | tf_op jit(solution)/shard_map/ppermute | solution.py:360
  13.4 3.2 %collective-permute-start.8 = (bf16[64,1024]{1,0:T(8,128)(2,1)S(1)}, bf16[64,1024]{1,0:T(8,128)(2,1)S(1)}, u32[]{:S(2)}, u32[]{:S(2)}) collective-permute-start(bf16[64,1024]{1,0:T(8,128)(2,1)S(1)} %get-tuple-element.51.refs_3_), channel_id=1, source_target_pairs={{16,0},{17,1},{18,2},{19,3}} | collective-permute-start | bytes 393224 | tf_op jit(solution)/shard_map/ppermute | solution.py:373
  14.0 15.0 %collective-permute-start = (bf16[272,1024]{1,0:T(8,128)(2,1)S(1)}, bf16[272,1024]{1,0:T(8,128)(2,1)S(1)}, u32[]{:S(2)}, u32[]{:S(2)}) collective-permute-start(bf16[272,1024]{1,0:T(8,128)(2,1)S(1)} %hold.2.refs_2_.refs_1_.refs_7_.refs_3_), channel_id=1, source_target_pairs={{0,1},{1,0},{2,3},{3,2},{4,5},{5,4},{6,7},{7,6},{8,9},{9,8},{10,11... | collective-permute-start | bytes 1671176 | tf_op jit(solution)/shard_map/ppermute | solution.py:288
  15.9 6.7 %collective-permute-start.7 = (bf16[64,1024]{1,0:T(8,128)(2,1)S(1)}, bf16[64,1024]{1,0:T(8,128)(2,1)S(1)}, u32[]{:S(2)}, u32[]{:S(2)}) collective-permute-start(bf16[64,1024]{1,0:T(8,128)(2,1)S(1)} %get-tuple-element.52.refs_1_), channel_id=1, source_target_pairs={{16,0},{17,1},{18,2},{19,3}} | collective-permute-start | bytes 393224 | tf_op jit(solution)/shard_map/ppermute | solution.py:373
  16.7 8.7 %collective-permute-start.13 = (bf16[64,1024]{1,0:T(8,128)(2,1)S(1)}, bf16[64,1024]{1,0:T(8,128)(2,1)S(1)}, u32[]{:S(2)}, u32[]{:S(2)}) collective-permute-start(bf16[64,1024]{1,0:T(8,128)(2,1)S(1)} %get-tuple-element.63.refs_5_), channel_id=1, source_target_pairs={{0,16},{1,17},{2,18},{3,19}} | collective-permute-start | bytes 393224 | tf_op jit(solution)/shard_map/ppermute | solution.py:397
  20.6 11.5 %collective-permute-start.6 = (bf16[272,1024]{1,0:T(8,128)(2,1)S(1)}, bf16[272,1024]{1,0:T(8,128)(2,1)S(1)}, u32[]{:S(2)}, u32[]{:S(2)}) collective-permute-start(bf16[272,1024]{1,0:T(8,128)(2,1)S(1)} %hold.3), channel_id=1, source_target_pairs={{0,1},{1,0},{2,3},{3,2},{4,5},{5,4},{6,7},{7,6},{8,9},{9,8},{10,11... | collective-permute-start | bytes 1671176 | tf_op jit(solution)/shard_map/ppermute | solution.py:288
  22.7 4.2 %collective-permute-start.12 = (bf16[64,1024]{1,0:T(8,128)(2,1)S(1)}, bf16[64,1024]{1,0:T(8,128)(2,1)S(1)}, u32[]{:S(2)}, u32[]{:S(2)}) collective-permute-start(bf16[64,1024]{1,0:T(8,128)(2,1)S(1)} %get-tuple-element.60.refs_5_), channel_id=1, source_target_pairs={{0,16},{1,17},{2,18},{3,19}} | collective-permute-start | bytes 393224 | tf_op jit(solution)/shard_map/ppermute | solution.py:397
  23.4 8.0 %collective-permute-start.10 = (bf16[128,1024]{1,0:T(8,128)(2,1)S(1)}, bf16[128,1024]{1,0:T(8,128)(2,1)S(1)}, u32[]{:S(2)}, u32[]{:S(2)}) collective-permute-start(bf16[128,1024]{1,0:T(8,128)(2,1)S(1)} %get-tuple-element.59.refs_10_.refs_7_), channel_id=1, source_target_pairs={{0,2},{1,3},{2,0},{3,1},{4,6},{5,7},{6,4},{7,5},{8,10},{9,11},{10,... | collective-permute-start | bytes 786440 | tf_op jit(solution)/shard_map/ppermute | solution.py:288
  25.5 2.2 %collective-permute-start.15 = (bf16[64,1024]{1,0:T(8,128)(2,1)S(1)}, bf16[64,1024]{1,0:T(8,128)(2,1)S(1)}, u32[]{:S(2)}, u32[]{:S(2)}) collective-permute-start(bf16[64,1024]{1,0:T(8,128)(2,1)S(1)} %get-tuple-element.65.refs_6_.refs_5_), channel_id=1, source_target_pairs={{0,8},{16,24},{1,9},{17,25},{2,10},{18,26},{3,11},{19,27}} | collective-permute-start | bytes 393224 | tf_op jit(solution)/shard_map/ppermute | solution.py:397
  27.0 5.2 %collective-permute-start.14 = (bf16[64,1024]{1,0:T(8,128)(2,1)S(1)}, bf16[64,1024]{1,0:T(8,128)(2,1)S(1)}, u32[]{:S(2)}, u32[]{:S(2)}) collective-permute-start(bf16[64,1024]{1,0:T(8,128)(2,1)S(1)} %get-tuple-element.66.refs_5_), channel_id=1, source_target_pairs={{0,8},{16,24},{1,9},{17,25},{2,10},{18,26},{3,11},{19,27}} | collective-permute-start | bytes 393224 | tf_op jit(solution)/shard_map/ppermute | solution.py:397
  27.7 16.8 %collective-permute-start.17 = (bf16[64,1024]{1,0:T(8,128)(2,1)S(1)}, bf16[64,1024]{1,0:T(8,128)(2,1)S(1)}, u32[]{:S(2)}, u32[]{:S(2)}) collective-permute-start(bf16[64,1024]{1,0:T(8,128)(2,1)S(1)} %get-tuple-element.69.refs_6_), channel_id=1, source_target_pairs={{0,4},{8,12},{16,20},{24,28},{1,5},{9,13},{17,21},{25,29},{2,6},{1... | collective-permute-start | bytes 393224 | tf_op jit(solution)/shard_map/ppermute | solution.py:407
  29.0 23.1 %collective-permute-start.9 = (bf16[128,1024]{1,0:T(8,128)(2,1)S(1)}, bf16[128,1024]{1,0:T(8,128)(2,1)S(1)}, u32[]{:S(2)}, u32[]{:S(2)}) collective-permute-start(bf16[128,1024]{1,0:T(8,128)(2,1)S(1)} %get-tuple-element.59.refs_10_.refs_7_), channel_id=1, source_target_pairs={{0,1},{1,0},{2,3},{3,2},{4,5},{5,4},{6,7},{7,6},{8,9},{9,8},{10,11... | collective-permute-start | bytes 786440 | tf_op jit(solution)/shard_map/ppermute | solution.py:288
  31.4 21.4 %collective-permute-start.11 = (bf16[128,1024]{1,0:T(8,128)(2,1)S(1)}, bf16[128,1024]{1,0:T(8,128)(2,1)S(1)}, u32[]{:S(2)}, u32[]{:S(2)}) collective-permute-start(bf16[128,1024]{1,0:T(8,128)(2,1)S(1)} %collective-permute-done.10.refs_12_.refs_9_), channel_id=1, source_target_pairs={{0,1},{1,0},{2,3},{3,2},{4,5},{5,4},{6,7},{7,6},{8,9},{9,8},{10,11... | collective-permute-start | bytes 786440 | tf_op jit(solution)/shard_map/ppermute | solution.py:288
  32.2 12.3 %copy-start = (s32[3]{0:T(128)S(1)}, s32[3]{0:T(128)}, u32[]{:S(2)}) copy-start(s32[3]{0:T(128)} %refs_0_.9) | copy-start | bytes 40
  32.2 20.6 %collective-permute-start.16 = (bf16[64,1024]{1,0:T(8,128)(2,1)S(1)}, bf16[64,1024]{1,0:T(8,128)(2,1)S(1)}, u32[]{:S(2)}, u32[]{:S(2)}) collective-permute-start(bf16[64,1024]{1,0:T(8,128)(2,1)S(1)} %get-tuple-element.70.refs_6_), channel_id=1, source_target_pairs={{0,4},{8,12},{16,20},{24,28},{1,5},{9,13},{17,21},{25,29},{2,6},{1... | collective-permute-start | bytes 393224 | tf_op jit(solution)/shard_map/ppermute | solution.py:407
  46.5 9.7 %collective-permute-start.21 = (bf16[4,64,256]{2,1,0:T(8,128)(2,1)S(1)}, bf16[4,64,256]{2,1,0:T(8,128)(2,1)S(1)}, u32[]{:S(2)}, u32[]{:S(2)}) collective-permute-start(bf16[4,64,256]{2,1,0:T(8,128)(2,1)S(1)} %get-tuple-element.79), channel_id=1, source_target_pairs={{0,1},{1,0},{2,3},{3,2},{4,5},{5,4},{6,7},{7,6},{8,9},{9,8},{10,11... | collective-permute-start | bytes 393224 | tf_op jit(solution)/shard_map/ppermute | solution.py:288
  50.1 7.0 %collective-permute-start.22 = (bf16[4,64,256]{2,1,0:T(8,128)(2,1)S(1)}, bf16[4,64,256]{2,1,0:T(8,128)(2,1)S(1)}, u32[]{:S(2)}, u32[]{:S(2)}) collective-permute-start(bf16[4,64,256]{2,1,0:T(8,128)(2,1)S(1)} %get-tuple-element.80), channel_id=1, source_target_pairs={{0,2},{1,3},{2,0},{3,1},{4,6},{5,7},{6,4},{7,5},{8,10},{9,11},{10,... | collective-permute-start | bytes 393224 | tf_op jit(solution)/shard_map/ppermute | solution.py:288
  52.1 6.4 %collective-permute-start.23 = (bf16[4,64,256]{2,1,0:T(8,128)(2,1)S(1)}, bf16[4,64,256]{2,1,0:T(8,128)(2,1)S(1)}, u32[]{:S(2)}, u32[]{:S(2)}) collective-permute-start(bf16[4,64,256]{2,1,0:T(8,128)(2,1)S(1)} %get-tuple-element.81), channel_id=1, source_target_pairs={{0,3},{1,2},{2,1},{3,0},{4,7},{5,6},{6,5},{7,4},{8,11},{9,10},{10,... | collective-permute-start | bytes 393224 | tf_op jit(solution)/shard_map/ppermute | solution.py:288
  54.9 5.0 %collective-permute-start.18 = (bf16[4,64,256]{2,1,0:T(8,128)(2,1)S(1)}, bf16[4,64,256]{2,1,0:T(8,128)(2,1)S(1)}, u32[]{:S(2)}, u32[]{:S(2)}) collective-permute-start(bf16[4,64,256]{2,1,0:T(8,128)(2,1)S(1)} %get-tuple-element.76), channel_id=1, source_target_pairs={{0,1},{1,0},{2,3},{3,2},{4,5},{5,4},{6,7},{7,6},{8,9},{9,8},{10,11... | collective-permute-start | bytes 393224 | tf_op jit(solution)/shard_map/ppermute | solution.py:288
  55.1 5.7 %collective-permute-start.19 = (bf16[4,64,256]{2,1,0:T(8,128)(2,1)S(1)}, bf16[4,64,256]{2,1,0:T(8,128)(2,1)S(1)}, u32[]{:S(2)}, u32[]{:S(2)}) collective-permute-start(bf16[4,64,256]{2,1,0:T(8,128)(2,1)S(1)} %get-tuple-element.77), channel_id=1, source_target_pairs={{0,2},{1,3},{2,0},{3,1},{4,6},{5,7},{6,4},{7,5},{8,10},{9,11},{10,... | collective-permute-start | bytes 393224 | tf_op jit(solution)/shard_map/ppermute | solution.py:288
  56.2 7.5 %collective-permute-start.20 = (bf16[4,64,256]{2,1,0:T(8,128)(2,1)S(1)}, bf16[4,64,256]{2,1,0:T(8,128)(2,1)S(1)}, u32[]{:S(2)}, u32[]{:S(2)}) collective-permute-start(bf16[4,64,256]{2,1,0:T(8,128)(2,1)S(1)} %get-tuple-element.78), channel_id=1, source_target_pairs={{0,3},{1,2},{2,1},{3,0},{4,7},{5,6},{6,5},{7,4},{8,11},{9,10},{10,... | collective-permute-start | bytes 393224 | tf_op jit(solution)/shard_map/ppermute | solution.py:288

commit v8 on v7

--- a/solution.py
+++ b/solution.py
@@ -219,42 +219,42 @@
         packs[mask][...] = posts[:, :, pl.ds(start, share)]
 
 
-def ready_body(nodes, groups, w_ref, *refs):
-    lams, (raw_ref, hot_ref) = refs[:groups], refs[groups:]
-    chunks, merged, share = raw_ref.shape[1:]
+def ready_body(nodes, groups, *refs):
+    lams, hot_ref = refs[:groups], refs[groups]
+    chunks, _, merged = hot_ref.shape[1:]
     part = merged // groups
     rows = part * chunks
     values = hot_ref.shape[2]
     base = (nodes - 1) * rows
-    start = pl.multiple_of(lax.axis_index("rows") * share, share)
     for n in range(nodes):
         observed = [lam[base : base + PAD, :rows].astype(F32).astype(jnp.int32)[n : n + 1] for lam in lams]
         for c in range(chunks):
             row = jnp.concatenate([item[:, c * part : (c + 1) * part] for item in observed], axis=1)
             hot_ref[n, c] = one_hot(row, values)
-        if n > 0:
-            weight = w_ref[n, pl.ds(start, share), :]
-            for c in range(chunks):
-                low = (n - 1) * rows + c * part
-                lam = jnp.concatenate([item[low : low + part, :] for item in lams], axis=0)
-                raw_ref[n - 1, c] = lax.dot_general(lam, weight, (((1,), (1,)), ((), ())), preferred_element_type=F32)
-
-
-def counts_body(nodes, groups, chunk, parent_ref, raw_ref, hot_ref, *refs):
+
+
+def counts_body(nodes, groups, chunk, parent_ref, w_ref, hot_ref, *refs):
     lams, tops, posts = refs[:groups], refs[groups : 2 * groups], refs[2 * groups : 3 * groups]
     refs = refs[3 * groups :]
-    chunks = raw_ref.shape[1]
-    part = raw_ref.shape[2] // groups
+    chunks = hot_ref.shape[1]
+    part = hot_ref.shape[3] // groups
     rows = part * chunks
-    before = refs[:2] if chunk > 0 else None
-    refs = refs[2:] if chunk > 0 else refs
+    before = refs[:3] if chunk > 0 else None
+    refs = refs[3:] if chunk > 0 else refs
     final = chunk == chunks - 1
     copies = []
     if final:
-        w_ref, homes, refs, sems = refs[0], refs[1:3], refs[3:5], refs[5]
-        share = refs[0].shape[1]
+        homes, refs, sems = refs[:2], refs[2:4], refs[4]
         samples = rows * groups
-        start = pl.multiple_of(lax.axis_index("rows") * share, share)
+    share = refs[0].shape[1]
+    start = pl.multiple_of(lax.axis_index("rows") * share, share)
+
+    def own_message(n, c):
+        low = (n - 1) * rows + c * part
+        lam = jnp.concatenate([item[low : low + part, :] for item in lams], axis=0)
+        weight = w_ref[n, pl.ds(start, share), :]
+        return lax.dot_general(lam, weight, (((1,), (1,)), ((), ())), preferred_element_type=F32)
+
     for n in range(nodes):
         low = (n - 1) * rows + chunk * part if n > 0 else chunk * part
         lam = jnp.concatenate([item[low : low + part, :] for item in (lams if n > 0 else tops)], axis=0)
@@ -263,7 +263,7 @@
         else:
             slot = local_slot(parent_ref, n, nodes)
             q_par = jnp.concatenate([item[slot] for item in posts], axis=0)
-            ratio = (q_par.astype(F32) / raw_ref[n - 1, chunk]).astype(BF16)
+            ratio = (q_par.astype(F32) / (own_message(n, chunk) if before is None else before[2][n - 1, chunk - 1])).astype(BF16)
         flow = lax.dot_general(ratio, lam, (((0,), (0,)), ((), ())), preferred_element_type=F32)
         post = jnp.concatenate([item[n] for item in posts], axis=0)
         tally = jnp.dot(hot_ref[n, chunk], post, preferred_element_type=F32)
@@ -280,6 +280,10 @@
             if final:
                 copies.append(pltpu.make_async_copy(refs[k].at[n], homes[k].at[n], sems.at[k, n]))
                 copies[-1].start()
+    if before is None:
+        for n in range(1, nodes):
+            for c in range(1, chunks):
+                refs[2][n - 1, c - 1] = own_message(n, c)
     for copy in copies:
         copy.wait()
 
@@ -381,12 +385,11 @@
         (top_msg[c],) = run(top_body, "top", (top_lam[c], weights), (half(F32),), work=1.0)
     all_tops = gather(far(merged[0]))
     all_lams = gather(near, send[-1:])
-    raw_own, hots = run(
+    (hots,) = run(
         functools.partial(ready_body, nodes, groups),
         "ready",
-        (weights, *all_lams),
+        (*all_lams,),
         (
-            pltpu.VMEM((nodes - 1, CHUNKS, groups * part, share), F32),
             pltpu.VMEM((nodes, CHUNKS, values, groups * part), BF16),
         ),
         after=(),
@@ -412,7 +415,7 @@
             (pltpu.VMEM((nodes + 1, part, share), BF16),) * groups,
             (pltpu.VMEM((nodes + 1, part, states), BF16),),
             [SM] + [VM] * 8,
-            after=[own_posts[-1][0], *all_tops, raw_own] if c > 0 else [],
+            after=[own_posts[-1][0], *all_tops, hots] if c > 0 else [],
         )
         order = sorted(range(1, groups), reverse=True)
         moved = {mask: swap(packs[mask], mask) for mask in order}
@@ -420,13 +423,14 @@
     sums = ()
     for c in every:
         final = c == CHUNKS - 1
-        ins = (parent, raw_own, hots, *all_lams, *all_tops, *own_posts[c], *sums) + ((weights,) if final else ())
+        ins = (parent, weights, hots, *all_lams, *all_tops, *own_posts[c], *sums)
         shapes = ((nodes, share, states), (nodes, values, share))
         sums = run(
             functools.partial(counts_body, nodes, groups, c),
             "counts",
             ins,
-            tuple(jax.ShapeDtypeStruct(x, BF16) if final else pltpu.VMEM(x, F32) for x in shapes),
+            tuple(jax.ShapeDtypeStruct(x, BF16) if final else pltpu.VMEM(x, F32) for x in shapes)
+            + (() if final else (pltpu.VMEM((nodes - 1, CHUNKS - 1, groups * part, share), F32),)),
             tuple(pltpu.VMEM(x, BF16) for x in shapes) + (pltpu.SemaphoreType.DMA((2, nodes)),) if final else (),
             [SM] + [VM] * (len(ins) - 1),
             (ANY, ANY) if final else None,

time: 66.4 us -> 66.6 us (level)
  waiting for transfers between devices: 22.7 us -> 21.8 us
  Pallas kernels: 16.8 us -> 17.6 us
    ppermute x12, waiting for transfers between devices: 10.6 us -> 9.63 us  [swap(): lax.ppermute(value, 'rows', [(s, s ^ mask) for s in range(lax.axis_size('...]
    pallas_call x22, Pallas kernels: 16.8 us -> 17.6 us  [run(): pl.pallas_call(lambda *refs: body(*refs[:count], *refs[idle:]), name=name...]
  transfers between devices with their start and end apart: 24 -> 24, of which waited for: 7 -> 6; matrix products, arithmetic and copies ran while one was open for 0% -> 0% of each run, Pallas kernels for 14% -> 15%
where the time goes in v8:
time: 66.6 us; the launch traced here: 66.2 us
  starting transfers between devices  25.7 us (39%)
  waiting for transfers between devices  21.8 us (33%)
  Pallas kernels  17.6 us (26%)
  between operations  1.11 us (2%)
    pallas_call x22, Pallas kernels, run(): pl.pallas_call(lambda *refs: body(*refs[:count], *refs[idle:]), name=name...  17.6 us
    ppermute x12, starting transfers between devices, swap(): lax.ppermute(value, 'rows', [(s, s ^ mask) for s in range(lax.axis_size('...  15.1 us
    ppermute x2, waiting for transfers between devices, per_device(): recv = lax.ppermute(post[c], 'leaf', down_pairs(0))  10.9 us
    ppermute x12, waiting for transfers between devices, swap(): lax.ppermute(value, 'rows', [(s, s ^ mask) for s in range(lax.axis_size('...  9.63 us
    ppermute x4, starting transfers between devices, per_device(): recv = lax.ppermute(send[c], 'leaf', up_pairs(level))  3.96 us
    ppermute x4, starting transfers between devices, per_device(): recv = lax.ppermute(post[c], 'leaf', down_pairs(level))  2.68 us
    ppermute x2, starting transfers between devices, per_device(): recv = lax.ppermute(post[c], 'leaf', down_pairs(0))  2.58 us
  transfers between devices with their start and end apart: 24, of which 6 were waited for; matrix products, arithmetic and copies ran while one was open for 0% of the time, Pallas kernels for 15%

profile of v8, /device:TPU:13, one launch (start us, length us, event | category | flops | bytes accessed | tf_op | source)
XLA Modules:
  0.0 66.2 jit_solution(17384478830387236834)
XLA Ops:
  0.6 4.5 %prep.1 = (bf16[3,1024,1024]{2,1,0:T(8,128)(2,1)S(1)}, bf16[272,1024]{1,0:T(8,128)(2,1)S(1)}, f32[2,128,1024]{2,1,0:T(8,128)S(1)}, f32[8,1024]{1,0:T(8,128)S(1)}...) custom-call(s32[3]{0:T(128)} %refs_0_.9, s32[3,128]{1,0:T(4,128)} %refs_1_.1, bf16[3,256,1024]{2,1,0:T(8,128)(2,1)} %refs_2_.1, ...), custom_call_target="tpu_custom_call" | custom-call | flops 1000000000 | bytes 2097152 | tf_op jit(solution)/shard_map/prep/pallas_call | solution.py:22
  5.2 0.8 %first.2.refs_1_ = bf16[64,1024]{1,0:T(8,128)(2,1)S(1)} custom-call(f32[64,1024]{1,0:T(8,128)S(1)} %get-tuple-element.44.refs_0_, bf16[3,1024,1024]{2,1,0:T(8,128)(2,1)S(1)} %get-tuple-element.42.refs_1_.refs_2_.refs_3_.refs_4_), custom_call_target="tpu_custom_call" | custom-call | flops 1000000000 | bytes 2097152 | tf_op jit(solution)/shard_map/first/pallas_call | solution.py:22
  6.0 1.3 %collective-permute-start.3 = (bf16[64,1024]{1,0:T(8,128)(2,1)S(1)}, bf16[64,1024]{1,0:T(8,128)(2,1)S(1)}, u32[]{:S(2)}, u32[]{:S(2)}) collective-permute-start(bf16[64,1024]{1,0:T(8,128)(2,1)S(1)} %first.2.refs_1_), channel_id=1, source_target_pairs={{4,0},{12,8},{20,16},{28,24},{5,1},{13,9},{21,17},{29,25},{6,2},{1... | collective-permute-start | bytes 393224 | tf_op jit(solution)/shard_map/ppermute | solution.py:364
  7.3 1.3 %collective-permute-start.1 = (bf16[272,1024]{1,0:T(8,128)(2,1)S(1)}, bf16[272,1024]{1,0:T(8,128)(2,1)S(1)}, u32[]{:S(2)}, u32[]{:S(2)}) collective-permute-start(bf16[272,1024]{1,0:T(8,128)(2,1)S(1)} %hold.2.refs_2_.refs_0_.refs_7_.refs_3_), channel_id=1, source_target_pairs={{0,2},{1,3},{2,0},{3,1},{4,6},{5,7},{6,4},{7,5},{8,10},{9,11},{10,... | collective-permute-start | bytes 1671176 | tf_op jit(solution)/shard_map/ppermute | solution.py:292
  8.6 0.8 %first.3 = bf16[64,1024]{1,0:T(8,128)(2,1)S(1)} custom-call(f32[64,1024]{1,0:T(8,128)S(1)} %get-tuple-element.45.refs_0_, bf16[3,1024,1024]{2,1,0:T(8,128)(2,1)S(1)} %get-tuple-element.42.refs_1_.refs_2_.refs_3_.refs_4_, bf16[272,1024]{1,0:T(8,128)(2,1)S(1)} %hold.2.refs_2_.refs_0_.refs_7_.refs_3_), custom_call_target="tpu_custom_call" | custom-call | flops 1000000000 | bytes 2097152 | tf_op jit(solution)/shard_map/first/pallas_call | solution.py:22
  9.4 1.3 %collective-permute-start.2 = (bf16[64,1024]{1,0:T(8,128)(2,1)S(1)}, bf16[64,1024]{1,0:T(8,128)(2,1)S(1)}, u32[]{:S(2)}, u32[]{:S(2)}) collective-permute-start(bf16[64,1024]{1,0:T(8,128)(2,1)S(1)} %first.3), channel_id=1, source_target_pairs={{4,0},{12,8},{20,16},{28,24},{5,1},{13,9},{21,17},{29,25},{6,2},{1... | collective-permute-start | bytes 393224 | tf_op jit(solution)/shard_map/ppermute | solution.py:364
  10.7 0.0 collective-permute-done.3.refs_1_
  10.8 0.7 %collective-permute-start.5 = (bf16[64,1024]{1,0:T(8,128)(2,1)S(1)}, bf16[64,1024]{1,0:T(8,128)(2,1)S(1)}, u32[]{:S(2)}, u32[]{:S(2)}) collective-permute-start(bf16[64,1024]{1,0:T(8,128)(2,1)S(1)} %get-tuple-element.46.refs_3_), channel_id=1, source_target_pairs={{8,0},{24,16},{9,1},{25,17},{10,2},{26,18},{11,3},{27,19}} | collective-permute-start | bytes 393224 | tf_op jit(solution)/shard_map/ppermute | solution.py:364
  11.5 1.2 %collective-permute-done.2.refs_1_ = bf16[64,1024]{1,0:T(8,128)(2,1)S(1)} collective-permute-done((bf16[64,1024]{1,0:T(8,128)(2,1)S(1)}, bf16[64,1024]{1,0:T(8,128)(2,1)S(1)}, u32[]{:S(2)}, u32[]{:S(2)}) %collective-permute-start.2) | collective-permute-done | bytes 131104 | tf_op jit(solution)/shard_map/ppermute | solution.py:364
  12.7 0.7 collective-permute-start.4
  13.3 0.0 collective-permute-done.5.refs_1_
  13.4 0.7 %collective-permute-start.8 = (bf16[64,1024]{1,0:T(8,128)(2,1)S(1)}, bf16[64,1024]{1,0:T(8,128)(2,1)S(1)}, u32[]{:S(2)}, u32[]{:S(2)}) collective-permute-start(bf16[64,1024]{1,0:T(8,128)(2,1)S(1)} %get-tuple-element.50.refs_3_), channel_id=1, source_target_pairs={{16,0},{17,1},{18,2},{19,3}} | collective-permute-start | bytes 393224 | tf_op jit(solution)/shard_map/ppermute | solution.py:377
  14.1 1.9 %collective-permute-start = (bf16[272,1024]{1,0:T(8,128)(2,1)S(1)}, bf16[272,1024]{1,0:T(8,128)(2,1)S(1)}, u32[]{:S(2)}, u32[]{:S(2)}) collective-permute-start(bf16[272,1024]{1,0:T(8,128)(2,1)S(1)} %hold.2.refs_2_.refs_0_.refs_7_.refs_3_), channel_id=1, source_target_pairs={{0,1},{1,0},{2,3},{3,2},{4,5},{5,4},{6,7},{7,6},{8,9},{9,8},{10,11... | collective-permute-start | bytes 1671176 | tf_op jit(solution)/shard_map/ppermute | solution.py:292
  15.9 0.7 collective-permute-start.7
  16.6 0.1 root.2
  16.7 0.7 %collective-permute-start.13 = (bf16[64,1024]{1,0:T(8,128)(2,1)S(1)}, bf16[64,1024]{1,0:T(8,128)(2,1)S(1)}, u32[]{:S(2)}, u32[]{:S(2)}) collective-permute-start(bf16[64,1024]{1,0:T(8,128)(2,1)S(1)} %get-tuple-element.60.refs_5_), channel_id=1, source_target_pairs={{0,16},{1,17},{2,18},{3,19}} | collective-permute-start | bytes 393224 | tf_op jit(solution)/shard_map/ppermute | solution.py:400
  17.4 3.2 %collective-permute-done.1.refs_2_.refs_9_.refs_5_ = bf16[272,1024]{1,0:T(8,128)(2,1)S(1)} collective-permute-done((bf16[272,1024]{1,0:T(8,128)(2,1)S(1)}, bf16[272,1024]{1,0:T(8,128)(2,1)S(1)}, u32[]{:S(2)}, u32[]{:S(2)}) %collective-permute-start.1) | collective-permute-done | bytes 557088 | tf_op jit(solution)/shard_map/ppermute | solution.py:292
  20.6 1.9 %collective-permute-start.6 = (bf16[272,1024]{1,0:T(8,128)(2,1)S(1)}, bf16[272,1024]{1,0:T(8,128)(2,1)S(1)}, u32[]{:S(2)}, u32[]{:S(2)}) collective-permute-start(bf16[272,1024]{1,0:T(8,128)(2,1)S(1)} %hold.3), channel_id=1, source_target_pairs={{0,1},{1,0},{2,3},{3,2},{4,5},{5,4},{6,7},{7,6},{8,9},{9,8},{10,11... | collective-permute-start | bytes 1671176 | tf_op jit(solution)/shard_map/ppermute | solution.py:292
  22.6 0.0 collective-permute-done.7.refs_1_
  22.6 0.1 root.3
  22.7 0.7 %collective-permute-start.12 = (bf16[64,1024]{1,0:T(8,128)(2,1)S(1)}, bf16[64,1024]{1,0:T(8,128)(2,1)S(1)}, u32[]{:S(2)}, u32[]{:S(2)}) collective-permute-start(bf16[64,1024]{1,0:T(8,128)(2,1)S(1)} %get-tuple-element.57.refs_5_), channel_id=1, source_target_pairs={{0,16},{1,17},{2,18},{3,19}} | collective-permute-start | bytes 393224 | tf_op jit(solution)/shard_map/ppermute | solution.py:400
  23.4 1.3 %collective-permute-start.10 = (bf16[128,1024]{1,0:T(8,128)(2,1)S(1)}, bf16[128,1024]{1,0:T(8,128)(2,1)S(1)}, u32[]{:S(2)}, u32[]{:S(2)}) collective-permute-start(bf16[128,1024]{1,0:T(8,128)(2,1)S(1)} %get-tuple-element.56.refs_10_.refs_7_), channel_id=1, source_target_pairs={{0,2},{1,3},{2,0},{3,1},{4,6},{5,7},{6,4},{7,5},{8,10},{9,11},{10,... | collective-permute-start | bytes 786440 | tf_op jit(solution)/shard_map/ppermute | solution.py:292
  24.7 0.8 %top.3.refs_2_.refs_3_ = f32[64,1024]{1,0:T(8,128)S(1)} custom-call(bf16[64,1024]{1,0:T(8,128)(2,1)S(1)} %get-tuple-element.55.refs_3_.refs_0_.refs_1_.refs_2_, bf16[3,1024,1024]{2,1,0:T(8,128)(2,1)S(1)} %get-tuple-element.42.refs_1_.refs_2_.refs_3_.refs_4_), custom_call_target="tpu_custom_call" | custom-call | flops 1000000000 | bytes 2097152 | tf_op jit(solution)/shard_map/top/pallas_call | solution.py:22
  25.4 0.0 collective-permute-done.13.refs_0_
  25.5 0.7 %collective-permute-start.15 = (bf16[64,1024]{1,0:T(8,128)(2,1)S(1)}, bf16[64,1024]{1,0:T(8,128)(2,1)S(1)}, u32[]{:S(2)}, u32[]{:S(2)}) collective-permute-start(bf16[64,1024]{1,0:T(8,128)(2,1)S(1)} %get-tuple-element.62.refs_6_.refs_5_), channel_id=1, source_target_pairs={{0,8},{16,24},{1,9},{17,25},{2,10},{18,26},{3,11},{19,27}} | collective-permute-start | bytes 393224 | tf_op jit(solution)/shard_map/ppermute | solution.py:400
  26.2 0.8 %top.2.refs_2_.refs_3_ = f32[64,1024]{1,0:T(8,128)S(1)} custom-call(bf16[64,1024]{1,0:T(8,128)(2,1)S(1)} %get-tuple-element.58.refs_0_.refs_1_.refs_2_, bf16[3,1024,1024]{2,1,0:T(8,128)(2,1)S(1)} %get-tuple-element.42.refs_1_.refs_2_.refs_3_.refs_4_), custom_call_target="tpu_custom_call" | custom-call | flops 1000000000 | bytes 2097152 | tf_op jit(solution)/shard_map/top/pallas_call | solution.py:22
  27.0 0.7 %collective-permute-start.14 = (bf16[64,1024]{1,0:T(8,128)(2,1)S(1)}, bf16[64,1024]{1,0:T(8,128)(2,1)S(1)}, u32[]{:S(2)}, u32[]{:S(2)}) collective-permute-start(bf16[64,1024]{1,0:T(8,128)(2,1)S(1)} %get-tuple-element.63.refs_5_), channel_id=1, source_target_pairs={{0,8},{16,24},{1,9},{17,25},{2,10},{18,26},{3,11},{19,27}} | collective-permute-start | bytes 393224 | tf_op jit(solution)/shard_map/ppermute | solution.py:400
  27.6 0.0 collective-permute-done.15.refs_0_
  27.7 1.3 %collective-permute-start.17 = (bf16[64,1024]{1,0:T(8,128)(2,1)S(1)}, bf16[64,1024]{1,0:T(8,128)(2,1)S(1)}, u32[]{:S(2)}, u32[]{:S(2)}) collective-permute-start(bf16[64,1024]{1,0:T(8,128)(2,1)S(1)} %get-tuple-element.66.refs_6_), channel_id=1, source_target_pairs={{0,4},{8,12},{16,20},{24,28},{1,5},{9,13},{17,21},{25,29},{2,6},{1... | collective-permute-start | bytes 393224 | tf_op jit(solution)/shard_map/ppermute | solution.py:410
  29.0 0.0 collective-permute-done.refs_1_.refs_8_.refs_4_
  29.0 0.4 collective-permute-start.9
  29.4 2.0 %collective-permute-done.10.refs_12_.refs_9_ = bf16[128,1024]{1,0:T(8,128)(2,1)S(1)} collective-permute-done((bf16[128,1024]{1,0:T(8,128)(2,1)S(1)}, bf16[128,1024]{1,0:T(8,128)(2,1)S(1)}, u32[]{:S(2)}, u32[]{:S(2)}) %collective-permute-start.10) | collective-permute-done | bytes 262176 | tf_op jit(solution)/shard_map/ppermute | solution.py:292
  31.4 0.8 %collective-permute-start.11 = (bf16[128,1024]{1,0:T(8,128)(2,1)S(1)}, bf16[128,1024]{1,0:T(8,128)(2,1)S(1)}, u32[]{:S(2)}, u32[]{:S(2)}) collective-permute-start(bf16[128,1024]{1,0:T(8,128)(2,1)S(1)} %collective-permute-done.10.refs_12_.refs_9_), channel_id=1, source_target_pairs={{0,1},{1,0},{2,3},{3,2},{4,5},{5,4},{6,7},{7,6},{8,9},{9,8},{10,11... | collective-permute-start | bytes 786440 | tf_op jit(solution)/shard_map/ppermute | solution.py:292
  32.2 1.3 %collective-permute-start.16 = (bf16[64,1024]{1,0:T(8,128)(2,1)S(1)}, bf16[64,1024]{1,0:T(8,128)(2,1)S(1)}, u32[]{:S(2)}, u32[]{:S(2)}) collective-permute-start(bf16[64,1024]{1,0:T(8,128)(2,1)S(1)} %get-tuple-element.67.refs_6_), channel_id=1, source_target_pairs={{0,4},{8,12},{16,20},{24,28},{1,5},{9,13},{17,21},{25,29},{2,6},{1... | collective-permute-start | bytes 393224 | tf_op jit(solution)/shard_map/ppermute | solution.py:410
  33.5 10.9 %collective-permute-done.17.refs_1_ = bf16[64,1024]{1,0:T(8,128)(2,1)S(1)} collective-permute-done((bf16[64,1024]{1,0:T(8,128)(2,1)S(1)}, bf16[64,1024]{1,0:T(8,128)(2,1)S(1)}, u32[]{:S(2)}, u32[]{:S(2)}) %collective-permute-start.17) | collective-permute-done | bytes 131104 | tf_op jit(solution)/shard_map/ppermute | solution.py:410
  44.4 2.1 %last.2 = (bf16[4,64,256]{2,1,0:T(8,128)(2,1)S(1)}, bf16[4,64,256]{2,1,0:T(8,128)(2,1)S(1)}, bf16[4,64,256]{2,1,0:T(8,128)(2,1)S(1)}, bf16[4,64,256]{2,1,0:T(8,128)(2,1)S(1)}) custom-call(s32[3]{0:T(128)S(1)} %copy-done, bf16[64,1024]{1,0:T(8,128)(2,1)S(1)} %collective-permute-done.17.refs_1_, ...), custom_call_target="tpu_custom_call" | custom-call | flops 1000000000 | bytes 2097152 | tf_op jit(solution)/shard_map/last/pallas_call | solution.py:22
  46.5 3.6 %collective-permute-start.21 = (bf16[4,64,256]{2,1,0:T(8,128)(2,1)S(1)}, bf16[4,64,256]{2,1,0:T(8,128)(2,1)S(1)}, u32[]{:S(2)}, u32[]{:S(2)}) collective-permute-start(bf16[4,64,256]{2,1,0:T(8,128)(2,1)S(1)} %get-tuple-element.76), channel_id=1, source_target_pairs={{0,1},{1,0},{2,3},{3,2},{4,5},{5,4},{6,7},{7,6},{8,9},{9,8},{10,11... | collective-permute-start | bytes 393224 | tf_op jit(solution)/shard_map/ppermute | solution.py:292
  50.1 1.1 %collective-permute-start.22 = (bf16[4,64,256]{2,1,0:T(8,128)(2,1)S(1)}, bf16[4,64,256]{2,1,0:T(8,128)(2,1)S(1)}, u32[]{:S(2)}, u32[]{:S(2)}) collective-permute-start(bf16[4,64,256]{2,1,0:T(8,128)(2,1)S(1)} %get-tuple-element.77), channel_id=1, source_target_pairs={{0,2},{1,3},{2,0},{3,1},{4,6},{5,7},{6,4},{7,5},{8,10},{9,11},{10,... | collective-permute-start | bytes 393224 | tf_op jit(solution)/shard_map/ppermute | solution.py:292
  51.2 0.3 ready.1.refs_14_.refs_2_
  51.5 0.7 collective-permute-start.23
  52.2 2.2 %last.3 = (bf16[4,64,256]{2,1,0:T(8,128)(2,1)S(1)}, bf16[4,64,256]{2,1,0:T(8,128)(2,1)S(1)}, bf16[4,64,256]{2,1,0:T(8,128)(2,1)S(1)}, bf16[4,64,256]{2,1,0:T(8,128)(2,1)S(1)}) custom-call(s32[3]{0:T(128)S(1)} %copy-done, bf16[64,1024]{1,0:T(8,128)(2,1)S(1)} %collective-permute-done.16.refs_1_, ...), custom_call_target="tpu_custom_call" | custom-call | flops 1000000000 | bytes 2097152 | tf_op jit(solution)/shard_map/last/pallas_call | solution.py:22
  54.4 0.2 collective-permute-start.18
  54.7 1.1 %collective-permute-start.19 = (bf16[4,64,256]{2,1,0:T(8,128)(2,1)S(1)}, bf16[4,64,256]{2,1,0:T(8,128)(2,1)S(1)}, u32[]{:S(2)}, u32[]{:S(2)}) collective-permute-start(bf16[4,64,256]{2,1,0:T(8,128)(2,1)S(1)} %get-tuple-element.74), channel_id=1, source_target_pairs={{0,2},{1,3},{2,0},{3,1},{4,6},{5,7},{6,4},{7,5},{8,10},{9,11},{10,... | collective-permute-start | bytes 393224 | tf_op jit(solution)/shard_map/ppermute | solution.py:292
  55.8 0.9 %collective-permute-start.20 = (bf16[4,64,256]{2,1,0:T(8,128)(2,1)S(1)}, bf16[4,64,256]{2,1,0:T(8,128)(2,1)S(1)}, u32[]{:S(2)}, u32[]{:S(2)}) collective-permute-start(bf16[4,64,256]{2,1,0:T(8,128)(2,1)S(1)} %get-tuple-element.75), channel_id=1, source_target_pairs={{0,3},{1,2},{2,1},{3,0},{4,7},{5,6},{6,5},{7,4},{8,11},{9,10},{10,... | collective-permute-start | bytes 393224 | tf_op jit(solution)/shard_map/ppermute | solution.py:292
  56.7 1.9 %collective-permute-done.23.refs_14_ = bf16[4,64,256]{2,1,0:T(8,128)(2,1)S(1)} collective-permute-done((bf16[4,64,256]{2,1,0:T(8,128)(2,1)S(1)}, bf16[4,64,256]{2,1,0:T(8,128)(2,1)S(1)}, u32[]{:S(2)}, u32[]{:S(2)}) %collective-permute-start.23) | collective-permute-done | bytes 131104 | tf_op jit(solution)/shard_map/ppermute | solution.py:292
  58.6 2.6 %counts.2 = (f32[3,256,1024]{2,1,0:T(8,128)S(1)}, f32[3,256,256]{2,1,0:T(8,128)S(1)}, f32[2,1,256,256]{3,2,1,0:T(8,128)S(1)}) custom-call(s32[3]{0:T(128)S(1)} %copy-done, bf16[3,1024,1024]{2,1,0:T(8,128)(2,1)S(1)} %get-tuple-element.42.refs_1_.refs_2_.refs_3_.refs_4_, bf16[3,2,256,256]{3,2,1,0:T(8,128)(2,1)S(1)} %ready.1.refs_14_.refs_2_, ...), custom_call_target="tpu_custom_call" | custom-call | flops 1000000000 | bytes 2097152 | tf_op jit(solution)/shard_map/counts/pallas_call | solution.py:22
  61.2 2.6 %collective-permute-done.20.refs_14_ = bf16[4,64,256]{2,1,0:T(8,128)(2,1)S(1)} collective-permute-done((bf16[4,64,256]{2,1,0:T(8,128)(2,1)S(1)}, bf16[4,64,256]{2,1,0:T(8,128)(2,1)S(1)}, u32[]{:S(2)}, u32[]{:S(2)}) %collective-permute-start.20) | collective-permute-done | bytes 131104 | tf_op jit(solution)/shard_map/ppermute | solution.py:292
  63.7 2.3 %counts.3 = (bf16[3,256,1024]{2,1,0:T(8,128)(2,1)}, bf16[3,256,256]{2,1,0:T(8,128)(2,1)}) custom-call(s32[3]{0:T(128)S(1)} %copy-done, bf16[3,1024,1024]{2,1,0:T(8,128)(2,1)S(1)} %get-tuple-element.42.refs_1_.refs_2_.refs_3_.refs_4_, bf16[3,2,256,256]{3,2,1,0:T(8,128)(2,1)S(1)} %ready.1.refs_14_.refs_2_, ...), custom_call_target="tpu_custom_call" | custom-call | flops 1000000000 | bytes 2097152 | tf_op jit(solution)/shard_map/counts/pallas_call | solution.py:22
  (25 shorter events, 0.3 us)
Async XLA Ops:
  6.0 4.8 %collective-permute-start.3 = (bf16[64,1024]{1,0:T(8,128)(2,1)S(1)}, bf16[64,1024]{1,0:T(8,128)(2,1)S(1)}, u32[]{:S(2)}, u32[]{:S(2)}) collective-permute-start(bf16[64,1024]{1,0:T(8,128)(2,1)S(1)} %first.2.refs_1_), channel_id=1, source_target_pairs={{4,0},{12,8},{20,16},{28,24},{5,1},{13,9},{21,17},{29,25},{6,2},{1... | collective-permute-start | bytes 393224 | tf_op jit(solution)/shard_map/ppermute | solution.py:364
  7.3 13.2 %collective-permute-start.1 = (bf16[272,1024]{1,0:T(8,128)(2,1)S(1)}, bf16[272,1024]{1,0:T(8,128)(2,1)S(1)}, u32[]{:S(2)}, u32[]{:S(2)}) collective-permute-start(bf16[272,1024]{1,0:T(8,128)(2,1)S(1)} %hold.2.refs_2_.refs_0_.refs_7_.refs_3_), channel_id=1, source_target_pairs={{0,2},{1,3},{2,0},{3,1},{4,6},{5,7},{6,4},{7,5},{8,10},{9,11},{10,... | collective-permute-start | bytes 1671176 | tf_op jit(solution)/shard_map/ppermute | solution.py:292
  9.4 3.2 %collective-permute-start.2 = (bf16[64,1024]{1,0:T(8,128)(2,1)S(1)}, bf16[64,1024]{1,0:T(8,128)(2,1)S(1)}, u32[]{:S(2)}, u32[]{:S(2)}) collective-permute-start(bf16[64,1024]{1,0:T(8,128)(2,1)S(1)} %first.3), channel_id=1, source_target_pairs={{4,0},{12,8},{20,16},{28,24},{5,1},{13,9},{21,17},{29,25},{6,2},{1... | collective-permute-start | bytes 393224 | tf_op jit(solution)/shard_map/ppermute | solution.py:364
  10.8 2.6 %collective-permute-start.5 = (bf16[64,1024]{1,0:T(8,128)(2,1)S(1)}, bf16[64,1024]{1,0:T(8,128)(2,1)S(1)}, u32[]{:S(2)}, u32[]{:S(2)}) collective-permute-start(bf16[64,1024]{1,0:T(8,128)(2,1)S(1)} %get-tuple-element.46.refs_3_), channel_id=1, source_target_pairs={{8,0},{24,16},{9,1},{25,17},{10,2},{26,18},{11,3},{27,19}} | collective-permute-start | bytes 393224 | tf_op jit(solution)/shard_map/ppermute | solution.py:364
  12.7 3.3 %collective-permute-start.4 = (bf16[64,1024]{1,0:T(8,128)(2,1)S(1)}, bf16[64,1024]{1,0:T(8,128)(2,1)S(1)}, u32[]{:S(2)}, u32[]{:S(2)}) collective-permute-start(bf16[64,1024]{1,0:T(8,128)(2,1)S(1)} %get-tuple-element.48), channel_id=1, source_target_pairs={{8,0},{24,16},{9,1},{25,17},{10,2},{26,18},{11,3},{27,19}} | collective-permute-start | bytes 393224 | tf_op jit(solution)/shard_map/ppermute | solution.py:364
  13.4 3.2 %collective-permute-start.8 = (bf16[64,1024]{1,0:T(8,128)(2,1)S(1)}, bf16[64,1024]{1,0:T(8,128)(2,1)S(1)}, u32[]{:S(2)}, u32[]{:S(2)}) collective-permute-start(bf16[64,1024]{1,0:T(8,128)(2,1)S(1)} %get-tuple-element.50.refs_3_), channel_id=1, source_target_pairs={{16,0},{17,1},{18,2},{19,3}} | collective-permute-start | bytes 393224 | tf_op jit(solution)/shard_map/ppermute | solution.py:377
  14.1 15.0 %collective-permute-start = (bf16[272,1024]{1,0:T(8,128)(2,1)S(1)}, bf16[272,1024]{1,0:T(8,128)(2,1)S(1)}, u32[]{:S(2)}, u32[]{:S(2)}) collective-permute-start(bf16[272,1024]{1,0:T(8,128)(2,1)S(1)} %hold.2.refs_2_.refs_0_.refs_7_.refs_3_), channel_id=1, source_target_pairs={{0,1},{1,0},{2,3},{3,2},{4,5},{5,4},{6,7},{7,6},{8,9},{9,8},{10,11... | collective-permute-start | bytes 1671176 | tf_op jit(solution)/shard_map/ppermute | solution.py:292
  15.9 6.6 %collective-permute-start.7 = (bf16[64,1024]{1,0:T(8,128)(2,1)S(1)}, bf16[64,1024]{1,0:T(8,128)(2,1)S(1)}, u32[]{:S(2)}, u32[]{:S(2)}) collective-permute-start(bf16[64,1024]{1,0:T(8,128)(2,1)S(1)} %get-tuple-element.51.refs_1_), channel_id=1, source_target_pairs={{16,0},{17,1},{18,2},{19,3}} | collective-permute-start | bytes 393224 | tf_op jit(solution)/shard_map/ppermute | solution.py:377
  16.7 8.7 %collective-permute-start.13 = (bf16[64,1024]{1,0:T(8,128)(2,1)S(1)}, bf16[64,1024]{1,0:T(8,128)(2,1)S(1)}, u32[]{:S(2)}, u32[]{:S(2)}) collective-permute-start(bf16[64,1024]{1,0:T(8,128)(2,1)S(1)} %get-tuple-element.60.refs_5_), channel_id=1, source_target_pairs={{0,16},{1,17},{2,18},{3,19}} | collective-permute-start | bytes 393224 | tf_op jit(solution)/shard_map/ppermute | solution.py:400
  20.6 11.5 %collective-permute-start.6 = (bf16[272,1024]{1,0:T(8,128)(2,1)S(1)}, bf16[272,1024]{1,0:T(8,128)(2,1)S(1)}, u32[]{:S(2)}, u32[]{:S(2)}) collective-permute-start(bf16[272,1024]{1,0:T(8,128)(2,1)S(1)} %hold.3), channel_id=1, source_target_pairs={{0,1},{1,0},{2,3},{3,2},{4,5},{5,4},{6,7},{7,6},{8,9},{9,8},{10,11... | collective-permute-start | bytes 1671176 | tf_op jit(solution)/shard_map/ppermute | solution.py:292
  22.7 4.2 %collective-permute-start.12 = (bf16[64,1024]{1,0:T(8,128)(2,1)S(1)}, bf16[64,1024]{1,0:T(8,128)(2,1)S(1)}, u32[]{:S(2)}, u32[]{:S(2)}) collective-permute-start(bf16[64,1024]{1,0:T(8,128)(2,1)S(1)} %get-tuple-element.57.refs_5_), channel_id=1, source_target_pairs={{0,16},{1,17},{2,18},{3,19}} | collective-permute-start | bytes 393224 | tf_op jit(solution)/shard_map/ppermute | solution.py:400
  23.4 8.0 %collective-permute-start.10 = (bf16[128,1024]{1,0:T(8,128)(2,1)S(1)}, bf16[128,1024]{1,0:T(8,128)(2,1)S(1)}, u32[]{:S(2)}, u32[]{:S(2)}) collective-permute-start(bf16[128,1024]{1,0:T(8,128)(2,1)S(1)} %get-tuple-element.56.refs_10_.refs_7_), channel_id=1, source_target_pairs={{0,2},{1,3},{2,0},{3,1},{4,6},{5,7},{6,4},{7,5},{8,10},{9,11},{10,... | collective-permute-start | bytes 786440 | tf_op jit(solution)/shard_map/ppermute | solution.py:292
  25.5 2.2 %collective-permute-start.15 = (bf16[64,1024]{1,0:T(8,128)(2,1)S(1)}, bf16[64,1024]{1,0:T(8,128)(2,1)S(1)}, u32[]{:S(2)}, u32[]{:S(2)}) collective-permute-start(bf16[64,1024]{1,0:T(8,128)(2,1)S(1)} %get-tuple-element.62.refs_6_.refs_5_), channel_id=1, source_target_pairs={{0,8},{16,24},{1,9},{17,25},{2,10},{18,26},{3,11},{19,27}} | collective-permute-start | bytes 393224 | tf_op jit(solution)/shard_map/ppermute | solution.py:400
  27.0 5.2 %collective-permute-start.14 = (bf16[64,1024]{1,0:T(8,128)(2,1)S(1)}, bf16[64,1024]{1,0:T(8,128)(2,1)S(1)}, u32[]{:S(2)}, u32[]{:S(2)}) collective-permute-start(bf16[64,1024]{1,0:T(8,128)(2,1)S(1)} %get-tuple-element.63.refs_5_), channel_id=1, source_target_pairs={{0,8},{16,24},{1,9},{17,25},{2,10},{18,26},{3,11},{19,27}} | collective-permute-start | bytes 393224 | tf_op jit(solution)/shard_map/ppermute | solution.py:400
  27.7 16.7 %collective-permute-start.17 = (bf16[64,1024]{1,0:T(8,128)(2,1)S(1)}, bf16[64,1024]{1,0:T(8,128)(2,1)S(1)}, u32[]{:S(2)}, u32[]{:S(2)}) collective-permute-start(bf16[64,1024]{1,0:T(8,128)(2,1)S(1)} %get-tuple-element.66.refs_6_), channel_id=1, source_target_pairs={{0,4},{8,12},{16,20},{24,28},{1,5},{9,13},{17,21},{25,29},{2,6},{1... | collective-permute-start | bytes 393224 | tf_op jit(solution)/shard_map/ppermute | solution.py:410
  29.0 22.5 %collective-permute-start.9 = (bf16[128,1024]{1,0:T(8,128)(2,1)S(1)}, bf16[128,1024]{1,0:T(8,128)(2,1)S(1)}, u32[]{:S(2)}, u32[]{:S(2)}) collective-permute-start(bf16[128,1024]{1,0:T(8,128)(2,1)S(1)} %get-tuple-element.56.refs_10_.refs_7_), channel_id=1, source_target_pairs={{0,1},{1,0},{2,3},{3,2},{4,5},{5,4},{6,7},{7,6},{8,9},{9,8},{10,11... | collective-permute-start | bytes 786440 | tf_op jit(solution)/shard_map/ppermute | solution.py:292
  31.4 20.8 %collective-permute-start.11 = (bf16[128,1024]{1,0:T(8,128)(2,1)S(1)}, bf16[128,1024]{1,0:T(8,128)(2,1)S(1)}, u32[]{:S(2)}, u32[]{:S(2)}) collective-permute-start(bf16[128,1024]{1,0:T(8,128)(2,1)S(1)} %collective-permute-done.10.refs_12_.refs_9_), channel_id=1, source_target_pairs={{0,1},{1,0},{2,3},{3,2},{4,5},{5,4},{6,7},{7,6},{8,9},{9,8},{10,11... | collective-permute-start | bytes 786440 | tf_op jit(solution)/shard_map/ppermute | solution.py:292
  32.2 12.3 %copy-start = (s32[3]{0:T(128)S(1)}, s32[3]{0:T(128)}, u32[]{:S(2)}) copy-start(s32[3]{0:T(128)} %refs_0_.9) | copy-start | bytes 40
  32.2 20.0 %collective-permute-start.16 = (bf16[64,1024]{1,0:T(8,128)(2,1)S(1)}, bf16[64,1024]{1,0:T(8,128)(2,1)S(1)}, u32[]{:S(2)}, u32[]{:S(2)}) collective-permute-start(bf16[64,1024]{1,0:T(8,128)(2,1)S(1)} %get-tuple-element.67.refs_6_), channel_id=1, source_target_pairs={{0,4},{8,12},{16,20},{24,28},{1,5},{9,13},{17,21},{25,29},{2,6},{1... | collective-permute-start | bytes 393224 | tf_op jit(solution)/shard_map/ppermute | solution.py:410
  46.5 9.3 %collective-permute-start.21 = (bf16[4,64,256]{2,1,0:T(8,128)(2,1)S(1)}, bf16[4,64,256]{2,1,0:T(8,128)(2,1)S(1)}, u32[]{:S(2)}, u32[]{:S(2)}) collective-permute-start(bf16[4,64,256]{2,1,0:T(8,128)(2,1)S(1)} %get-tuple-element.76), channel_id=1, source_target_pairs={{0,1},{1,0},{2,3},{3,2},{4,5},{5,4},{6,7},{7,6},{8,9},{9,8},{10,11... | collective-permute-start | bytes 393224 | tf_op jit(solution)/shard_map/ppermute | solution.py:292
  50.1 6.6 %collective-permute-start.22 = (bf16[4,64,256]{2,1,0:T(8,128)(2,1)S(1)}, bf16[4,64,256]{2,1,0:T(8,128)(2,1)S(1)}, u32[]{:S(2)}, u32[]{:S(2)}) collective-permute-start(bf16[4,64,256]{2,1,0:T(8,128)(2,1)S(1)} %get-tuple-element.77), channel_id=1, source_target_pairs={{0,2},{1,3},{2,0},{3,1},{4,6},{5,7},{6,4},{7,5},{8,10},{9,11},{10,... | collective-permute-start | bytes 393224 | tf_op jit(solution)/shard_map/ppermute | solution.py:292
  51.5 7.0 %collective-permute-start.23 = (bf16[4,64,256]{2,1,0:T(8,128)(2,1)S(1)}, bf16[4,64,256]{2,1,0:T(8,128)(2,1)S(1)}, u32[]{:S(2)}, u32[]{:S(2)}) collective-permute-start(bf16[4,64,256]{2,1,0:T(8,128)(2,1)S(1)} %get-tuple-element.78), channel_id=1, source_target_pairs={{0,3},{1,2},{2,1},{3,0},{4,7},{5,6},{6,5},{7,4},{8,11},{9,10},{10,... | collective-permute-start | bytes 393224 | tf_op jit(solution)/shard_map/ppermute | solution.py:292
  54.4 6.7 %collective-permute-start.18 = (bf16[4,64,256]{2,1,0:T(8,128)(2,1)S(1)}, bf16[4,64,256]{2,1,0:T(8,128)(2,1)S(1)}, u32[]{:S(2)}, u32[]{:S(2)}) collective-permute-start(bf16[4,64,256]{2,1,0:T(8,128)(2,1)S(1)} %get-tuple-element.73), channel_id=1, source_target_pairs={{0,1},{1,0},{2,3},{3,2},{4,5},{5,4},{6,7},{7,6},{8,9},{9,8},{10,11... | collective-permute-start | bytes 393224 | tf_op jit(solution)/shard_map/ppermute | solution.py:292
  54.7 6.5 %collective-permute-start.19 = (bf16[4,64,256]{2,1,0:T(8,128)(2,1)S(1)}, bf16[4,64,256]{2,1,0:T(8,128)(2,1)S(1)}, u32[]{:S(2)}, u32[]{:S(2)}) collective-permute-start(bf16[4,64,256]{2,1,0:T(8,128)(2,1)S(1)} %get-tuple-element.74), channel_id=1, source_target_pairs={{0,2},{1,3},{2,0},{3,1},{4,6},{5,7},{6,4},{7,5},{8,10},{9,11},{10,... | collective-permute-start | bytes 393224 | tf_op jit(solution)/shard_map/ppermute | solution.py:292
  55.8 8.0 %collective-permute-start.20 = (bf16[4,64,256]{2,1,0:T(8,128)(2,1)S(1)}, bf16[4,64,256]{2,1,0:T(8,128)(2,1)S(1)}, u32[]{:S(2)}, u32[]{:S(2)}) collective-permute-start(bf16[4,64,256]{2,1,0:T(8,128)(2,1)S(1)} %get-tuple-element.75), channel_id=1, source_target_pairs={{0,3},{1,2},{2,1},{3,0},{4,7},{5,6},{6,5},{7,4},{8,11},{9,10},{10,... | collective-permute-start | bytes 393224 | tf_op jit(solution)/shard_map/ppermute | solution.py:292

commit v9 on v8

--- a/solution.py
+++ b/solution.py
@@ -417,7 +417,7 @@
             [SM] + [VM] * 8,
             after=[own_posts[-1][0], *all_tops, hots] if c > 0 else [],
         )
-        order = sorted(range(1, groups), reverse=True)
+        order = sorted(range(1, groups), reverse=c == CHUNKS - 1)
         moved = {mask: swap(packs[mask], mask) for mask in order}
         own_posts.append([packs[0]] + [moved[mask] for mask in range(1, groups)])
     sums = ()

time: 66.6 us -> 66.6 us (level)
  no operation moved by 1% of the time
where the time goes in v9:
time: 66.6 us; the launch traced here: 66.2 us
  starting transfers between devices  25.7 us (39%)
  waiting for transfers between devices  21.8 us (33%)
  Pallas kernels  17.6 us (26%)
  between operations  1.11 us (2%)
    pallas_call x22, Pallas kernels, run(): pl.pallas_call(lambda *refs: body(*refs[:count], *refs[idle:]), name=name...  17.6 us
    ppermute x12, starting transfers between devices, swap(): lax.ppermute(value, 'rows', [(s, s ^ mask) for s in range(lax.axis_size('...  15.1 us
    ppermute x2, waiting for transfers between devices, per_device(): recv = lax.ppermute(post[c], 'leaf', down_pairs(0))  10.9 us
    ppermute x12, waiting for transfers between devices, swap(): lax.ppermute(value, 'rows', [(s, s ^ mask) for s in range(lax.axis_size('...  9.63 us
    ppermute x4, starting transfers between devices, per_device(): recv = lax.ppermute(send[c], 'leaf', up_pairs(level))  3.96 us
    ppermute x4, starting transfers between devices, per_device(): recv = lax.ppermute(post[c], 'leaf', down_pairs(level))  2.68 us
    ppermute x2, starting transfers between devices, per_device(): recv = lax.ppermute(post[c], 'leaf', down_pairs(0))  2.58 us
  transfers between devices with their start and end apart: 24, of which 6 were waited for; matrix products, arithmetic and copies ran while one was open for 0% of the time, Pallas kernels for 15%

profile of v9, /device:TPU:13, one launch (start us, length us, event | category | flops | bytes accessed | tf_op | source)
XLA Modules:
  0.0 66.2 jit_solution(17384478830387236834)
XLA Ops:
  0.6 4.5 %prep.1 = (bf16[3,1024,1024]{2,1,0:T(8,128)(2,1)S(1)}, bf16[272,1024]{1,0:T(8,128)(2,1)S(1)}, f32[2,128,1024]{2,1,0:T(8,128)S(1)}, f32[8,1024]{1,0:T(8,128)S(1)}...) custom-call(s32[3]{0:T(128)} %refs_0_.9, s32[3,128]{1,0:T(4,128)} %refs_1_.1, bf16[3,256,1024]{2,1,0:T(8,128)(2,1)} %refs_2_.1, ...), custom_call_target="tpu_custom_call" | custom-call | flops 1000000000 | bytes 2097152 | tf_op jit(solution)/shard_map/prep/pallas_call | solution.py:22
  5.2 0.8 %first.2.refs_1_ = bf16[64,1024]{1,0:T(8,128)(2,1)S(1)} custom-call(f32[64,1024]{1,0:T(8,128)S(1)} %get-tuple-element.44.refs_0_, bf16[3,1024,1024]{2,1,0:T(8,128)(2,1)S(1)} %get-tuple-element.42.refs_1_.refs_2_.refs_3_.refs_4_), custom_call_target="tpu_custom_call" | custom-call | flops 1000000000 | bytes 2097152 | tf_op jit(solution)/shard_map/first/pallas_call | solution.py:22
  6.0 1.3 %collective-permute-start.3 = (bf16[64,1024]{1,0:T(8,128)(2,1)S(1)}, bf16[64,1024]{1,0:T(8,128)(2,1)S(1)}, u32[]{:S(2)}, u32[]{:S(2)}) collective-permute-start(bf16[64,1024]{1,0:T(8,128)(2,1)S(1)} %first.2.refs_1_), channel_id=1, source_target_pairs={{4,0},{12,8},{20,16},{28,24},{5,1},{13,9},{21,17},{29,25},{6,2},{1... | collective-permute-start | bytes 393224 | tf_op jit(solution)/shard_map/ppermute | solution.py:364
  7.3 1.3 %collective-permute-start.1 = (bf16[272,1024]{1,0:T(8,128)(2,1)S(1)}, bf16[272,1024]{1,0:T(8,128)(2,1)S(1)}, u32[]{:S(2)}, u32[]{:S(2)}) collective-permute-start(bf16[272,1024]{1,0:T(8,128)(2,1)S(1)} %hold.2.refs_2_.refs_0_.refs_7_.refs_3_), channel_id=1, source_target_pairs={{0,2},{1,3},{2,0},{3,1},{4,6},{5,7},{6,4},{7,5},{8,10},{9,11},{10,... | collective-permute-start | bytes 1671176 | tf_op jit(solution)/shard_map/ppermute | solution.py:292
  8.6 0.8 %first.3 = bf16[64,1024]{1,0:T(8,128)(2,1)S(1)} custom-call(f32[64,1024]{1,0:T(8,128)S(1)} %get-tuple-element.45.refs_0_, bf16[3,1024,1024]{2,1,0:T(8,128)(2,1)S(1)} %get-tuple-element.42.refs_1_.refs_2_.refs_3_.refs_4_, bf16[272,1024]{1,0:T(8,128)(2,1)S(1)} %hold.2.refs_2_.refs_0_.refs_7_.refs_3_), custom_call_target="tpu_custom_call" | custom-call | flops 1000000000 | bytes 2097152 | tf_op jit(solution)/shard_map/first/pallas_call | solution.py:22
  9.4 1.3 %collective-permute-start.2 = (bf16[64,1024]{1,0:T(8,128)(2,1)S(1)}, bf16[64,1024]{1,0:T(8,128)(2,1)S(1)}, u32[]{:S(2)}, u32[]{:S(2)}) collective-permute-start(bf16[64,1024]{1,0:T(8,128)(2,1)S(1)} %first.3), channel_id=1, source_target_pairs={{4,0},{12,8},{20,16},{28,24},{5,1},{13,9},{21,17},{29,25},{6,2},{1... | collective-permute-start | bytes 393224 | tf_op jit(solution)/shard_map/ppermute | solution.py:364
  10.7 0.0 collective-permute-done.3.refs_1_
  10.8 0.7 %collective-permute-start.5 = (bf16[64,1024]{1,0:T(8,128)(2,1)S(1)}, bf16[64,1024]{1,0:T(8,128)(2,1)S(1)}, u32[]{:S(2)}, u32[]{:S(2)}) collective-permute-start(bf16[64,1024]{1,0:T(8,128)(2,1)S(1)} %get-tuple-element.46.refs_3_), channel_id=1, source_target_pairs={{8,0},{24,16},{9,1},{25,17},{10,2},{26,18},{11,3},{27,19}} | collective-permute-start | bytes 393224 | tf_op jit(solution)/shard_map/ppermute | solution.py:364
  11.5 1.2 %collective-permute-done.2.refs_1_ = bf16[64,1024]{1,0:T(8,128)(2,1)S(1)} collective-permute-done((bf16[64,1024]{1,0:T(8,128)(2,1)S(1)}, bf16[64,1024]{1,0:T(8,128)(2,1)S(1)}, u32[]{:S(2)}, u32[]{:S(2)}) %collective-permute-start.2) | collective-permute-done | bytes 131104 | tf_op jit(solution)/shard_map/ppermute | solution.py:364
  12.7 0.7 collective-permute-start.4
  13.3 0.0 collective-permute-done.5.refs_1_
  13.4 0.7 %collective-permute-start.8 = (bf16[64,1024]{1,0:T(8,128)(2,1)S(1)}, bf16[64,1024]{1,0:T(8,128)(2,1)S(1)}, u32[]{:S(2)}, u32[]{:S(2)}) collective-permute-start(bf16[64,1024]{1,0:T(8,128)(2,1)S(1)} %get-tuple-element.50.refs_3_), channel_id=1, source_target_pairs={{16,0},{17,1},{18,2},{19,3}} | collective-permute-start | bytes 393224 | tf_op jit(solution)/shard_map/ppermute | solution.py:377
  14.1 1.9 %collective-permute-start = (bf16[272,1024]{1,0:T(8,128)(2,1)S(1)}, bf16[272,1024]{1,0:T(8,128)(2,1)S(1)}, u32[]{:S(2)}, u32[]{:S(2)}) collective-permute-start(bf16[272,1024]{1,0:T(8,128)(2,1)S(1)} %hold.2.refs_2_.refs_0_.refs_7_.refs_3_), channel_id=1, source_target_pairs={{0,1},{1,0},{2,3},{3,2},{4,5},{5,4},{6,7},{7,6},{8,9},{9,8},{10,11... | collective-permute-start | bytes 1671176 | tf_op jit(solution)/shard_map/ppermute | solution.py:292
  15.9 0.7 collective-permute-start.7
  16.6 0.1 root.2
  16.7 0.7 %collective-permute-start.13 = (bf16[64,1024]{1,0:T(8,128)(2,1)S(1)}, bf16[64,1024]{1,0:T(8,128)(2,1)S(1)}, u32[]{:S(2)}, u32[]{:S(2)}) collective-permute-start(bf16[64,1024]{1,0:T(8,128)(2,1)S(1)} %get-tuple-element.60.refs_5_), channel_id=1, source_target_pairs={{0,16},{1,17},{2,18},{3,19}} | collective-permute-start | bytes 393224 | tf_op jit(solution)/shard_map/ppermute | solution.py:400
  17.4 3.2 %collective-permute-done.1.refs_2_.refs_9_.refs_5_ = bf16[272,1024]{1,0:T(8,128)(2,1)S(1)} collective-permute-done((bf16[272,1024]{1,0:T(8,128)(2,1)S(1)}, bf16[272,1024]{1,0:T(8,128)(2,1)S(1)}, u32[]{:S(2)}, u32[]{:S(2)}) %collective-permute-start.1) | collective-permute-done | bytes 557088 | tf_op jit(solution)/shard_map/ppermute | solution.py:292
  20.6 1.9 %collective-permute-start.6 = (bf16[272,1024]{1,0:T(8,128)(2,1)S(1)}, bf16[272,1024]{1,0:T(8,128)(2,1)S(1)}, u32[]{:S(2)}, u32[]{:S(2)}) collective-permute-start(bf16[272,1024]{1,0:T(8,128)(2,1)S(1)} %hold.3), channel_id=1, source_target_pairs={{0,1},{1,0},{2,3},{3,2},{4,5},{5,4},{6,7},{7,6},{8,9},{9,8},{10,11... | collective-permute-start | bytes 1671176 | tf_op jit(solution)/shard_map/ppermute | solution.py:292
  22.6 0.0 collective-permute-done.7.refs_1_
  22.6 0.1 root.3
  22.7 0.7 %collective-permute-start.12 = (bf16[64,1024]{1,0:T(8,128)(2,1)S(1)}, bf16[64,1024]{1,0:T(8,128)(2,1)S(1)}, u32[]{:S(2)}, u32[]{:S(2)}) collective-permute-start(bf16[64,1024]{1,0:T(8,128)(2,1)S(1)} %get-tuple-element.57.refs_5_), channel_id=1, source_target_pairs={{0,16},{1,17},{2,18},{3,19}} | collective-permute-start | bytes 393224 | tf_op jit(solution)/shard_map/ppermute | solution.py:400
  23.4 1.3 %collective-permute-start.10 = (bf16[128,1024]{1,0:T(8,128)(2,1)S(1)}, bf16[128,1024]{1,0:T(8,128)(2,1)S(1)}, u32[]{:S(2)}, u32[]{:S(2)}) collective-permute-start(bf16[128,1024]{1,0:T(8,128)(2,1)S(1)} %get-tuple-element.56.refs_10_.refs_7_), channel_id=1, source_target_pairs={{0,2},{1,3},{2,0},{3,1},{4,6},{5,7},{6,4},{7,5},{8,10},{9,11},{10,... | collective-permute-start | bytes 786440 | tf_op jit(solution)/shard_map/ppermute | solution.py:292
  24.7 0.8 %top.3.refs_2_.refs_3_ = f32[64,1024]{1,0:T(8,128)S(1)} custom-call(bf16[64,1024]{1,0:T(8,128)(2,1)S(1)} %get-tuple-element.55.refs_3_.refs_0_.refs_1_.refs_2_, bf16[3,1024,1024]{2,1,0:T(8,128)(2,1)S(1)} %get-tuple-element.42.refs_1_.refs_2_.refs_3_.refs_4_), custom_call_target="tpu_custom_call" | custom-call | flops 1000000000 | bytes 2097152 | tf_op jit(solution)/shard_map/top/pallas_call | solution.py:22
  25.4 0.0 collective-permute-done.13.refs_0_
  25.5 0.7 %collective-permute-start.15 = (bf16[64,1024]{1,0:T(8,128)(2,1)S(1)}, bf16[64,1024]{1,0:T(8,128)(2,1)S(1)}, u32[]{:S(2)}, u32[]{:S(2)}) collective-permute-start(bf16[64,1024]{1,0:T(8,128)(2,1)S(1)} %get-tuple-element.62.refs_6_.refs_5_), channel_id=1, source_target_pairs={{0,8},{16,24},{1,9},{17,25},{2,10},{18,26},{3,11},{19,27}} | collective-permute-start | bytes 393224 | tf_op jit(solution)/shard_map/ppermute | solution.py:400
  26.2 0.8 %top.2.refs_2_.refs_3_ = f32[64,1024]{1,0:T(8,128)S(1)} custom-call(bf16[64,1024]{1,0:T(8,128)(2,1)S(1)} %get-tuple-element.58.refs_0_.refs_1_.refs_2_, bf16[3,1024,1024]{2,1,0:T(8,128)(2,1)S(1)} %get-tuple-element.42.refs_1_.refs_2_.refs_3_.refs_4_), custom_call_target="tpu_custom_call" | custom-call | flops 1000000000 | bytes 2097152 | tf_op jit(solution)/shard_map/top/pallas_call | solution.py:22
  27.0 0.7 %collective-permute-start.14 = (bf16[64,1024]{1,0:T(8,128)(2,1)S(1)}, bf16[64,1024]{1,0:T(8,128)(2,1)S(1)}, u32[]{:S(2)}, u32[]{:S(2)}) collective-permute-start(bf16[64,1024]{1,0:T(8,128)(2,1)S(1)} %get-tuple-element.63.refs_5_), channel_id=1, source_target_pairs={{0,8},{16,24},{1,9},{17,25},{2,10},{18,26},{3,11},{19,27}} | collective-permute-start | bytes 393224 | tf_op jit(solution)/shard_map/ppermute | solution.py:400
  27.6 0.0 collective-permute-done.15.refs_0_
  27.7 1.3 %collective-permute-start.17 = (bf16[64,1024]{1,0:T(8,128)(2,1)S(1)}, bf16[64,1024]{1,0:T(8,128)(2,1)S(1)}, u32[]{:S(2)}, u32[]{:S(2)}) collective-permute-start(bf16[64,1024]{1,0:T(8,128)(2,1)S(1)} %get-tuple-element.66.refs_6_), channel_id=1, source_target_pairs={{0,4},{8,12},{16,20},{24,28},{1,5},{9,13},{17,21},{25,29},{2,6},{1... | collective-permute-start | bytes 393224 | tf_op jit(solution)/shard_map/ppermute | solution.py:410
  29.0 0.0 collective-permute-done.refs_1_.refs_8_.refs_4_
  29.0 0.4 collective-permute-start.9
  29.4 2.0 %collective-permute-done.10.refs_12_.refs_9_ = bf16[128,1024]{1,0:T(8,128)(2,1)S(1)} collective-permute-done((bf16[128,1024]{1,0:T(8,128)(2,1)S(1)}, bf16[128,1024]{1,0:T(8,128)(2,1)S(1)}, u32[]{:S(2)}, u32[]{:S(2)}) %collective-permute-start.10) | collective-permute-done | bytes 262176 | tf_op jit(solution)/shard_map/ppermute | solution.py:292
  31.4 0.8 %collective-permute-start.11 = (bf16[128,1024]{1,0:T(8,128)(2,1)S(1)}, bf16[128,1024]{1,0:T(8,128)(2,1)S(1)}, u32[]{:S(2)}, u32[]{:S(2)}) collective-permute-start(bf16[128,1024]{1,0:T(8,128)(2,1)S(1)} %collective-permute-done.10.refs_12_.refs_9_), channel_id=1, source_target_pairs={{0,1},{1,0},{2,3},{3,2},{4,5},{5,4},{6,7},{7,6},{8,9},{9,8},{10,11... | collective-permute-start | bytes 786440 | tf_op jit(solution)/shard_map/ppermute | solution.py:292
  32.2 1.3 %collective-permute-start.16 = (bf16[64,1024]{1,0:T(8,128)(2,1)S(1)}, bf16[64,1024]{1,0:T(8,128)(2,1)S(1)}, u32[]{:S(2)}, u32[]{:S(2)}) collective-permute-start(bf16[64,1024]{1,0:T(8,128)(2,1)S(1)} %get-tuple-element.67.refs_6_), channel_id=1, source_target_pairs={{0,4},{8,12},{16,20},{24,28},{1,5},{9,13},{17,21},{25,29},{2,6},{1... | collective-permute-start | bytes 393224 | tf_op jit(solution)/shard_map/ppermute | solution.py:410
  33.5 10.9 %collective-permute-done.17.refs_1_ = bf16[64,1024]{1,0:T(8,128)(2,1)S(1)} collective-permute-done((bf16[64,1024]{1,0:T(8,128)(2,1)S(1)}, bf16[64,1024]{1,0:T(8,128)(2,1)S(1)}, u32[]{:S(2)}, u32[]{:S(2)}) %collective-permute-start.17) | collective-permute-done | bytes 131104 | tf_op jit(solution)/shard_map/ppermute | solution.py:410
  44.4 2.1 %last.2 = (bf16[4,64,256]{2,1,0:T(8,128)(2,1)S(1)}, bf16[4,64,256]{2,1,0:T(8,128)(2,1)S(1)}, bf16[4,64,256]{2,1,0:T(8,128)(2,1)S(1)}, bf16[4,64,256]{2,1,0:T(8,128)(2,1)S(1)}) custom-call(s32[3]{0:T(128)S(1)} %copy-done, bf16[64,1024]{1,0:T(8,128)(2,1)S(1)} %collective-permute-done.17.refs_1_, ...), custom_call_target="tpu_custom_call" | custom-call | flops 1000000000 | bytes 2097152 | tf_op jit(solution)/shard_map/last/pallas_call | solution.py:22
  46.5 3.6 %collective-permute-start.21 = (bf16[4,64,256]{2,1,0:T(8,128)(2,1)S(1)}, bf16[4,64,256]{2,1,0:T(8,128)(2,1)S(1)}, u32[]{:S(2)}, u32[]{:S(2)}) collective-permute-start(bf16[4,64,256]{2,1,0:T(8,128)(2,1)S(1)} %get-tuple-element.76), channel_id=1, source_target_pairs={{0,1},{1,0},{2,3},{3,2},{4,5},{5,4},{6,7},{7,6},{8,9},{9,8},{10,11... | collective-permute-start | bytes 393224 | tf_op jit(solution)/shard_map/ppermute | solution.py:292
  50.1 1.1 %collective-permute-start.22 = (bf16[4,64,256]{2,1,0:T(8,128)(2,1)S(1)}, bf16[4,64,256]{2,1,0:T(8,128)(2,1)S(1)}, u32[]{:S(2)}, u32[]{:S(2)}) collective-permute-start(bf16[4,64,256]{2,1,0:T(8,128)(2,1)S(1)} %get-tuple-element.77), channel_id=1, source_target_pairs={{0,2},{1,3},{2,0},{3,1},{4,6},{5,7},{6,4},{7,5},{8,10},{9,11},{10,... | collective-permute-start | bytes 393224 | tf_op jit(solution)/shard_map/ppermute | solution.py:292
  51.2 0.3 ready.1.refs_14_.refs_2_
  51.5 0.7 collective-permute-start.23
  52.2 2.2 %last.3 = (bf16[4,64,256]{2,1,0:T(8,128)(2,1)S(1)}, bf16[4,64,256]{2,1,0:T(8,128)(2,1)S(1)}, bf16[4,64,256]{2,1,0:T(8,128)(2,1)S(1)}, bf16[4,64,256]{2,1,0:T(8,128)(2,1)S(1)}) custom-call(s32[3]{0:T(128)S(1)} %copy-done, bf16[64,1024]{1,0:T(8,128)(2,1)S(1)} %collective-permute-done.16.refs_1_, ...), custom_call_target="tpu_custom_call" | custom-call | flops 1000000000 | bytes 2097152 | tf_op jit(solution)/shard_map/last/pallas_call | solution.py:22
  54.4 0.2 collective-permute-start.18
  54.7 1.1 %collective-permute-start.19 = (bf16[4,64,256]{2,1,0:T(8,128)(2,1)S(1)}, bf16[4,64,256]{2,1,0:T(8,128)(2,1)S(1)}, u32[]{:S(2)}, u32[]{:S(2)}) collective-permute-start(bf16[4,64,256]{2,1,0:T(8,128)(2,1)S(1)} %get-tuple-element.74), channel_id=1, source_target_pairs={{0,2},{1,3},{2,0},{3,1},{4,6},{5,7},{6,4},{7,5},{8,10},{9,11},{10,... | collective-permute-start | bytes 393224 | tf_op jit(solution)/shard_map/ppermute | solution.py:292
  55.8 0.9 %collective-permute-start.20 = (bf16[4,64,256]{2,1,0:T(8,128)(2,1)S(1)}, bf16[4,64,256]{2,1,0:T(8,128)(2,1)S(1)}, u32[]{:S(2)}, u32[]{:S(2)}) collective-permute-start(bf16[4,64,256]{2,1,0:T(8,128)(2,1)S(1)} %get-tuple-element.75), channel_id=1, source_target_pairs={{0,3},{1,2},{2,1},{3,0},{4,7},{5,6},{6,5},{7,4},{8,11},{9,10},{10,... | collective-permute-start | bytes 393224 | tf_op jit(solution)/shard_map/ppermute | solution.py:292
  56.7 1.9 %collective-permute-done.23.refs_14_ = bf16[4,64,256]{2,1,0:T(8,128)(2,1)S(1)} collective-permute-done((bf16[4,64,256]{2,1,0:T(8,128)(2,1)S(1)}, bf16[4,64,256]{2,1,0:T(8,128)(2,1)S(1)}, u32[]{:S(2)}, u32[]{:S(2)}) %collective-permute-start.23) | collective-permute-done | bytes 131104 | tf_op jit(solution)/shard_map/ppermute | solution.py:292
  58.6 2.6 %counts.2 = (f32[3,256,1024]{2,1,0:T(8,128)S(1)}, f32[3,256,256]{2,1,0:T(8,128)S(1)}, f32[2,1,256,256]{3,2,1,0:T(8,128)S(1)}) custom-call(s32[3]{0:T(128)S(1)} %copy-done, bf16[3,1024,1024]{2,1,0:T(8,128)(2,1)S(1)} %get-tuple-element.42.refs_1_.refs_2_.refs_3_.refs_4_, bf16[3,2,256,256]{3,2,1,0:T(8,128)(2,1)S(1)} %ready.1.refs_14_.refs_2_, ...), custom_call_target="tpu_custom_call" | custom-call | flops 1000000000 | bytes 2097152 | tf_op jit(solution)/shard_map/counts/pallas_call | solution.py:22
  61.2 2.6 %collective-permute-done.20.refs_14_ = bf16[4,64,256]{2,1,0:T(8,128)(2,1)S(1)} collective-permute-done((bf16[4,64,256]{2,1,0:T(8,128)(2,1)S(1)}, bf16[4,64,256]{2,1,0:T(8,128)(2,1)S(1)}, u32[]{:S(2)}, u32[]{:S(2)}) %collective-permute-start.20) | collective-permute-done | bytes 131104 | tf_op jit(solution)/shard_map/ppermute | solution.py:292
  63.7 2.3 %counts.3 = (bf16[3,256,1024]{2,1,0:T(8,128)(2,1)}, bf16[3,256,256]{2,1,0:T(8,128)(2,1)}) custom-call(s32[3]{0:T(128)S(1)} %copy-done, bf16[3,1024,1024]{2,1,0:T(8,128)(2,1)S(1)} %get-tuple-element.42.refs_1_.refs_2_.refs_3_.refs_4_, bf16[3,2,256,256]{3,2,1,0:T(8,128)(2,1)S(1)} %ready.1.refs_14_.refs_2_, ...), custom_call_target="tpu_custom_call" | custom-call | flops 1000000000 | bytes 2097152 | tf_op jit(solution)/shard_map/counts/pallas_call | solution.py:22
  (25 shorter events, 0.3 us)
Async XLA Ops:
  6.0 4.8 %collective-permute-start.3 = (bf16[64,1024]{1,0:T(8,128)(2,1)S(1)}, bf16[64,1024]{1,0:T(8,128)(2,1)S(1)}, u32[]{:S(2)}, u32[]{:S(2)}) collective-permute-start(bf16[64,1024]{1,0:T(8,128)(2,1)S(1)} %first.2.refs_1_), channel_id=1, source_target_pairs={{4,0},{12,8},{20,16},{28,24},{5,1},{13,9},{21,17},{29,25},{6,2},{1... | collective-permute-start | bytes 393224 | tf_op jit(solution)/shard_map/ppermute | solution.py:364
  7.3 13.2 %collective-permute-start.1 = (bf16[272,1024]{1,0:T(8,128)(2,1)S(1)}, bf16[272,1024]{1,0:T(8,128)(2,1)S(1)}, u32[]{:S(2)}, u32[]{:S(2)}) collective-permute-start(bf16[272,1024]{1,0:T(8,128)(2,1)S(1)} %hold.2.refs_2_.refs_0_.refs_7_.refs_3_), channel_id=1, source_target_pairs={{0,2},{1,3},{2,0},{3,1},{4,6},{5,7},{6,4},{7,5},{8,10},{9,11},{10,... | collective-permute-start | bytes 1671176 | tf_op jit(solution)/shard_map/ppermute | solution.py:292
  9.4 3.2 %collective-permute-start.2 = (bf16[64,1024]{1,0:T(8,128)(2,1)S(1)}, bf16[64,1024]{1,0:T(8,128)(2,1)S(1)}, u32[]{:S(2)}, u32[]{:S(2)}) collective-permute-start(bf16[64,1024]{1,0:T(8,128)(2,1)S(1)} %first.3), channel_id=1, source_target_pairs={{4,0},{12,8},{20,16},{28,24},{5,1},{13,9},{21,17},{29,25},{6,2},{1... | collective-permute-start | bytes 393224 | tf_op jit(solution)/shard_map/ppermute | solution.py:364
  10.8 2.6 %collective-permute-start.5 = (bf16[64,1024]{1,0:T(8,128)(2,1)S(1)}, bf16[64,1024]{1,0:T(8,128)(2,1)S(1)}, u32[]{:S(2)}, u32[]{:S(2)}) collective-permute-start(bf16[64,1024]{1,0:T(8,128)(2,1)S(1)} %get-tuple-element.46.refs_3_), channel_id=1, source_target_pairs={{8,0},{24,16},{9,1},{25,17},{10,2},{26,18},{11,3},{27,19}} | collective-permute-start | bytes 393224 | tf_op jit(solution)/shard_map/ppermute | solution.py:364
  12.7 3.3 %collective-permute-start.4 = (bf16[64,1024]{1,0:T(8,128)(2,1)S(1)}, bf16[64,1024]{1,0:T(8,128)(2,1)S(1)}, u32[]{:S(2)}, u32[]{:S(2)}) collective-permute-start(bf16[64,1024]{1,0:T(8,128)(2,1)S(1)} %get-tuple-element.48), channel_id=1, source_target_pairs={{8,0},{24,16},{9,1},{25,17},{10,2},{26,18},{11,3},{27,19}} | collective-permute-start | bytes 393224 | tf_op jit(solution)/shard_map/ppermute | solution.py:364
  13.4 3.2 %collective-permute-start.8 = (bf16[64,1024]{1,0:T(8,128)(2,1)S(1)}, bf16[64,1024]{1,0:T(8,128)(2,1)S(1)}, u32[]{:S(2)}, u32[]{:S(2)}) collective-permute-start(bf16[64,1024]{1,0:T(8,128)(2,1)S(1)} %get-tuple-element.50.refs_3_), channel_id=1, source_target_pairs={{16,0},{17,1},{18,2},{19,3}} | collective-permute-start | bytes 393224 | tf_op jit(solution)/shard_map/ppermute | solution.py:377
  14.1 15.0 %collective-permute-start = (bf16[272,1024]{1,0:T(8,128)(2,1)S(1)}, bf16[272,1024]{1,0:T(8,128)(2,1)S(1)}, u32[]{:S(2)}, u32[]{:S(2)}) collective-permute-start(bf16[272,1024]{1,0:T(8,128)(2,1)S(1)} %hold.2.refs_2_.refs_0_.refs_7_.refs_3_), channel_id=1, source_target_pairs={{0,1},{1,0},{2,3},{3,2},{4,5},{5,4},{6,7},{7,6},{8,9},{9,8},{10,11... | collective-permute-start | bytes 1671176 | tf_op jit(solution)/shard_map/ppermute | solution.py:292
  15.9 6.6 %collective-permute-start.7 = (bf16[64,1024]{1,0:T(8,128)(2,1)S(1)}, bf16[64,1024]{1,0:T(8,128)(2,1)S(1)}, u32[]{:S(2)}, u32[]{:S(2)}) collective-permute-start(bf16[64,1024]{1,0:T(8,128)(2,1)S(1)} %get-tuple-element.51.refs_1_), channel_id=1, source_target_pairs={{16,0},{17,1},{18,2},{19,3}} | collective-permute-start | bytes 393224 | tf_op jit(solution)/shard_map/ppermute | solution.py:377
  16.7 8.7 %collective-permute-start.13 = (bf16[64,1024]{1,0:T(8,128)(2,1)S(1)}, bf16[64,1024]{1,0:T(8,128)(2,1)S(1)}, u32[]{:S(2)}, u32[]{:S(2)}) collective-permute-start(bf16[64,1024]{1,0:T(8,128)(2,1)S(1)} %get-tuple-element.60.refs_5_), channel_id=1, source_target_pairs={{0,16},{1,17},{2,18},{3,19}} | collective-permute-start | bytes 393224 | tf_op jit(solution)/shard_map/ppermute | solution.py:400
  20.6 11.5 %collective-permute-start.6 = (bf16[272,1024]{1,0:T(8,128)(2,1)S(1)}, bf16[272,1024]{1,0:T(8,128)(2,1)S(1)}, u32[]{:S(2)}, u32[]{:S(2)}) collective-permute-start(bf16[272,1024]{1,0:T(8,128)(2,1)S(1)} %hold.3), channel_id=1, source_target_pairs={{0,1},{1,0},{2,3},{3,2},{4,5},{5,4},{6,7},{7,6},{8,9},{9,8},{10,11... | collective-permute-start | bytes 1671176 | tf_op jit(solution)/shard_map/ppermute | solution.py:292
  22.7 4.2 %collective-permute-start.12 = (bf16[64,1024]{1,0:T(8,128)(2,1)S(1)}, bf16[64,1024]{1,0:T(8,128)(2,1)S(1)}, u32[]{:S(2)}, u32[]{:S(2)}) collective-permute-start(bf16[64,1024]{1,0:T(8,128)(2,1)S(1)} %get-tuple-element.57.refs_5_), channel_id=1, source_target_pairs={{0,16},{1,17},{2,18},{3,19}} | collective-permute-start | bytes 393224 | tf_op jit(solution)/shard_map/ppermute | solution.py:400
  23.4 8.0 %collective-permute-start.10 = (bf16[128,1024]{1,0:T(8,128)(2,1)S(1)}, bf16[128,1024]{1,0:T(8,128)(2,1)S(1)}, u32[]{:S(2)}, u32[]{:S(2)}) collective-permute-start(bf16[128,1024]{1,0:T(8,128)(2,1)S(1)} %get-tuple-element.56.refs_10_.refs_7_), channel_id=1, source_target_pairs={{0,2},{1,3},{2,0},{3,1},{4,6},{5,7},{6,4},{7,5},{8,10},{9,11},{10,... | collective-permute-start | bytes 786440 | tf_op jit(solution)/shard_map/ppermute | solution.py:292
  25.5 2.2 %collective-permute-start.15 = (bf16[64,1024]{1,0:T(8,128)(2,1)S(1)}, bf16[64,1024]{1,0:T(8,128)(2,1)S(1)}, u32[]{:S(2)}, u32[]{:S(2)}) collective-permute-start(bf16[64,1024]{1,0:T(8,128)(2,1)S(1)} %get-tuple-element.62.refs_6_.refs_5_), channel_id=1, source_target_pairs={{0,8},{16,24},{1,9},{17,25},{2,10},{18,26},{3,11},{19,27}} | collective-permute-start | bytes 393224 | tf_op jit(solution)/shard_map/ppermute | solution.py:400
  27.0 5.2 %collective-permute-start.14 = (bf16[64,1024]{1,0:T(8,128)(2,1)S(1)}, bf16[64,1024]{1,0:T(8,128)(2,1)S(1)}, u32[]{:S(2)}, u32[]{:S(2)}) collective-permute-start(bf16[64,1024]{1,0:T(8,128)(2,1)S(1)} %get-tuple-element.63.refs_5_), channel_id=1, source_target_pairs={{0,8},{16,24},{1,9},{17,25},{2,10},{18,26},{3,11},{19,27}} | collective-permute-start | bytes 393224 | tf_op jit(solution)/shard_map/ppermute | solution.py:400
  27.7 16.7 %collective-permute-start.17 = (bf16[64,1024]{1,0:T(8,128)(2,1)S(1)}, bf16[64,1024]{1,0:T(8,128)(2,1)S(1)}, u32[]{:S(2)}, u32[]{:S(2)}) collective-permute-start(bf16[64,1024]{1,0:T(8,128)(2,1)S(1)} %get-tuple-element.66.refs_6_), channel_id=1, source_target_pairs={{0,4},{8,12},{16,20},{24,28},{1,5},{9,13},{17,21},{25,29},{2,6},{1... | collective-permute-start | bytes 393224 | tf_op jit(solution)/shard_map/ppermute | solution.py:410
  29.0 22.5 %collective-permute-start.9 = (bf16[128,1024]{1,0:T(8,128)(2,1)S(1)}, bf16[128,1024]{1,0:T(8,128)(2,1)S(1)}, u32[]{:S(2)}, u32[]{:S(2)}) collective-permute-start(bf16[128,1024]{1,0:T(8,128)(2,1)S(1)} %get-tuple-element.56.refs_10_.refs_7_), channel_id=1, source_target_pairs={{0,1},{1,0},{2,3},{3,2},{4,5},{5,4},{6,7},{7,6},{8,9},{9,8},{10,11... | collective-permute-start | bytes 786440 | tf_op jit(solution)/shard_map/ppermute | solution.py:292
  31.4 20.8 %collective-permute-start.11 = (bf16[128,1024]{1,0:T(8,128)(2,1)S(1)}, bf16[128,1024]{1,0:T(8,128)(2,1)S(1)}, u32[]{:S(2)}, u32[]{:S(2)}) collective-permute-start(bf16[128,1024]{1,0:T(8,128)(2,1)S(1)} %collective-permute-done.10.refs_12_.refs_9_), channel_id=1, source_target_pairs={{0,1},{1,0},{2,3},{3,2},{4,5},{5,4},{6,7},{7,6},{8,9},{9,8},{10,11... | collective-permute-start | bytes 786440 | tf_op jit(solution)/shard_map/ppermute | solution.py:292
  32.2 12.3 %copy-start = (s32[3]{0:T(128)S(1)}, s32[3]{0:T(128)}, u32[]{:S(2)}) copy-start(s32[3]{0:T(128)} %refs_0_.9) | copy-start | bytes 40
  32.2 20.0 %collective-permute-start.16 = (bf16[64,1024]{1,0:T(8,128)(2,1)S(1)}, bf16[64,1024]{1,0:T(8,128)(2,1)S(1)}, u32[]{:S(2)}, u32[]{:S(2)}) collective-permute-start(bf16[64,1024]{1,0:T(8,128)(2,1)S(1)} %get-tuple-element.67.refs_6_), channel_id=1, source_target_pairs={{0,4},{8,12},{16,20},{24,28},{1,5},{9,13},{17,21},{25,29},{2,6},{1... | collective-permute-start | bytes 393224 | tf_op jit(solution)/shard_map/ppermute | solution.py:410
  46.5 9.3 %collective-permute-start.21 = (bf16[4,64,256]{2,1,0:T(8,128)(2,1)S(1)}, bf16[4,64,256]{2,1,0:T(8,128)(2,1)S(1)}, u32[]{:S(2)}, u32[]{:S(2)}) collective-permute-start(bf16[4,64,256]{2,1,0:T(8,128)(2,1)S(1)} %get-tuple-element.76), channel_id=1, source_target_pairs={{0,1},{1,0},{2,3},{3,2},{4,5},{5,4},{6,7},{7,6},{8,9},{9,8},{10,11... | collective-permute-start | bytes 393224 | tf_op jit(solution)/shard_map/ppermute | solution.py:292
  50.1 6.6 %collective-permute-start.22 = (bf16[4,64,256]{2,1,0:T(8,128)(2,1)S(1)}, bf16[4,64,256]{2,1,0:T(8,128)(2,1)S(1)}, u32[]{:S(2)}, u32[]{:S(2)}) collective-permute-start(bf16[4,64,256]{2,1,0:T(8,128)(2,1)S(1)} %get-tuple-element.77), channel_id=1, source_target_pairs={{0,2},{1,3},{2,0},{3,1},{4,6},{5,7},{6,4},{7,5},{8,10},{9,11},{10,... | collective-permute-start | bytes 393224 | tf_op jit(solution)/shard_map/ppermute | solution.py:292
  51.5 7.0 %collective-permute-start.23 = (bf16[4,64,256]{2,1,0:T(8,128)(2,1)S(1)}, bf16[4,64,256]{2,1,0:T(8,128)(2,1)S(1)}, u32[]{:S(2)}, u32[]{:S(2)}) collective-permute-start(bf16[4,64,256]{2,1,0:T(8,128)(2,1)S(1)} %get-tuple-element.78), channel_id=1, source_target_pairs={{0,3},{1,2},{2,1},{3,0},{4,7},{5,6},{6,5},{7,4},{8,11},{9,10},{10,... | collective-permute-start | bytes 393224 | tf_op jit(solution)/shard_map/ppermute | solution.py:292
  54.4 6.7 %collective-permute-start.18 = (bf16[4,64,256]{2,1,0:T(8,128)(2,1)S(1)}, bf16[4,64,256]{2,1,0:T(8,128)(2,1)S(1)}, u32[]{:S(2)}, u32[]{:S(2)}) collective-permute-start(bf16[4,64,256]{2,1,0:T(8,128)(2,1)S(1)} %get-tuple-element.73), channel_id=1, source_target_pairs={{0,1},{1,0},{2,3},{3,2},{4,5},{5,4},{6,7},{7,6},{8,9},{9,8},{10,11... | collective-permute-start | bytes 393224 | tf_op jit(solution)/shard_map/ppermute | solution.py:292
  54.7 6.5 %collective-permute-start.19 = (bf16[4,64,256]{2,1,0:T(8,128)(2,1)S(1)}, bf16[4,64,256]{2,1,0:T(8,128)(2,1)S(1)}, u32[]{:S(2)}, u32[]{:S(2)}) collective-permute-start(bf16[4,64,256]{2,1,0:T(8,128)(2,1)S(1)} %get-tuple-element.74), channel_id=1, source_target_pairs={{0,2},{1,3},{2,0},{3,1},{4,6},{5,7},{6,4},{7,5},{8,10},{9,11},{10,... | collective-permute-start | bytes 393224 | tf_op jit(solution)/shard_map/ppermute | solution.py:292
  55.8 8.0 %collective-permute-start.20 = (bf16[4,64,256]{2,1,0:T(8,128)(2,1)S(1)}, bf16[4,64,256]{2,1,0:T(8,128)(2,1)S(1)}, u32[]{:S(2)}, u32[]{:S(2)}) collective-permute-start(bf16[4,64,256]{2,1,0:T(8,128)(2,1)S(1)} %get-tuple-element.75), channel_id=1, source_target_pairs={{0,3},{1,2},{2,1},{3,0},{4,7},{5,6},{6,5},{7,4},{8,11},{9,10},{10,... | collective-permute-start | bytes 393224 | tf_op jit(solution)/shard_map/ppermute | solution.py:292
